TPU v7x, 32 devices: a whole 2x2x4 slice. The times are simulated.
32 devices in a mesh: sta: 4 (over y, x), clu: 8 (over z, core).
Axes of the slice: x: 2, y: 2, z: 4, core: 2. Of those that a mesh axis runs over, the one named last changes fastest.
Arguments:
- spectra: bfloat16 [256, 256, 128], P('clu', 'sta'), may hold values from -6 to 6
- partials: bfloat16 [256, 4, 256], P('clu', None, 'sta')
- pair_list: int32 [256, 50], P('clu'), may hold values from -1 to 103, as said below
- station_mask: int32 [256, 50, 256], P('clu', None, 'sta'), may hold values 0 or 1
- exports: int32 [48, 12], P('clu'), may hold values from 0 to 31
Outputs:
- normal_blocks: float32 [16, 51, 256], P('sta', None, 'clu')
- right_sides: float32 [4, 256], P('sta', 'clu')
Inputs may be any that keep to these rules, and one draw needn't show every extreme that they name: `pair_list`: each event's valid entries come first and the rest are -1; every event has 25 to 50 valid entries and the first event of every cluster has all 50. A valid entry below 32 names an event of the same cluster; entry 32 + h * 12 + c names the c-th event sent to this cluster by the cluster at cycle offset -o(h) from it, o(h) as for exports.
All inputs are finite; a program needn't handle non-finite values. No bound on the sum of `station_mask` on one device may be relied on, other than what follows from the above.
Results may differ from a plain program's by a relative error of at most 0.0047.
Values may be sent and summed in bfloat16 or wider, within the bound.
No kernel may reach another device: no remote copies, remote signals or barrier semaphores. Data moves between devices by JAX's collectives and lax.ppermute only.
A program may use at most 64 MiB of HBM per device.

v0:
```python
import math

import jax
import jax.numpy as jnp
from jax import lax
from jax.sharding import PartitionSpec as P


def shifted(block, axis, distance):
    devices = range(lax.axis_size(axis))
    route = [((i - distance) % len(devices), i) for i in devices]
    return lax.ppermute(block, axis, route)


def lag_tables(freq_count):
    freq_values = jnp.arange(freq_count, dtype=jnp.float32) * (math.pi / freq_count)
    lag_values = jnp.arange(2 * freq_count - 1, dtype=jnp.float32) - (freq_count - 1)
    phase_grid = freq_values[:, None] * lag_values[None, :]
    cosine_grid = jnp.cos(phase_grid)
    sine_grid = jnp.sin(phase_grid)
    real_rows = jnp.concatenate([cosine_grid, -freq_values[:, None] * sine_grid], axis=1)
    imag_rows = jnp.concatenate([-sine_grid, -freq_values[:, None] * cosine_grid], axis=1)
    lag_table = jnp.concatenate([real_rows, imag_rows], axis=0).astype(jnp.bfloat16)
    return (lag_table, lag_values)


def pair_weights(spec_one, spec_two, energy_one, energy_two, lag_table, lag_values, freq_count):
    first_vals = spec_one.astype(jnp.float32)
    second_vals = spec_two.astype(jnp.float32)
    real_a = first_vals[..., :freq_count]
    imag_a = first_vals[..., freq_count:]
    real_b = second_vals[..., :freq_count]
    imag_b = second_vals[..., freq_count:]
    cross_spec = jnp.concatenate(
        [real_a * real_b + imag_a * imag_b, imag_a * real_b - real_a * imag_b], axis=-1
    ).astype(jnp.bfloat16)
    lead_shape = cross_spec.shape[:-1]
    lagged = jnp.dot(
        cross_spec.reshape(-1, 2 * freq_count), lag_table, preferred_element_type=jnp.float32
    )
    lag_count = lag_values.shape[0]
    inverse = lax.rsqrt((energy_one * energy_two).reshape(-1) + 1e-06)
    correlation = lagged[:, :lag_count] * inverse[:, None]
    slope_fn = lagged[:, lag_count:] * inverse[:, None]
    power_sum = jnp.sum(correlation * correlation, axis=1)
    rough_sum = jnp.sum(slope_fn * slope_fn, axis=1)
    delay_lag = jnp.sum(correlation * correlation * lag_values[None, :], axis=1) / (
        power_sum + 1e-06
    )
    weight = power_sum / (power_sum + 0.125 * rough_sum + 1e-06)
    return (weight.reshape(lead_shape), delay_lag.reshape(lead_shape))


def on_device(spectra, partials, pair_list, station_mask, exports):
    highest = lax.Precision.HIGHEST
    event_count, station_count, two_freq = spectra.shape
    freq_count = two_freq // 2
    sta_groups = lax.axis_size("sta")
    groups_out = exports.shape[0]
    half_span = groups_out // 2
    capacity = exports.shape[1]
    neighbours = pair_list.shape[1]
    all_stations = station_count * sta_groups
    offsets = [h - half_span + (1 if h >= half_span else 0) for h in range(groups_out)]
    lag_table, lag_values = lag_tables(freq_count)
    energy = jnp.sum(jnp.square(spectra.astype(jnp.float32)), axis=-1)
    spec_len = station_count * two_freq
    outgoing = jnp.concatenate(
        [
            spectra[exports].reshape(groups_out, capacity, spec_len),
            partials[exports].reshape(groups_out, capacity, 4 * station_count),
        ],
        axis=2,
    )
    received = [None] * groups_out
    for h in range(groups_out):
        received[h] = shifted(outgoing[h], "clu", offsets[h])
    got_rows = jnp.stack(received, axis=0)
    imported = groups_out * capacity
    got_spec = got_rows[..., :spec_len].reshape(imported, station_count, two_freq)
    got_geo = got_rows[..., spec_len:].reshape(imported, 4, station_count)
    got_energy = jnp.sum(jnp.square(got_spec.astype(jnp.float32)), axis=-1)
    cand_spec = jnp.concatenate([spectra, got_spec], axis=0)
    cand_geo = jnp.concatenate([partials, got_geo], axis=0)
    cand_energy = jnp.concatenate([energy, got_energy], axis=0)
    cand_total = event_count + imported
    cand_ids = jnp.arange(cand_total, dtype=jnp.int32)
    live_pairs = (pair_list >= 0).astype(jnp.float32)[..., None] * station_mask.astype(jnp.float32)
    clipped = jnp.maximum(pair_list, 0)
    block_size = max(event_count // 16, 1)
    rounds = event_count // block_size

    def one_round(accumulated, inputs):
        acc_diag, acc_right = accumulated
        spec_a, geo_a, energy_a, partner_b, live_b = inputs
        weight, delay_lag = pair_weights(
            spec_a[:, None],
            cand_spec[partner_b],
            energy_a[:, None],
            cand_energy[partner_b],
            lag_table,
            lag_values,
            freq_count,
        )
        scaled = weight * live_b / all_stations
        geo_one = geo_a.astype(jnp.float32)
        geo_two = cand_geo[partner_b].astype(jnp.float32)
        diag_one = jnp.einsum(
            "rks,ris,rjs->ijr", scaled, geo_one, geo_one, precision=highest
        ).reshape(16, -1)
        off_diag = -jnp.einsum(
            "rks,ris,rkjs->ijkr", scaled, geo_one, geo_two, precision=highest
        ).reshape(16, neighbours, -1)
        right_one = jnp.einsum("rks,ris->ir", scaled * delay_lag, geo_one, precision=highest)
        diag_two = jnp.einsum(
            "rks,rkis,rkjs->rkij", scaled, geo_two, geo_two, precision=highest
        ).reshape(-1, 16)
        right_two = -jnp.einsum(
            "rks,rkis->rki", scaled * delay_lag, geo_two, precision=highest
        ).reshape(-1, 4)
        onehot = (partner_b.reshape(-1)[:, None] == cand_ids[None, :]).astype(jnp.float32)
        acc_diag = acc_diag + jnp.dot(diag_two.T, onehot, precision=highest)
        acc_right = acc_right + jnp.dot(right_two.T, onehot, precision=highest)
        return ((acc_diag, acc_right), (diag_one, off_diag, right_one))

    round_inputs = (
        spectra.reshape(rounds, block_size, station_count, two_freq),
        partials.reshape(rounds, block_size, 4, station_count),
        energy.reshape(rounds, block_size, station_count),
        clipped.reshape(rounds, block_size, neighbours),
        live_pairs.reshape(rounds, block_size, neighbours, station_count),
    )
    start_acc = (jnp.zeros((16, cand_total), jnp.float32), jnp.zeros((4, cand_total), jnp.float32))
    (acc_diag, acc_right), (diag_rows, off_rows, right_rows) = lax.scan(
        one_round, start_acc, round_inputs
    )
    diagonal = diag_rows.transpose(1, 0, 2).reshape(16, event_count) + acc_diag[:, :event_count]
    off_blocks = off_rows.transpose(1, 2, 0, 3).reshape(16, neighbours, event_count)
    right_hand = right_rows.transpose(1, 0, 2).reshape(4, event_count) + acc_right[:, :event_count]
    import_diag = acc_diag[:, event_count:].reshape(16, groups_out, capacity)
    import_right = acc_right[:, event_count:].reshape(4, groups_out, capacity)
    owner_hot = (
        exports.reshape(-1)[:, None] == jnp.arange(event_count, dtype=jnp.int32)[None, :]
    ).astype(jnp.float32)

    def spread(values):
        return jnp.dot(values.reshape(values.shape[0], -1), owner_hot, precision=highest)

    import_terms = jnp.concatenate([import_diag, import_right], axis=0)
    back_list = [shifted(import_terms[:, h], "clu", -offsets[h]) for h in range(groups_out)]
    back_terms = jnp.stack(back_list, axis=1)
    diagonal = diagonal + spread(back_terms[:16])
    right_hand = right_hand + spread(back_terms[16:])
    normal_part = jnp.concatenate([diagonal[:, None, :], off_blocks], axis=1)
    total_normal, total_right = lax.psum((normal_part, right_hand), "sta")
    sta_place = lax.axis_index("sta")
    normal_share = lax.dynamic_slice_in_dim(
        total_normal, sta_place * (16 // sta_groups), 16 // sta_groups, 0
    )
    right_share = lax.dynamic_slice_in_dim(
        total_right, sta_place * (4 // sta_groups), 4 // sta_groups, 0
    )
    return (normal_share, right_share)


def solution(mesh):
    return jax.shard_map(
        on_device,
        mesh=mesh,
        in_specs=(
            P("clu", "sta", None),
            P("clu", None, "sta"),
            P("clu", None),
            P("clu", None, "sta"),
            P("clu", None),
        ),
        out_specs=(P("sta", None, "clu"), P("sta", "clu")),
        check_vma=False,
    )
```

profile of v0, /device:TPU:0, one launch (start us, length us, event | category | flops | bytes accessed | tf_op | source)
XLA Modules:
  0.0 468.8 jit_solution(14140332511440352107)
XLA Ops:
  8.0 1.8 gather_fusion.3
  13.2 3.5 collective-permute-start
  16.6 1.6 collective-permute-start.1
  25.8 2.9 collective-permute-done.1
  28.7 5.8 %collective-permute-done.2 = bf16[12,8448]{1,0:T(8,128)(2,1)S(1)} collective-permute-done((bf16[12,8448]{1,0:T(8,128)(2,1)}, bf16[12,8448]{1,0:T(8,128)(2,1)S(1)}, u32[]{:S(2)}, u32[]{:S(2)}) %collective-permute-start.2) | collective-permute-done | bytes 202784 | tf_op jit(solution)/shard_map/ppermute | solution.py:12
  34.5 2.6 collective-permute-done.3
  37.1 6.0 %collective-permute-done.4 = bf16[12,8448]{1,0:T(8,128)(2,1)S(1)} collective-permute-done((bf16[12,8448]{1,0:T(8,128)(2,1)S(1)}, bf16[12,8448]{1,0:T(8,128)(2,1)S(1)}, u32[]{:S(2)}, u32[]{:S(2)}) %collective-permute-start.4) | collective-permute-done | bytes 202784 | tf_op jit(solution)/shard_map/ppermute | solution.py:12
  43.1 10.3 %collective-permute-done.5 = bf16[12,8448]{1,0:T(8,128)(2,1)S(1)} collective-permute-done((bf16[12,8448]{1,0:T(8,128)(2,1)S(1)}, bf16[12,8448]{1,0:T(8,128)(2,1)S(1)}, u32[]{:S(2)}, u32[]{:S(2)}) %collective-permute-start.5) | collective-permute-done | bytes 202784 | tf_op jit(solution)/shard_map/ppermute | solution.py:12
  58.6 332.7 %while.19 = (s32[]{:T(128)}, f32[16,104]{1,0:T(8,128)}, f32[4,104]{1,0:T(4,128)}, f32[16,16,2]{1,2,0:T(2,128)}, f32[16,16,50,2]{2,1,3,0:T(8,128)}, /*index=5*/f3...) while((s32[]{:T(128)}, f32[16,104]{1,0:T(8,128)}, ...), condition=%wide.region_8.9_spmd.clone, body=%wide.region_2.8_spmd.clone.sunk | while | flops 435276384 | bytes 30170480 | solution.py:134
  62.7 3.9 fusion.76
  67.8 4.2 multiply_reduce_fusion.6
  83.5 3.9 fusion.76
  88.6 4.2 multiply_reduce_fusion.6
  104.2 3.9 fusion.76
  109.3 4.2 multiply_reduce_fusion.6
  125.0 3.9 fusion.76
  130.1 4.2 multiply_reduce_fusion.6
  145.8 3.9 fusion.76
  151.0 4.2 multiply_reduce_fusion.6
  166.6 3.9 fusion.76
  171.7 4.2 multiply_reduce_fusion.6
  187.4 3.9 fusion.76
  192.5 4.2 multiply_reduce_fusion.6
  208.2 3.9 fusion.76
  213.3 4.2 multiply_reduce_fusion.6
  229.0 3.9 fusion.76
  234.2 4.2 multiply_reduce_fusion.6
  249.8 3.9 fusion.76
  255.0 4.2 multiply_reduce_fusion.6
  270.6 3.9 fusion.76
  275.7 4.2 multiply_reduce_fusion.6
  291.4 3.9 fusion.76
  296.5 4.2 multiply_reduce_fusion.6
  312.1 3.9 fusion.76
  317.3 4.2 multiply_reduce_fusion.6
  332.9 3.9 fusion.76
  338.0 4.2 multiply_reduce_fusion.6
  353.7 3.9 fusion.76
  358.8 4.2 multiply_reduce_fusion.6
  374.5 3.9 fusion.76
  379.7 4.2 multiply_reduce_fusion.6
  393.8 2.0 collective-permute-start.7
  395.9 1.4 collective-permute-start.8
  397.4 2.1 collective-permute-start.9
  403.2 2.3 collective-permute-done.11
  406.7 10.0 %psum.15 = f32[4,32]{1,0:T(4,128)S(1)} all-reduce(f32[4,32]{1,0:T(4,128)S(1)} %convolution_add_fusion.3), channel_id=1, replica_groups=mesh['sta'=4,'clu'=8] {'sta'}, use_global_device_ids=true, to_apply=%region_10.11 | all-reduce | flops 128 | bytes 1024 | tf_op jit(solution)/shard_map/psum | solution.py:155
  419.2 41.3 %all-reduce.2.cloned.1.call-done = f32[16,51,32]{1,2,0:T(8,128)} async-done(((f32[16,51,32]{1,2,0:T(8,128)}), f32[16,51,32]{1,2,0:T(8,128)}) %all-reduce.2.cloned.1.call-update) | async-done | bytes 104464 | tf_op jit(solution)/shard_map/psum | solution.py:155
  460.5 1.5 constant_dynamic-slice_fusion.4
  (1198 shorter events, 227.6 us)
Async XLA Ops:
  7.2 453.3 %all-reduce.2.cloned.1.call-start = ((), (), s32[]{:S(2)}) async-start(), calls=%async_computation | async-start | bytes 524288 | tf_op jit(solution)/shard_map/psum | solution.py:155
  12.2 9.4 %copy-start.8 = (s32[6,12]{1,0:T(8,128)S(1)}, s32[6,12]{1,0:T(8,128)}, u32[]{:S(2)}) copy-start(s32[6,12]{1,0:T(8,128)} %param.11) | copy-start | bytes 868
  12.2 10.0 %copy-start.4 = (s32[32,50]{1,0:T(8,128)S(1)}, s32[32,50]{1,0:T(8,128)}, u32[]{:S(2)}) copy-start(s32[32,50]{1,0:T(8,128)} %param.9) | copy-start | bytes 19204
  12.2 10.1 %copy-start.2 = (s32[32,50,64]{2,0,1:T(8,128)S(1)}, s32[32,50,64]{2,0,1:T(8,128)}, u32[]{:S(2)}) copy-start(s32[32,50,64]{2,0,1:T(8,128)} %param.10) | copy-start | bytes 1228804
  13.2 11.3 %collective-permute-start = (bf16[12,8448]{1,0:T(8,128)(2,1)}, bf16[12,8448]{1,0:T(8,128)(2,1)S(1)}, u32[]{:S(2)}, u32[]{:S(2)}) collective-permute-start(bf16[12,8448]{1,0:T(8,128)(2,1)} %get-tuple-element.287), channel_id=1, source_target_pairs={{3,0},{4,1},{5,2},{6,3},{7,4},{0,5},{1,6},{2,7},{11,8},{12,9},{13,... | collective-permute-start | bytes 608264 | tf_op jit(solution)/shard_map/ppermute | solution.py:12
  16.6 12.0 %collective-permute-start.1 = (bf16[12,8448]{1,0:T(8,128)(2,1)}, bf16[12,8448]{1,0:T(8,128)(2,1)S(1)}, u32[]{:S(2)}, u32[]{:S(2)}) collective-permute-start(bf16[12,8448]{1,0:T(8,128)(2,1)} %get-tuple-element.286), channel_id=1, source_target_pairs={{2,0},{3,1},{4,2},{5,3},{6,4},{7,5},{0,6},{1,7},{10,8},{11,9},{12,... | collective-permute-start | bytes 608264 | tf_op jit(solution)/shard_map/ppermute | solution.py:12
  18.2 16.2 %collective-permute-start.2 = (bf16[12,8448]{1,0:T(8,128)(2,1)}, bf16[12,8448]{1,0:T(8,128)(2,1)S(1)}, u32[]{:S(2)}, u32[]{:S(2)}) collective-permute-start(bf16[12,8448]{1,0:T(8,128)(2,1)} %get-tuple-element.285), channel_id=1, source_target_pairs={{1,0},{2,1},{3,2},{4,3},{5,4},{6,5},{7,6},{0,7},{9,8},{10,9},{11,1... | collective-permute-start | bytes 608264 | tf_op jit(solution)/shard_map/ppermute | solution.py:12
  18.5 18.5 %collective-permute-start.3 = (bf16[12,8448]{1,0:T(8,128)(2,1)S(1)}, bf16[12,8448]{1,0:T(8,128)(2,1)S(1)}, u32[]{:S(2)}, u32[]{:S(2)}) collective-permute-start(bf16[12,8448]{1,0:T(8,128)(2,1)S(1)} %get-tuple-element.284), channel_id=1, source_target_pairs={{7,0},{0,1},{1,2},{2,3},{3,4},{4,5},{5,6},{6,7},{15,8},{8,9},{9,10... | collective-permute-start | bytes 608264 | tf_op jit(solution)/shard_map/ppermute | solution.py:12
  18.7 24.4 %collective-permute-start.4 = (bf16[12,8448]{1,0:T(8,128)(2,1)S(1)}, bf16[12,8448]{1,0:T(8,128)(2,1)S(1)}, u32[]{:S(2)}, u32[]{:S(2)}) collective-permute-start(bf16[12,8448]{1,0:T(8,128)(2,1)S(1)} %get-tuple-element.283), channel_id=1, source_target_pairs={{6,0},{7,1},{0,2},{1,3},{2,4},{3,5},{4,6},{5,7},{14,8},{15,9},{8,1... | collective-permute-start | bytes 608264 | tf_op jit(solution)/shard_map/ppermute | solution.py:12
  24.4 29.0 %collective-permute-start.5 = (bf16[12,8448]{1,0:T(8,128)(2,1)S(1)}, bf16[12,8448]{1,0:T(8,128)(2,1)S(1)}, u32[]{:S(2)}, u32[]{:S(2)}) collective-permute-start(bf16[12,8448]{1,0:T(8,128)(2,1)S(1)} %get-tuple-element.282), channel_id=1, source_target_pairs={{5,0},{6,1},{7,2},{0,3},{1,4},{2,5},{3,6},{4,7},{13,8},{14,9},{15,... | collective-permute-start | bytes 608264 | tf_op jit(solution)/shard_map/ppermute | solution.py:12
  72.5 4.9 %copy-start.11 = (f32[4,104]{1,0:T(4,128)S(1)}, f32[4,104]{1,0:T(4,128)}, u32[]{:S(2)}) copy-start(f32[4,104]{1,0:T(4,128)} %get-tuple-element.435) | copy-start | bytes 4996 | tf_op jit(solution)/shard_map/while
  73.4 6.1 %copy-start.6 = (s32[16,2,50]{2,1,0:T(2,128)S(1)}, s32[16,2,50]{2,1,0:T(2,128)}, u32[]{:S(2)}) copy-start(s32[16,2,50]{2,1,0:T(2,128)} %copy-done.5) | copy-start | bytes 19204 | tf_op jit(solution)/shard_map/while
  93.3 4.9 %copy-start.11 = (f32[4,104]{1,0:T(4,128)S(1)}, f32[4,104]{1,0:T(4,128)}, u32[]{:S(2)}) copy-start(f32[4,104]{1,0:T(4,128)} %get-tuple-element.435) | copy-start | bytes 4996 | tf_op jit(solution)/shard_map/while
  94.2 6.0 %copy-start.6 = (s32[16,2,50]{2,1,0:T(2,128)S(1)}, s32[16,2,50]{2,1,0:T(2,128)}, u32[]{:S(2)}) copy-start(s32[16,2,50]{2,1,0:T(2,128)} %copy-done.5) | copy-start | bytes 19204 | tf_op jit(solution)/shard_map/while
  114.0 4.9 %copy-start.11 = (f32[4,104]{1,0:T(4,128)S(1)}, f32[4,104]{1,0:T(4,128)}, u32[]{:S(2)}) copy-start(f32[4,104]{1,0:T(4,128)} %get-tuple-element.435) | copy-start | bytes 4996 | tf_op jit(solution)/shard_map/while
  114.9 6.1 %copy-start.6 = (s32[16,2,50]{2,1,0:T(2,128)S(1)}, s32[16,2,50]{2,1,0:T(2,128)}, u32[]{:S(2)}) copy-start(s32[16,2,50]{2,1,0:T(2,128)} %copy-done.5) | copy-start | bytes 19204 | tf_op jit(solution)/shard_map/while
  134.8 4.9 %copy-start.11 = (f32[4,104]{1,0:T(4,128)S(1)}, f32[4,104]{1,0:T(4,128)}, u32[]{:S(2)}) copy-start(f32[4,104]{1,0:T(4,128)} %get-tuple-element.435) | copy-start | bytes 4996 | tf_op jit(solution)/shard_map/while
  135.7 6.1 %copy-start.6 = (s32[16,2,50]{2,1,0:T(2,128)S(1)}, s32[16,2,50]{2,1,0:T(2,128)}, u32[]{:S(2)}) copy-start(s32[16,2,50]{2,1,0:T(2,128)} %copy-done.5) | copy-start | bytes 19204 | tf_op jit(solution)/shard_map/while
  155.6 4.9 %copy-start.11 = (f32[4,104]{1,0:T(4,128)S(1)}, f32[4,104]{1,0:T(4,128)}, u32[]{:S(2)}) copy-start(f32[4,104]{1,0:T(4,128)} %get-tuple-element.435) | copy-start | bytes 4996 | tf_op jit(solution)/shard_map/while
  156.6 6.0 %copy-start.6 = (s32[16,2,50]{2,1,0:T(2,128)S(1)}, s32[16,2,50]{2,1,0:T(2,128)}, u32[]{:S(2)}) copy-start(s32[16,2,50]{2,1,0:T(2,128)} %copy-done.5) | copy-start | bytes 19204 | tf_op jit(solution)/shard_map/while
  176.4 4.9 %copy-start.11 = (f32[4,104]{1,0:T(4,128)S(1)}, f32[4,104]{1,0:T(4,128)}, u32[]{:S(2)}) copy-start(f32[4,104]{1,0:T(4,128)} %get-tuple-element.435) | copy-start | bytes 4996 | tf_op jit(solution)/shard_map/while
  177.3 6.1 %copy-start.6 = (s32[16,2,50]{2,1,0:T(2,128)S(1)}, s32[16,2,50]{2,1,0:T(2,128)}, u32[]{:S(2)}) copy-start(s32[16,2,50]{2,1,0:T(2,128)} %copy-done.5) | copy-start | bytes 19204 | tf_op jit(solution)/shard_map/while
  197.2 4.9 %copy-start.11 = (f32[4,104]{1,0:T(4,128)S(1)}, f32[4,104]{1,0:T(4,128)}, u32[]{:S(2)}) copy-start(f32[4,104]{1,0:T(4,128)} %get-tuple-element.435) | copy-start | bytes 4996 | tf_op jit(solution)/shard_map/while
  198.1 6.1 %copy-start.6 = (s32[16,2,50]{2,1,0:T(2,128)S(1)}, s32[16,2,50]{2,1,0:T(2,128)}, u32[]{:S(2)}) copy-start(s32[16,2,50]{2,1,0:T(2,128)} %copy-done.5) | copy-start | bytes 19204 | tf_op jit(solution)/shard_map/while
  218.0 4.9 %copy-start.11 = (f32[4,104]{1,0:T(4,128)S(1)}, f32[4,104]{1,0:T(4,128)}, u32[]{:S(2)}) copy-start(f32[4,104]{1,0:T(4,128)} %get-tuple-element.435) | copy-start | bytes 4996 | tf_op jit(solution)/shard_map/while
  218.9 6.1 %copy-start.6 = (s32[16,2,50]{2,1,0:T(2,128)S(1)}, s32[16,2,50]{2,1,0:T(2,128)}, u32[]{:S(2)}) copy-start(s32[16,2,50]{2,1,0:T(2,128)} %copy-done.5) | copy-start | bytes 19204 | tf_op jit(solution)/shard_map/while
  238.8 4.9 %copy-start.11 = (f32[4,104]{1,0:T(4,128)S(1)}, f32[4,104]{1,0:T(4,128)}, u32[]{:S(2)}) copy-start(f32[4,104]{1,0:T(4,128)} %get-tuple-element.435) | copy-start | bytes 4996 | tf_op jit(solution)/shard_map/while
  239.7 6.1 %copy-start.6 = (s32[16,2,50]{2,1,0:T(2,128)S(1)}, s32[16,2,50]{2,1,0:T(2,128)}, u32[]{:S(2)}) copy-start(s32[16,2,50]{2,1,0:T(2,128)} %copy-done.5) | copy-start | bytes 19204 | tf_op jit(solution)/shard_map/while
  259.7 4.9 %copy-start.11 = (f32[4,104]{1,0:T(4,128)S(1)}, f32[4,104]{1,0:T(4,128)}, u32[]{:S(2)}) copy-start(f32[4,104]{1,0:T(4,128)} %get-tuple-element.435) | copy-start | bytes 4996 | tf_op jit(solution)/shard_map/while
  260.6 6.0 %copy-start.6 = (s32[16,2,50]{2,1,0:T(2,128)S(1)}, s32[16,2,50]{2,1,0:T(2,128)}, u32[]{:S(2)}) copy-start(s32[16,2,50]{2,1,0:T(2,128)} %copy-done.5) | copy-start | bytes 19204 | tf_op jit(solution)/shard_map/while
  280.4 4.9 %copy-start.11 = (f32[4,104]{1,0:T(4,128)S(1)}, f32[4,104]{1,0:T(4,128)}, u32[]{:S(2)}) copy-start(f32[4,104]{1,0:T(4,128)} %get-tuple-element.435) | copy-start | bytes 4996 | tf_op jit(solution)/shard_map/while
  281.3 6.1 %copy-start.6 = (s32[16,2,50]{2,1,0:T(2,128)S(1)}, s32[16,2,50]{2,1,0:T(2,128)}, u32[]{:S(2)}) copy-start(s32[16,2,50]{2,1,0:T(2,128)} %copy-done.5) | copy-start | bytes 19204 | tf_op jit(solution)/shard_map/while
  301.2 4.9 %copy-start.11 = (f32[4,104]{1,0:T(4,128)S(1)}, f32[4,104]{1,0:T(4,128)}, u32[]{:S(2)}) copy-start(f32[4,104]{1,0:T(4,128)} %get-tuple-element.435) | copy-start | bytes 4996 | tf_op jit(solution)/shard_map/while
  302.1 6.0 %copy-start.6 = (s32[16,2,50]{2,1,0:T(2,128)S(1)}, s32[16,2,50]{2,1,0:T(2,128)}, u32[]{:S(2)}) copy-start(s32[16,2,50]{2,1,0:T(2,128)} %copy-done.5) | copy-start | bytes 19204 | tf_op jit(solution)/shard_map/while
  322.0 4.9 %copy-start.11 = (f32[4,104]{1,0:T(4,128)S(1)}, f32[4,104]{1,0:T(4,128)}, u32[]{:S(2)}) copy-start(f32[4,104]{1,0:T(4,128)} %get-tuple-element.435) | copy-start | bytes 4996 | tf_op jit(solution)/shard_map/while
  322.9 6.0 %copy-start.6 = (s32[16,2,50]{2,1,0:T(2,128)S(1)}, s32[16,2,50]{2,1,0:T(2,128)}, u32[]{:S(2)}) copy-start(s32[16,2,50]{2,1,0:T(2,128)} %copy-done.5) | copy-start | bytes 19204 | tf_op jit(solution)/shard_map/while
  342.7 4.9 %copy-start.11 = (f32[4,104]{1,0:T(4,128)S(1)}, f32[4,104]{1,0:T(4,128)}, u32[]{:S(2)}) copy-start(f32[4,104]{1,0:T(4,128)} %get-tuple-element.435) | copy-start | bytes 4996 | tf_op jit(solution)/shard_map/while
  343.6 6.1 %copy-start.6 = (s32[16,2,50]{2,1,0:T(2,128)S(1)}, s32[16,2,50]{2,1,0:T(2,128)}, u32[]{:S(2)}) copy-start(s32[16,2,50]{2,1,0:T(2,128)} %copy-done.5) | copy-start | bytes 19204 | tf_op jit(solution)/shard_map/while
  363.5 4.9 %copy-start.11 = (f32[4,104]{1,0:T(4,128)S(1)}, f32[4,104]{1,0:T(4,128)}, u32[]{:S(2)}) copy-start(f32[4,104]{1,0:T(4,128)} %get-tuple-element.435) | copy-start | bytes 4996 | tf_op jit(solution)/shard_map/while
  364.4 6.1 %copy-start.6 = (s32[16,2,50]{2,1,0:T(2,128)S(1)}, s32[16,2,50]{2,1,0:T(2,128)}, u32[]{:S(2)}) copy-start(s32[16,2,50]{2,1,0:T(2,128)} %copy-done.5) | copy-start | bytes 19204 | tf_op jit(solution)/shard_map/while
  384.3 4.9 %copy-start.11 = (f32[4,104]{1,0:T(4,128)S(1)}, f32[4,104]{1,0:T(4,128)}, u32[]{:S(2)}) copy-start(f32[4,104]{1,0:T(4,128)} %get-tuple-element.435) | copy-start | bytes 4996 | tf_op jit(solution)/shard_map/while
  385.3 6.1 %copy-start.6 = (s32[16,2,50]{2,1,0:T(2,128)S(1)}, s32[16,2,50]{2,1,0:T(2,128)}, u32[]{:S(2)}) copy-start(s32[16,2,50]{2,1,0:T(2,128)} %copy-done.5) | copy-start | bytes 19204 | tf_op jit(solution)/shard_map/while
  393.2 9.2 %collective-permute-start.6 = (f32[20,12]{0,1:T(8,128)S(1)}, f32[20,12]{0,1:T(8,128)S(1)}, u32[]{:S(2)}, u32[]{:S(2)}) collective-permute-start(f32[20,12]{0,1:T(8,128)S(1)} %bitcast.202), channel_id=1, source_target_pairs={{5,0},{6,1},{7,2},{0,3},{1,4},{2,5},{3,6},{4,7},{13,8},{14,9},{15,... | collective-permute-start | bytes 2888 | tf_op jit(solution)/shard_map/ppermute | solution.py:12
  393.8 8.7 %collective-permute-start.7 = (f32[20,12]{0,1:T(8,128)S(1)}, f32[20,12]{0,1:T(8,128)S(1)}, u32[]{:S(2)}, u32[]{:S(2)}) collective-permute-start(f32[20,12]{0,1:T(8,128)S(1)} %bitcast.201), channel_id=1, source_target_pairs={{6,0},{7,1},{0,2},{1,3},{2,4},{3,5},{4,6},{5,7},{14,8},{15,9},{8,1... | collective-permute-start | bytes 2888 | tf_op jit(solution)/shard_map/ppermute | solution.py:12
  395.9 6.6 %collective-permute-start.8 = (f32[20,12]{0,1:T(8,128)S(1)}, f32[20,12]{0,1:T(8,128)S(1)}, u32[]{:S(2)}, u32[]{:S(2)}) collective-permute-start(f32[20,12]{0,1:T(8,128)S(1)} %bitcast.200), channel_id=1, source_target_pairs={{7,0},{0,1},{1,2},{2,3},{3,4},{4,5},{5,6},{6,7},{15,8},{8,9},{9,10... | collective-permute-start | bytes 2888 | tf_op jit(solution)/shard_map/ppermute | solution.py:12
  397.4 5.2 %collective-permute-start.9 = (f32[20,12]{0,1:T(8,128)S(1)}, f32[20,12]{0,1:T(8,128)S(1)}, u32[]{:S(2)}, u32[]{:S(2)}) collective-permute-start(f32[20,12]{0,1:T(8,128)S(1)} %bitcast.199), channel_id=1, source_target_pairs={{1,0},{2,1},{3,2},{4,3},{5,4},{6,5},{7,6},{0,7},{9,8},{10,9},{11,1... | collective-permute-start | bytes 2888 | tf_op jit(solution)/shard_map/ppermute | solution.py:12
  399.6 3.7 collective-permute-start.10
  402.4 3.1 collective-permute-start.11
  (98 other events, 250.6 us)
Sparse Core Ops, SparseCore 0:
  418.8 41.6 all-reduce.1
where the time goes:
time: 471 us; the launch traced here: 469 us
  other arithmetic  133 us (28%)
  local copies, waits for them, and re-layouts  133 us (28%)
  matrix products  89.2 us (19%)
  waiting for transfers between devices  71.9 us (15%)
  starting transfers between devices  14.5 us (3%)
  between operations  14.3 us (3%)
  blocking collectives  9.99 us (2%)
    reduce_sum x16, other arithmetic, pair_weights(): jnp.sum(correlation * correlation * lag_values[None, :], axis=1)  67.3 us
    dot_general x16, matrix products, pair_weights(): jnp.dot(cross_spec.reshape(-1, 2 * freq_count), lag_table, preferred_elem...  61.8 us
    psum x1, waiting for transfers between devices, on_device(): total_normal, total_right = lax.psum((normal_part, right_hand), 'sta')  41.3 us
    ppermute x12, waiting for transfers between devices, shifted(): return lax.ppermute(block, axis, route)  30.6 us
    dynamic_update_slice x48, local copies, waits for them, and re-layouts, on_device(): lax.scan(one_round, start_acc, round_inputs)  28.6 us
    another operation x17, other arithmetic  19.5 us
    dynamic_slice x32, local copies, waits for them, and re-layouts, on_device(): lax.scan(one_round, start_acc, round_inputs)  14.6 us
    ppermute x12, starting transfers between devices, shifted(): return lax.ppermute(block, axis, route)  14.4 us
  transfers between devices with their start and end apart: 13, of which 8 were waited for; matrix products, arithmetic and copies ran while one was open for 2% of the time, Pallas kernels for 0%

commit v1 on v0

v1 whole, which is shorter than its diff:
```python
import functools
import math

import jax
import jax.numpy as jnp
import numpy as np
from jax import lax
from jax.experimental import pallas as pl
from jax.experimental.pallas import tpu as pltpu
from jax.sharding import PartitionSpec as P

F32 = jnp.float32
BF16 = jnp.bfloat16
VMEM_LIMIT = 56 * 1024 * 1024
SLOT_ROWS = 64
GROUP_ROWS = 16


def shifted(block, axis, distance):
    devices = range(lax.axis_size(axis))
    route = [((i - distance) % len(devices), i) for i in devices]
    return lax.ppermute(block, axis, route)


def moment_table(freq_count):
    f = np.arange(freq_count)

    def edge(k):
        out = np.zeros(k.shape)
        live = (k % (2 * freq_count)) != 0
        sign = 1.0 - 2.0 * (k[live] % 2)
        out[live] = -freq_count * sign / np.tan(np.pi * k[live] / (2 * freq_count))
        return out

    table = np.zeros((freq_count + 16, 2 * freq_count), np.float32)
    table[:freq_count, :freq_count] = -(edge(f[:, None] + f[None, :]) + edge(f[None, :] - f[:, None]))
    w = f * math.pi / freq_count
    table[freq_count, :freq_count] = (1.0 - 2.0 * (f % 2)) * w
    high = jnp.asarray(w * w, F32).astype(BF16)
    low = (jnp.asarray(w * w, F32) - high.astype(F32)).astype(BF16)
    table = jnp.asarray(table, F32).astype(BF16)
    table = table.at[freq_count + 1, freq_count:].set(high)
    return table.at[freq_count + 2, freq_count:].set(low)


def low_half(shape):
    return lax.broadcasted_iota(jnp.int32, shape, len(shape) - 1) < shape[-1] // 2


def outgoing_kernel(cap, exports_ref, spec_ref, geo_ref, *refs):
    outs, rows = refs[:-1], refs[-1]
    stations = spec_ref.shape[1]
    half = cap // 2
    body = cap * stations
    for h, out in enumerate(outs):
        rows[...] = jnp.zeros_like(rows)
        for c in range(cap):
            event = exports_ref[h, c]
            out[c * stations : (c + 1) * stations, :] = spec_ref[event]
            place = (c % 2) * half + c // 2
            rows[place : place + 1, :] = geo_ref[0, pl.ds(event, 1), :]
            rows[GROUP_ROWS + place : GROUP_ROWS + place + 1, :] = geo_ref[1, pl.ds(event, 1), :]
        out[body : body + 2 * GROUP_ROWS, :] = rows[...].astype(BF16)


def fold(x):
    rows = x.shape[0] // 8
    total = x[0:8]
    for r in range(1, rows):
        total = total + x[8 * r : 8 * r + 8]
    return total


def prepare(natural, bp, bb, eb, pairs, freq):
    for j in range(pairs):
        turned = natural(j).astype(F32).T
        bp[j] = turned
        re, im = turned[:freq], turned[freq:]
        square = re * re + im * im
        bb[j] = square
        eb[j : j + 1, :] = jnp.sum(square, axis=0, keepdims=True)


def dense_pairs(da, ea, bp, bb, eb, table, rm, rs, rt, rz, out, pairs, columns, freq, events, scale, batch):
    lead = lax.broadcasted_iota(jnp.int32, (8, 1), 0) == 0

    def one_event(e, js):
        a = da[e].astype(F32)
        ar, ai = a[:freq], a[freq:]
        square = ar * ar + ai * ai
        xs, reals, totals, alternates = [], [], [], []
        for j in js:
            br, bi = bp[j, :freq, :], bp[j, freq:, :]
            cr = ar * br + ai * bi
            ci = ai * br - ar * bi
            both = square * bb[j]
            xs.append(jnp.concatenate([ci.astype(BF16), both.astype(BF16)], axis=0))
            reals.append(cr.astype(BF16))
            edge = cr[0:8] * cr[0:8] - ci[0:8] * ci[0:8]
            totals.append(fold(both) + jnp.where(lead, edge, 0.0))
            alternates.append(fold(cr))
        z = jnp.dot(table[...], jnp.concatenate(xs, axis=1), preferred_element_type=F32)
        for i, j in enumerate(js):
            part = z[:, i * 128 : (i + 1) * 128]
            row = pl.ds(pl.multiple_of((j * events + e) * 8, 8), 8)
            rm[row, :] = fold(reals[i].astype(F32) * part[:freq])
            rs[row, :] = totals[i]
            rt[row, :] = alternates[i]
            rz[row, :] = part[freq : freq + 8]

    @pl.loop(0, events)
    def _(e):
        for start in range(0, pairs, batch):
            one_event(e, list(range(start, min(start + batch, pairs))))

    low = low_half((8, 128))

    @pl.loop(0, pairs)
    def _(j):
        energy_b = eb[pl.ds(j, 1), :]
        for e0 in range(0, events, 8):
            base = (j * events + e0) * 8

            def pick(ref, k):
                return ref[pl.ds(base + k, 8, stride=8), :]

            moment, total, alternate = pick(rm, 0), pick(rs, 0), pick(rt, 0)
            for k in range(1, 8):
                moment = moment + pick(rm, k)
                total = total + pick(rs, k)
                alternate = alternate + (1 - 2 * (k % 2)) * pick(rt, k)
            tilt = pick(rz, 0)
            bend = pick(rz, 1) + pick(rz, 2)
            inverse = 1.0 / (ea[e0 : e0 + 8, :] * energy_b + 1e-06)
            power = (freq * total - alternate * alternate) * inverse
            rough = (freq * bend - tilt * tilt) * inverse
            weight = power / (power + 0.125 * rough + 1e-06) * scale
            moved = weight * (moment * inverse / (power + 1e-06))
            even = jnp.where(low, weight, pltpu.roll(moved, 64, 1))
            odd = jnp.where(low, pltpu.roll(weight, 64, 1), moved)
            out[pl.ds(e0 * columns + j, 8, stride=columns), :] = even
            out[pl.ds(e0 * columns + pairs + j, 8, stride=columns), :] = odd


def local_kernel(freq, events, scale, spec_ref, table, out, da, ea, bp, bb, eb, rm, rs, rt, rz):
    pairs = events // 2
    prepare(lambda j: spec_ref[j], bp, bb, eb, pairs, freq)
    low = low_half((128, 128))
    for j in range(pairs):
        both = bp[j]
        other = pltpu.roll(both, 64, 1)
        da[2 * j] = jnp.where(low, both, other).astype(BF16)
        da[2 * j + 1] = jnp.where(low, other, both).astype(BF16)
    energy = eb[...]
    other = pltpu.roll(energy, 64, 1)
    low = low_half(energy.shape)
    ea[pl.ds(0, pairs, stride=2), :] = jnp.where(low, energy, other)
    ea[pl.ds(1, pairs, stride=2), :] = jnp.where(low, other, energy)
    dense_pairs(da, ea, bp, bb, eb, table, rm, rs, rt, rz, out, pairs, events, freq, events, scale, 4)


def import_kernel(freq, events, cap, scale, got_ref, da, ea, table, out, tail, bp, bb, eb, rm, rs, rt, rz):
    pairs = cap // 2
    prepare(lambda j: got_ref[j * 128 : (j + 1) * 128, :], bp, bb, eb, pairs, freq)
    out[...] = jnp.zeros_like(out)
    tail[...] = got_ref[cap // 2 * 128 :, :]
    dense_pairs(da, ea, bp, bb, eb, table, rm, rs, rt, rz, out, pairs, GROUP_ROWS, freq, events, scale, pairs)


def weight_scratch(pairs, events, freq):
    rows = pairs * events * 8
    return [
        pltpu.VMEM((pairs, 2 * freq, 128), F32),
        pltpu.VMEM((pairs, freq, 128), F32),
        pltpu.VMEM((-(-pairs // 8) * 8, 128), F32),
    ] + [pltpu.VMEM((rows, 128), F32)] * 4


def candidate_geo(own0, own1, tails):
    first = jnp.concatenate([own0] + [t[:GROUP_ROWS, :] for t in tails], axis=0)
    second = jnp.concatenate([own1] + [t[GROUP_ROWS:, :] for t in tails], axis=0)
    return first, second


def sums_kernel(groups, events, hot, hot_turned, mask, own_geo, *refs):
    tables, tails = refs[: groups + 1], refs[groups + 1 : 2 * groups + 1]
    slots_out, terms_out, geo_out, own = refs[2 * groups + 1 :]
    cands = hot.shape[1]

    @pl.loop(0, events)
    def _(e):
        parts = [tables[0][pl.ds(pl.multiple_of(e * events, 8), events), :]]
        for t in tables[1:]:
            parts.append(t[pl.ds(pl.multiple_of(e * GROUP_ROWS, 8), GROUP_ROWS), :])
        every = jnp.concatenate(parts, axis=0).astype(BF16)
        rows = pl.ds(pl.multiple_of(e * SLOT_ROWS, SLOT_ROWS), SLOT_ROWS)
        slots = jnp.dot(hot[rows, :], every, preferred_element_type=F32) * mask[rows, :].astype(F32)
        slots_out[rows, :] = slots.astype(BF16)
        place = (e % 2) * (events // 2) + e // 2
        own[pl.ds(place, 1), :] = jnp.sum(slots, axis=0, keepdims=True)

    gathered = jnp.dot(hot_turned[...], slots_out[...], preferred_element_type=F32)
    low = low_half((cands, 128))
    gathered = jnp.where(low, gathered, -gathered)
    totals = jnp.concatenate([gathered[:events] + own[...], gathered[events:]], axis=0)
    turned = pltpu.roll(totals, 64, 1)
    weights = jnp.where(low, totals, turned)
    moves = jnp.where(low, turned, totals)
    first, second = candidate_geo(own_geo[0], own_geo[1], [t[...] for t in tails])
    geo_out[:, :128] = first
    geo_out[:, 128:] = second
    blocks = [first.astype(F32), second.astype(F32)]
    singles = []
    for block in blocks:
        other = pltpu.roll(block, 64, 1)
        singles += [jnp.where(low, block, other), jnp.where(low, other, block)]
    half_row = lax.broadcasted_iota(jnp.int32, (8, 128), 0)
    half_lane = lax.broadcasted_iota(jnp.int32, (8, 128), 1) // 64
    picker = jnp.where(half_row == half_lane, 1.0, 0.0).astype(F32)

    def halves(values):
        return lax.dot_general(
            picker, values, (((1,), (1,)), ((), ())), precision=lax.Precision.HIGHEST, preferred_element_type=F32
        )[:2]

    rows = []
    for i in range(4):
        left = weights * singles[i]
        rows += [halves(left * blocks[0]), halves(left * blocks[1])]
    rows += [halves(moves * blocks[0]), halves(moves * blocks[1])]
    rows.append(jnp.zeros((4, 128), F32))
    terms_out[...] = jnp.concatenate(rows, axis=0)


def blocks_kernel(events, hot, slots, geo, left, out, turned):
    turned[...] = jnp.zeros_like(turned)
    low = low_half((SLOT_ROWS, 128))

    @pl.loop(0, events)
    def _(e):
        rows = pl.ds(pl.multiple_of(e * SLOT_ROWS, SLOT_ROWS), SLOT_ROWS)
        partner = jnp.dot(hot[rows, :], geo[...], preferred_element_type=F32)
        pair = slots[rows, :].astype(F32)
        weights = jnp.where(low, pair, pltpu.roll(pair, 64, 1))
        weighted = jnp.concatenate([weights * partner[:, :128], weights * partner[:, 128:]], axis=1).astype(BF16)
        entry = lax.dot_general(left[e], weighted, (((1,), (1,)), ((), ())), preferred_element_type=F32)
        turned[pl.ds(e, 16, stride=events), 0:SLOT_ROWS] = entry

    for i in range(4):
        out[i] = turned[i * 4 * events : (i + 1) * 4 * events, :].T[:SLOT_ROWS]


def message_kernel(groups, events, slots, place, blocks, owners, *refs):
    terms, outs, rows = refs[: groups + 1], refs[groups + 1 : -1], refs[-1]
    stacked = jnp.concatenate([t[...] for t in terms], axis=1)
    spread = jnp.dot(stacked, owners[...], precision=lax.Precision.HIGHEST, preferred_element_type=F32)
    block = lax.broadcasted_iota(jnp.int32, (1, 128), 1) // events
    for i in range(4):
        diagonal = jnp.zeros((1, 128), F32)
        for j in range(4):
            diagonal = jnp.where(block == j, spread[4 * i + j : 4 * i + j + 1], diagonal)
        rows[i, 0:1, :] = diagonal
        rows[i, 1:2, :] = spread[16 + i : 17 + i]
    for d, out in enumerate(outs):
        share = lax.rem(place[0] + d, 4)
        out[...] = blocks[share, 0 : out.shape[0], :]
        out[0:1, :] = rows[share, 0:1, :]
        out[slots + 1 : slots + 2, :] = rows[share, 1:2, :]


def total_kernel(events, slots, *refs):
    parts, normal, right = refs[:4], refs[4], refs[5]
    total = (parts[0][...] + parts[1][...]) + (parts[2][...] + parts[3][...])
    for j in range(4):
        moved = total if j == 0 else pltpu.roll(total, 128 - j * events, 1)
        normal[j] = moved[: slots + 1, :events]
    right[...] = total[slots + 1 : slots + 2, :events]


def vmem(n):
    return [pl.BlockSpec(memory_space=pltpu.VMEM)] * n


def call(kernel, outs, inputs, scratch=(), specs=None, micros=1.0):
    shapes = [jax.ShapeDtypeStruct(s, t) for s, t in outs]
    return pl.pallas_call(
        kernel,
        out_shape=shapes,
        in_specs=specs if specs is not None else vmem(len(inputs)),
        out_specs=vmem(len(outs)),
        scratch_shapes=list(scratch),
        compiler_params=pltpu.CompilerParams(vmem_limit_bytes=VMEM_LIMIT),
        cost_estimate=pl.CostEstimate(flops=int(micros * 1e9), bytes_accessed=1024, transcendentals=0),
    )(*inputs)


def on_device(spectra, partials, pair_list, station_mask, exports):
    events, stations, two_freq = spectra.shape
    freq = two_freq // 2
    groups, cap = exports.shape
    half_span = groups // 2
    slots = pair_list.shape[1]
    sta_groups = lax.axis_size("sta")
    scale = 1.0 / (stations * sta_groups)
    offsets = [h - half_span + (1 if h >= half_span else 0) for h in range(groups)]
    cands = events + groups * GROUP_ROWS
    half = cap // 2
    table = moment_table(freq)
    smem = pl.BlockSpec(memory_space=pltpu.SMEM)

    geo_rows = partials.reshape(events, 2, 2 * stations).transpose(1, 0, 2)
    out_rows = cap * stations + 2 * GROUP_ROWS
    outgoing = call(
        functools.partial(outgoing_kernel, cap),
        [((out_rows, 128), BF16)] * groups,
        (exports, spectra, geo_rows.astype(F32)),
        scratch=[pltpu.VMEM((2 * GROUP_ROWS, 128), F32)],
        specs=[smem] + vmem(2),
        micros=2.0,
    )
    order = sorted(range(groups), key=lambda h: -abs(offsets[h]))
    got = [None] * groups
    for h in order:
        got[h] = shifted(outgoing[h], "clu", offsets[h])

    local, dup, energy = call(
        functools.partial(local_kernel, freq, events, scale),
        [((events * events, 128), F32), ((events, 128, 128), BF16), ((events, 128), F32)],
        (spectra.reshape(events // 2, 2 * stations, two_freq), table),
        scratch=weight_scratch(events // 2, events, freq),
        micros=8.0,
    )

    m = pair_list
    near = (m % 2) * (events // 2) + m // 2
    far = jnp.maximum(m - events, 0)
    entry = far % cap
    far = events + GROUP_ROWS * (far // cap) + (entry % 2) * half + entry // 2
    column = jnp.where(m < 0, -1, jnp.where(m < events, near, far))
    column = jnp.pad(column, ((0, 0), (1, SLOT_ROWS - 1 - slots)), constant_values=-1).reshape(-1)
    cand_ids = jnp.arange(cands, dtype=jnp.int32)
    hot = (column[:, None] == cand_ids[None, :]).astype(BF16)
    hot_turned = (cand_ids[:, None] == column[None, :]).astype(BF16)
    mask = jnp.pad(station_mask, ((0, 0), (1, SLOT_ROWS - 1 - slots), (0, 0))).astype(BF16)
    mask = jnp.concatenate([mask, mask], axis=2).reshape(events * SLOT_ROWS, 128)
    own_geo = geo_rows.reshape(2, events // 2, 2, 128).transpose(0, 2, 1, 3).reshape(2, events, 128)
    eye = jnp.eye(4, dtype=BF16)
    left = -(partials[:, :, None, None, :] * eye[None, None, :, :, None]).reshape(events, 16, 4 * stations)
    cand_rank = np.arange(GROUP_ROWS)
    cand_entry = np.where(cand_rank < cap, 2 * (cand_rank % half) + cand_rank // half, 0)
    owner = jnp.where(jnp.asarray(cand_rank < cap)[None, :], exports[:, cand_entry], -1)
    local_rank = np.arange(cands)
    local_owner = np.where(local_rank < events, 2 * (local_rank % (events // 2)) + local_rank // (events // 2), -1)
    owner_rows = [jnp.asarray(local_owner, jnp.int32)]
    for h in range(groups):
        start = events + GROUP_ROWS * h
        owner_rows.append(jnp.pad(owner[h], (start, cands - start - GROUP_ROWS), constant_values=-1))
    owners = jnp.concatenate(owner_rows)[:, None] == (jnp.arange(128, dtype=jnp.int32) % events)[None, :]
    owners = owners.astype(F32)

    tables, tails = [None] * groups, [None] * groups
    for h in order[::-1]:
        tables[h], tails[h] = call(
            functools.partial(import_kernel, freq, events, cap, scale),
            [((events * GROUP_ROWS, 128), F32), ((2 * GROUP_ROWS, 128), BF16)],
            (got[h], dup, energy, table),
            scratch=weight_scratch(half, events, freq),
            micros=3.0,
        )

    weights, terms, geo = call(
        functools.partial(sums_kernel, groups, events),
        [((events * SLOT_ROWS, 128), BF16), ((24, 128), F32), ((cands, 256), BF16)],
        (hot, hot_turned, mask, own_geo, local, *tables, *tails),
        scratch=[pltpu.VMEM((events, 128), F32)],
        micros=2.0,
    )
    back = [shifted(terms, "clu", -offsets[h]) for h in range(groups)]
    (blocks,) = call(
        functools.partial(blocks_kernel, events),
        [((4, SLOT_ROWS, 128), F32)],
        (hot, weights, geo, left),
        scratch=[pltpu.VMEM((16 * events, 128), F32)],
        micros=3.0,
    )
    message_rows = -(-(slots + 2) // 8) * 8
    place = lax.axis_index("sta").astype(jnp.int32).reshape(1)
    messages = call(
        functools.partial(message_kernel, groups, events, slots),
        [((message_rows, 128), F32)] * 4,
        (place, blocks, owners, terms, *back),
        scratch=[pltpu.VMEM((4, 8, 128), F32)],
        specs=[smem] + vmem(3 + groups),
    )
    shares = [messages[0]] + [shifted(messages[d], "sta", d) for d in range(1, 4)]
    normal, right = call(
        functools.partial(total_kernel, events, slots),
        [((4, slots + 1, events), F32), ((1, events), F32)],
        shares,
    )
    return (normal, right)


def solution(mesh):
    return jax.shard_map(
        on_device,
        mesh=mesh,
        in_specs=(
            P("clu", "sta", None),
            P("clu", None, "sta"),
            P("clu", None),
            P("clu", None, "sta"),
            P("clu", None),
        ),
        out_specs=(P("sta", None, "clu"), P("sta", "clu")),
        check_vma=False,
    )
```

time: 471 us -> 138 us (0.29)
  other arithmetic: 133 us -> 4.93 us
  local copies, waits for them, and re-layouts: 133 us -> 11.9 us
  Pallas kernels: 0 us -> 95.6 us
  matrix products: 89.2 us -> 0 us
  waiting for transfers between devices: 71.9 us -> 2.67 us
  between operations: 14.3 us -> 0.82 us
  blocking collectives: 9.99 us -> 0 us
  starting transfers between devices: 14.5 us -> 21.6 us
    pallas_call x0 -> x12, Pallas kernels: none -> 95.6 us  [call(): pl.pallas_call(kernel, out_shape=shapes, in_specs=specs if specs is not N...]
    dot_general x114 -> x0, matrix products: 89.2 us -> none  [the longest x16 61.8 us: pair_weights(): jnp.dot(cross_spec.reshape(-1, 2 * freq_count), lag_table, preferred_elem...]
    reduce_sum x50 -> x0, other arithmetic: 75.2 us -> none  [the longest x16 67.3 us: pair_weights(): jnp.sum(correlation * correlation * lag_values[None, :], axis=1)]
    psum x1 -> x0, waiting for transfers between devices: 41.3 us -> none  [on_device(): total_normal, total_right = lax.psum((normal_part, right_hand), 'sta')]
    gather x82 -> x1, local copies, waits for them, and re-layouts: 40.5 us -> 0.56 us  [on_device(): exports[:, cand_entry]]
    dynamic_update_slice x48 -> x0, local copies, waits for them, and re-layouts: 28.6 us -> none  [on_device(): lax.scan(one_round, start_acc, round_inputs)]
    ppermute x12 -> x15, waiting for transfers between devices: 30.6 us -> 2.67 us  [shifted(): return lax.ppermute(block, axis, route)]
    another operation x17 -> x1, other arithmetic: 19.5 us -> 0.07 us
  transfers between devices with their start and end apart: 13 -> 15, of which waited for: 8 -> 3; matrix products, arithmetic and copies ran while one was open for 2% -> 6% of each run, Pallas kernels for 0% -> 52%
where the time goes in v1:
time: 138 us
  Pallas kernels  95.6 us (69%)
  starting transfers between devices  21.6 us (16%)
  local copies, waits for them, and re-layouts  11.9 us (9%)
  other arithmetic  4.93 us (4%)
  waiting for transfers between devices  2.67 us (2%)
    pallas_call x12, Pallas kernels, call(): pl.pallas_call(kernel, out_shape=shapes, in_specs=specs if specs is not N...  95.6 us
    ppermute x15, starting transfers between devices, shifted(): return lax.ppermute(block, axis, route)  21.6 us
    unnamed x55, local copies, waits for them, and re-layouts  6.13 us
  transfers between devices with their start and end apart: 15, of which 3 were waited for; matrix products, arithmetic and copies ran while one was open for 6% of the time, Pallas kernels for 52%

profile of v1, /device:TPU:0, one launch (start us, length us, event | category | flops | bytes accessed | tf_op | source)
XLA Modules:
  0.0 137.6 jit_solution(13109890998908499351)
XLA Ops:
  0.6 0.8 reshape.109
  1.5 0.6 bitcast_convert_fusion
  2.1 2.2 %shard_map.132 = (bf16[800,128]{1,0:T(8,128)(2,1)}, bf16[800,128]{1,0:T(8,128)(2,1)}, bf16[800,128]{1,0:T(8,128)(2,1)}, bf16[800,128]{1,0:T(8,128)(2,1)}, bf16[8...) custom-call(s32[6,12]{1,0:T(8,128)} %exports_ref.1, bf16[32,64,128]{2,1,0:T(8,128)(2,1)} %spec_ref.1, ...), custom_call_target="tpu_custom_call" | custom-call | flops 2000000000 | bytes 1024 | tf_op jit(solution)/shard_map/pallas_call | solution.py:286
  4.3 3.5 %collective-permute-start = (bf16[800,128]{1,0:T(8,128)(2,1)}, bf16[800,128]{1,0:T(8,128)(2,1)S(1)}, u32[]{:S(2)}, u32[]{:S(2)}) collective-permute-start(bf16[800,128]{1,0:T(8,128)(2,1)} %get-tuple-element.55), channel_id=1, source_target_pairs={{3,0},{4,1},{5,2},{6,3},{7,4},{0,5},{1,6},{2,7},{11,8},{12,9},{13,... | collective-permute-start | bytes 614408 | tf_op jit(solution)/shard_map/ppermute | solution.py:22
  7.8 1.6 %collective-permute-start.1 = (bf16[800,128]{1,0:T(8,128)(2,1)}, bf16[800,128]{1,0:T(8,128)(2,1)S(1)}, u32[]{:S(2)}, u32[]{:S(2)}) collective-permute-start(bf16[800,128]{1,0:T(8,128)(2,1)} %get-tuple-element.59), channel_id=1, source_target_pairs={{2,0},{3,1},{4,2},{5,3},{6,4},{7,5},{0,6},{1,7},{10,8},{11,9},{12,... | collective-permute-start | bytes 614408 | tf_op jit(solution)/shard_map/ppermute | solution.py:22
  9.4 0.3 collective-permute-start.2
  9.9 1.4 %collective-permute-start.4 = (bf16[800,128]{1,0:T(8,128)(2,1)}, bf16[800,128]{1,0:T(8,128)(2,1)S(1)}, u32[]{:S(2)}, u32[]{:S(2)}) collective-permute-start(bf16[800,128]{1,0:T(8,128)(2,1)} %get-tuple-element.65), channel_id=1, source_target_pairs={{6,0},{7,1},{0,2},{1,3},{2,4},{3,5},{4,6},{5,7},{14,8},{15,9},{8,1... | collective-permute-start | bytes 614408 | tf_op jit(solution)/shard_map/ppermute | solution.py:22
  11.5 1.1 fusion.hot
  12.6 0.9 fusion.1.hot_turned
  13.6 0.6 copy.20
  14.4 0.3 pad_maximum_fusion
  14.7 1.0 copy.18
  15.9 0.3 mul.37
  16.4 0.6 copy-done.5
  17.0 0.6 gather_fusion
  17.7 0.3 slice_reduce_fusion
  18.0 14.0 %shard_map.131 = (f32[1024,128]{1,0:T(8,128)}, bf16[32,128,128]{2,1,0:T(8,128)(2,1)}, f32[32,128]{1,0:T(8,128)}) custom-call(bf16[16,128,128]{2,1,0:T(8,128)(2,1)} %bitcast.15, bf16[80,128]{1,0:T(8,128)(2,1)} %constant.183.table), custom_call_target="tpu_custom_call" | custom-call | flops 8000000000 | bytes 1024 | tf_op jit(solution)/shard_map/pallas_call | solution.py:286
  32.5 0.7 multiply_negate_fusion.left
  33.2 0.3 copy-done.6
  33.5 1.3 collective-permute-start.5
  34.8 9.4 %shard_map.133 = (f32[512,128]{1,0:T(8,128)}, bf16[32,128]{1,0:T(8,128)(2,1)}) custom-call(bf16[800,128]{1,0:T(8,128)(2,1)} %copy-done.11, bf16[32,128,128]{2,1,0:T(8,128)(2,1)} %get-tuple-element.56.da, f32[32,128]{1,0:T(8,128)} %get-tuple-element.57.ea, bf16[80,128]{1,0:T(8,128)(2,1)} %constant.183.table), custom_call_target="tpu_custom_call" | custom-call | flops 3000000000 | bytes 1024 | tf_op jit(solution)/shard_map/pallas_call | solution.py:286
  44.1 0.7 copy-done.10
  44.8 9.3 %shard_map.134 = (f32[512,128]{1,0:T(8,128)}, bf16[32,128]{1,0:T(8,128)(2,1)}) custom-call(bf16[800,128]{1,0:T(8,128)(2,1)} %copy-done.10, bf16[32,128,128]{2,1,0:T(8,128)(2,1)} %get-tuple-element.56.da, f32[32,128]{1,0:T(8,128)} %get-tuple-element.57.ea, bf16[80,128]{1,0:T(8,128)(2,1)} %constant.183.table), custom_call_target="tpu_custom_call" | custom-call | flops 3000000000 | bytes 1024 | tf_op jit(solution)/shard_map/pallas_call | solution.py:286
  54.2 0.7 copy-done.9
  54.9 9.4 %shard_map.135 = (f32[512,128]{1,0:T(8,128)}, bf16[32,128]{1,0:T(8,128)(2,1)}) custom-call(bf16[800,128]{1,0:T(8,128)(2,1)} %copy-done.9, bf16[32,128,128]{2,1,0:T(8,128)(2,1)} %get-tuple-element.56.da, f32[32,128]{1,0:T(8,128)} %get-tuple-element.57.ea, bf16[80,128]{1,0:T(8,128)(2,1)} %constant.183.table), custom_call_target="tpu_custom_call" | custom-call | flops 3000000000 | bytes 1024 | tf_op jit(solution)/shard_map/pallas_call | solution.py:286
  64.2 0.7 copy-done.8
  64.9 9.4 %shard_map.136 = (f32[512,128]{1,0:T(8,128)}, bf16[32,128]{1,0:T(8,128)(2,1)}) custom-call(bf16[800,128]{1,0:T(8,128)(2,1)} %copy-done.8, bf16[32,128,128]{2,1,0:T(8,128)(2,1)} %get-tuple-element.56.da, f32[32,128]{1,0:T(8,128)} %get-tuple-element.57.ea, bf16[80,128]{1,0:T(8,128)(2,1)} %constant.183.table), custom_call_target="tpu_custom_call" | custom-call | flops 3000000000 | bytes 1024 | tf_op jit(solution)/shard_map/pallas_call | solution.py:286
  74.3 0.7 copy-done.7
  75.0 9.4 %shard_map.137 = (f32[512,128]{1,0:T(8,128)}, bf16[32,128]{1,0:T(8,128)(2,1)}) custom-call(bf16[800,128]{1,0:T(8,128)(2,1)} %copy-done.7, bf16[32,128,128]{2,1,0:T(8,128)(2,1)} %get-tuple-element.56.da, f32[32,128]{1,0:T(8,128)} %get-tuple-element.57.ea, bf16[80,128]{1,0:T(8,128)(2,1)} %constant.183.table), custom_call_target="tpu_custom_call" | custom-call | flops 3000000000 | bytes 1024 | tf_op jit(solution)/shard_map/pallas_call | solution.py:286
  84.4 0.7 copy-done.12
  85.0 9.3 %shard_map.138 = (f32[512,128]{1,0:T(8,128)}, bf16[32,128]{1,0:T(8,128)(2,1)}) custom-call(bf16[800,128]{1,0:T(8,128)(2,1)} %copy-done.12, bf16[32,128,128]{2,1,0:T(8,128)(2,1)} %get-tuple-element.56.da, f32[32,128]{1,0:T(8,128)} %get-tuple-element.57.ea, bf16[80,128]{1,0:T(8,128)(2,1)} %constant.183.table), custom_call_target="tpu_custom_call" | custom-call | flops 3000000000 | bytes 1024 | tf_op jit(solution)/shard_map/pallas_call | solution.py:286
  94.4 9.0 %shard_map.139 = (bf16[2048,128]{1,0:T(8,128)(2,1)}, f32[24,128]{1,0:T(8,128)}, bf16[128,256]{1,0:T(8,128)(2,1)}) custom-call(bf16[2048,128]{1,0:T(8,128)(2,1)} %fusion.hot, bf16[128,2048]{1,0:T(8,128)(2,1)} %fusion.1.hot_turned, bf16[2048,128]{1,0:T(8,128)(2,1)} %bitcast.12, bf16[2,32,128]{2,1,0:T(8,128)(2,1)} %bitcast.14, ...), custom_call_target="tpu_custom_call" | custom-call | flops 2000000000 | bytes 1024 | tf_op jit(solution)/shard_map/pallas_call | solution.py:286
  103.3 3.5 %collective-permute-start.10 = (f32[24,128]{1,0:T(8,128)}, f32[24,128]{1,0:T(8,128)S(1)}, u32[]{:S(2)}, u32[]{:S(2)}) collective-permute-start(f32[24,128]{1,0:T(8,128)} %get-tuple-element.77.refs_0_), channel_id=1, source_target_pairs={{2,0},{3,1},{4,2},{5,3},{6,4},{7,5},{0,6},{1,7},{10,8},{11,9},{12,... | collective-permute-start | bytes 36872 | tf_op jit(solution)/shard_map/ppermute | solution.py:22
  106.9 1.0 compare_convert_fusion.owners
  107.9 1.7 %collective-permute-start.6 = (f32[24,128]{1,0:T(8,128)S(1)}, f32[24,128]{1,0:T(8,128)S(1)}, u32[]{:S(2)}, u32[]{:S(2)}) collective-permute-start(f32[24,128]{1,0:T(8,128)S(1)} %copy-done.16), channel_id=1, source_target_pairs={{5,0},{6,1},{7,2},{0,3},{1,4},{2,5},{3,6},{4,7},{13,8},{14,9},{15,... | collective-permute-start | bytes 36872 | tf_op jit(solution)/shard_map/ppermute | solution.py:22
  109.8 3.4 %collective-permute-start.9 = (f32[24,128]{1,0:T(8,128)S(1)}, f32[24,128]{1,0:T(8,128)S(1)}, u32[]{:S(2)}, u32[]{:S(2)}) collective-permute-start(f32[24,128]{1,0:T(8,128)S(1)} %copy-done.16), channel_id=1, source_target_pairs={{1,0},{2,1},{3,2},{4,3},{5,4},{6,5},{7,6},{0,7},{9,8},{10,9},{11,1... | collective-permute-start | bytes 36872 | tf_op jit(solution)/shard_map/ppermute | solution.py:22
  113.2 10.7 %shard_map.140.blocks = f32[4,64,128]{2,1,0:T(8,128)} custom-call(bf16[2048,128]{1,0:T(8,128)(2,1)} %fusion.hot, bf16[2048,128]{1,0:T(8,128)(2,1)} %get-tuple-element.75.slots, bf16[128,256]{1,0:T(8,128)(2,1)} %get-tuple-element.76.geo, bf16[32,16,256]{2,1,0:T(8,128)(2,1)} %multiply_negate_fusion.left), custom_call_target="tpu_custom_call" | custom-call | flops 3000000000 | bytes 1024 | tf_op jit(solution)/shard_map/pallas_call | solution.py:286
  124.0 0.5 copy-done.18
  124.6 2.1 %shard_map.141 = (f32[56,128]{1,0:T(8,128)}, f32[56,128]{1,0:T(8,128)}, f32[56,128]{1,0:T(8,128)}, f32[56,128]{1,0:T(8,128)}) custom-call(s32[1]{0:T(128)} %bitcast.place, f32[4,64,128]{2,1,0:T(8,128)} %shard_map.140.blocks, f32[896,128]{1,0:T(8,128)} %compare_convert_fusion.owners, f32[24,128]{1,0:T(8,128)} %get-tuple-element.77.refs_0_, ...), custom_call_target="tpu_custom_call" | custom-call | flops 1000000000 | bytes 1024 | tf_op jit(solution)/shard_map/pallas_call | solution.py:286
  126.7 1.5 %collective-permute-start.12 = (f32[56,128]{1,0:T(8,128)}, f32[56,128]{1,0:T(8,128)S(1)}, u32[]{:S(2)}, u32[]{:S(2)}) collective-permute-start(f32[56,128]{1,0:T(8,128)} %get-tuple-element.79), channel_id=1, source_target_pairs={{24,0},{0,8},{8,16},{16,24},{25,1},{1,9},{9,17},{17,25},{26,2},{2,... | collective-permute-start | bytes 86024 | tf_op jit(solution)/shard_map/ppermute | solution.py:22
  128.2 1.5 %collective-permute-start.13 = (f32[56,128]{1,0:T(8,128)}, f32[56,128]{1,0:T(8,128)S(1)}, u32[]{:S(2)}, u32[]{:S(2)}) collective-permute-start(f32[56,128]{1,0:T(8,128)} %get-tuple-element.80), channel_id=1, source_target_pairs={{16,0},{24,8},{0,16},{8,24},{17,1},{25,9},{1,17},{9,25},{18,2},{26... | collective-permute-start | bytes 86024 | tf_op jit(solution)/shard_map/ppermute | solution.py:22
  129.7 1.4 %collective-permute-start.14 = (f32[56,128]{1,0:T(8,128)}, f32[56,128]{1,0:T(8,128)S(1)}, u32[]{:S(2)}, u32[]{:S(2)}) collective-permute-start(f32[56,128]{1,0:T(8,128)} %get-tuple-element.81), channel_id=1, source_target_pairs={{8,0},{16,8},{24,16},{0,24},{9,1},{17,9},{25,17},{1,25},{10,2},{18... | collective-permute-start | bytes 86024 | tf_op jit(solution)/shard_map/ppermute | solution.py:22
  131.2 0.5 collective-permute-done.12.refs_1_
  131.7 0.6 collective-permute-done.13.refs_2_
  132.3 1.5 %collective-permute-done.14.refs_3_ = f32[56,128]{1,0:T(8,128)S(1)} collective-permute-done((f32[56,128]{1,0:T(8,128)}, f32[56,128]{1,0:T(8,128)S(1)}, u32[]{:S(2)}, u32[]{:S(2)}) %collective-permute-start.14) | collective-permute-done | bytes 28704 | tf_op jit(solution)/shard_map/ppermute | solution.py:22
  133.8 0.6 copy-done.15
  134.4 1.5 %shard_map.142 = (f32[4,51,32]{2,1,0:T(8,128)}, f32[1,32]{1,0:T(1,128)}) custom-call(f32[56,128]{1,0:T(8,128)} %get-tuple-element.78.refs_0_, f32[56,128]{1,0:T(8,128)} %copy-done.13, f32[56,128]{1,0:T(8,128)} %copy-done.14, f32[56,128]{1,0:T(8,128)} %copy-done.15), custom_call_target="tpu_custom_call" | custom-call | flops 1000000000 | bytes 1024 | tf_op jit(solution)/shard_map/pallas_call | solution.py:286
  135.9 1.6 %copy.22 = f32[4,51,32]{1,2,0:T(8,128)} copy(f32[4,51,32]{2,1,0:T(8,128)} %get-tuple-element.84) | data formatting | bytes 52224 | tf_op jit(solution)/shard_map/pallas_call | solution.py:286
  (75 shorter events, 2.0 us)
Async XLA Ops:
  2.1 9.2 %copy-start.2 = (s32[32,50]{1,0:T(8,128)S(1)}, s32[32,50]{1,0:T(8,128)}, u32[]{:S(2)}) copy-start(s32[32,50]{1,0:T(8,128)} %param.18) | copy-start | bytes 19204
  4.3 10.0 %copy-start = (s32[32,50,64]{2,0,1:T(8,128)S(1)}, s32[32,50,64]{2,0,1:T(8,128)}, u32[]{:S(2)}) copy-start(s32[32,50,64]{2,0,1:T(8,128)} %param.19) | copy-start | bytes 1228804
  4.3 28.9 %collective-permute-start = (bf16[800,128]{1,0:T(8,128)(2,1)}, bf16[800,128]{1,0:T(8,128)(2,1)S(1)}, u32[]{:S(2)}, u32[]{:S(2)}) collective-permute-start(bf16[800,128]{1,0:T(8,128)(2,1)} %get-tuple-element.55), channel_id=1, source_target_pairs={{3,0},{4,1},{5,2},{6,3},{7,4},{0,5},{1,6},{2,7},{11,8},{12,9},{13,... | collective-permute-start | bytes 614408 | tf_op jit(solution)/shard_map/ppermute | solution.py:22
  7.8 36.4 %collective-permute-start.1 = (bf16[800,128]{1,0:T(8,128)(2,1)}, bf16[800,128]{1,0:T(8,128)(2,1)S(1)}, u32[]{:S(2)}, u32[]{:S(2)}) collective-permute-start(bf16[800,128]{1,0:T(8,128)(2,1)} %get-tuple-element.59), channel_id=1, source_target_pairs={{2,0},{3,1},{4,2},{5,3},{6,4},{7,5},{0,6},{1,7},{10,8},{11,9},{12,... | collective-permute-start | bytes 614408 | tf_op jit(solution)/shard_map/ppermute | solution.py:22
  9.4 44.8 %collective-permute-start.2 = (bf16[800,128]{1,0:T(8,128)(2,1)}, bf16[800,128]{1,0:T(8,128)(2,1)S(1)}, u32[]{:S(2)}, u32[]{:S(2)}) collective-permute-start(bf16[800,128]{1,0:T(8,128)(2,1)} %get-tuple-element.61), channel_id=1, source_target_pairs={{1,0},{2,1},{3,2},{4,3},{5,4},{6,5},{7,6},{0,7},{9,8},{10,9},{11,1... | collective-permute-start | bytes 614408 | tf_op jit(solution)/shard_map/ppermute | solution.py:22
  9.7 54.6 %collective-permute-start.3 = (bf16[800,128]{1,0:T(8,128)(2,1)}, bf16[800,128]{1,0:T(8,128)(2,1)S(1)}, u32[]{:S(2)}, u32[]{:S(2)}) collective-permute-start(bf16[800,128]{1,0:T(8,128)(2,1)} %get-tuple-element.63), channel_id=1, source_target_pairs={{7,0},{0,1},{1,2},{2,3},{3,4},{4,5},{5,6},{6,7},{15,8},{8,9},{9,10... | collective-permute-start | bytes 614408 | tf_op jit(solution)/shard_map/ppermute | solution.py:22
  9.9 64.4 %collective-permute-start.4 = (bf16[800,128]{1,0:T(8,128)(2,1)}, bf16[800,128]{1,0:T(8,128)(2,1)S(1)}, u32[]{:S(2)}, u32[]{:S(2)}) collective-permute-start(bf16[800,128]{1,0:T(8,128)(2,1)} %get-tuple-element.65), channel_id=1, source_target_pairs={{6,0},{7,1},{0,2},{1,3},{2,4},{3,5},{4,6},{5,7},{14,8},{15,9},{8,1... | collective-permute-start | bytes 614408 | tf_op jit(solution)/shard_map/ppermute | solution.py:22
  12.6 0.9 copy-start.3
  14.7 1.0 copy-start.1
  16.3 0.7 copy-start.5
  17.0 0.7 copy-start.4
  18.0 14.0 %copy-start.23 = (s32[128]{0:T(128)S(1)}, s32[128]{0:T(128)}, u32[]{:S(2)}) copy-start(s32[128]{0:T(128)} %constant.157.clone) | copy-start | bytes 1540
  32.5 1.0 copy-start.6
  33.2 1.6 %copy-start.11 = (bf16[800,128]{1,0:T(8,128)(2,1)}, bf16[800,128]{1,0:T(8,128)(2,1)S(1)}, u32[]{:S(2)}) copy-start(bf16[800,128]{1,0:T(8,128)(2,1)S(1)} %collective-permute-done.got_ref) | copy-start | bytes 614404
  33.5 50.8 %collective-permute-start.5 = (bf16[800,128]{1,0:T(8,128)(2,1)S(1)}, bf16[800,128]{1,0:T(8,128)(2,1)S(1)}, u32[]{:S(2)}, u32[]{:S(2)}) collective-permute-start(bf16[800,128]{1,0:T(8,128)(2,1)S(1)} %copy-done.6), channel_id=1, source_target_pairs={{5,0},{6,1},{7,2},{0,3},{1,4},{2,5},{3,6},{4,7},{13,8},{14,9},{15,... | collective-permute-start | bytes 614408 | tf_op jit(solution)/shard_map/ppermute | solution.py:22
  44.1 0.7 copy-start.10
  54.2 0.7 copy-start.9
  64.2 0.7 copy-start.8
  74.3 0.7 copy-start.7
  84.3 0.7 copy-start.12
  103.3 6.4 %collective-permute-start.10 = (f32[24,128]{1,0:T(8,128)}, f32[24,128]{1,0:T(8,128)S(1)}, u32[]{:S(2)}, u32[]{:S(2)}) collective-permute-start(f32[24,128]{1,0:T(8,128)} %get-tuple-element.77.refs_0_), channel_id=1, source_target_pairs={{2,0},{3,1},{4,2},{5,3},{6,4},{7,5},{0,6},{1,7},{10,8},{11,9},{12,... | collective-permute-start | bytes 36872 | tf_op jit(solution)/shard_map/ppermute | solution.py:22
  106.9 1.0 copy-start.16
  107.9 16.1 %collective-permute-start.11 = (f32[24,128]{1,0:T(8,128)S(1)}, f32[24,128]{1,0:T(8,128)S(1)}, u32[]{:S(2)}, u32[]{:S(2)}) collective-permute-start(f32[24,128]{1,0:T(8,128)S(1)} %copy-done.16), channel_id=1, source_target_pairs={{3,0},{4,1},{5,2},{6,3},{7,4},{0,5},{1,6},{2,7},{11,8},{12,9},{13,... | collective-permute-start | bytes 36872 | tf_op jit(solution)/shard_map/ppermute | solution.py:22
  107.9 16.1 %collective-permute-start.6 = (f32[24,128]{1,0:T(8,128)S(1)}, f32[24,128]{1,0:T(8,128)S(1)}, u32[]{:S(2)}, u32[]{:S(2)}) collective-permute-start(f32[24,128]{1,0:T(8,128)S(1)} %copy-done.16), channel_id=1, source_target_pairs={{5,0},{6,1},{7,2},{0,3},{1,4},{2,5},{3,6},{4,7},{13,8},{14,9},{15,... | collective-permute-start | bytes 36872 | tf_op jit(solution)/shard_map/ppermute | solution.py:22
  109.6 14.4 %collective-permute-start.7 = (f32[24,128]{1,0:T(8,128)S(1)}, f32[24,128]{1,0:T(8,128)S(1)}, u32[]{:S(2)}, u32[]{:S(2)}) collective-permute-start(f32[24,128]{1,0:T(8,128)S(1)} %copy-done.16), channel_id=1, source_target_pairs={{6,0},{7,1},{0,2},{1,3},{2,4},{3,5},{4,6},{5,7},{14,8},{15,9},{8,1... | collective-permute-start | bytes 36872 | tf_op jit(solution)/shard_map/ppermute | solution.py:22
  109.6 14.4 %collective-permute-start.8 = (f32[24,128]{1,0:T(8,128)S(1)}, f32[24,128]{1,0:T(8,128)S(1)}, u32[]{:S(2)}, u32[]{:S(2)}) collective-permute-start(f32[24,128]{1,0:T(8,128)S(1)} %copy-done.16), channel_id=1, source_target_pairs={{7,0},{0,1},{1,2},{2,3},{3,4},{4,5},{5,6},{6,7},{15,8},{8,9},{9,10... | collective-permute-start | bytes 36872 | tf_op jit(solution)/shard_map/ppermute | solution.py:22
  109.8 14.2 %copy-start.17 = (f32[24,128]{1,0:T(8,128)}, f32[24,128]{1,0:T(8,128)S(1)}, u32[]{:S(2)}) copy-start(f32[24,128]{1,0:T(8,128)S(1)} %collective-permute-done.10.refs_5_) | copy-start | bytes 36868
  109.8 14.2 %collective-permute-start.9 = (f32[24,128]{1,0:T(8,128)S(1)}, f32[24,128]{1,0:T(8,128)S(1)}, u32[]{:S(2)}, u32[]{:S(2)}) collective-permute-start(f32[24,128]{1,0:T(8,128)S(1)} %copy-done.16), channel_id=1, source_target_pairs={{1,0},{2,1},{3,2},{4,3},{5,4},{6,5},{7,6},{0,7},{9,8},{10,9},{11,1... | collective-permute-start | bytes 36872 | tf_op jit(solution)/shard_map/ppermute | solution.py:22
  123.9 0.6 copy-start.18
  124.0 0.6 copy-start.19
  124.0 0.6 copy-start.20
  124.0 0.6 copy-start.21
  124.0 0.6 copy-start.22
  126.7 5.0 %collective-permute-start.12 = (f32[56,128]{1,0:T(8,128)}, f32[56,128]{1,0:T(8,128)S(1)}, u32[]{:S(2)}, u32[]{:S(2)}) collective-permute-start(f32[56,128]{1,0:T(8,128)} %get-tuple-element.79), channel_id=1, source_target_pairs={{24,0},{0,8},{8,16},{16,24},{25,1},{1,9},{9,17},{17,25},{26,2},{2,... | collective-permute-start | bytes 86024 | tf_op jit(solution)/shard_map/ppermute | solution.py:22
  128.2 4.1 %collective-permute-start.13 = (f32[56,128]{1,0:T(8,128)}, f32[56,128]{1,0:T(8,128)S(1)}, u32[]{:S(2)}, u32[]{:S(2)}) collective-permute-start(f32[56,128]{1,0:T(8,128)} %get-tuple-element.80), channel_id=1, source_target_pairs={{16,0},{24,8},{0,16},{8,24},{17,1},{25,9},{1,17},{9,25},{18,2},{26... | collective-permute-start | bytes 86024 | tf_op jit(solution)/shard_map/ppermute | solution.py:22
  129.7 4.1 %collective-permute-start.14 = (f32[56,128]{1,0:T(8,128)}, f32[56,128]{1,0:T(8,128)S(1)}, u32[]{:S(2)}, u32[]{:S(2)}) collective-permute-start(f32[56,128]{1,0:T(8,128)} %get-tuple-element.81), channel_id=1, source_target_pairs={{8,0},{16,8},{24,16},{0,24},{9,1},{17,9},{25,17},{1,25},{10,2},{18... | collective-permute-start | bytes 86024 | tf_op jit(solution)/shard_map/ppermute | solution.py:22
  131.7 2.1 %copy-start.13 = (f32[56,128]{1,0:T(8,128)}, f32[56,128]{1,0:T(8,128)S(1)}, u32[]{:S(2)}) copy-start(f32[56,128]{1,0:T(8,128)S(1)} %collective-permute-done.12.refs_1_) | copy-start | bytes 86020
  132.3 1.5 %copy-start.14 = (f32[56,128]{1,0:T(8,128)}, f32[56,128]{1,0:T(8,128)S(1)}, u32[]{:S(2)}) copy-start(f32[56,128]{1,0:T(8,128)S(1)} %collective-permute-done.13.refs_2_) | copy-start | bytes 86020
  133.8 0.6 copy-start.15

commit v2 on v1

v2 whole, which is shorter than its diff:
```python
import functools
import math

import jax
import jax.numpy as jnp
import numpy as np
from jax import lax
from jax.experimental import pallas as pl
from jax.experimental.pallas import tpu as pltpu
from jax.sharding import PartitionSpec as P

F32 = jnp.float32
BF16 = jnp.bfloat16
VMEM_LIMIT = 24 * 1024 * 1024
SLOT_ROWS = 64
GROUP_ROWS = 16
BATCH = 8
WIDE = 4
PAIR_BASE = 64
UNROLL = 4


def shifted(block, axis, distance):
    devices = range(lax.axis_size(axis))
    route = [((i - distance) % len(devices), i) for i in devices]
    return lax.ppermute(block, axis, route)


def moment_table(freq_count):
    f = np.arange(freq_count)

    def edge(k):
        out = np.zeros(k.shape)
        live = (k % (2 * freq_count)) != 0
        sign = 1.0 - 2.0 * (k[live] % 2)
        out[live] = -freq_count * sign / np.tan(np.pi * k[live] / (2 * freq_count))
        return out

    table = np.zeros((freq_count + 16, 2 * freq_count), np.float32)
    table[:freq_count, :freq_count] = -(edge(f[:, None] + f[None, :]) + edge(f[None, :] - f[:, None]))
    w = f * math.pi / freq_count
    table[freq_count, :freq_count] = (1.0 - 2.0 * (f % 2)) * w
    high = jnp.asarray(w * w, F32).astype(BF16)
    low = (jnp.asarray(w * w, F32) - high.astype(F32)).astype(BF16)
    table = jnp.asarray(table, F32).astype(BF16)
    table = table.at[freq_count + 1, freq_count:].set(high)
    return table.at[freq_count + 2, freq_count:].set(low)


def low_half(shape):
    return lax.broadcasted_iota(jnp.int32, shape, len(shape) - 1) < shape[-1] // 2


def outgoing_kernel(cap, exports_ref, spec_ref, geo_ref, *refs):
    outs, rows = refs[:-1], refs[-1]
    stations = spec_ref.shape[1]
    half = cap // 2
    body = cap * stations
    rows[...] = jnp.zeros_like(rows)
    for h, out in enumerate(outs):
        for c in range(cap):
            event = exports_ref[h, c]
            out[c * stations : (c + 1) * stations, :] = spec_ref[event]
            place = (c % 2) * half + c // 2
            geo = geo_ref[event].astype(F32)
            rows[place : place + 1, :] = jnp.concatenate([geo[0:1], geo[1:2]], axis=1)
            place += GROUP_ROWS
            rows[place : place + 1, :] = jnp.concatenate([geo[2:3], geo[3:4]], axis=1)
        out[body : body + 2 * GROUP_ROWS, :] = rows[...].astype(BF16)


def fold(x):
    rows = x.shape[0] // 8
    total = x[0:8]
    for r in range(1, rows):
        total = total + x[8 * r : 8 * r + 8]
    return total


def prepare(natural, bp, bb, eb, pairs, freq):
    for j in range(pairs):
        turned = natural(j).astype(F32).T
        bp[j] = turned
        re, im = turned[:freq], turned[freq:]
        square = re * re + im * im
        bb[j] = square
        eb[j : j + 1, :] = jnp.sum(square, axis=0, keepdims=True)


def listed_pairs(ids, batches, da, sq, ea, bp, bb, eb, table, work, store, freq, scale):
    xs, reals, rm, rs, rt, rz, re = work
    lead = lax.broadcasted_iota(jnp.int32, (8, 1), 0) == 0

    def split(t, u):
        code = ids[t * BATCH + u]
        return code >> 6, code & (PAIR_BASE - 1)

    def rows_of(t, u):
        return pl.ds(pl.multiple_of((t * BATCH + u) * 8, 8), 8)

    def cross_stage(t, slot):
        for u in range(BATCH):
            e, j = split(t, u)
            ar, ai = da[e, :freq, :], da[e, freq:, :]
            br, bi = bp[j, :freq, :], bp[j, freq:, :]
            cr = ar * br + ai * bi
            ci = ai * br - ar * bi
            both = sq[e] * bb[j]
            lanes = slice(u * 128, (u + 1) * 128)
            xs[slot, :freq, lanes] = ci.astype(BF16)
            xs[slot, freq:, lanes] = both.astype(BF16)
            reals[slot, :, lanes] = cr.astype(BF16)
            edge = cr[0:8] * cr[0:8] - ci[0:8] * ci[0:8]
            rs[rows_of(t, u), :] = fold(both) + jnp.where(lead, edge, 0.0)
            rt[rows_of(t, u), :] = fold(cr)
            re[pl.ds(t * BATCH + u, 1), :] = ea[pl.ds(e, 1), :] * eb[pl.ds(j, 1), :]

    def moment_stage(t, slot):
        for start in range(0, BATCH, WIDE):
            lanes = slice(start * 128, (start + WIDE) * 128)
            z = jnp.dot(table[...], xs[slot, :, lanes], preferred_element_type=F32)
            for i in range(WIDE):
                part = z[:, i * 128 : (i + 1) * 128]
                real = reals[slot, :, (start + i) * 128 : (start + i + 1) * 128].astype(F32)
                rm[rows_of(t, start + i), :] = fold(real * part[:freq])
                rz[rows_of(t, start + i), :] = part[freq : freq + 8]

    cross_stage(0, 0)

    @pl.loop(0, (batches + 1) // 2)
    def _(i):
        cross_stage(2 * i + 1, 1)
        moment_stage(2 * i, 0)
        cross_stage(2 * i + 2, 0)
        moment_stage(2 * i + 1, 1)

    low = low_half((8, 128))

    @pl.loop(0, batches)
    def _(t):
        base = t * BATCH * 8

        def pick(ref, k):
            return ref[pl.ds(base + k, 8, stride=8), :]

        moment, total, alternate = pick(rm, 0), pick(rs, 0), pick(rt, 0)
        for k in range(1, 8):
            moment = moment + pick(rm, k)
            total = total + pick(rs, k)
            alternate = alternate + (1 - 2 * (k % 2)) * pick(rt, k)
        tilt = pick(rz, 0)
        bend = pick(rz, 1) + pick(rz, 2)
        inverse = 1.0 / (re[pl.ds(pl.multiple_of(t * BATCH, 8), 8), :] + 1e-06)
        power = (freq * total - alternate * alternate) * inverse
        rough = (freq * bend - tilt * tilt) * inverse
        weight = power / (power + 0.125 * rough + 1e-06) * scale
        moved = weight * (moment * inverse / (power + 1e-06))
        even = jnp.where(low, weight, pltpu.roll(moved, 64, 1))
        odd = jnp.where(low, pltpu.roll(weight, 64, 1), moved)
        for u in range(BATCH):
            e, j = split(t, u)
            store(e, j, even[u : u + 1], odd[u : u + 1])


def local_kernel(freq, events, scale, items, ids, spec_ref, table, out, da, sq, ea, bp, bb, eb, *work):
    pairs = events // 2
    prepare(lambda j: spec_ref[j], bp, bb, eb, pairs, freq)
    low = low_half((128, 128))
    for j in range(pairs):
        both = bp[j]
        other = pltpu.roll(both, 64, 1)
        da[2 * j] = jnp.where(low, both, other)
        da[2 * j + 1] = jnp.where(low, other, both)
        both = bb[j]
        other = pltpu.roll(both, 64, 1)
        sq[2 * j] = jnp.where(low[:freq], both, other)
        sq[2 * j + 1] = jnp.where(low[:freq], other, both)
    energy = eb[...]
    other = pltpu.roll(energy, 64, 1)
    low = low_half(energy.shape)
    ea[pl.ds(0, pairs, stride=2), :] = jnp.where(low, energy, other)
    ea[pl.ds(1, pairs, stride=2), :] = jnp.where(low, other, energy)
    row = low_half((1, 128))

    def store(e, j, even, odd):
        own = (e & 1) * pairs + (e >> 1)
        out[pl.ds(e * events + j, 1), :] = even
        out[pl.ds(e * events + pairs + j, 1), :] = odd
        out[pl.ds(2 * j * events + own, 1), :] = jnp.where(row, even, -even)
        out[pl.ds((2 * j + 1) * events + own, 1), :] = jnp.where(row, odd, -odd)

    listed_pairs(ids, items // BATCH, da, sq, ea, bp, bb, eb, table, work, store, freq, scale)


def import_kernel(group, freq, events, cap, scale, ids, counts, got_ref, da, sq, ea, table, out, tail, bp, bb, eb, *work):
    pairs = cap // 2
    prepare(lambda j: got_ref[j * 128 : (j + 1) * 128, :], bp, bb, eb, pairs, freq)
    out[...] = jnp.zeros_like(out)
    tail[...] = got_ref[cap // 2 * 128 :, :]

    def store(e, j, even, odd):
        out[pl.ds(e * GROUP_ROWS + j, 1), :] = even
        out[pl.ds(e * GROUP_ROWS + pairs + j, 1), :] = odd

    batches = (counts[group] + BATCH - 1) // BATCH
    listed_pairs(ids.at[group], batches, da, sq, ea, bp, bb, eb, table, work, store, freq, scale)


def weight_scratch(pairs, items, freq):
    items = items + 2 * BATCH
    return [
        pltpu.VMEM((pairs, 2 * freq, 128), F32),
        pltpu.VMEM((pairs, freq, 128), F32),
        pltpu.VMEM((-(-pairs // 8) * 8, 128), F32),
        pltpu.VMEM((2, 2 * freq, BATCH * 128), BF16),
        pltpu.VMEM((2, freq, BATCH * 128), BF16),
    ] + [pltpu.VMEM((items * 8, 128), F32)] * 4 + [pltpu.VMEM((items, 128), F32)]


def candidate_geo(own0, own1, tails):
    first = jnp.concatenate([own0] + [t[:GROUP_ROWS, :] for t in tails], axis=0)
    second = jnp.concatenate([own1] + [t[GROUP_ROWS:, :] for t in tails], axis=0)
    return first, second


def sums_kernel(groups, events, hot, hot_turned, mask, own_geo, *refs):
    tables, tails = refs[: groups + 1], refs[groups + 1 : 2 * groups + 1]
    slots_out, terms_out, geo_out, own = refs[2 * groups + 1 :]
    cands = hot.shape[1]

    @pl.loop(0, events // UNROLL)
    def _(step):
        for u in range(UNROLL):
            e = step * UNROLL + u
            parts = [tables[0][pl.ds(pl.multiple_of(e * events, 8), events), :]]
            for t in tables[1:]:
                parts.append(t[pl.ds(pl.multiple_of(e * GROUP_ROWS, 8), GROUP_ROWS), :])
            every = jnp.concatenate(parts, axis=0).astype(BF16)
            rows = pl.ds(pl.multiple_of(e * SLOT_ROWS, SLOT_ROWS), SLOT_ROWS)
            slots = jnp.dot(hot[rows, :], every, preferred_element_type=F32) * mask[rows, :].astype(F32)
            slots_out[rows, :] = slots.astype(BF16)
            place = (u % 2) * (events // 2) + (e >> 1)
            own[pl.ds(place, 1), :] = jnp.sum(slots, axis=0, keepdims=True)

    gathered = jnp.dot(hot_turned[...], slots_out[...], preferred_element_type=F32)
    low = low_half((cands, 128))
    gathered = jnp.where(low, gathered, -gathered)
    totals = jnp.concatenate([gathered[:events] + own[...], gathered[events:]], axis=0)
    turned = pltpu.roll(totals, 64, 1)
    weights = jnp.where(low, totals, turned)
    moves = jnp.where(low, turned, totals)
    first, second = candidate_geo(own_geo[0], own_geo[1], [t[...] for t in tails])
    geo_out[:, :128] = first
    geo_out[:, 128:] = second
    blocks = [first.astype(F32), second.astype(F32)]
    singles = []
    for block in blocks:
        other = pltpu.roll(block, 64, 1)
        singles += [jnp.where(low, block, other), jnp.where(low, other, block)]
    half_row = lax.broadcasted_iota(jnp.int32, (8, 128), 0)
    half_lane = lax.broadcasted_iota(jnp.int32, (8, 128), 1) // 64
    picker = jnp.where(half_row == half_lane, 1.0, 0.0).astype(F32)

    def halves(values):
        return lax.dot_general(
            picker, values, (((1,), (1,)), ((), ())), precision=lax.Precision.HIGHEST, preferred_element_type=F32
        )[:2]

    rights = [halves(moves * blocks[0]), halves(moves * blocks[1])]
    for i in range(4):
        scaled = weights * singles[i]
        rows = [halves(scaled * blocks[0]), halves(scaled * blocks[1]), rights[i // 2][i % 2 : i % 2 + 1]]
        share = jnp.concatenate(rows + [jnp.zeros((3, 128), F32)], axis=0)
        for q in range(terms_out.shape[1]):
            terms_out[i, q] = share


def blocks_kernel(events, hot, slots, geo, left, out, turned):
    turned[...] = jnp.zeros_like(turned)
    low = low_half((SLOT_ROWS, 128))

    @pl.loop(0, events // UNROLL)
    def _(step):
        for u in range(UNROLL):
            e = step * UNROLL + u
            rows = pl.ds(pl.multiple_of(e * SLOT_ROWS, SLOT_ROWS), SLOT_ROWS)
            partner = jnp.dot(hot[rows, :], geo[...], preferred_element_type=F32)
            pair = slots[rows, :].astype(F32)
            weights = jnp.where(low, pair, pltpu.roll(pair, 64, 1))
            weighted = jnp.concatenate([weights * partner[:, :128], weights * partner[:, 128:]], axis=1).astype(BF16)
            entry = lax.dot_general(left[e], weighted, (((1,), (1,)), ((), ())), preferred_element_type=F32)
            turned[pl.ds(e, 16, stride=events), 0:SLOT_ROWS] = entry

    for i in range(4):
        out[i] = turned[i * 4 * events : (i + 1) * 4 * events, :].T[: out.shape[1]]


def total_kernel(groups, events, slots, clusters, blocks, received, owners, normal, right):
    parts = []
    for g in range(groups + 1):
        part = received[clusters[g]]
        for t in range(1, 4):
            part = part + received[t * (received.shape[0] // 4) + clusters[g]]
        parts.append(part)
    spread = jnp.dot(
        jnp.concatenate(parts, axis=1), owners[...], precision=lax.Precision.HIGHEST, preferred_element_type=F32
    )
    block = lax.broadcasted_iota(jnp.int32, (1, 128), 1) // events
    diagonal = jnp.zeros((1, 128), F32)
    for j in range(4):
        diagonal = jnp.where(block == j, spread[j : j + 1], diagonal)
    right[...] = spread[4:5, :events]
    total = (blocks[0] + blocks[1]) + (blocks[2] + blocks[3])
    top = lax.broadcasted_iota(jnp.int32, total.shape, 0) == 0
    total = jnp.where(top, diagonal, total)
    turned = total.T
    for j in range(4):
        normal[j] = turned[j * events : (j + 1) * events, : slots + 1]


def vmem(n):
    return [pl.BlockSpec(memory_space=pltpu.VMEM)] * n


def call(kernel, outs, inputs, scratch=(), specs=None, micros=1.0):
    shapes = [jax.ShapeDtypeStruct(s, t) for s, t in outs]
    return pl.pallas_call(
        kernel,
        out_shape=shapes,
        in_specs=specs if specs is not None else vmem(len(inputs)),
        out_specs=vmem(len(outs)),
        scratch_shapes=list(scratch),
        compiler_params=pltpu.CompilerParams(vmem_limit_bytes=VMEM_LIMIT),
        cost_estimate=pl.CostEstimate(flops=int(micros * 1e9), bytes_accessed=1024, transcendentals=0),
    )(*inputs)


def on_device(spectra, partials, pair_list, station_mask, exports):
    events, stations, two_freq = spectra.shape
    freq = two_freq // 2
    groups, cap = exports.shape
    half_span = groups // 2
    slots = pair_list.shape[1]
    sta_groups = lax.axis_size("sta")
    scale = 1.0 / (stations * sta_groups)
    offsets = [h - half_span + (1 if h >= half_span else 0) for h in range(groups)]
    cands = events + groups * GROUP_ROWS
    half = cap // 2
    table = moment_table(freq)
    smem = pl.BlockSpec(memory_space=pltpu.SMEM)
    clusters = lax.axis_size("clu")

    out_rows = cap * stations + 2 * GROUP_ROWS
    outgoing = call(
        functools.partial(outgoing_kernel, cap),
        [((out_rows, 128), BF16)] * groups,
        (exports, spectra, partials),
        scratch=[pltpu.VMEM((2 * GROUP_ROWS, 128), F32)],
        specs=[smem] + vmem(2),
        micros=2.0,
    )
    order = sorted(range(groups), key=lambda h: -abs(offsets[h]))
    got = [None] * groups
    for h in order:
        got[h] = shifted(outgoing[h], "clu", offsets[h])

    codes = [e * PAIR_BASE + j for e in range(events) for j in range(e // 2, events // 2)]
    items = -(-len(codes) // (2 * BATCH)) * 2 * BATCH
    codes = codes + [0] * (items + 2 * BATCH - len(codes))
    local, dup, square, energy = call(
        functools.partial(local_kernel, freq, events, scale, items),
        [
            ((events * events, 128), F32),
            ((events, 128, 128), F32),
            ((events, freq, 128), F32),
            ((events, 128), F32),
        ],
        (jnp.asarray(codes, jnp.int32), spectra.reshape(events // 2, 2 * stations, two_freq), table),
        scratch=weight_scratch(events // 2, items, freq),
        specs=[smem] + vmem(2),
        micros=8.0,
    )

    far = jnp.maximum(pair_list - events, 0)
    named = jnp.where(pair_list < events, -1, (far // cap) * half + (far % cap) // 2)
    wanted = jnp.any(named[:, :, None] == jnp.arange(groups * half, dtype=jnp.int32)[None, None, :], axis=1)
    wanted = wanted.reshape(events, groups, half).transpose(1, 0, 2).reshape(groups, events * half)
    item = np.arange(events * half)
    before = jnp.asarray(item[:, None] < item[None, :], BF16)
    rank = jnp.dot(wanted.astype(BF16), before, preferred_element_type=F32).astype(jnp.int32)
    item_code = jnp.asarray((item // half) * PAIR_BASE + item % half, jnp.int32)
    spot = jnp.where(wanted, rank, -1)
    longest = events * half + 3 * BATCH
    lists = jnp.sum(
        jnp.where(spot[:, None, :] == jnp.arange(longest, dtype=jnp.int32)[None, :, None], item_code[None, None, :], 0),
        axis=2,
    ).astype(jnp.int32)
    counts = jnp.sum(wanted.astype(jnp.int32), axis=1)

    m = pair_list
    near = (m % 2) * (events // 2) + m // 2
    entry = far % cap
    far = events + GROUP_ROWS * (far // cap) + (entry % 2) * half + entry // 2
    column = jnp.where(m < 0, -1, jnp.where(m < events, near, far))
    column = jnp.pad(column, ((0, 0), (1, SLOT_ROWS - 1 - slots)), constant_values=-1).reshape(-1)
    cand_ids = jnp.arange(cands, dtype=jnp.int32)
    hot = (column[:, None] == cand_ids[None, :]).astype(BF16)
    hot_turned = (cand_ids[:, None] == column[None, :]).astype(BF16)
    mask = jnp.pad(station_mask, ((0, 0), (1, SLOT_ROWS - 1 - slots), (0, 0))).astype(BF16)
    mask = jnp.concatenate([mask, mask], axis=2).reshape(events * SLOT_ROWS, 128)
    own_geo = partials.reshape(events // 2, 2, 2, 128).transpose(2, 1, 0, 3).reshape(2, events, 128)
    eye = jnp.eye(4, dtype=BF16)
    left = -(partials[:, :, None, None, :] * eye[None, None, :, :, None]).reshape(events, 16, 4 * stations)
    cand_rank = np.arange(GROUP_ROWS)
    cand_entry = np.where(cand_rank < cap, 2 * (cand_rank % half) + cand_rank // half, 0)
    owner = jnp.where(jnp.asarray(cand_rank < cap)[None, :], exports[:, cand_entry], -1)
    local_rank = np.arange(cands)
    local_owner = np.where(local_rank < events, 2 * (local_rank % (events // 2)) + local_rank // (events // 2), -1)
    owner_rows = [jnp.asarray(local_owner, jnp.int32)]
    for h in range(groups):
        start = events + GROUP_ROWS * h
        owner_rows.append(jnp.pad(owner[h], (start, cands - start - GROUP_ROWS), constant_values=-1))
    owners = jnp.concatenate(owner_rows)[:, None] == (jnp.arange(128, dtype=jnp.int32) % events)[None, :]
    owners = owners.astype(F32)

    tables, tails = [None] * groups, [None] * groups
    for h in order[::-1]:
        tables[h], tails[h] = call(
            functools.partial(import_kernel, h, freq, events, cap, scale),
            [((events * GROUP_ROWS, 128), F32), ((2 * GROUP_ROWS, 128), BF16)],
            (lists, counts, got[h], dup, square, energy, table),
            scratch=weight_scratch(half, events * half, freq),
            specs=[smem] * 2 + vmem(5),
            micros=3.0,
        )

    weights, terms, geo = call(
        functools.partial(sums_kernel, groups, events),
        [((events * SLOT_ROWS, 128), BF16), ((4, clusters, 8, 128), F32), ((cands, 256), BF16)],
        (hot, hot_turned, mask, own_geo, local, *tables, *tails),
        scratch=[pltpu.VMEM((events, 128), F32)],
        micros=2.0,
    )
    terms = lax.all_to_all(
        terms.reshape(4 * clusters, 8, 128), ("sta", "clu"), split_axis=0, concat_axis=0, tiled=True
    )
    message_rows = -(-(slots + 1) // 8) * 8
    (blocks,) = call(
        functools.partial(blocks_kernel, events),
        [((4, message_rows, 128), F32)],
        (hot, weights, geo, left),
        scratch=[pltpu.VMEM((16 * events, 128), F32)],
        micros=3.0,
    )
    blocks = lax.all_to_all(blocks, "sta", split_axis=0, concat_axis=0, tiled=True)
    sources = (lax.axis_index("clu") + jnp.asarray([0] + offsets, jnp.int32)) % clusters
    normal, right = call(
        functools.partial(total_kernel, groups, events, slots),
        [((4, events, slots + 1), F32), ((1, events), F32)],
        (sources.astype(jnp.int32), blocks, terms, owners),
        specs=[smem] + vmem(3),
    )
    return (normal.transpose(0, 2, 1), right)


def solution(mesh):
    return jax.shard_map(
        on_device,
        mesh=mesh,
        in_specs=(
            P("clu", "sta", None),
            P("clu", None, "sta"),
            P("clu", None),
            P("clu", None, "sta"),
            P("clu", None),
        ),
        out_specs=(P("sta", None, "clu"), P("sta", "clu")),
        check_vma=False,
    )
```

time: 138 us -> 91.4 us (0.66)
  Pallas kernels: 95.6 us -> 49.2 us
  waiting for transfers between devices: 2.67 us -> 13 us
  starting transfers between devices: 21.6 us -> 14.8 us
  local copies, waits for them, and re-layouts: 11.9 us -> 7.94 us
    pallas_call x12 -> x11, Pallas kernels: 95.6 us -> 49.2 us  [call(): pl.pallas_call(kernel, out_shape=shapes, in_specs=specs if specs is not N...]
    ppermute x15 -> x6, starting transfers between devices: 21.6 us -> 8.09 us  [shifted(): return lax.ppermute(block, axis, route)]
    all_to_all x0 -> x2, waiting for transfers between devices: none -> 13 us  [the longest x1 7.9 us: on_device(): lax.all_to_all(terms.reshape(4 * clusters, 8, 128), ('sta', 'clu'), split...]
    all_to_all x0 -> x2, starting transfers between devices: none -> 6.66 us  [the longest x1 3.72 us: on_device(): lax.all_to_all(blocks, 'sta', split_axis=0, concat_axis=0, tiled=True)]
    unnamed x55 -> x37, local copies, waits for them, and re-layouts: 6.13 us -> 3.04 us
    ppermute x15 -> x6, waiting for transfers between devices: 2.67 us -> 0.03 us  [shifted(): return lax.ppermute(block, axis, route)]
    mul x4, local copies, waits for them, and re-layouts: 0.63 us -> 3.25 us  [on_device(): partials[:, :, None, None, :] * eye[None, None, :, :, None]]
    pallas_call x1 -> x0, local copies, waits for them, and re-layouts: 1.62 us -> none  [call(): pl.pallas_call(kernel, out_shape=shapes, in_specs=specs if specs is not N...]
  transfers between devices with their start and end apart: 15 -> 8, of which waited for: 3 -> 2; matrix products, arithmetic and copies ran while one was open for 6% -> 11% of each run, Pallas kernels for 52% -> 38%
where the time goes in v2:
time: 91.4 us; the launch traced here: 90.6 us
  Pallas kernels  49.2 us (54%)
  starting transfers between devices  14.8 us (16%)
  waiting for transfers between devices  13 us (14%)
  local copies, waits for them, and re-layouts  7.94 us (9%)
  other arithmetic  4.51 us (5%)
  between operations  0.96 us (1%)
    pallas_call x11, Pallas kernels, call(): pl.pallas_call(kernel, out_shape=shapes, in_specs=specs if specs is not N...  49.2 us
    ppermute x6, starting transfers between devices, shifted(): return lax.ppermute(block, axis, route)  8.09 us
    all_to_all x1, waiting for transfers between devices, on_device(): lax.all_to_all(terms.reshape(4 * clusters, 8, 128), ('sta', 'clu'), split...  7.9 us
    all_to_all x1, waiting for transfers between devices, on_device(): lax.all_to_all(blocks, 'sta', split_axis=0, concat_axis=0, tiled=True)  5.12 us
    all_to_all x1, starting transfers between devices, on_device(): lax.all_to_all(blocks, 'sta', split_axis=0, concat_axis=0, tiled=True)  3.72 us
    mul x4, local copies, waits for them, and re-layouts, on_device(): partials[:, :, None, None, :] * eye[None, None, :, :, None]  3.25 us
    unnamed x37, local copies, waits for them, and re-layouts  3.04 us
    all_to_all x1, starting transfers between devices, on_device(): lax.all_to_all(terms.reshape(4 * clusters, 8, 128), ('sta', 'clu'), split...  2.95 us
  transfers between devices with their start and end apart: 8, of which 2 were waited for; matrix products, arithmetic and copies ran while one was open for 11% of the time, Pallas kernels for 38%

profile of v2, /device:TPU:0, one launch (start us, length us, event | category | flops | bytes accessed | tf_op | source)
XLA Modules:
  0.0 90.6 jit_solution(15857434167726778079)
XLA Ops:
  0.6 0.7 copy-done
  1.4 0.7 copy-done.2
  2.1 1.0 %copy-done.4 = bf16[32,64,128]{2,1,0:T(8,128)(2,1)S(1)} copy-done((bf16[32,64,128]{2,1,0:T(8,128)(2,1)S(1)}, bf16[32,64,128]{2,1,0:T(8,128)(2,1)}, u32[]{:S(2)}) %copy-start.4) | copy-done | bytes 524312
  3.1 1.6 %shard_map.168 = (bf16[800,128]{1,0:T(8,128)(2,1)S(1)}, bf16[800,128]{1,0:T(8,128)(2,1)S(1)}, bf16[800,128]{1,0:T(8,128)(2,1)S(1)}, bf16[800,128]{1,0:T(8,128)(2...) custom-call(s32[6,12]{1,0:T(8,128)S(1)} %copy-done.2, bf16[32,64,128]{2,1,0:T(8,128)(2,1)S(1)} %copy-done.4, ...), custom_call_target="tpu_custom_call" | custom-call | flops 2000000000 | bytes 1024 | tf_op jit(solution)/shard_map/pallas_call | solution.py:327
  4.7 2.5 %collective-permute-start.5 = (bf16[800,128]{1,0:T(8,128)(2,1)}, bf16[800,128]{1,0:T(8,128)(2,1)}, u32[]{:S(2)}, u32[]{:S(2)}) collective-permute-start(bf16[800,128]{1,0:T(8,128)(2,1)} %get-tuple-element.67), channel_id=1, source_target_pairs={{5,0},{6,1},{7,2},{0,3},{1,4},{2,5},{3,6},{4,7},{13,8},{14,9},{15,... | collective-permute-start | bytes 614408 | tf_op jit(solution)/shard_map/ppermute | solution.py:26
  7.2 1.6 %collective-permute-start.4 = (bf16[800,128]{1,0:T(8,128)(2,1)}, bf16[800,128]{1,0:T(8,128)(2,1)}, u32[]{:S(2)}, u32[]{:S(2)}) collective-permute-start(bf16[800,128]{1,0:T(8,128)(2,1)} %get-tuple-element.65), channel_id=1, source_target_pairs={{6,0},{7,1},{0,2},{1,3},{2,4},{3,5},{4,6},{5,7},{14,8},{15,9},{8,1... | collective-permute-start | bytes 614408 | tf_op jit(solution)/shard_map/ppermute | solution.py:26
  8.7 1.4 %collective-permute-start.3 = (bf16[800,128]{1,0:T(8,128)(2,1)S(1)}, bf16[800,128]{1,0:T(8,128)(2,1)}, u32[]{:S(2)}, u32[]{:S(2)}) collective-permute-start(bf16[800,128]{1,0:T(8,128)(2,1)S(1)} %get-tuple-element.63), channel_id=1, source_target_pairs={{7,0},{0,1},{1,2},{2,3},{3,4},{4,5},{5,6},{6,7},{15,8},{8,9},{9,10... | collective-permute-start | bytes 614408 | tf_op jit(solution)/shard_map/ppermute | solution.py:26
  10.1 2.1 %collective-permute-start.2 = (bf16[800,128]{1,0:T(8,128)(2,1)S(1)}, bf16[800,128]{1,0:T(8,128)(2,1)S(1)}, u32[]{:S(2)}, u32[]{:S(2)}) collective-permute-start(bf16[800,128]{1,0:T(8,128)(2,1)S(1)} %get-tuple-element.61), channel_id=1, source_target_pairs={{1,0},{2,1},{3,2},{4,3},{5,4},{6,5},{7,6},{0,7},{9,8},{10,9},{11,1... | collective-permute-start | bytes 614408 | tf_op jit(solution)/shard_map/ppermute | solution.py:26
  12.3 0.5 collective-permute-start.1
  12.9 0.3 fusion.1.hot
  13.3 0.1 fusion.2.hot_turned
  13.4 0.1 reshape.114
  13.5 0.1 copy.28
  13.6 0.7 fusion.3
  14.3 0.2 convert_reduce_fusion.counts
  14.6 0.1 copy.27
  14.7 0.1 reshape.120
  14.8 1.2 %convert.4 = bf16[32,50,64]{2,0,1:T(8,128)(2,1)S(1)} convert(s32[32,50,64]{2,0,1:T(8,128)} %param.23) | non-fusion elementwise | flops 102400 | bytes 614400 | tf_op jit(solution)/shard_map/convert
  16.0 0.1 pad.40
  16.1 0.3 pad_maximum_fusion
  16.5 0.2 copy.25
  16.8 0.9 %mul.36 = bf16[32,4,4,4,64]{4,3,2,1,0:T(4,128)(2,1)} broadcast(bf16[32,4,64]{2,1,0:T(4,128)(2,1)S(1)} %copy-done.1), dimensions={0,1,4} | broadcast | bytes 278528 | tf_op jit(solution)/shard_map/mul | solution.py:413
  17.7 2.2 %mul.37 = bf16[32,16,256]{2,1,0:T(8,128)(2,1)} reshape(bf16[32,4,4,4,64]{4,3,2,1,0:T(4,128)(2,1)} %mul.36) | data formatting | bytes 524288 | tf_op jit(solution)/shard_map/mul | solution.py:413
  19.9 0.1 mul.39
  20.0 0.6 gather_fusion
  20.7 0.3 slice_reduce_fusion
  21.0 0.1 fusion
  21.1 0.3 select_reduce_fusion.ids
  21.4 1.0 %multiply_negate_fusion.left = bf16[32,16,256]{2,1,0:T(8,128)(2,1)S(1)} fusion(bf16[32,16,256]{2,1,0:T(8,128)(2,1)} %mul.37, bf16[16,256]{1,0:T(8,128)(2,1)S(1)} %mul.39), kind=kLoop, calls=%fused_computation.13 | loop fusion | flops 262144 | bytes 532480 | tf_op jit(solution)/shard_map/neg | solution.py:413
  22.4 0.1 constant_dynamic-update-slice_fusion.4
  22.5 0.1 constant_dynamic-update-slice_fusion.3
  22.6 0.1 constant_dynamic-update-slice_fusion.2
  22.7 13.2 %shard_map.167 = (f32[1024,128]{1,0:T(8,128)S(1)}, f32[32,128,128]{2,1,0:T(8,128)S(1)}, f32[32,64,128]{2,1,0:T(8,128)S(1)}, f32[32,128]{1,0:T(8,128)S(1)}) custom-call(s32[288]{0:T(512)S(1)} %copy-done.7, bf16[16,128,128]{2,1,0:T(8,128)(2,1)S(1)} %bitcast.17, bf16[80,128]{1,0:T(8,128)(2,1)S(1)} %copy-done.6), custom_call_target="tpu_custom_call" | custom-call | flops 8000000000 | bytes 1024 | tf_op jit(solution)/shard_map/pallas_call | solution.py:327
  36.0 4.6 %shard_map.174 = (f32[512,128]{1,0:T(8,128)S(1)}, bf16[32,128]{1,0:T(8,128)(2,1)S(1)}) custom-call(s32[6,216]{1,0:T(8,128)S(1)} %select_reduce_fusion.ids, s32[6]{0:T(128)S(1)} %convert_reduce_fusion.counts, bf16[800,128]{1,0:T(8,128)(2,1)} %collective-permute-done.5.got_ref, f32[32,128,128]{2,1,0:T(8,128)S(1)} %get-tuple-element.55.da, ...), custom_call_target="tpu_custom_call" | custom-call | flops 3000000000 | bytes 1024 | tf_op jit(solution)/shard_map/pallas_call | solution.py:327
  40.6 4.7 %shard_map.173 = (f32[512,128]{1,0:T(8,128)S(1)}, bf16[32,128]{1,0:T(8,128)(2,1)S(1)}) custom-call(s32[6,216]{1,0:T(8,128)S(1)} %select_reduce_fusion.ids, s32[6]{0:T(128)S(1)} %convert_reduce_fusion.counts, bf16[800,128]{1,0:T(8,128)(2,1)} %collective-permute-done.4.got_ref, f32[32,128,128]{2,1,0:T(8,128)S(1)} %get-tuple-element.55.da, ...), custom_call_target="tpu_custom_call" | custom-call | flops 3000000000 | bytes 1024 | tf_op jit(solution)/shard_map/pallas_call | solution.py:327
  45.4 4.0 %shard_map.172 = (f32[512,128]{1,0:T(8,128)S(1)}, bf16[32,128]{1,0:T(8,128)(2,1)S(1)}) custom-call(s32[6,216]{1,0:T(8,128)S(1)} %select_reduce_fusion.ids, s32[6]{0:T(128)S(1)} %convert_reduce_fusion.counts, bf16[800,128]{1,0:T(8,128)(2,1)} %collective-permute-done.3.got_ref, f32[32,128,128]{2,1,0:T(8,128)S(1)} %get-tuple-element.55.da, ...), custom_call_target="tpu_custom_call" | custom-call | flops 3000000000 | bytes 1024 | tf_op jit(solution)/shard_map/pallas_call | solution.py:327
  49.4 4.4 %shard_map.171 = (f32[512,128]{1,0:T(8,128)S(1)}, bf16[32,128]{1,0:T(8,128)(2,1)S(1)}) custom-call(s32[6,216]{1,0:T(8,128)S(1)} %select_reduce_fusion.ids, s32[6]{0:T(128)S(1)} %convert_reduce_fusion.counts, bf16[800,128]{1,0:T(8,128)(2,1)S(1)} %collective-permute-done.2.got_ref, f32[32,128,128]{2,1,0:T(8,128)S(1)} %get-tuple-element.55.da, ...), custom_call_target="tpu_custom_call" | custom-call | flops 3000000000 | bytes 1024 | tf_op jit(solution)/shard_map/pallas_call | solution.py:327
  53.8 3.8 %shard_map.170 = (f32[512,128]{1,0:T(8,128)S(1)}, bf16[32,128]{1,0:T(8,128)(2,1)S(1)}) custom-call(s32[6,216]{1,0:T(8,128)S(1)} %select_reduce_fusion.ids, s32[6]{0:T(128)S(1)} %convert_reduce_fusion.counts, bf16[800,128]{1,0:T(8,128)(2,1)S(1)} %collective-permute-done.1.got_ref, f32[32,128,128]{2,1,0:T(8,128)S(1)} %get-tuple-element.55.da, ...), custom_call_target="tpu_custom_call" | custom-call | flops 3000000000 | bytes 1024 | tf_op jit(solution)/shard_map/pallas_call | solution.py:327
  57.6 4.4 %shard_map.169 = (f32[512,128]{1,0:T(8,128)S(1)}, bf16[32,128]{1,0:T(8,128)(2,1)S(1)}) custom-call(s32[6,216]{1,0:T(8,128)S(1)} %select_reduce_fusion.ids, s32[6]{0:T(128)S(1)} %convert_reduce_fusion.counts, bf16[800,128]{1,0:T(8,128)(2,1)S(1)} %collective-permute-done.got_ref, f32[32,128,128]{2,1,0:T(8,128)S(1)} %get-tuple-element.55.da, ...), custom_call_target="tpu_custom_call" | custom-call | flops 3000000000 | bytes 1024 | tf_op jit(solution)/shard_map/pallas_call | solution.py:327
  61.9 3.6 %shard_map.175 = (bf16[2048,128]{1,0:T(8,128)(2,1)S(1)}, f32[4,8,8,128]{3,2,1,0:T(8,128)}, bf16[128,256]{1,0:T(8,128)(2,1)S(1)}) custom-call(bf16[2048,128]{1,0:T(8,128)(2,1)S(1)} %fusion.1.hot, bf16[128,2048]{1,0:T(8,128)(2,1)S(1)} %fusion.2.hot_turned, bf16[2048,128]{1,0:T(8,128)(2,1)S(1)} %bitcast.15, bf16[2,32,128]{2,1,0:T(8,128)(2,1)S(1)} %bitcast.16, ...), custom_call_target="tpu_custom_call" | custom-call | flops 2000000000 | bytes 1024 | tf_op jit(solution)/shard_map/pallas_call | solution.py:327
  65.5 3.4 %shard_map.176 = f32[4,56,128]{2,1,0:T(8,128)} custom-call(bf16[2048,128]{1,0:T(8,128)(2,1)S(1)} %fusion.1.hot, bf16[2048,128]{1,0:T(8,128)(2,1)S(1)} %get-tuple-element.75.slots, bf16[128,256]{1,0:T(8,128)(2,1)S(1)} %get-tuple-element.76.geo, bf16[32,16,256]{2,1,0:T(8,128)(2,1)S(1)} %multiply_negate_fusion.left), custom_call_target="tpu_custom_call" | custom-call | flops 3000000000 | bytes 1024 | tf_op jit(solution)/shard_map/pallas_call | solution.py:327
  68.9 3.7 %all-to-all-start = ((f32[4,56,128]{2,1,0:T(8,128)}), f32[4,56,128]{2,1,0:T(8,128)S(1)}, u32[]{:S(2)}, u32[]{:S(2)}) async-start(f32[4,56,128]{2,1,0:T(8,128)} %shard_map.176), calls=%async_computation | async-start | bytes 229376 | tf_op jit(solution)/shard_map/all_to_all | solution.py:455
  72.7 5.1 %all-to-all-done.blocks = f32[4,56,128]{2,1,0:T(8,128)S(1)} async-done(((f32[4,56,128]{2,1,0:T(8,128)}), f32[4,56,128]{2,1,0:T(8,128)S(1)}, u32[]{:S(2)}, u32[]{:S(2)}) %all-to-all-start) | async-done | bytes 114720 | tf_op jit(solution)/shard_map/all_to_all | solution.py:455
  77.8 2.9 %all-to-all-start.1 = ((f32[32,8,128]{2,1,0:T(8,128)}), f32[32,8,128]{2,1,0:T(8,128)S(1)}, u32[]{:S(2)}, u32[]{:S(2)}) async-start(f32[32,8,128]{2,1,0:T(8,128)} %bitcast.5), calls=%async_computation.1 | async-start | bytes 262144 | tf_op jit(solution)/shard_map/all_to_all | solution.py:444
  80.8 0.1 constant_dynamic-update-slice_fusion
  80.9 0.2 compare_convert_fusion.owners
  81.1 7.9 %all-to-all-done.1.received = f32[32,8,128]{2,1,0:T(8,128)S(1)} async-done(((f32[32,8,128]{2,1,0:T(8,128)}), f32[32,8,128]{2,1,0:T(8,128)S(1)}, u32[]{:S(2)}, u32[]{:S(2)}) %all-to-all-start.1) | async-done | bytes 131104 | tf_op jit(solution)/shard_map/all_to_all | solution.py:444
  89.0 1.6 %shard_map.177 = (f32[4,32,51]{2,1,0:T(8,128)}, f32[1,32]{1,0:T(1,128)}) custom-call(s32[7]{0:T(128)S(1)} %and_select_fusion.1.clusters, f32[4,56,128]{2,1,0:T(8,128)S(1)} %all-to-all-done.blocks, f32[32,8,128]{2,1,0:T(8,128)S(1)} %all-to-all-done.1.received, f32[896,128]{1,0:T(8,128)S(1)} %compare_convert_fusion.owners), custom_call_target="tpu_custom_call" | custom-call | flops 1000000000 | bytes 1024 | tf_op jit(solution)/shard_map/pallas_call | solution.py:327
  (48 shorter events, 0.7 us)
Async XLA Ops:
  0.6 0.8 copy-start
  1.4 0.7 copy-start.2
  2.1 1.0 %copy-start.4 = (bf16[32,64,128]{2,1,0:T(8,128)(2,1)S(1)}, bf16[32,64,128]{2,1,0:T(8,128)(2,1)}, u32[]{:S(2)}) copy-start(bf16[32,64,128]{2,1,0:T(8,128)(2,1)} %spec_ref.1) | copy-start | bytes 1572868
  3.1 9.6 %copy-start.9 = (s32[32,50]{1,0:T(8,128)S(1)}, s32[32,50]{1,0:T(8,128)}, u32[]{:S(2)}) copy-start(s32[32,50]{1,0:T(8,128)} %param.22) | copy-start | bytes 19204
  4.7 8.7 %copy-start.1 = (bf16[32,4,64]{2,1,0:T(4,128)(2,1)S(1)}, bf16[32,4,64]{2,1,0:T(4,128)(2,1)}, u32[]{:S(2)}) copy-start(bf16[32,4,64]{2,1,0:T(4,128)(2,1)} %geo_ref.1) | copy-start | bytes 49156
  4.7 8.8 %copy-start.3 = (s32[6,12]{1,0:T(8,128)S(1)}, s32[6,12]{1,0:T(8,128)}, u32[]{:S(2)}) copy-start(s32[6,12]{1,0:T(8,128)} %exports_ref.1) | copy-start | bytes 868
  4.7 31.2 %collective-permute-start.5 = (bf16[800,128]{1,0:T(8,128)(2,1)}, bf16[800,128]{1,0:T(8,128)(2,1)}, u32[]{:S(2)}, u32[]{:S(2)}) collective-permute-start(bf16[800,128]{1,0:T(8,128)(2,1)} %get-tuple-element.67), channel_id=1, source_target_pairs={{5,0},{6,1},{7,2},{0,3},{1,4},{2,5},{3,6},{4,7},{13,8},{14,9},{15,... | collective-permute-start | bytes 614408 | tf_op jit(solution)/shard_map/ppermute | solution.py:26
  7.2 33.5 %collective-permute-start.4 = (bf16[800,128]{1,0:T(8,128)(2,1)}, bf16[800,128]{1,0:T(8,128)(2,1)}, u32[]{:S(2)}, u32[]{:S(2)}) collective-permute-start(bf16[800,128]{1,0:T(8,128)(2,1)} %get-tuple-element.65), channel_id=1, source_target_pairs={{6,0},{7,1},{0,2},{1,3},{2,4},{3,5},{4,6},{5,7},{14,8},{15,9},{8,1... | collective-permute-start | bytes 614408 | tf_op jit(solution)/shard_map/ppermute | solution.py:26
  8.7 36.6 %collective-permute-start.3 = (bf16[800,128]{1,0:T(8,128)(2,1)S(1)}, bf16[800,128]{1,0:T(8,128)(2,1)}, u32[]{:S(2)}, u32[]{:S(2)}) collective-permute-start(bf16[800,128]{1,0:T(8,128)(2,1)S(1)} %get-tuple-element.63), channel_id=1, source_target_pairs={{7,0},{0,1},{1,2},{2,3},{3,4},{4,5},{5,6},{6,7},{15,8},{8,9},{9,10... | collective-permute-start | bytes 614408 | tf_op jit(solution)/shard_map/ppermute | solution.py:26
  10.1 39.3 %collective-permute-start.2 = (bf16[800,128]{1,0:T(8,128)(2,1)S(1)}, bf16[800,128]{1,0:T(8,128)(2,1)S(1)}, u32[]{:S(2)}, u32[]{:S(2)}) collective-permute-start(bf16[800,128]{1,0:T(8,128)(2,1)S(1)} %get-tuple-element.61), channel_id=1, source_target_pairs={{1,0},{2,1},{3,2},{4,3},{5,4},{6,5},{7,6},{0,7},{9,8},{10,9},{11,1... | collective-permute-start | bytes 614408 | tf_op jit(solution)/shard_map/ppermute | solution.py:26
  12.3 41.5 %collective-permute-start.1 = (bf16[800,128]{1,0:T(8,128)(2,1)S(1)}, bf16[800,128]{1,0:T(8,128)(2,1)S(1)}, u32[]{:S(2)}, u32[]{:S(2)}) collective-permute-start(bf16[800,128]{1,0:T(8,128)(2,1)S(1)} %get-tuple-element.59), channel_id=1, source_target_pairs={{2,0},{3,1},{4,2},{5,3},{6,4},{7,5},{0,6},{1,7},{10,8},{11,9},{12,... | collective-permute-start | bytes 614408 | tf_op jit(solution)/shard_map/ppermute | solution.py:26
  16.4 3.6 %copy-start.12 = (s32[16]{0:T(128)S(1)}, s32[16]{0:T(128)}, u32[]{:S(2)}) copy-start(s32[16]{0:T(128)} %constant.219) | copy-start | bytes 196
  16.5 4.1 %copy-start.11 = (pred[16]{0:T(512)(128)(4,1)S(1)}, pred[16]{0:T(512)(128)(4,1)}, u32[]{:S(2)}) copy-start(pred[16]{0:T(512)(128)(4,1)} %constant.187.clone) | copy-start | bytes 52
  16.5 4.5 %copy-start.8 = (bf16[192,192]{1,0:T(8,128)(2,1)S(1)}, bf16[192,192]{1,0:T(8,128)(2,1)}, u32[]{:S(2)}) copy-start(bf16[192,192]{1,0:T(8,128)(2,1)} %constant.185.clone) | copy-start | bytes 221188
  16.5 4.6 %copy-start.10 = (s32[192]{0:T(256)S(1)}, s32[192]{0:T(256)}, u32[]{:S(2)}) copy-start(s32[192]{0:T(256)} %constant.186.clone) | copy-start | bytes 2308
  16.7 5.6 %copy-start.14 = (s32[128]{0:T(128)S(1)}, s32[128]{0:T(128)}, u32[]{:S(2)}) copy-start(s32[128]{0:T(128)} %constant.190.clone) | copy-start | bytes 1540
  16.7 6.0 %copy-start.5 = (bf16[32,64,128]{2,1,0:T(8,128)(2,1)S(1)}, bf16[32,64,128]{2,1,0:T(8,128)(2,1)}, u32[]{:S(2)}) copy-start(bf16[32,64,128]{2,1,0:T(8,128)(2,1)} %spec_ref.1) | copy-start | bytes 1572868
  16.7 6.0 %copy-start.6 = (bf16[80,128]{1,0:T(8,128)(2,1)S(1)}, bf16[80,128]{1,0:T(8,128)(2,1)}, u32[]{:S(2)}) copy-start(bf16[80,128]{1,0:T(8,128)(2,1)} %constant.217.table) | copy-start | bytes 61444
  16.7 5.9 %copy-start.7 = (s32[288]{0:T(512)S(1)}, s32[288]{0:T(512)}, u32[]{:S(2)}) copy-start(s32[288]{0:T(512)} %constant.184.clone.ids) | copy-start | bytes 3460
  22.7 13.2 %copy-start.13 = (s32[7]{0:T(128)S(1)}, s32[7]{0:T(128)}, u32[]{:S(2)}) copy-start(s32[7]{0:T(128)} %constant.191.clone) | copy-start | bytes 88
  35.9 21.7 %collective-permute-start = (bf16[800,128]{1,0:T(8,128)(2,1)S(1)}, bf16[800,128]{1,0:T(8,128)(2,1)S(1)}, u32[]{:S(2)}, u32[]{:S(2)}) collective-permute-start(bf16[800,128]{1,0:T(8,128)(2,1)S(1)} %get-tuple-element.54), channel_id=1, source_target_pairs={{3,0},{4,1},{5,2},{6,3},{7,4},{0,5},{1,6},{2,7},{11,8},{12,9},{13,... | collective-permute-start | bytes 614408 | tf_op jit(solution)/shard_map/ppermute | solution.py:26
  68.9 8.9 %all-to-all-start = ((f32[4,56,128]{2,1,0:T(8,128)}), f32[4,56,128]{2,1,0:T(8,128)S(1)}, u32[]{:S(2)}, u32[]{:S(2)}) async-start(f32[4,56,128]{2,1,0:T(8,128)} %shard_map.176), calls=%async_computation | async-start | bytes 229376 | tf_op jit(solution)/shard_map/all_to_all | solution.py:455
  77.8 11.1 %all-to-all-start.1 = ((f32[32,8,128]{2,1,0:T(8,128)}), f32[32,8,128]{2,1,0:T(8,128)S(1)}, u32[]{:S(2)}, u32[]{:S(2)}) async-start(f32[32,8,128]{2,1,0:T(8,128)} %bitcast.5), calls=%async_computation.1 | async-start | bytes 262144 | tf_op jit(solution)/shard_map/all_to_all | solution.py:444

commit v3 on v2

--- a/solution.py
+++ b/solution.py
@@ -54,14 +54,13 @@
 def outgoing_kernel(cap, exports_ref, spec_ref, geo_ref, *refs):
     outs, rows = refs[:-1], refs[-1]
     stations = spec_ref.shape[1]
-    half = cap // 2
     body = cap * stations
     rows[...] = jnp.zeros_like(rows)
     for h, out in enumerate(outs):
         for c in range(cap):
             event = exports_ref[h, c]
             out[c * stations : (c + 1) * stations, :] = spec_ref[event]
-            place = (c % 2) * half + c // 2
+            place = c
             geo = geo_ref[event].astype(F32)
             rows[place : place + 1, :] = jnp.concatenate([geo[0:1], geo[1:2]], axis=1)
             place += GROUP_ROWS
@@ -90,13 +89,11 @@
 def listed_pairs(ids, batches, da, sq, ea, bp, bb, eb, table, work, store, freq, scale):
     xs, reals, rm, rs, rt, rz, re = work
     lead = lax.broadcasted_iota(jnp.int32, (8, 1), 0) == 0
+    low = low_half((8, 128))
 
     def split(t, u):
         code = ids[t * BATCH + u]
         return code >> 6, code & (PAIR_BASE - 1)
-
-    def rows_of(t, u):
-        return pl.ds(pl.multiple_of((t * BATCH + u) * 8, 8), 8)
 
     def cross_stage(t, slot):
         for u in range(BATCH):
@@ -107,50 +104,38 @@
             ci = ai * br - ar * bi
             both = sq[e] * bb[j]
             lanes = slice(u * 128, (u + 1) * 128)
+            rows = slice(u * 8, (u + 1) * 8)
             xs[slot, :freq, lanes] = ci.astype(BF16)
             xs[slot, freq:, lanes] = both.astype(BF16)
             reals[slot, :, lanes] = cr.astype(BF16)
             edge = cr[0:8] * cr[0:8] - ci[0:8] * ci[0:8]
-            rs[rows_of(t, u), :] = fold(both) + jnp.where(lead, edge, 0.0)
-            rt[rows_of(t, u), :] = fold(cr)
-            re[pl.ds(t * BATCH + u, 1), :] = ea[pl.ds(e, 1), :] * eb[pl.ds(j, 1), :]
-
-    def moment_stage(t, slot):
+            rs[slot, rows, :] = fold(both) + jnp.where(lead, edge, 0.0)
+            rt[slot, rows, :] = fold(cr)
+            re[slot, u : u + 1, :] = ea[pl.ds(e, 1), :] * eb[pl.ds(j, 1), :]
+
+    def moment_stage(slot):
         for start in range(0, BATCH, WIDE):
             lanes = slice(start * 128, (start + WIDE) * 128)
             z = jnp.dot(table[...], xs[slot, :, lanes], preferred_element_type=F32)
             for i in range(WIDE):
                 part = z[:, i * 128 : (i + 1) * 128]
                 real = reals[slot, :, (start + i) * 128 : (start + i + 1) * 128].astype(F32)
-                rm[rows_of(t, start + i), :] = fold(real * part[:freq])
-                rz[rows_of(t, start + i), :] = part[freq : freq + 8]
-
-    cross_stage(0, 0)
-
-    @pl.loop(0, (batches + 1) // 2)
-    def _(i):
-        cross_stage(2 * i + 1, 1)
-        moment_stage(2 * i, 0)
-        cross_stage(2 * i + 2, 0)
-        moment_stage(2 * i + 1, 1)
-
-    low = low_half((8, 128))
-
-    @pl.loop(0, batches)
-    def _(t):
-        base = t * BATCH * 8
-
+                rows = slice((start + i) * 8, (start + i + 1) * 8)
+                rm[slot, rows, :] = fold(real * part[:freq])
+                rz[slot, rows, :] = part[freq : freq + 8]
+
+    def finish_stage(t, slot):
         def pick(ref, k):
-            return ref[pl.ds(base + k, 8, stride=8), :]
+            return ref[slot, pl.ds(k, 8, stride=8), :]
 
         moment, total, alternate = pick(rm, 0), pick(rs, 0), pick(rt, 0)
         for k in range(1, 8):
             moment = moment + pick(rm, k)
             total = total + pick(rs, k)
-            alternate = alternate + (1 - 2 * (k % 2)) * pick(rt, k)
+            alternate = alternate + pick(rt, k) if k % 2 == 0 else alternate - pick(rt, k)
         tilt = pick(rz, 0)
         bend = pick(rz, 1) + pick(rz, 2)
-        inverse = 1.0 / (re[pl.ds(pl.multiple_of(t * BATCH, 8), 8), :] + 1e-06)
+        inverse = 1.0 / (re[slot] + 1e-06)
         power = (freq * total - alternate * alternate) * inverse
         rough = (freq * bend - tilt * tilt) * inverse
         weight = power / (power + 0.125 * rough + 1e-06) * scale
@@ -160,6 +145,17 @@
         for u in range(BATCH):
             e, j = split(t, u)
             store(e, j, even[u : u + 1], odd[u : u + 1])
+
+    cross_stage(0, 0)
+
+    @pl.loop(0, (batches + 1) // 2)
+    def _(i):
+        cross_stage(2 * i + 1, 1)
+        moment_stage(0)
+        finish_stage(2 * i, 0)
+        cross_stage(2 * i + 2, 0)
+        moment_stage(1)
+        finish_stage(2 * i + 1, 1)
 
 
 def local_kernel(freq, events, scale, items, ids, spec_ref, table, out, da, sq, ea, bp, bb, eb, *work):
@@ -183,11 +179,10 @@
     row = low_half((1, 128))
 
     def store(e, j, even, odd):
-        own = (e & 1) * pairs + (e >> 1)
-        out[pl.ds(e * events + j, 1), :] = even
-        out[pl.ds(e * events + pairs + j, 1), :] = odd
-        out[pl.ds(2 * j * events + own, 1), :] = jnp.where(row, even, -even)
-        out[pl.ds((2 * j + 1) * events + own, 1), :] = jnp.where(row, odd, -odd)
+        out[pl.ds(e * events + 2 * j, 1), :] = even
+        out[pl.ds(e * events + 2 * j + 1, 1), :] = odd
+        out[pl.ds(2 * j * events + e, 1), :] = jnp.where(row, even, -even)
+        out[pl.ds((2 * j + 1) * events + e, 1), :] = jnp.where(row, odd, -odd)
 
     listed_pairs(ids, items // BATCH, da, sq, ea, bp, bb, eb, table, work, store, freq, scale)
 
@@ -199,34 +194,32 @@
     tail[...] = got_ref[cap // 2 * 128 :, :]
 
     def store(e, j, even, odd):
-        out[pl.ds(e * GROUP_ROWS + j, 1), :] = even
-        out[pl.ds(e * GROUP_ROWS + pairs + j, 1), :] = odd
+        out[pl.ds(e * GROUP_ROWS + 2 * j, 1), :] = even
+        out[pl.ds(e * GROUP_ROWS + 2 * j + 1, 1), :] = odd
 
     batches = (counts[group] + BATCH - 1) // BATCH
     listed_pairs(ids.at[group], batches, da, sq, ea, bp, bb, eb, table, work, store, freq, scale)
 
 
-def weight_scratch(pairs, items, freq):
-    items = items + 2 * BATCH
-    return [
-        pltpu.VMEM((pairs, 2 * freq, 128), F32),
-        pltpu.VMEM((pairs, freq, 128), F32),
-        pltpu.VMEM((-(-pairs // 8) * 8, 128), F32),
-        pltpu.VMEM((2, 2 * freq, BATCH * 128), BF16),
-        pltpu.VMEM((2, freq, BATCH * 128), BF16),
-    ] + [pltpu.VMEM((items * 8, 128), F32)] * 4 + [pltpu.VMEM((items, 128), F32)]
-
-
-def candidate_geo(own0, own1, tails):
-    first = jnp.concatenate([own0] + [t[:GROUP_ROWS, :] for t in tails], axis=0)
-    second = jnp.concatenate([own1] + [t[GROUP_ROWS:, :] for t in tails], axis=0)
-    return first, second
-
-
-def sums_kernel(groups, events, hot, hot_turned, mask, own_geo, *refs):
+def weight_scratch(pairs, freq):
+    return (
+        [
+            pltpu.VMEM((pairs, 2 * freq, 128), F32),
+            pltpu.VMEM((pairs, freq, 128), F32),
+            pltpu.VMEM((-(-pairs // 8) * 8, 128), F32),
+            pltpu.VMEM((2, 2 * freq, BATCH * 128), BF16),
+            pltpu.VMEM((2, freq, BATCH * 128), BF16),
+        ]
+        + [pltpu.VMEM((2, BATCH * 8, 128), F32)] * 4
+        + [pltpu.VMEM((2, BATCH, 128), F32)]
+    )
+
+
+def sums_kernel(groups, events, slots, hot, hot_turned, mask, partials, *refs):
     tables, tails = refs[: groups + 1], refs[groups + 1 : 2 * groups + 1]
-    slots_out, terms_out, geo_out, own = refs[2 * groups + 1 :]
+    slots_out, terms_out, geo_out, own, own_geo = refs[2 * groups + 1 :]
     cands = hot.shape[1]
+    rest = jnp.zeros((SLOT_ROWS - slots, 128), F32)
 
     @pl.loop(0, events // UNROLL)
     def _(step):
@@ -237,10 +230,14 @@
                 parts.append(t[pl.ds(pl.multiple_of(e * GROUP_ROWS, 8), GROUP_ROWS), :])
             every = jnp.concatenate(parts, axis=0).astype(BF16)
             rows = pl.ds(pl.multiple_of(e * SLOT_ROWS, SLOT_ROWS), SLOT_ROWS)
-            slots = jnp.dot(hot[rows, :], every, preferred_element_type=F32) * mask[rows, :].astype(F32)
-            slots_out[rows, :] = slots.astype(BF16)
-            place = (u % 2) * (events // 2) + (e >> 1)
-            own[pl.ds(place, 1), :] = jnp.sum(slots, axis=0, keepdims=True)
+            live = mask[pl.ds(e, slots, stride=events), :].astype(F32)
+            live = jnp.concatenate([jnp.concatenate([live, live], axis=1), rest], axis=0)
+            picked = jnp.dot(hot[rows, :], every, preferred_element_type=F32) * live
+            slots_out[rows, :] = picked.astype(BF16)
+            own[pl.ds(e, 1), :] = jnp.sum(picked, axis=0, keepdims=True)
+            geo = partials[e].astype(F32)
+            own_geo[pl.ds(e, 1), :] = jnp.concatenate([geo[0:1], geo[1:2]], axis=1)
+            own_geo[pl.ds(events + e, 1), :] = jnp.concatenate([geo[2:3], geo[3:4]], axis=1)
 
     gathered = jnp.dot(hot_turned[...], slots_out[...], preferred_element_type=F32)
     low = low_half((cands, 128))
@@ -249,7 +246,9 @@
     turned = pltpu.roll(totals, 64, 1)
     weights = jnp.where(low, totals, turned)
     moves = jnp.where(low, turned, totals)
-    first, second = candidate_geo(own_geo[0], own_geo[1], [t[...] for t in tails])
+    ends = [t[...] for t in tails]
+    first = jnp.concatenate([own_geo[:events].astype(BF16)] + [t[:GROUP_ROWS] for t in ends], axis=0)
+    second = jnp.concatenate([own_geo[events:].astype(BF16)] + [t[GROUP_ROWS:] for t in ends], axis=0)
     geo_out[:, :128] = first
     geo_out[:, 128:] = second
     blocks = [first.astype(F32), second.astype(F32)]
@@ -275,9 +274,12 @@
             terms_out[i, q] = share
 
 
-def blocks_kernel(events, hot, slots, geo, left, out, turned):
+def blocks_kernel(events, place, hot, slots, geo, partials, *refs):
+    outs, turned = refs[:-1], refs[-1]
     turned[...] = jnp.zeros_like(turned)
     low = low_half((SLOT_ROWS, 128))
+    column = lax.broadcasted_iota(jnp.int32, (16, 128), 0) % 4
+    block = lax.broadcasted_iota(jnp.int32, (16, 128), 1) // 64
 
     @pl.loop(0, events // UNROLL)
     def _(step):
@@ -288,14 +290,21 @@
             pair = slots[rows, :].astype(F32)
             weights = jnp.where(low, pair, pltpu.roll(pair, 64, 1))
             weighted = jnp.concatenate([weights * partner[:, :128], weights * partner[:, 128:]], axis=1).astype(BF16)
-            entry = lax.dot_general(left[e], weighted, (((1,), (1,)), ((), ())), preferred_element_type=F32)
+            own = partials[e].astype(F32)
+            own = jnp.concatenate([own, own], axis=1)
+            own = jnp.concatenate([jnp.broadcast_to(-own[i : i + 1], (4, 128)) for i in range(4)], axis=0)
+            left = [jnp.where(column == block, own, 0.0), jnp.where(column == block + 2, own, 0.0)]
+            left = jnp.concatenate(left, axis=1).astype(BF16)
+            entry = lax.dot_general(left, weighted, (((1,), (1,)), ((), ())), preferred_element_type=F32)
             turned[pl.ds(e, 16, stride=events), 0:SLOT_ROWS] = entry
 
-    for i in range(4):
-        out[i] = turned[i * 4 * events : (i + 1) * 4 * events, :].T[: out.shape[1]]
-
-
-def total_kernel(groups, events, slots, clusters, blocks, received, owners, normal, right):
+    for d, out in enumerate(outs):
+        share = lax.rem(place[0] + d, 4)
+        rows = pl.ds(pl.multiple_of(share * 4 * events, 128), 4 * events)
+        out[...] = turned[rows, :].T[: out.shape[0]]
+
+
+def total_kernel(groups, events, slots, clusters, own, one, two, three, received, owners, normal, right):
     parts = []
     for g in range(groups + 1):
         part = received[clusters[g]]
@@ -310,7 +319,7 @@
     for j in range(4):
         diagonal = jnp.where(block == j, spread[j : j + 1], diagonal)
     right[...] = spread[4:5, :events]
-    total = (blocks[0] + blocks[1]) + (blocks[2] + blocks[3])
+    total = pltpu.roll((own[...] + one[...]) + (two[...] + three[...]), 1, 0)
     top = lax.broadcasted_iota(jnp.int32, total.shape, 0) == 0
     total = jnp.where(top, diagonal, total)
     turned = total.T
@@ -359,7 +368,7 @@
         specs=[smem] + vmem(2),
         micros=2.0,
     )
-    order = sorted(range(groups), key=lambda h: -abs(offsets[h]))
+    order = sorted(range(groups), key=lambda h: abs(offsets[h]))
     got = [None] * groups
     for h in order:
         got[h] = shifted(outgoing[h], "clu", offsets[h])
@@ -367,6 +376,7 @@
     codes = [e * PAIR_BASE + j for e in range(events) for j in range(e // 2, events // 2)]
     items = -(-len(codes) // (2 * BATCH)) * 2 * BATCH
     codes = codes + [0] * (items + 2 * BATCH - len(codes))
+    natural, got[order[0]] = lax.optimization_barrier((spectra, got[order[0]]))
     local, dup, square, energy = call(
         functools.partial(local_kernel, freq, events, scale, items),
         [
@@ -375,8 +385,8 @@
             ((events, freq, 128), F32),
             ((events, 128), F32),
         ],
-        (jnp.asarray(codes, jnp.int32), spectra.reshape(events // 2, 2 * stations, two_freq), table),
-        scratch=weight_scratch(events // 2, items, freq),
+        (jnp.asarray(codes, jnp.int32), natural.reshape(events // 2, 2 * stations, two_freq), table),
+        scratch=weight_scratch(events // 2, freq),
         specs=[smem] + vmem(2),
         micros=8.0,
     )
@@ -397,68 +407,57 @@
     ).astype(jnp.int32)
     counts = jnp.sum(wanted.astype(jnp.int32), axis=1)
 
-    m = pair_list
-    near = (m % 2) * (events // 2) + m // 2
-    entry = far % cap
-    far = events + GROUP_ROWS * (far // cap) + (entry % 2) * half + entry // 2
-    column = jnp.where(m < 0, -1, jnp.where(m < events, near, far))
-    column = jnp.pad(column, ((0, 0), (1, SLOT_ROWS - 1 - slots)), constant_values=-1).reshape(-1)
+    column = jnp.where(pair_list < events, pair_list, events + GROUP_ROWS * (far // cap) + far % cap)
+    column = jnp.pad(column, ((0, 0), (0, SLOT_ROWS - slots)), constant_values=-1).reshape(-1)
     cand_ids = jnp.arange(cands, dtype=jnp.int32)
     hot = (column[:, None] == cand_ids[None, :]).astype(BF16)
     hot_turned = (cand_ids[:, None] == column[None, :]).astype(BF16)
-    mask = jnp.pad(station_mask, ((0, 0), (1, SLOT_ROWS - 1 - slots), (0, 0))).astype(BF16)
-    mask = jnp.concatenate([mask, mask], axis=2).reshape(events * SLOT_ROWS, 128)
-    own_geo = partials.reshape(events // 2, 2, 2, 128).transpose(2, 1, 0, 3).reshape(2, events, 128)
-    eye = jnp.eye(4, dtype=BF16)
-    left = -(partials[:, :, None, None, :] * eye[None, None, :, :, None]).reshape(events, 16, 4 * stations)
-    cand_rank = np.arange(GROUP_ROWS)
-    cand_entry = np.where(cand_rank < cap, 2 * (cand_rank % half) + cand_rank // half, 0)
-    owner = jnp.where(jnp.asarray(cand_rank < cap)[None, :], exports[:, cand_entry], -1)
-    local_rank = np.arange(cands)
-    local_owner = np.where(local_rank < events, 2 * (local_rank % (events // 2)) + local_rank // (events // 2), -1)
-    owner_rows = [jnp.asarray(local_owner, jnp.int32)]
+    mask = station_mask.transpose(1, 0, 2).reshape(slots * events, stations)
+    owner_rows = [jnp.asarray(np.where(np.arange(cands) < events, np.arange(cands), -1), jnp.int32)]
     for h in range(groups):
         start = events + GROUP_ROWS * h
-        owner_rows.append(jnp.pad(owner[h], (start, cands - start - GROUP_ROWS), constant_values=-1))
+        owner_rows.append(jnp.pad(exports[h], (start, cands - start - cap), constant_values=-1))
     owners = jnp.concatenate(owner_rows)[:, None] == (jnp.arange(128, dtype=jnp.int32) % events)[None, :]
     owners = owners.astype(F32)
 
     tables, tails = [None] * groups, [None] * groups
-    for h in order[::-1]:
+    for h in order:
         tables[h], tails[h] = call(
             functools.partial(import_kernel, h, freq, events, cap, scale),
             [((events * GROUP_ROWS, 128), F32), ((2 * GROUP_ROWS, 128), BF16)],
             (lists, counts, got[h], dup, square, energy, table),
-            scratch=weight_scratch(half, events * half, freq),
+            scratch=weight_scratch(half, freq),
             specs=[smem] * 2 + vmem(5),
             micros=3.0,
         )
 
     weights, terms, geo = call(
-        functools.partial(sums_kernel, groups, events),
+        functools.partial(sums_kernel, groups, events, slots),
         [((events * SLOT_ROWS, 128), BF16), ((4, clusters, 8, 128), F32), ((cands, 256), BF16)],
-        (hot, hot_turned, mask, own_geo, local, *tables, *tails),
-        scratch=[pltpu.VMEM((events, 128), F32)],
+        (hot, hot_turned, mask, partials, local, *tables, *tails),
+        scratch=[pltpu.VMEM((events, 128), F32), pltpu.VMEM((2 * events, 128), F32)],
         micros=2.0,
     )
     terms = lax.all_to_all(
         terms.reshape(4 * clusters, 8, 128), ("sta", "clu"), split_axis=0, concat_axis=0, tiled=True
     )
     message_rows = -(-(slots + 1) // 8) * 8
-    (blocks,) = call(
+    place = lax.axis_index("sta").astype(jnp.int32).reshape(1)
+    shares = call(
         functools.partial(blocks_kernel, events),
-        [((4, message_rows, 128), F32)],
-        (hot, weights, geo, left),
+        [((message_rows, 128), F32)] * 4,
+        (place, hot, weights, geo, partials),
         scratch=[pltpu.VMEM((16 * events, 128), F32)],
+        specs=[smem] + vmem(4),
         micros=3.0,
     )
-    blocks = lax.all_to_all(blocks, "sta", split_axis=0, concat_axis=0, tiled=True)
+    shares = [shares[0]] + [shifted(shares[d], "sta", d) for d in range(1, 4)]
     sources = (lax.axis_index("clu") + jnp.asarray([0] + offsets, jnp.int32)) % clusters
     normal, right = call(
         functools.partial(total_kernel, groups, events, slots),
         [((4, events, slots + 1), F32), ((1, events), F32)],
-        (sources.astype(jnp.int32), blocks, terms, owners),
-        specs=[smem] + vmem(3),
+        (sources.astype(jnp.int32), *shares, terms, owners),
+        specs=[smem] + vmem(6),
     )
     return (normal.transpose(0, 2, 1), right)
 

time: 91.4 us -> 78.5 us (0.86); the launches traced: 90.6 us -> 78.7 us
  starting transfers between devices: 14.8 us -> 27.9 us
  waiting for transfers between devices: 13 us -> 2.41 us
  Pallas kernels: 49.2 us -> 42.1 us
  local copies, waits for them, and re-layouts: 7.94 us -> 3.31 us
  other arithmetic: 4.51 us -> 1.92 us
    all_to_all x1, starting transfers between devices: 2.95 us -> 14.5 us  [on_device(): lax.all_to_all(terms.reshape(4 * clusters, 8, 128), ('sta', 'clu'), split...]
    all_to_all x1, waiting for transfers between devices: 7.9 us -> 0.01 us  [on_device(): lax.all_to_all(terms.reshape(4 * clusters, 8, 128), ('sta', 'clu'), split...]
    pallas_call x11, Pallas kernels: 49.2 us -> 42.1 us  [call(): pl.pallas_call(kernel, out_shape=shapes, in_specs=specs if specs is not N...]
    ppermute x6 -> x9, starting transfers between devices: 8.09 us -> 13.5 us  [shifted(): return lax.ppermute(block, axis, route)]
    all_to_all x1 -> x0, waiting for transfers between devices: 5.12 us -> none  [on_device(): lax.all_to_all(blocks, 'sta', split_axis=0, concat_axis=0, tiled=True)]
    all_to_all x1 -> x0, starting transfers between devices: 3.72 us -> none  [on_device(): lax.all_to_all(blocks, 'sta', split_axis=0, concat_axis=0, tiled=True)]
    mul x4 -> x0, local copies, waits for them, and re-layouts: 3.25 us -> none  [on_device(): partials[:, :, None, None, :] * eye[None, None, :, :, None]]
    ppermute x6 -> x9, waiting for transfers between devices: 0.03 us -> 2.41 us  [shifted(): return lax.ppermute(block, axis, route)]
  transfers between devices with their start and end apart: 8 -> 10, of which waited for: 2 -> 3; matrix products, arithmetic and copies ran while one was open for 11% -> 4% of each run, Pallas kernels for 38% -> 41%
where the time goes in v3:
time: 78.5 us; the launch traced here: 78.7 us
  Pallas kernels  42.1 us (54%)
  starting transfers between devices  27.9 us (36%)
  local copies, waits for them, and re-layouts  3.31 us (4%)
  waiting for transfers between devices  2.41 us (3%)
  other arithmetic  1.92 us (2%)
  between operations  0.88 us (1%)
    pallas_call x11, Pallas kernels, call(): pl.pallas_call(kernel, out_shape=shapes, in_specs=specs if specs is not N...  42.1 us
    all_to_all x1, starting transfers between devices, on_device(): lax.all_to_all(terms.reshape(4 * clusters, 8, 128), ('sta', 'clu'), split...  14.5 us
    ppermute x9, starting transfers between devices, shifted(): return lax.ppermute(block, axis, route)  13.5 us
    unnamed x34, local copies, waits for them, and re-layouts  2.94 us
    ppermute x9, waiting for transfers between devices, shifted(): return lax.ppermute(block, axis, route)  2.41 us
  transfers between devices with their start and end apart: 10, of which 3 were waited for; matrix products, arithmetic and copies ran while one was open for 4% of the time, Pallas kernels for 41%

profile of v3, /device:TPU:0, one launch (start us, length us, event | category | flops | bytes accessed | tf_op | source)
XLA Modules:
  0.0 78.7 jit_solution(17587602662026839732)
XLA Ops:
  0.6 0.0 copy-start
  0.6 0.7 copy-done
  1.3 1.0 %copy-done.3 = bf16[32,64,128]{2,1,0:T(8,128)(2,1)S(1)} copy-done((bf16[32,64,128]{2,1,0:T(8,128)(2,1)S(1)}, bf16[32,64,128]{2,1,0:T(8,128)(2,1)}, u32[]{:S(2)}) %copy-start.3) | copy-done | bytes 524312
  2.4 0.8 copy-done.5
  3.1 1.5 %shard_map.140 = (bf16[800,128]{1,0:T(8,128)(2,1)S(1)}, bf16[800,128]{1,0:T(8,128)(2,1)S(1)}, bf16[800,128]{1,0:T(8,128)(2,1)}, bf16[800,128]{1,0:T(8,128)(2,1)S...) custom-call(s32[6,12]{1,0:T(8,128)S(1)} %copy-done, bf16[32,64,128]{2,1,0:T(8,128)(2,1)S(1)} %copy-done.3, ...), custom_call_target="tpu_custom_call" | custom-call | flops 2000000000 | bytes 1024 | tf_op jit(solution)/shard_map/pallas_call | solution.py:336
  4.6 0.0 copy-start.4
  4.6 0.0 copy-start.7
  4.6 0.0 copy-start.8
  4.6 4.5 %collective-permute-start = (bf16[800,128]{1,0:T(8,128)(2,1)}, bf16[800,128]{1,0:T(8,128)(2,1)}, u32[]{:S(2)}, u32[]{:S(2)}) collective-permute-start(bf16[800,128]{1,0:T(8,128)(2,1)} %get-tuple-element.59), channel_id=1, source_target_pairs={{1,0},{2,1},{3,2},{4,3},{5,4},{6,5},{7,6},{0,7},{9,8},{10,9},{11,1... | collective-permute-start | bytes 614408 | tf_op jit(solution)/shard_map/ppermute | solution.py:26
  9.2 0.2 collective-permute-start.4
  9.4 0.8 %collective-permute-start.3 = (bf16[800,128]{1,0:T(8,128)(2,1)S(1)}, bf16[800,128]{1,0:T(8,128)(2,1)S(1)}, u32[]{:S(2)}, u32[]{:S(2)}) collective-permute-start(bf16[800,128]{1,0:T(8,128)(2,1)S(1)} %get-tuple-element.71), channel_id=1, source_target_pairs={{7,0},{0,1},{1,2},{2,3},{3,4},{4,5},{5,6},{6,7},{15,8},{8,9},{9,10... | collective-permute-start | bytes 614408 | tf_op jit(solution)/shard_map/ppermute | solution.py:26
  10.2 2.8 %collective-permute-start.2 = (bf16[800,128]{1,0:T(8,128)(2,1)S(1)}, bf16[800,128]{1,0:T(8,128)(2,1)S(1)}, u32[]{:S(2)}, u32[]{:S(2)}) collective-permute-start(bf16[800,128]{1,0:T(8,128)(2,1)S(1)} %get-tuple-element.67), channel_id=1, source_target_pairs={{2,0},{3,1},{4,2},{5,3},{6,4},{7,5},{0,6},{1,7},{10,8},{11,9},{12,... | collective-permute-start | bytes 614408 | tf_op jit(solution)/shard_map/ppermute | solution.py:26
  13.1 0.1 eq.38
  13.1 0.3 fusion.1.hot
  13.5 0.1 fusion.2.hot_turned
  13.6 0.7 fusion.3
  14.3 0.2 convert_reduce_fusion.counts
  14.5 0.1 copy.16
  14.7 0.1 reshape.103
  14.8 0.1 fusion
  15.0 0.3 select_reduce_fusion.ids
  15.3 0.1 constant_dynamic-update-slice_fusion.5
  15.3 0.1 constant_dynamic-update-slice_fusion.4
  15.4 0.1 constant_dynamic-update-slice_fusion.3
  15.5 0.1 constant_dynamic-update-slice_fusion.2
  15.6 0.1 constant_dynamic-update-slice_fusion.1
  15.7 0.1 constant_dynamic-update-slice_fusion
  15.7 0.2 compare_convert_fusion.owners
  15.9 0.3 collective-permute-start.1
  16.3 11.0 %shard_map.141 = (f32[1024,128]{1,0:T(8,128)S(1)}, f32[32,128,128]{2,1,0:T(8,128)S(1)}, f32[32,64,128]{2,1,0:T(8,128)S(1)}, f32[32,128]{1,0:T(8,128)S(1)}) custom-call(s32[288]{0:T(512)S(1)} %copy-done.8, bf16[16,128,128]{2,1,0:T(8,128)(2,1)S(1)} %bitcast.26, bf16[80,128]{1,0:T(8,128)(2,1)S(1)} %copy-done.7), custom_call_target="tpu_custom_call" | custom-call | flops 8000000000 | bytes 1024 | tf_op jit(solution)/shard_map/pallas_call | solution.py:336
  27.3 4.1 %shard_map.144 = (f32[512,128]{1,0:T(8,128)S(1)}, bf16[32,128]{1,0:T(8,128)(2,1)S(1)}) custom-call(s32[6,216]{1,0:T(8,128)S(1)} %select_reduce_fusion.ids, s32[6]{0:T(128)S(1)} %convert_reduce_fusion.counts, bf16[800,128]{1,0:T(8,128)(2,1)} %collective-permute-done.got_ref, f32[32,128,128]{2,1,0:T(8,128)S(1)} %get-tuple-element.63.da, ...), custom_call_target="tpu_custom_call" | custom-call | flops 3000000000 | bytes 1024 | tf_op jit(solution)/shard_map/pallas_call | solution.py:336
  31.4 3.6 %shard_map.147 = (f32[512,128]{1,0:T(8,128)S(1)}, bf16[32,128]{1,0:T(8,128)(2,1)S(1)}) custom-call(s32[6,216]{1,0:T(8,128)S(1)} %select_reduce_fusion.ids, s32[6]{0:T(128)S(1)} %convert_reduce_fusion.counts, bf16[800,128]{1,0:T(8,128)(2,1)} %collective-permute-done.5.got_ref, f32[32,128,128]{2,1,0:T(8,128)S(1)} %get-tuple-element.63.da, ...), custom_call_target="tpu_custom_call" | custom-call | flops 3000000000 | bytes 1024 | tf_op jit(solution)/shard_map/pallas_call | solution.py:336
  35.0 3.6 %shard_map.146 = (f32[512,128]{1,0:T(8,128)S(1)}, bf16[32,128]{1,0:T(8,128)(2,1)S(1)}) custom-call(s32[6,216]{1,0:T(8,128)S(1)} %select_reduce_fusion.ids, s32[6]{0:T(128)S(1)} %convert_reduce_fusion.counts, bf16[800,128]{1,0:T(8,128)(2,1)} %collective-permute-done.4.got_ref, f32[32,128,128]{2,1,0:T(8,128)S(1)} %get-tuple-element.63.da, ...), custom_call_target="tpu_custom_call" | custom-call | flops 3000000000 | bytes 1024 | tf_op jit(solution)/shard_map/pallas_call | solution.py:336
  38.5 3.3 %shard_map.145 = (f32[512,128]{1,0:T(8,128)S(1)}, bf16[32,128]{1,0:T(8,128)(2,1)S(1)}) custom-call(s32[6,216]{1,0:T(8,128)S(1)} %select_reduce_fusion.ids, s32[6]{0:T(128)S(1)} %convert_reduce_fusion.counts, bf16[800,128]{1,0:T(8,128)(2,1)S(1)} %collective-permute-done.3.got_ref, f32[32,128,128]{2,1,0:T(8,128)S(1)} %get-tuple-element.63.da, ...), custom_call_target="tpu_custom_call" | custom-call | flops 3000000000 | bytes 1024 | tf_op jit(solution)/shard_map/pallas_call | solution.py:336
  41.8 3.8 %shard_map.143 = (f32[512,128]{1,0:T(8,128)S(1)}, bf16[32,128]{1,0:T(8,128)(2,1)S(1)}) custom-call(s32[6,216]{1,0:T(8,128)S(1)} %select_reduce_fusion.ids, s32[6]{0:T(128)S(1)} %convert_reduce_fusion.counts, bf16[800,128]{1,0:T(8,128)(2,1)S(1)} %collective-permute-done.2.got_ref, f32[32,128,128]{2,1,0:T(8,128)S(1)} %get-tuple-element.63.da, ...), custom_call_target="tpu_custom_call" | custom-call | flops 3000000000 | bytes 1024 | tf_op jit(solution)/shard_map/pallas_call | solution.py:336
  45.7 0.0 copy-start.6
  45.7 3.3 %shard_map.142 = (f32[512,128]{1,0:T(8,128)S(1)}, bf16[32,128]{1,0:T(8,128)(2,1)S(1)}) custom-call(s32[6,216]{1,0:T(8,128)S(1)} %select_reduce_fusion.ids, s32[6]{0:T(128)S(1)} %convert_reduce_fusion.counts, bf16[800,128]{1,0:T(8,128)(2,1)S(1)} %collective-permute-done.1.got_ref, f32[32,128,128]{2,1,0:T(8,128)S(1)} %get-tuple-element.63.da, ...), custom_call_target="tpu_custom_call" | custom-call | flops 3000000000 | bytes 1024 | tf_op jit(solution)/shard_map/pallas_call | solution.py:336
  49.0 3.7 %shard_map.148 = (bf16[2048,128]{1,0:T(8,128)(2,1)S(1)}, f32[4,8,8,128]{3,2,1,0:T(8,128)}, bf16[128,256]{1,0:T(8,128)(2,1)S(1)}) custom-call(bf16[2048,128]{1,0:T(8,128)(2,1)S(1)} %fusion.1.hot, bf16[128,2048]{1,0:T(8,128)(2,1)S(1)} %fusion.2.hot_turned, s32[1600,64]{1,0:T(8,128)S(1)} %bitcast.25, bf16[32,4,64]{2,1,0:T(4,128)(2,1)S(1)} %copy-done.6, ...), custom_call_target="tpu_custom_call" | custom-call | flops 2000000000 | bytes 1024 | tf_op jit(solution)/shard_map/pallas_call | solution.py:336
  52.7 14.5 %all-to-all-start = ((f32[32,8,128]{2,1,0:T(8,128)}), f32[32,8,128]{2,1,0:T(8,128)S(1)}, u32[]{:S(2)}, u32[]{:S(2)}) async-start(f32[32,8,128]{2,1,0:T(8,128)} %bitcast.5), calls=%async_computation | async-start | bytes 262144 | tf_op jit(solution)/shard_map/all_to_all | solution.py:441
  67.1 0.0 copy-start.12
  67.2 2.7 %shard_map.149 = (f32[56,128]{1,0:T(8,128)S(1)}, f32[56,128]{1,0:T(8,128)S(1)}, f32[56,128]{1,0:T(8,128)S(1)}, f32[56,128]{1,0:T(8,128)S(1)}) custom-call(s32[1]{0:T(128)} %bitcast.place, bf16[2048,128]{1,0:T(8,128)(2,1)S(1)} %fusion.1.hot, bf16[2048,128]{1,0:T(8,128)(2,1)S(1)} %get-tuple-element.83.slots, bf16[128,256]{1,0:T(8,128)(2,1)S(1)} %get-tuple-element.84.geo, ...), custom_call_target="tpu_custom_call" | custom-call | flops 3000000000 | bytes 1024 | tf_op jit(solution)/shard_map/pallas_call | solution.py:336
  69.9 1.8 %collective-permute-start.6 = (f32[56,128]{1,0:T(8,128)S(1)}, f32[56,128]{1,0:T(8,128)S(1)}, u32[]{:S(2)}, u32[]{:S(2)}) collective-permute-start(f32[56,128]{1,0:T(8,128)S(1)} %get-tuple-element.86), channel_id=1, source_target_pairs={{24,0},{0,8},{8,16},{16,24},{25,1},{1,9},{9,17},{17,25},{26,2},{2,... | collective-permute-start | bytes 86024 | tf_op jit(solution)/shard_map/ppermute | solution.py:26
  71.7 1.5 %collective-permute-start.7 = (f32[56,128]{1,0:T(8,128)S(1)}, f32[56,128]{1,0:T(8,128)S(1)}, u32[]{:S(2)}, u32[]{:S(2)}) collective-permute-start(f32[56,128]{1,0:T(8,128)S(1)} %get-tuple-element.87), channel_id=1, source_target_pairs={{16,0},{24,8},{0,16},{8,24},{17,1},{25,9},{1,17},{9,25},{18,2},{26... | collective-permute-start | bytes 86024 | tf_op jit(solution)/shard_map/ppermute | solution.py:26
  73.2 1.5 %collective-permute-start.8 = (f32[56,128]{1,0:T(8,128)S(1)}, f32[56,128]{1,0:T(8,128)S(1)}, u32[]{:S(2)}, u32[]{:S(2)}) collective-permute-start(f32[56,128]{1,0:T(8,128)S(1)} %get-tuple-element.88), channel_id=1, source_target_pairs={{8,0},{16,8},{24,16},{0,24},{9,1},{17,9},{25,17},{1,25},{10,2},{18... | collective-permute-start | bytes 86024 | tf_op jit(solution)/shard_map/ppermute | solution.py:26
  74.7 0.3 collective-permute-done.6.one
  74.9 0.7 collective-permute-done.7.two
  75.6 1.4 %collective-permute-done.8.three = f32[56,128]{1,0:T(8,128)S(1)} collective-permute-done((f32[56,128]{1,0:T(8,128)S(1)}, f32[56,128]{1,0:T(8,128)S(1)}, u32[]{:S(2)}, u32[]{:S(2)}) %collective-permute-start.8) | collective-permute-done | bytes 28704 | tf_op jit(solution)/shard_map/ppermute | solution.py:26
  77.1 1.6 %shard_map.150 = (f32[4,32,51]{2,1,0:T(8,128)}, f32[1,32]{1,0:T(1,128)}) custom-call(s32[7]{0:T(128)S(1)} %and_select_fusion.1.clusters, f32[56,128]{1,0:T(8,128)S(1)} %get-tuple-element.85.own, f32[56,128]{1,0:T(8,128)S(1)} %collective-permute-done.6.one, f32[56,128]{1,0:T(8,128)S(1)} %collective-permute-done.7.two, ...), custom_call_target="tpu_custom_call" | custom-call | flops 1000000000 | bytes 1024 | tf_op jit(solution)/shard_map/pallas_call | solution.py:336
  (34 shorter events, 0.1 us)
Async XLA Ops:
  0.6 0.7 copy-start
  1.3 1.0 %copy-start.3 = (bf16[32,64,128]{2,1,0:T(8,128)(2,1)S(1)}, bf16[32,64,128]{2,1,0:T(8,128)(2,1)}, u32[]{:S(2)}) copy-start(bf16[32,64,128]{2,1,0:T(8,128)(2,1)} %spec_ref.1) | copy-start | bytes 1572868
  2.4 0.8 copy-start.5
  3.1 9.9 %copy-start.10 = (s32[32,50]{1,0:T(8,128)S(1)}, s32[32,50]{1,0:T(8,128)}, u32[]{:S(2)}) copy-start(s32[32,50]{1,0:T(8,128)} %param.19) | copy-start | bytes 19204
  4.6 9.0 %copy-start.1 = (s32[6,12]{1,0:T(8,128)S(1)}, s32[6,12]{1,0:T(8,128)}, u32[]{:S(2)}) copy-start(s32[6,12]{1,0:T(8,128)} %exports_ref.1) | copy-start | bytes 868
  4.6 10.2 %copy-start.9 = (bf16[192,192]{1,0:T(8,128)(2,1)S(1)}, bf16[192,192]{1,0:T(8,128)(2,1)}, u32[]{:S(2)}) copy-start(bf16[192,192]{1,0:T(8,128)(2,1)} %constant.157.clone) | copy-start | bytes 221188
  4.6 10.4 %copy-start.11 = (s32[192]{0:T(256)S(1)}, s32[192]{0:T(256)}, u32[]{:S(2)}) copy-start(s32[192]{0:T(256)} %constant.158.clone) | copy-start | bytes 2308
  4.6 10.7 %copy-start.13 = (s32[128]{0:T(128)S(1)}, s32[128]{0:T(128)}, u32[]{:S(2)}) copy-start(s32[128]{0:T(128)} %constant.159.clone) | copy-start | bytes 1540
  4.6 11.7 %copy-start.4 = (bf16[32,64,128]{2,1,0:T(8,128)(2,1)S(1)}, bf16[32,64,128]{2,1,0:T(8,128)(2,1)}, u32[]{:S(2)}) copy-start(bf16[32,64,128]{2,1,0:T(8,128)(2,1)} %spec_ref.1) | copy-start | bytes 1572868
  4.6 11.7 %copy-start.7 = (bf16[80,128]{1,0:T(8,128)(2,1)S(1)}, bf16[80,128]{1,0:T(8,128)(2,1)}, u32[]{:S(2)}) copy-start(bf16[80,128]{1,0:T(8,128)(2,1)} %constant.184.table) | copy-start | bytes 61444
  4.6 11.7 %copy-start.8 = (s32[288]{0:T(512)S(1)}, s32[288]{0:T(512)}, u32[]{:S(2)}) copy-start(s32[288]{0:T(512)} %constant.156.clone.ids) | copy-start | bytes 3460
  4.6 11.3 %collective-permute-start = (bf16[800,128]{1,0:T(8,128)(2,1)}, bf16[800,128]{1,0:T(8,128)(2,1)}, u32[]{:S(2)}, u32[]{:S(2)}) collective-permute-start(bf16[800,128]{1,0:T(8,128)(2,1)} %get-tuple-element.59), channel_id=1, source_target_pairs={{1,0},{2,1},{3,2},{4,3},{5,4},{6,5},{7,6},{0,7},{9,8},{10,9},{11,1... | collective-permute-start | bytes 614408 | tf_op jit(solution)/shard_map/ppermute | solution.py:26
  9.2 22.3 %collective-permute-start.5 = (bf16[800,128]{1,0:T(8,128)(2,1)S(1)}, bf16[800,128]{1,0:T(8,128)(2,1)}, u32[]{:S(2)}, u32[]{:S(2)}) collective-permute-start(bf16[800,128]{1,0:T(8,128)(2,1)S(1)} %get-tuple-element.75), channel_id=1, source_target_pairs={{5,0},{6,1},{7,2},{0,3},{1,4},{2,5},{3,6},{4,7},{13,8},{14,9},{15,... | collective-permute-start | bytes 614408 | tf_op jit(solution)/shard_map/ppermute | solution.py:26
  9.2 25.8 %collective-permute-start.4 = (bf16[800,128]{1,0:T(8,128)(2,1)S(1)}, bf16[800,128]{1,0:T(8,128)(2,1)}, u32[]{:S(2)}, u32[]{:S(2)}) collective-permute-start(bf16[800,128]{1,0:T(8,128)(2,1)S(1)} %get-tuple-element.73), channel_id=1, source_target_pairs={{6,0},{7,1},{0,2},{1,3},{2,4},{3,5},{4,6},{5,7},{14,8},{15,9},{8,1... | collective-permute-start | bytes 614408 | tf_op jit(solution)/shard_map/ppermute | solution.py:26
  9.4 29.2 %collective-permute-start.3 = (bf16[800,128]{1,0:T(8,128)(2,1)S(1)}, bf16[800,128]{1,0:T(8,128)(2,1)S(1)}, u32[]{:S(2)}, u32[]{:S(2)}) collective-permute-start(bf16[800,128]{1,0:T(8,128)(2,1)S(1)} %get-tuple-element.71), channel_id=1, source_target_pairs={{7,0},{0,1},{1,2},{2,3},{3,4},{4,5},{5,6},{6,7},{15,8},{8,9},{9,10... | collective-permute-start | bytes 614408 | tf_op jit(solution)/shard_map/ppermute | solution.py:26
  10.2 31.6 %collective-permute-start.2 = (bf16[800,128]{1,0:T(8,128)(2,1)S(1)}, bf16[800,128]{1,0:T(8,128)(2,1)S(1)}, u32[]{:S(2)}, u32[]{:S(2)}) collective-permute-start(bf16[800,128]{1,0:T(8,128)(2,1)S(1)} %get-tuple-element.67), channel_id=1, source_target_pairs={{2,0},{3,1},{4,2},{5,3},{6,4},{7,5},{0,6},{1,7},{10,8},{11,9},{12,... | collective-permute-start | bytes 614408 | tf_op jit(solution)/shard_map/ppermute | solution.py:26
  15.9 29.8 %collective-permute-start.1 = (bf16[800,128]{1,0:T(8,128)(2,1)S(1)}, bf16[800,128]{1,0:T(8,128)(2,1)S(1)}, u32[]{:S(2)}, u32[]{:S(2)}) collective-permute-start(bf16[800,128]{1,0:T(8,128)(2,1)S(1)} %get-tuple-element.62), channel_id=1, source_target_pairs={{3,0},{4,1},{5,2},{6,3},{7,4},{0,5},{1,6},{2,7},{11,8},{12,9},{13,... | collective-permute-start | bytes 614408 | tf_op jit(solution)/shard_map/ppermute | solution.py:26
  45.7 3.3 %copy-start.2 = (s32[32,50,64]{2,0,1:T(8,128)S(1)}, s32[32,50,64]{2,0,1:T(8,128)}, u32[]{:S(2)}) copy-start(s32[32,50,64]{2,0,1:T(8,128)} %param.20) | copy-start | bytes 1228804
  45.7 3.3 %copy-start.6 = (bf16[32,4,64]{2,1,0:T(4,128)(2,1)S(1)}, bf16[32,4,64]{2,1,0:T(4,128)(2,1)}, u32[]{:S(2)}) copy-start(bf16[32,4,64]{2,1,0:T(4,128)(2,1)} %partials.3) | copy-start | bytes 49156
  52.7 24.4 %all-to-all-start = ((f32[32,8,128]{2,1,0:T(8,128)}), f32[32,8,128]{2,1,0:T(8,128)S(1)}, u32[]{:S(2)}, u32[]{:S(2)}) async-start(f32[32,8,128]{2,1,0:T(8,128)} %bitcast.5), calls=%async_computation | async-start | bytes 262144 | tf_op jit(solution)/shard_map/all_to_all | solution.py:441
  67.1 7.5 %copy-start.12 = (s32[7]{0:T(128)S(1)}, s32[7]{0:T(128)}, u32[]{:S(2)}) copy-start(s32[7]{0:T(128)} %constant.160.clone) | copy-start | bytes 88
  69.9 5.0 %collective-permute-start.6 = (f32[56,128]{1,0:T(8,128)S(1)}, f32[56,128]{1,0:T(8,128)S(1)}, u32[]{:S(2)}, u32[]{:S(2)}) collective-permute-start(f32[56,128]{1,0:T(8,128)S(1)} %get-tuple-element.86), channel_id=1, source_target_pairs={{24,0},{0,8},{8,16},{16,24},{25,1},{1,9},{9,17},{17,25},{26,2},{2,... | collective-permute-start | bytes 86024 | tf_op jit(solution)/shard_map/ppermute | solution.py:26
  71.7 3.9 %collective-permute-start.7 = (f32[56,128]{1,0:T(8,128)S(1)}, f32[56,128]{1,0:T(8,128)S(1)}, u32[]{:S(2)}, u32[]{:S(2)}) collective-permute-start(f32[56,128]{1,0:T(8,128)S(1)} %get-tuple-element.87), channel_id=1, source_target_pairs={{16,0},{24,8},{0,16},{8,24},{17,1},{25,9},{1,17},{9,25},{18,2},{26... | collective-permute-start | bytes 86024 | tf_op jit(solution)/shard_map/ppermute | solution.py:26
  73.2 3.9 %collective-permute-start.8 = (f32[56,128]{1,0:T(8,128)S(1)}, f32[56,128]{1,0:T(8,128)S(1)}, u32[]{:S(2)}, u32[]{:S(2)}) collective-permute-start(f32[56,128]{1,0:T(8,128)S(1)} %get-tuple-element.88), channel_id=1, source_target_pairs={{8,0},{16,8},{24,16},{0,24},{9,1},{17,9},{25,17},{1,25},{10,2},{18... | collective-permute-start | bytes 86024 | tf_op jit(solution)/shard_map/ppermute | solution.py:26

commit v4 on v3

--- a/solution.py
+++ b/solution.py
@@ -36,27 +36,23 @@
         out[live] = -freq_count * sign / np.tan(np.pi * k[live] / (2 * freq_count))
         return out
 
-    table = np.zeros((freq_count + 16, 2 * freq_count), np.float32)
-    table[:freq_count, :freq_count] = -(edge(f[:, None] + f[None, :]) + edge(f[None, :] - f[:, None]))
-    w = f * math.pi / freq_count
-    table[freq_count, :freq_count] = (1.0 - 2.0 * (f % 2)) * w
-    high = jnp.asarray(w * w, F32).astype(BF16)
-    low = (jnp.asarray(w * w, F32) - high.astype(F32)).astype(BF16)
-    table = jnp.asarray(table, F32).astype(BF16)
-    table = table.at[freq_count + 1, freq_count:].set(high)
-    return table.at[freq_count + 2, freq_count:].set(low)
+    table = np.zeros((freq_count + 16, freq_count), np.float32)
+    table[:freq_count] = -(edge(f[:, None] + f[None, :]) + edge(f[None, :] - f[:, None]))
+    table[freq_count] = (1.0 - 2.0 * (f % 2)) * f * math.pi / freq_count
+    return jnp.asarray(table, F32).astype(BF16)
 
 
 def low_half(shape):
     return lax.broadcasted_iota(jnp.int32, shape, len(shape) - 1) < shape[-1] // 2
 
 
-def outgoing_kernel(cap, exports_ref, spec_ref, geo_ref, *refs):
+def outgoing_kernel(cap, send_group, exports_ref, spec_ref, geo_ref, *refs):
     outs, rows = refs[:-1], refs[-1]
     stations = spec_ref.shape[1]
     body = cap * stations
     rows[...] = jnp.zeros_like(rows)
-    for h, out in enumerate(outs):
+    for g, out in enumerate(outs):
+        h = send_group(g, lax.axis_index("clu"))
         for c in range(cap):
             event = exports_ref[h, c]
             out[c * stations : (c + 1) * stations, :] = spec_ref[event]
@@ -87,31 +83,51 @@
 
 
 def listed_pairs(ids, batches, da, sq, ea, bp, bb, eb, table, work, store, freq, scale):
-    xs, reals, rm, rs, rt, rz, re = work
+    xs, reals, rm, rs, rt, rb, rz, re = work
     lead = lax.broadcasted_iota(jnp.int32, (8, 1), 0) == 0
+    step = lax.broadcasted_iota(jnp.int32, (8, 1), 0).astype(F32)
     low = low_half((8, 128))
-
-    def split(t, u):
-        code = ids[t * BATCH + u]
-        return code >> 6, code & (PAIR_BASE - 1)
+    unit = (math.pi / freq) ** 2
+
+    def split(t, d):
+        code = ids[t * (BATCH // 2) + d]
+        return code >> 12, ((code >> 6) & 63, code & 63)
 
     def cross_stage(t, slot):
-        for u in range(BATCH):
-            e, j = split(t, u)
-            ar, ai = da[e, :freq, :], da[e, freq:, :]
-            br, bi = bp[j, :freq, :], bp[j, freq:, :]
-            cr = ar * br + ai * bi
-            ci = ai * br - ar * bi
-            both = sq[e] * bb[j]
-            lanes = slice(u * 128, (u + 1) * 128)
-            rows = slice(u * 8, (u + 1) * 8)
-            xs[slot, :freq, lanes] = ci.astype(BF16)
-            xs[slot, freq:, lanes] = both.astype(BF16)
-            reals[slot, :, lanes] = cr.astype(BF16)
-            edge = cr[0:8] * cr[0:8] - ci[0:8] * ci[0:8]
-            rs[slot, rows, :] = fold(both) + jnp.where(lead, edge, 0.0)
-            rt[slot, rows, :] = fold(cr)
-            re[slot, u : u + 1, :] = ea[pl.ds(e, 1), :] * eb[pl.ds(j, 1), :]
+        for d in range(BATCH // 2):
+            j, duo = split(t, d)
+            squares, sums = [[], []], [None, None]
+            for v in range(0, freq, 16):
+                br, bi = bp[j, v : v + 16, :], bp[j, freq + v : freq + v + 16, :]
+                b2 = bb[j, v : v + 16, :]
+                for i, e in enumerate(duo):
+                    ar, ai = da[e, v : v + 16, :], da[e, freq + v : freq + v + 16, :]
+                    cr = ar * br + ai * bi
+                    ci = ai * br - ar * bi
+                    both = sq[e, v : v + 16, :] * b2
+                    u = 2 * d + i
+                    lanes = slice(u * 128, (u + 1) * 128)
+                    xs[slot, v : v + 16, lanes] = ci.astype(BF16)
+                    reals[slot, v : v + 16, lanes] = cr.astype(BF16)
+                    squares[i] += [both[:8], both[8:]]
+                    part = cr[:8] + cr[8:]
+                    sums[i] = part if v == 0 else sums[i] + part
+                    if v == 0:
+                        edge = cr[:8] * cr[:8] - ci[:8] * ci[:8]
+                        rs[slot, u * 8 : u * 8 + 8, :] = jnp.where(lead, edge, 0.0)
+            for i, e in enumerate(duo):
+                u = 2 * d + i
+                rows = slice(u * 8, u * 8 + 8)
+                zero, one, two = squares[i][-1], squares[i][-1], squares[i][-1]
+                for v in range(freq // 8 - 2, 0, -1):
+                    zero = zero + squares[i][v]
+                    one = one + zero
+                    two = two + one
+                zero = zero + squares[i][0]
+                rs[slot, rows, :] += zero
+                rb[slot, rows, :] = unit * (64.0 * (2.0 * two - one) + step * (16.0 * one + step * zero))
+                rt[slot, rows, :] = sums[i]
+                re[slot, u : u + 1, :] = ea[pl.ds(e, 1), :] * eb[pl.ds(j, 1), :]
 
     def moment_stage(slot):
         for start in range(0, BATCH, WIDE):
@@ -128,13 +144,13 @@
         def pick(ref, k):
             return ref[slot, pl.ds(k, 8, stride=8), :]
 
-        moment, total, alternate = pick(rm, 0), pick(rs, 0), pick(rt, 0)
+        moment, total, alternate, bend = pick(rm, 0), pick(rs, 0), pick(rt, 0), pick(rb, 0)
         for k in range(1, 8):
             moment = moment + pick(rm, k)
             total = total + pick(rs, k)
+            bend = bend + pick(rb, k)
             alternate = alternate + pick(rt, k) if k % 2 == 0 else alternate - pick(rt, k)
         tilt = pick(rz, 0)
-        bend = pick(rz, 1) + pick(rz, 2)
         inverse = 1.0 / (re[slot] + 1e-06)
         power = (freq * total - alternate * alternate) * inverse
         rough = (freq * bend - tilt * tilt) * inverse
@@ -142,9 +158,11 @@
         moved = weight * (moment * inverse / (power + 1e-06))
         even = jnp.where(low, weight, pltpu.roll(moved, 64, 1))
         odd = jnp.where(low, pltpu.roll(weight, 64, 1), moved)
-        for u in range(BATCH):
-            e, j = split(t, u)
-            store(e, j, even[u : u + 1], odd[u : u + 1])
+        for d in range(BATCH // 2):
+            j, duo = split(t, d)
+            for i, e in enumerate(duo):
+                u = 2 * d + i
+                store(e, j, even[u : u + 1], odd[u : u + 1])
 
     cross_stage(0, 0)
 
@@ -158,7 +176,7 @@
         finish_stage(2 * i + 1, 1)
 
 
-def local_kernel(freq, events, scale, items, ids, spec_ref, table, out, da, sq, ea, bp, bb, eb, *work):
+def local_kernel(freq, events, scale, batches, ids, spec_ref, table, out, da, sq, ea, bp, bb, eb, *work):
     pairs = events // 2
     prepare(lambda j: spec_ref[j], bp, bb, eb, pairs, freq)
     low = low_half((128, 128))
@@ -184,7 +202,7 @@
         out[pl.ds(2 * j * events + e, 1), :] = jnp.where(row, even, -even)
         out[pl.ds((2 * j + 1) * events + e, 1), :] = jnp.where(row, odd, -odd)
 
-    listed_pairs(ids, items // BATCH, da, sq, ea, bp, bb, eb, table, work, store, freq, scale)
+    listed_pairs(ids, batches, da, sq, ea, bp, bb, eb, table, work, store, freq, scale)
 
 
 def import_kernel(group, freq, events, cap, scale, ids, counts, got_ref, da, sq, ea, table, out, tail, bp, bb, eb, *work):
@@ -197,7 +215,7 @@
         out[pl.ds(e * GROUP_ROWS + 2 * j, 1), :] = even
         out[pl.ds(e * GROUP_ROWS + 2 * j + 1, 1), :] = odd
 
-    batches = (counts[group] + BATCH - 1) // BATCH
+    batches = (counts[group] + BATCH // 2 - 1) // (BATCH // 2)
     listed_pairs(ids.at[group], batches, da, sq, ea, bp, bb, eb, table, work, store, freq, scale)
 
 
@@ -207,10 +225,10 @@
             pltpu.VMEM((pairs, 2 * freq, 128), F32),
             pltpu.VMEM((pairs, freq, 128), F32),
             pltpu.VMEM((-(-pairs // 8) * 8, 128), F32),
-            pltpu.VMEM((2, 2 * freq, BATCH * 128), BF16),
+            pltpu.VMEM((2, freq, BATCH * 128), BF16),
             pltpu.VMEM((2, freq, BATCH * 128), BF16),
         ]
-        + [pltpu.VMEM((2, BATCH * 8, 128), F32)] * 4
+        + [pltpu.VMEM((2, BATCH * 8, 128), F32)] * 5
         + [pltpu.VMEM((2, BATCH, 128), F32)]
     )
 
@@ -331,7 +349,7 @@
     return [pl.BlockSpec(memory_space=pltpu.VMEM)] * n
 
 
-def call(kernel, outs, inputs, scratch=(), specs=None, micros=1.0):
+def call(kernel, outs, inputs, scratch=(), specs=None, micros=1.0, limit=VMEM_LIMIT):
     shapes = [jax.ShapeDtypeStruct(s, t) for s, t in outs]
     return pl.pallas_call(
         kernel,
@@ -339,7 +357,7 @@
         in_specs=specs if specs is not None else vmem(len(inputs)),
         out_specs=vmem(len(outs)),
         scratch_shapes=list(scratch),
-        compiler_params=pltpu.CompilerParams(vmem_limit_bytes=VMEM_LIMIT),
+        compiler_params=pltpu.CompilerParams(vmem_limit_bytes=limit),
         cost_estimate=pl.CostEstimate(flops=int(micros * 1e9), bytes_accessed=1024, transcendentals=0),
     )(*inputs)
 
@@ -359,69 +377,102 @@
     smem = pl.BlockSpec(memory_space=pltpu.SMEM)
     clusters = lax.axis_size("clu")
 
+    paired = clusters == groups + 2 and clusters & (clusters - 1) == 0
+    if paired:
+        masks = [m for m in range(1, clusters) if m != clusters // 2]
+        routes = [[(i, i ^ m) for i in range(clusters)] for m in masks]
+    else:
+        order = sorted(range(groups), key=lambda h: abs(offsets[h]))
+        routes = [[(i, (i + offsets[h]) % clusters) for i in range(clusters)] for h in order]
+
+    def group_of(offset):
+        offset = offset & (clusters - 1)
+        return jnp.where(offset < clusters // 2, offset + half_span - 1, offset - clusters + half_span)
+
+    def send_group(g, p):
+        return group_of((p ^ masks[g]) - p) if paired else order[g]
+
+    def receive_group(g, p):
+        return group_of(p - (p ^ masks[g])) if paired else order[g]
+
+    def receiver(g, p):
+        return p ^ masks[g] if paired else (p + offsets[order[g]]) % clusters
+
     out_rows = cap * stations + 2 * GROUP_ROWS
     outgoing = call(
-        functools.partial(outgoing_kernel, cap),
+        functools.partial(outgoing_kernel, cap, send_group),
         [((out_rows, 128), BF16)] * groups,
         (exports, spectra, partials),
         scratch=[pltpu.VMEM((2 * GROUP_ROWS, 128), F32)],
         specs=[smem] + vmem(2),
         micros=2.0,
-    )
-    order = sorted(range(groups), key=lambda h: abs(offsets[h]))
+        limit=60 * 1024 * 1024,
+    )
     got = [None] * groups
-    for h in order:
-        got[h] = shifted(outgoing[h], "clu", offsets[h])
-
-    codes = [e * PAIR_BASE + j for e in range(events) for j in range(e // 2, events // 2)]
-    items = -(-len(codes) // (2 * BATCH)) * 2 * BATCH
-    codes = codes + [0] * (items + 2 * BATCH - len(codes))
-    natural, got[order[0]] = lax.optimization_barrier((spectra, got[order[0]]))
+    for g in [0] + list(range(groups - 1, 0, -1)):
+        got[g] = lax.ppermute(outgoing[g], "clu", routes[g])
+    me = lax.axis_index("clu").astype(jnp.int32)
+    sent = jnp.stack([jnp.asarray(send_group(g, me), jnp.int32) for g in range(groups)])
+    came = jnp.stack([jnp.asarray(receive_group(g, me), jnp.int32) for g in range(groups)])
+
+    duos = [j << 12 | e << 6 | e + 1 for j in range(events // 2) for e in range(0, 2 * j + 2, 2)]
+    batches = -(-len(duos) // BATCH) * 2
+    duos = duos + [1] * ((batches + 2) * (BATCH // 2) - len(duos))
+    natural, got[0] = lax.optimization_barrier((spectra, got[0]))
     local, dup, square, energy = call(
-        functools.partial(local_kernel, freq, events, scale, items),
+        functools.partial(local_kernel, freq, events, scale, batches),
         [
             ((events * events, 128), F32),
             ((events, 128, 128), F32),
             ((events, freq, 128), F32),
             ((events, 128), F32),
         ],
-        (jnp.asarray(codes, jnp.int32), natural.reshape(events // 2, 2 * stations, two_freq), table),
+        (jnp.asarray(duos, jnp.int32), natural.reshape(events // 2, 2 * stations, two_freq), table),
         scratch=weight_scratch(events // 2, freq),
         specs=[smem] + vmem(2),
         micros=8.0,
     )
 
     far = jnp.maximum(pair_list - events, 0)
-    named = jnp.where(pair_list < events, -1, (far // cap) * half + (far % cap) // 2)
+    far_group = far // cap
+    arrival = jnp.sum(jnp.where(far_group[:, :, None] == came[None, None, :], jnp.arange(groups, dtype=jnp.int32), 0), axis=2)
+    entry = far % cap
+    named = jnp.where(pair_list < events, -1, arrival * half + entry // 2)
     wanted = jnp.any(named[:, :, None] == jnp.arange(groups * half, dtype=jnp.int32)[None, None, :], axis=1)
-    wanted = wanted.reshape(events, groups, half).transpose(1, 0, 2).reshape(groups, events * half)
-    item = np.arange(events * half)
-    before = jnp.asarray(item[:, None] < item[None, :], BF16)
-    rank = jnp.dot(wanted.astype(BF16), before, preferred_element_type=F32).astype(jnp.int32)
-    item_code = jnp.asarray((item // half) * PAIR_BASE + item % half, jnp.int32)
-    spot = jnp.where(wanted, rank, -1)
-    longest = events * half + 3 * BATCH
+    wanted = wanted.astype(F32).T.reshape(groups, half, events)
+    ranks = np.arange(events)
+    rank = jnp.einsum("gje,ef->gjf", wanted, jnp.asarray(ranks[:, None] < ranks[None, :], F32))
+    rounded = jnp.ceil(jnp.sum(wanted, axis=2) * 0.5)
+    ranks = np.arange(half)
+    start = jnp.sum(rounded[:, :, None] * jnp.asarray(ranks[:, None] < ranks[None, :], F32)[None], axis=1)
+    rank = rank.astype(jnp.int32)
+    spot = jnp.where(wanted > 0, start.astype(jnp.int32)[:, :, None] + (rank >> 1), -1).reshape(groups, half * events)
+    event_ids = jnp.arange(events, dtype=jnp.int32)[None, None, :]
+    pair_ids = jnp.arange(half, dtype=jnp.int32)[None, :, None]
+    code = jnp.where(rank & 1 == 0, (pair_ids << 12) + (event_ids << 6), event_ids).reshape(groups, half * events)
+    longest = half * events // 2 + 3 * BATCH // 2
     lists = jnp.sum(
-        jnp.where(spot[:, None, :] == jnp.arange(longest, dtype=jnp.int32)[None, :, None], item_code[None, None, :], 0),
-        axis=2,
-    ).astype(jnp.int32)
-    counts = jnp.sum(wanted.astype(jnp.int32), axis=1)
-
-    column = jnp.where(pair_list < events, pair_list, events + GROUP_ROWS * (far // cap) + far % cap)
+        jnp.where(spot[:, None, :] == jnp.arange(longest, dtype=jnp.int32)[None, :, None], code[:, None, :], 0), axis=2
+    )
+    counts = jnp.sum(rounded, axis=1).astype(jnp.int32)
+
+    column = jnp.where(pair_list < events, pair_list, events + GROUP_ROWS * arrival + entry)
     column = jnp.pad(column, ((0, 0), (0, SLOT_ROWS - slots)), constant_values=-1).reshape(-1)
     cand_ids = jnp.arange(cands, dtype=jnp.int32)
     hot = (column[:, None] == cand_ids[None, :]).astype(BF16)
     hot_turned = (cand_ids[:, None] == column[None, :]).astype(BF16)
     mask = station_mask.transpose(1, 0, 2).reshape(slots * events, stations)
     owner_rows = [jnp.asarray(np.where(np.arange(cands) < events, np.arange(cands), -1), jnp.int32)]
-    for h in range(groups):
-        start = events + GROUP_ROWS * h
-        owner_rows.append(jnp.pad(exports[h], (start, cands - start - cap), constant_values=-1))
+    hot_sent = sent[:, None] == jnp.arange(groups, dtype=jnp.int32)[None, :]
+    rows_sent = jnp.sum(jnp.where(hot_sent[:, :, None], exports[None], 0), axis=1)
+    for g in range(groups):
+        start = events + GROUP_ROWS * g
+        owner_rows.append(jnp.pad(rows_sent[g], (start, cands - start - cap), constant_values=-1))
     owners = jnp.concatenate(owner_rows)[:, None] == (jnp.arange(128, dtype=jnp.int32) % events)[None, :]
     owners = owners.astype(F32)
 
     tables, tails = [None] * groups, [None] * groups
-    for h in order:
+    for h in range(groups):
         tables[h], tails[h] = call(
             functools.partial(import_kernel, h, freq, events, cap, scale),
             [((events * GROUP_ROWS, 128), F32), ((2 * GROUP_ROWS, 128), BF16)],
@@ -452,11 +503,11 @@
         micros=3.0,
     )
     shares = [shares[0]] + [shifted(shares[d], "sta", d) for d in range(1, 4)]
-    sources = (lax.axis_index("clu") + jnp.asarray([0] + offsets, jnp.int32)) % clusters
+    sources = jnp.stack([me] + [jnp.asarray(receiver(g, me), jnp.int32) for g in range(groups)])
     normal, right = call(
         functools.partial(total_kernel, groups, events, slots),
         [((4, events, slots + 1), F32), ((1, events), F32)],
-        (sources.astype(jnp.int32), *shares, terms, owners),
+        (sources, *shares, terms, owners),
         specs=[smem] + vmem(6),
     )
     return (normal.transpose(0, 2, 1), right)

time: 78.5 us -> 67.6 us (0.86); the launches traced: 78.7 us -> 67 us
  starting transfers between devices: 27.9 us -> 17.4 us
  local copies, waits for them, and re-layouts: 3.31 us -> 1.06 us
    all_to_all x1, starting transfers between devices: 14.5 us -> 3.28 us  [on_device(): lax.all_to_all(terms.reshape(4 * clusters, 8, 128), ('sta', 'clu'), split...]
    ppermute x0 -> x6, starting transfers between devices: none -> 9.35 us  [on_device(): got[g] = lax.ppermute(outgoing[g], 'clu', routes[g])]
    ppermute x9 -> x3, starting transfers between devices: 13.5 us -> 4.75 us  [shifted(): return lax.ppermute(block, axis, route)]
    unnamed x34 -> x26, local copies, waits for them, and re-layouts: 2.94 us -> 0.46 us
    ppermute x9 -> x3, waiting for transfers between devices: 2.41 us -> 2.13 us  [shifted(): return lax.ppermute(block, axis, route)]
  transfers between devices with their start and end apart: 10 -> 10, of which waited for: 3 -> 2; matrix products, arithmetic and copies ran while one was open for 4% -> 6% of each run, Pallas kernels for 41% -> 47%
where the time goes in v4:
time: 67.6 us; the launch traced here: 67 us
  Pallas kernels  42.5 us (63%)
  starting transfers between devices  17.4 us (26%)
  other arithmetic  2.59 us (4%)
  waiting for transfers between devices  2.16 us (3%)
  between operations  1.11 us (2%)
  local copies, waits for them, and re-layouts  1.06 us (2%)
    pallas_call x11, Pallas kernels, call(): pl.pallas_call(kernel, out_shape=shapes, in_specs=specs if specs is not N...  42.5 us
    ppermute x6, starting transfers between devices, on_device(): got[g] = lax.ppermute(outgoing[g], 'clu', routes[g])  9.35 us
    ppermute x3, starting transfers between devices, shifted(): return lax.ppermute(block, axis, route)  4.75 us
    all_to_all x1, starting transfers between devices, on_device(): lax.all_to_all(terms.reshape(4 * clusters, 8, 128), ('sta', 'clu'), split...  3.28 us
    ppermute x3, waiting for transfers between devices, shifted(): return lax.ppermute(block, axis, route)  2.13 us
  transfers between devices with their start and end apart: 10, of which 2 were waited for; matrix products, arithmetic and copies ran while one was open for 6% of the time, Pallas kernels for 47%

profile of v4, /device:TPU:0, one launch (start us, length us, event | category | flops | bytes accessed | tf_op | source)
XLA Modules:
  0.0 67.0 jit_solution(17005910172156511890)
XLA Ops:
  0.7 2.3 %shard_map.113 = (bf16[800,128]{1,0:T(8,128)(2,1)}, bf16[800,128]{1,0:T(8,128)(2,1)}, bf16[800,128]{1,0:T(8,128)(2,1)}, bf16[800,128]{1,0:T(8,128)(2,1)}, bf16[8...) custom-call(s32[6,12]{1,0:T(8,128)} %exports_ref.1, bf16[32,64,128]{2,1,0:T(8,128)(2,1)} %spec_ref.1, bf16[32,4,64]{2,1,0:T(4,128)(2,1)} %partials.3), custom_call_target="tpu_custom_call" | custom-call | flops 2000000000 | bytes 1024 | tf_op jit(solution)/shard_map/pallas_call | solution.py:354
  3.1 0.5 collective-permute-start
  3.5 4.7 %collective-permute-start.5 = (bf16[800,128]{1,0:T(8,128)(2,1)}, bf16[800,128]{1,0:T(8,128)(2,1)S(1)}, u32[]{:S(2)}, u32[]{:S(2)}) collective-permute-start(bf16[800,128]{1,0:T(8,128)(2,1)} %get-tuple-element.51), channel_id=1, source_target_pairs={{0,7},{1,6},{2,5},{3,4},{4,3},{5,2},{6,1},{7,0},{8,15},{9,14},{10,... | collective-permute-start | bytes 614408 | tf_op jit(solution)/shard_map/ppermute | solution.py:413
  8.2 0.3 collective-permute-start.3
  8.6 3.8 %collective-permute-start.2 = (bf16[800,128]{1,0:T(8,128)(2,1)}, bf16[800,128]{1,0:T(8,128)(2,1)S(1)}, u32[]{:S(2)}, u32[]{:S(2)}) collective-permute-start(bf16[800,128]{1,0:T(8,128)(2,1)} %get-tuple-element.45), channel_id=1, source_target_pairs={{0,3},{1,2},{2,1},{3,0},{4,7},{5,6},{6,5},{7,4},{8,11},{9,10},{10,... | collective-permute-start | bytes 614408 | tf_op jit(solution)/shard_map/ppermute | solution.py:413
  12.4 0.1 stack.80
  12.5 0.1 select_reduce_fusion.1
  12.6 0.7 %fusion.2 = pred[32,36]{0,1:T(8,128)(4,1)S(1)} fusion(s32[32,50]{1,0:T(8,128)S(1)} %get-tuple-element.68), kind=kLoop, calls=%fused_computation.8 | loop fusion | flops 114048 | bytes 7552 | tf_op jit(solution)/shard_map/reduce_or | solution.py:441
  13.3 0.1 convert_reduce_fusion
  13.5 0.1 eq.112
  13.6 0.3 fusion.hot
  13.9 0.1 fusion.1.hot_turned
  14.1 0.1 ceil.11
  14.2 0.1 multiply_reduce_fusion
  14.3 0.1 broadcast_add_fusion
  14.4 0.1 add_select_fusion
  14.5 0.1 broadcast_in_dim.87
  14.6 0.1 eq.122
  14.7 0.1 reduce_sum.58
  14.8 0.1 stack.87
  14.9 0.1 iota_compare_fusion.4
  15.0 0.1 select_reduce_fusion.2
  15.1 0.1 constant_dynamic-update-slice_fusion.5
  15.2 0.1 constant_dynamic-update-slice_fusion.4
  15.3 0.1 constant_dynamic-update-slice_fusion.3
  15.4 0.1 constant_dynamic-update-slice_fusion.2
  15.4 0.1 constant_dynamic-update-slice_fusion.1
  15.5 0.1 constant_dynamic-update-slice_fusion
  15.6 0.5 select_reduce_fusion.ids
  16.1 0.1 collective-permute-start.1
  16.2 10.5 %shard_map.114 = (f32[1024,128]{1,0:T(8,128)S(1)}, f32[32,128,128]{2,1,0:T(8,128)S(1)}, f32[32,64,128]{2,1,0:T(8,128)S(1)}, f32[32,128]{1,0:T(8,128)S(1)}) custom-call(s32[144]{0:T(256)S(1)} %copy-done.4, bf16[16,128,128]{2,1,0:T(8,128)(2,1)S(1)} %bitcast.45, bf16[80,64]{1,0:T(8,128)(2,1)S(1)} %copy-done.3), custom_call_target="tpu_custom_call" | custom-call | flops 8000000000 | bytes 1024 | tf_op jit(solution)/shard_map/pallas_call | solution.py:354
  26.7 3.6 %shard_map.115 = (f32[512,128]{1,0:T(8,128)S(1)}, bf16[32,128]{1,0:T(8,128)(2,1)S(1)}) custom-call(s32[6,108]{1,0:T(8,128)S(1)} %select_reduce_fusion.ids, s32[6]{0:T(128)S(1)} %convert_element_type.35.counts, bf16[800,128]{1,0:T(8,128)(2,1)S(1)} %collective-permute-done.got_ref, f32[32,128,128]{2,1,0:T(8,128)S(1)} %get-tuple-element.39.da, ...), custom_call_target="tpu_custom_call" | custom-call | flops 3000000000 | bytes 1024 | tf_op jit(solution)/shard_map/pallas_call | solution.py:354
  30.4 3.6 %shard_map.120 = (f32[512,128]{1,0:T(8,128)S(1)}, bf16[32,128]{1,0:T(8,128)(2,1)S(1)}) custom-call(s32[6,108]{1,0:T(8,128)S(1)} %select_reduce_fusion.ids, s32[6]{0:T(128)S(1)} %convert_element_type.35.counts, bf16[800,128]{1,0:T(8,128)(2,1)S(1)} %collective-permute-done.5.got_ref, f32[32,128,128]{2,1,0:T(8,128)S(1)} %get-tuple-element.39.da, ...), custom_call_target="tpu_custom_call" | custom-call | flops 3000000000 | bytes 1024 | tf_op jit(solution)/shard_map/pallas_call | solution.py:354
  34.0 3.6 %shard_map.119 = (f32[512,128]{1,0:T(8,128)S(1)}, bf16[32,128]{1,0:T(8,128)(2,1)S(1)}) custom-call(s32[6,108]{1,0:T(8,128)S(1)} %select_reduce_fusion.ids, s32[6]{0:T(128)S(1)} %convert_element_type.35.counts, bf16[800,128]{1,0:T(8,128)(2,1)S(1)} %collective-permute-done.4.got_ref, f32[32,128,128]{2,1,0:T(8,128)S(1)} %get-tuple-element.39.da, ...), custom_call_target="tpu_custom_call" | custom-call | flops 3000000000 | bytes 1024 | tf_op jit(solution)/shard_map/pallas_call | solution.py:354
  37.6 3.6 %shard_map.118 = (f32[512,128]{1,0:T(8,128)S(1)}, bf16[32,128]{1,0:T(8,128)(2,1)S(1)}) custom-call(s32[6,108]{1,0:T(8,128)S(1)} %select_reduce_fusion.ids, s32[6]{0:T(128)S(1)} %convert_element_type.35.counts, bf16[800,128]{1,0:T(8,128)(2,1)S(1)} %collective-permute-done.3.got_ref, f32[32,128,128]{2,1,0:T(8,128)S(1)} %get-tuple-element.39.da, ...), custom_call_target="tpu_custom_call" | custom-call | flops 3000000000 | bytes 1024 | tf_op jit(solution)/shard_map/pallas_call | solution.py:354
  41.2 3.6 %shard_map.117 = (f32[512,128]{1,0:T(8,128)S(1)}, bf16[32,128]{1,0:T(8,128)(2,1)S(1)}) custom-call(s32[6,108]{1,0:T(8,128)S(1)} %select_reduce_fusion.ids, s32[6]{0:T(128)S(1)} %convert_element_type.35.counts, bf16[800,128]{1,0:T(8,128)(2,1)S(1)} %collective-permute-done.2.got_ref, f32[32,128,128]{2,1,0:T(8,128)S(1)} %get-tuple-element.39.da, ...), custom_call_target="tpu_custom_call" | custom-call | flops 3000000000 | bytes 1024 | tf_op jit(solution)/shard_map/pallas_call | solution.py:354
  44.8 3.6 %shard_map.116 = (f32[512,128]{1,0:T(8,128)S(1)}, bf16[32,128]{1,0:T(8,128)(2,1)S(1)}) custom-call(s32[6,108]{1,0:T(8,128)S(1)} %select_reduce_fusion.ids, s32[6]{0:T(128)S(1)} %convert_element_type.35.counts, bf16[800,128]{1,0:T(8,128)(2,1)S(1)} %collective-permute-done.1.got_ref, f32[32,128,128]{2,1,0:T(8,128)S(1)} %get-tuple-element.39.da, ...), custom_call_target="tpu_custom_call" | custom-call | flops 3000000000 | bytes 1024 | tf_op jit(solution)/shard_map/pallas_call | solution.py:354
  48.5 3.7 %shard_map.121 = (bf16[2048,128]{1,0:T(8,128)(2,1)S(1)}, f32[4,8,8,128]{3,2,1,0:T(8,128)}, bf16[128,256]{1,0:T(8,128)(2,1)S(1)}) custom-call(bf16[2048,128]{1,0:T(8,128)(2,1)S(1)} %fusion.hot, bf16[128,2048]{1,0:T(8,128)(2,1)S(1)} %fusion.1.hot_turned, s32[1600,64]{1,0:T(8,128)S(1)} %bitcast.44, bf16[32,4,64]{2,1,0:T(4,128)(2,1)S(1)} %copy-done.2, ...), custom_call_target="tpu_custom_call" | custom-call | flops 2000000000 | bytes 1024 | tf_op jit(solution)/shard_map/pallas_call | solution.py:354
  52.1 3.3 %all-to-all-start = ((f32[32,8,128]{2,1,0:T(8,128)}), f32[32,8,128]{2,1,0:T(8,128)S(1)}, u32[]{:S(2)}, u32[]{:S(2)}) async-start(f32[32,8,128]{2,1,0:T(8,128)} %bitcast.19), calls=%async_computation | async-start | bytes 262144 | tf_op jit(solution)/shard_map/all_to_all | solution.py:492
  55.4 2.7 %shard_map.122 = (f32[56,128]{1,0:T(8,128)S(1)}, f32[56,128]{1,0:T(8,128)S(1)}, f32[56,128]{1,0:T(8,128)S(1)}, f32[56,128]{1,0:T(8,128)S(1)}) custom-call(s32[1]{0:T(128)} %bitcast.7.place, bf16[2048,128]{1,0:T(8,128)(2,1)S(1)} %fusion.hot, bf16[2048,128]{1,0:T(8,128)(2,1)S(1)} %get-tuple-element.59.slots, bf16[128,256]{1,0:T(8,128)(2,1)S(1)} %get-tuple-element.60.geo, ...), custom_call_target="tpu_custom_call" | custom-call | flops 3000000000 | bytes 1024 | tf_op jit(solution)/shard_map/pallas_call | solution.py:354
  58.2 1.8 %collective-permute-start.6 = (f32[56,128]{1,0:T(8,128)S(1)}, f32[56,128]{1,0:T(8,128)S(1)}, u32[]{:S(2)}, u32[]{:S(2)}) collective-permute-start(f32[56,128]{1,0:T(8,128)S(1)} %get-tuple-element.62), channel_id=1, source_target_pairs={{24,0},{0,8},{8,16},{16,24},{25,1},{1,9},{9,17},{17,25},{26,2},{2,... | collective-permute-start | bytes 86024 | tf_op jit(solution)/shard_map/ppermute | solution.py:26
  60.0 1.5 %collective-permute-start.7 = (f32[56,128]{1,0:T(8,128)S(1)}, f32[56,128]{1,0:T(8,128)S(1)}, u32[]{:S(2)}, u32[]{:S(2)}) collective-permute-start(f32[56,128]{1,0:T(8,128)S(1)} %get-tuple-element.63), channel_id=1, source_target_pairs={{16,0},{24,8},{0,16},{8,24},{17,1},{25,9},{1,17},{9,25},{18,2},{26... | collective-permute-start | bytes 86024 | tf_op jit(solution)/shard_map/ppermute | solution.py:26
  61.5 1.5 %collective-permute-start.8 = (f32[56,128]{1,0:T(8,128)S(1)}, f32[56,128]{1,0:T(8,128)S(1)}, u32[]{:S(2)}, u32[]{:S(2)}) collective-permute-start(f32[56,128]{1,0:T(8,128)S(1)} %get-tuple-element.64), channel_id=1, source_target_pairs={{8,0},{16,8},{24,16},{0,24},{9,1},{17,9},{25,17},{1,25},{10,2},{18... | collective-permute-start | bytes 86024 | tf_op jit(solution)/shard_map/ppermute | solution.py:26
  62.9 0.2 compare_convert_fusion.owners
  63.1 0.1 stack.73.clusters
  63.2 0.7 %collective-permute-done.7.two = f32[56,128]{1,0:T(8,128)S(1)} collective-permute-done((f32[56,128]{1,0:T(8,128)S(1)}, f32[56,128]{1,0:T(8,128)S(1)}, u32[]{:S(2)}, u32[]{:S(2)}) %collective-permute-start.7) | collective-permute-done | bytes 28704 | tf_op jit(solution)/shard_map/ppermute | solution.py:26
  63.9 1.4 %collective-permute-done.8.three = f32[56,128]{1,0:T(8,128)S(1)} collective-permute-done((f32[56,128]{1,0:T(8,128)S(1)}, f32[56,128]{1,0:T(8,128)S(1)}, u32[]{:S(2)}, u32[]{:S(2)}) %collective-permute-start.8) | collective-permute-done | bytes 28704 | tf_op jit(solution)/shard_map/ppermute | solution.py:26
  65.3 1.6 %shard_map.123 = (f32[4,32,51]{2,1,0:T(8,128)}, f32[1,32]{1,0:T(1,128)}) custom-call(s32[7]{0:T(128)S(1)} %stack.73.clusters, f32[56,128]{1,0:T(8,128)S(1)} %get-tuple-element.61.own, f32[56,128]{1,0:T(8,128)S(1)} %collective-permute-done.6.one, f32[56,128]{1,0:T(8,128)S(1)} %collective-permute-done.7.two, f32[56,128]{1,0:T(8,128)S(1)} %collective-permute-done.8.three, ...), custom_call_target="tpu_custom_call" | custom-call | flops 1000000000 | bytes 1024 | tf_op jit(solution)/shard_map/pallas_call | solution.py:354
  (43 shorter events, 0.2 us)
Async XLA Ops:
  0.6 13.5 %copy-start.6 = (f32[6,6]{1,0:T(8,128)S(1)}, f32[6,6]{1,0:T(8,128)}, u32[]{:S(2)}) copy-start(f32[6,6]{1,0:T(8,128)} %constant.147.clone) | copy-start | bytes 436
  0.6 13.7 %copy-start.8 = (bf16[32,32,1]{1,0,2:T(8,128)(2,1)S(1)}, bf16[32,32,1]{1,0,2:T(8,128)(2,1)}, u32[]{:S(2)}) copy-start(bf16[32,32,1]{1,0,2:T(8,128)(2,1)} %constant.201) | copy-start | bytes 6148
  0.7 14.5 %copy-start.9 = (s32[128]{0:T(128)S(1)}, s32[128]{0:T(128)}, u32[]{:S(2)}) copy-start(s32[128]{0:T(128)} %constant.148.clone) | copy-start | bytes 1540
  0.7 15.5 %copy-start.3 = (bf16[80,64]{1,0:T(8,128)(2,1)S(1)}, bf16[80,64]{1,0:T(8,128)(2,1)}, u32[]{:S(2)}) copy-start(bf16[80,64]{1,0:T(8,128)(2,1)} %constant.164.table) | copy-start | bytes 30724
  0.7 15.5 %copy-start.4 = (s32[144]{0:T(256)S(1)}, s32[144]{0:T(256)}, u32[]{:S(2)}) copy-start(s32[144]{0:T(256)} %constant.145.clone.ids) | copy-start | bytes 1732
  0.7 15.5 %copy-start.1 = (bf16[32,64,128]{2,1,0:T(8,128)(2,1)S(1)}, bf16[32,64,128]{2,1,0:T(8,128)(2,1)}, u32[]{:S(2)}) copy-start(bf16[32,64,128]{2,1,0:T(8,128)(2,1)} %spec_ref.1) | copy-start | bytes 1572868
  0.7 14.3 %copy-start.7 = (s32[6,12]{1,0:T(8,128)S(1)}, s32[6,12]{1,0:T(8,128)}, u32[]{:S(2)}) copy-start(s32[6,12]{1,0:T(8,128)} %exports_ref.1) | copy-start | bytes 868
  0.7 11.6 %copy-start.5 = (s32[32,50]{1,0:T(8,128)S(1)}, s32[32,50]{1,0:T(8,128)}, u32[]{:S(2)}) copy-start(s32[32,50]{1,0:T(8,128)} %param.12) | copy-start | bytes 19204
  3.1 13.0 %collective-permute-start = (bf16[800,128]{1,0:T(8,128)(2,1)}, bf16[800,128]{1,0:T(8,128)(2,1)S(1)}, u32[]{:S(2)}, u32[]{:S(2)}) collective-permute-start(bf16[800,128]{1,0:T(8,128)(2,1)} %get-tuple-element.35), channel_id=1, source_target_pairs={{0,1},{1,0},{2,3},{3,2},{4,5},{5,4},{6,7},{7,6},{8,9},{9,8},{10,11... | collective-permute-start | bytes 614408 | tf_op jit(solution)/shard_map/ppermute | solution.py:413
  3.5 26.8 %collective-permute-start.5 = (bf16[800,128]{1,0:T(8,128)(2,1)}, bf16[800,128]{1,0:T(8,128)(2,1)S(1)}, u32[]{:S(2)}, u32[]{:S(2)}) collective-permute-start(bf16[800,128]{1,0:T(8,128)(2,1)} %get-tuple-element.51), channel_id=1, source_target_pairs={{0,7},{1,6},{2,5},{3,4},{4,3},{5,2},{6,1},{7,0},{8,15},{9,14},{10,... | collective-permute-start | bytes 614408 | tf_op jit(solution)/shard_map/ppermute | solution.py:413
  8.2 25.7 %collective-permute-start.4 = (bf16[800,128]{1,0:T(8,128)(2,1)}, bf16[800,128]{1,0:T(8,128)(2,1)S(1)}, u32[]{:S(2)}, u32[]{:S(2)}) collective-permute-start(bf16[800,128]{1,0:T(8,128)(2,1)} %get-tuple-element.49), channel_id=1, source_target_pairs={{0,6},{1,7},{2,4},{3,5},{4,2},{5,3},{6,0},{7,1},{8,14},{9,15},{10,... | collective-permute-start | bytes 614408 | tf_op jit(solution)/shard_map/ppermute | solution.py:413
  8.2 29.3 %collective-permute-start.3 = (bf16[800,128]{1,0:T(8,128)(2,1)}, bf16[800,128]{1,0:T(8,128)(2,1)S(1)}, u32[]{:S(2)}, u32[]{:S(2)}) collective-permute-start(bf16[800,128]{1,0:T(8,128)(2,1)} %get-tuple-element.47), channel_id=1, source_target_pairs={{0,5},{1,4},{2,7},{3,6},{4,1},{5,0},{6,3},{7,2},{8,13},{9,12},{10,... | collective-permute-start | bytes 614408 | tf_op jit(solution)/shard_map/ppermute | solution.py:413
  8.6 32.6 %collective-permute-start.2 = (bf16[800,128]{1,0:T(8,128)(2,1)}, bf16[800,128]{1,0:T(8,128)(2,1)S(1)}, u32[]{:S(2)}, u32[]{:S(2)}) collective-permute-start(bf16[800,128]{1,0:T(8,128)(2,1)} %get-tuple-element.45), channel_id=1, source_target_pairs={{0,3},{1,2},{2,1},{3,0},{4,7},{5,6},{6,5},{7,4},{8,11},{9,10},{10,... | collective-permute-start | bytes 614408 | tf_op jit(solution)/shard_map/ppermute | solution.py:413
  16.1 28.7 %collective-permute-start.1 = (bf16[800,128]{1,0:T(8,128)(2,1)}, bf16[800,128]{1,0:T(8,128)(2,1)S(1)}, u32[]{:S(2)}, u32[]{:S(2)}) collective-permute-start(bf16[800,128]{1,0:T(8,128)(2,1)} %get-tuple-element.43), channel_id=1, source_target_pairs={{0,2},{1,3},{2,0},{3,1},{4,6},{5,7},{6,4},{7,5},{8,10},{9,11},{10,... | collective-permute-start | bytes 614408 | tf_op jit(solution)/shard_map/ppermute | solution.py:413
  44.8 3.6 %copy-start = (s32[32,50,64]{2,0,1:T(8,128)S(1)}, s32[32,50,64]{2,0,1:T(8,128)}, u32[]{:S(2)}) copy-start(s32[32,50,64]{2,0,1:T(8,128)} %param.13) | copy-start | bytes 1228804
  44.8 3.6 %copy-start.2 = (bf16[32,4,64]{2,1,0:T(4,128)(2,1)S(1)}, bf16[32,4,64]{2,1,0:T(4,128)(2,1)}, u32[]{:S(2)}) copy-start(bf16[32,4,64]{2,1,0:T(4,128)(2,1)} %partials.3) | copy-start | bytes 49156
  52.1 13.2 %all-to-all-start = ((f32[32,8,128]{2,1,0:T(8,128)}), f32[32,8,128]{2,1,0:T(8,128)S(1)}, u32[]{:S(2)}, u32[]{:S(2)}) async-start(f32[32,8,128]{2,1,0:T(8,128)} %bitcast.19), calls=%async_computation | async-start | bytes 262144 | tf_op jit(solution)/shard_map/all_to_all | solution.py:492
  58.2 5.0 %collective-permute-start.6 = (f32[56,128]{1,0:T(8,128)S(1)}, f32[56,128]{1,0:T(8,128)S(1)}, u32[]{:S(2)}, u32[]{:S(2)}) collective-permute-start(f32[56,128]{1,0:T(8,128)S(1)} %get-tuple-element.62), channel_id=1, source_target_pairs={{24,0},{0,8},{8,16},{16,24},{25,1},{1,9},{9,17},{17,25},{26,2},{2,... | collective-permute-start | bytes 86024 | tf_op jit(solution)/shard_map/ppermute | solution.py:26
  60.0 3.9 %collective-permute-start.7 = (f32[56,128]{1,0:T(8,128)S(1)}, f32[56,128]{1,0:T(8,128)S(1)}, u32[]{:S(2)}, u32[]{:S(2)}) collective-permute-start(f32[56,128]{1,0:T(8,128)S(1)} %get-tuple-element.63), channel_id=1, source_target_pairs={{16,0},{24,8},{0,16},{8,24},{17,1},{25,9},{1,17},{9,25},{18,2},{26... | collective-permute-start | bytes 86024 | tf_op jit(solution)/shard_map/ppermute | solution.py:26
  61.5 3.9 %collective-permute-start.8 = (f32[56,128]{1,0:T(8,128)S(1)}, f32[56,128]{1,0:T(8,128)S(1)}, u32[]{:S(2)}, u32[]{:S(2)}) collective-permute-start(f32[56,128]{1,0:T(8,128)S(1)} %get-tuple-element.64), channel_id=1, source_target_pairs={{8,0},{16,8},{24,16},{0,24},{9,1},{17,9},{25,17},{1,25},{10,2},{18... | collective-permute-start | bytes 86024 | tf_op jit(solution)/shard_map/ppermute | solution.py:26

commit v5 on v4

--- a/solution.py
+++ b/solution.py
@@ -16,14 +16,8 @@
 GROUP_ROWS = 16
 BATCH = 8
 WIDE = 4
-PAIR_BASE = 64
-UNROLL = 4
-
-
-def shifted(block, axis, distance):
-    devices = range(lax.axis_size(axis))
-    route = [((i - distance) % len(devices), i) for i in devices]
-    return lax.ppermute(block, axis, route)
+UNROLL = 8
+STAGES = 2
 
 
 def moment_table(freq_count):
@@ -91,11 +85,11 @@
 
     def split(t, d):
         code = ids[t * (BATCH // 2) + d]
-        return code >> 12, ((code >> 6) & 63, code & 63)
+        return (code >> 12) & 31, code >> 17, ((code >> 6) & 63, code & 63)
 
     def cross_stage(t, slot):
         for d in range(BATCH // 2):
-            j, duo = split(t, d)
+            j, _, duo = split(t, d)
             squares, sums = [[], []], [None, None]
             for v in range(0, freq, 16):
                 br, bi = bp[j, v : v + 16, :], bp[j, freq + v : freq + v + 16, :]
@@ -158,22 +152,29 @@
         moved = weight * (moment * inverse / (power + 1e-06))
         even = jnp.where(low, weight, pltpu.roll(moved, 64, 1))
         odd = jnp.where(low, pltpu.roll(weight, 64, 1), moved)
+        return even, odd
+
+    def put(t, even, odd):
         for d in range(BATCH // 2):
-            j, duo = split(t, d)
+            _, column, duo = split(t, d)
             for i, e in enumerate(duo):
                 u = 2 * d + i
-                store(e, j, even[u : u + 1], odd[u : u + 1])
+                store(e, column, even[u : u + 1], odd[u : u + 1])
 
     cross_stage(0, 0)
+    moment_stage(0)
+    cross_stage(1, 1)
 
     @pl.loop(0, (batches + 1) // 2)
     def _(i):
-        cross_stage(2 * i + 1, 1)
-        moment_stage(0)
-        finish_stage(2 * i, 0)
+        first = finish_stage(2 * i, 0)
         cross_stage(2 * i + 2, 0)
         moment_stage(1)
-        finish_stage(2 * i + 1, 1)
+        second = finish_stage(2 * i + 1, 1)
+        cross_stage(2 * i + 3, 1)
+        moment_stage(0)
+        put(2 * i, *first)
+        put(2 * i + 1, *second)
 
 
 def local_kernel(freq, events, scale, batches, ids, spec_ref, table, out, da, sq, ea, bp, bb, eb, *work):
@@ -196,27 +197,33 @@
     ea[pl.ds(1, pairs, stride=2), :] = jnp.where(low, other, energy)
     row = low_half((1, 128))
 
-    def store(e, j, even, odd):
-        out[pl.ds(e * events + 2 * j, 1), :] = even
-        out[pl.ds(e * events + 2 * j + 1, 1), :] = odd
-        out[pl.ds(2 * j * events + e, 1), :] = jnp.where(row, even, -even)
-        out[pl.ds((2 * j + 1) * events + e, 1), :] = jnp.where(row, odd, -odd)
+    def store(e, column, even, odd):
+        out[pl.ds(e * events + column, 1), :] = even
+        out[pl.ds(e * events + column + 1, 1), :] = odd
+        out[pl.ds(column * events + e, 1), :] = jnp.where(row, even, -even)
+        out[pl.ds((column + 1) * events + e, 1), :] = jnp.where(row, odd, -odd)
 
     listed_pairs(ids, batches, da, sq, ea, bp, bb, eb, table, work, store, freq, scale)
 
 
-def import_kernel(group, freq, events, cap, scale, ids, counts, got_ref, da, sq, ea, table, out, tail, bp, bb, eb, *work):
+def import_kernel(stage, arrivals, freq, events, cap, scale, ids, counts, *refs):
+    got, (da, sq, ea, table, out, tail, bp, bb, eb), work = refs[:arrivals], refs[arrivals : arrivals + 9], refs[arrivals + 9 :]
     pairs = cap // 2
-    prepare(lambda j: got_ref[j * 128 : (j + 1) * 128, :], bp, bb, eb, pairs, freq)
+
+    def natural(j):
+        return got[j // pairs][j % pairs * 128 : (j % pairs + 1) * 128, :]
+
+    prepare(natural, bp, bb, eb, arrivals * pairs, freq)
     out[...] = jnp.zeros_like(out)
-    tail[...] = got_ref[cap // 2 * 128 :, :]
-
-    def store(e, j, even, odd):
-        out[pl.ds(e * GROUP_ROWS + 2 * j, 1), :] = even
-        out[pl.ds(e * GROUP_ROWS + 2 * j + 1, 1), :] = odd
-
-    batches = (counts[group] + BATCH // 2 - 1) // (BATCH // 2)
-    listed_pairs(ids.at[group], batches, da, sq, ea, bp, bb, eb, table, work, store, freq, scale)
+    for g in range(arrivals):
+        tail[2 * GROUP_ROWS * g : 2 * GROUP_ROWS * (g + 1), :] = got[g][pairs * 128 :, :]
+
+    def store(e, column, even, odd):
+        out[pl.ds(e * arrivals * GROUP_ROWS + column, 1), :] = even
+        out[pl.ds(e * arrivals * GROUP_ROWS + column + 1, 1), :] = odd
+
+    batches = (counts[stage] + BATCH // 2 - 1) // (BATCH // 2)
+    listed_pairs(ids.at[stage], batches, da, sq, ea, bp, bb, eb, table, work, store, freq, scale)
 
 
 def weight_scratch(pairs, freq):
@@ -233,9 +240,15 @@
     )
 
 
+def two_parts(x):
+    high = x.astype(BF16)
+    return high, (x - high.astype(F32)).astype(BF16)
+
+
 def sums_kernel(groups, events, slots, hot, hot_turned, mask, partials, *refs):
-    tables, tails = refs[: groups + 1], refs[groups + 1 : 2 * groups + 1]
-    slots_out, terms_out, geo_out, own, own_geo = refs[2 * groups + 1 :]
+    tables, tails = refs[: STAGES + 1], refs[STAGES + 1 : 2 * STAGES + 1]
+    slots_out, terms_out, geo_out, own, own_geo = refs[2 * STAGES + 1 :]
+    import_rows = groups // STAGES * GROUP_ROWS
     cands = hot.shape[1]
     rest = jnp.zeros((SLOT_ROWS - slots, 128), F32)
 
@@ -245,7 +258,7 @@
             e = step * UNROLL + u
             parts = [tables[0][pl.ds(pl.multiple_of(e * events, 8), events), :]]
             for t in tables[1:]:
-                parts.append(t[pl.ds(pl.multiple_of(e * GROUP_ROWS, 8), GROUP_ROWS), :])
+                parts.append(t[pl.ds(pl.multiple_of(e * import_rows, 8), import_rows), :])
             every = jnp.concatenate(parts, axis=0).astype(BF16)
             rows = pl.ds(pl.multiple_of(e * SLOT_ROWS, SLOT_ROWS), SLOT_ROWS)
             live = mask[pl.ds(e, slots, stride=events), :].astype(F32)
@@ -264,7 +277,7 @@
     turned = pltpu.roll(totals, 64, 1)
     weights = jnp.where(low, totals, turned)
     moves = jnp.where(low, turned, totals)
-    ends = [t[...] for t in tails]
+    ends = [t[start : start + 2 * GROUP_ROWS, :] for t in tails for start in range(0, 2 * import_rows, 2 * GROUP_ROWS)]
     first = jnp.concatenate([own_geo[:events].astype(BF16)] + [t[:GROUP_ROWS] for t in ends], axis=0)
     second = jnp.concatenate([own_geo[events:].astype(BF16)] + [t[GROUP_ROWS:] for t in ends], axis=0)
     geo_out[:, :128] = first
@@ -276,12 +289,12 @@
         singles += [jnp.where(low, block, other), jnp.where(low, other, block)]
     half_row = lax.broadcasted_iota(jnp.int32, (8, 128), 0)
     half_lane = lax.broadcasted_iota(jnp.int32, (8, 128), 1) // 64
-    picker = jnp.where(half_row == half_lane, 1.0, 0.0).astype(F32)
+    picker = jnp.where(half_row == half_lane, 1.0, 0.0).astype(BF16)
+    picker = jnp.concatenate([picker, picker], axis=1)
 
     def halves(values):
-        return lax.dot_general(
-            picker, values, (((1,), (1,)), ((), ())), precision=lax.Precision.HIGHEST, preferred_element_type=F32
-        )[:2]
+        both = jnp.concatenate(two_parts(values), axis=1)
+        return lax.dot_general(picker, both, (((1,), (1,)), ((), ())), preferred_element_type=F32)[:2]
 
     rights = [halves(moves * blocks[0]), halves(moves * blocks[1])]
     for i in range(4):
@@ -317,7 +330,7 @@
             turned[pl.ds(e, 16, stride=events), 0:SLOT_ROWS] = entry
 
     for d, out in enumerate(outs):
-        share = lax.rem(place[0] + d, 4)
+        share = place[0] ^ d
         rows = pl.ds(pl.multiple_of(share * 4 * events, 128), 4 * events)
         out[...] = turned[rows, :].T[: out.shape[0]]
 
@@ -329,9 +342,8 @@
         for t in range(1, 4):
             part = part + received[t * (received.shape[0] // 4) + clusters[g]]
         parts.append(part)
-    spread = jnp.dot(
-        jnp.concatenate(parts, axis=1), owners[...], precision=lax.Precision.HIGHEST, preferred_element_type=F32
-    )
+    high, low = two_parts(jnp.concatenate(parts, axis=1))
+    spread = jnp.dot(high, owners[...], preferred_element_type=F32) + jnp.dot(low, owners[...], preferred_element_type=F32)
     block = lax.broadcasted_iota(jnp.int32, (1, 128), 1) // events
     diagonal = jnp.zeros((1, 128), F32)
     for j in range(4):
@@ -415,9 +427,9 @@
     sent = jnp.stack([jnp.asarray(send_group(g, me), jnp.int32) for g in range(groups)])
     came = jnp.stack([jnp.asarray(receive_group(g, me), jnp.int32) for g in range(groups)])
 
-    duos = [j << 12 | e << 6 | e + 1 for j in range(events // 2) for e in range(0, 2 * j + 2, 2)]
+    duos = [j << 18 | j << 12 | e << 6 | e + 1 for j in range(events // 2) for e in range(0, 2 * j + 2, 2)]
     batches = -(-len(duos) // BATCH) * 2
-    duos = duos + [1] * ((batches + 2) * (BATCH // 2) - len(duos))
+    duos = duos + [1] * ((batches + 3) * (BATCH // 2) - len(duos))
     natural, got[0] = lax.optimization_barrier((spectra, got[0]))
     local, dup, square, energy = call(
         functools.partial(local_kernel, freq, events, scale, batches),
@@ -439,18 +451,20 @@
     entry = far % cap
     named = jnp.where(pair_list < events, -1, arrival * half + entry // 2)
     wanted = jnp.any(named[:, :, None] == jnp.arange(groups * half, dtype=jnp.int32)[None, None, :], axis=1)
-    wanted = wanted.astype(F32).T.reshape(groups, half, events)
+    arrivals = groups // STAGES
+    pairs = arrivals * half
+    wanted = wanted.astype(F32).T.reshape(STAGES, pairs, events)
     ranks = np.arange(events)
     rank = jnp.einsum("gje,ef->gjf", wanted, jnp.asarray(ranks[:, None] < ranks[None, :], F32))
     rounded = jnp.ceil(jnp.sum(wanted, axis=2) * 0.5)
-    ranks = np.arange(half)
+    ranks = np.arange(pairs)
     start = jnp.sum(rounded[:, :, None] * jnp.asarray(ranks[:, None] < ranks[None, :], F32)[None], axis=1)
     rank = rank.astype(jnp.int32)
-    spot = jnp.where(wanted > 0, start.astype(jnp.int32)[:, :, None] + (rank >> 1), -1).reshape(groups, half * events)
+    spot = jnp.where(wanted > 0, start.astype(jnp.int32)[:, :, None] + (rank >> 1), -1).reshape(STAGES, pairs * events)
     event_ids = jnp.arange(events, dtype=jnp.int32)[None, None, :]
-    pair_ids = jnp.arange(half, dtype=jnp.int32)[None, :, None]
-    code = jnp.where(rank & 1 == 0, (pair_ids << 12) + (event_ids << 6), event_ids).reshape(groups, half * events)
-    longest = half * events // 2 + 3 * BATCH // 2
+    pair_codes = jnp.asarray(((ranks // half * GROUP_ROWS + ranks % half * 2) << 17) + (ranks << 12), jnp.int32)
+    code = jnp.where(rank & 1 == 0, pair_codes[None, :, None] + (event_ids << 6), event_ids).reshape(STAGES, pairs * events)
+    longest = pairs * events // 2 + 3 * BATCH // 2
     lists = jnp.sum(
         jnp.where(spot[:, None, :] == jnp.arange(longest, dtype=jnp.int32)[None, :, None], code[:, None, :], 0), axis=2
     )
@@ -469,17 +483,17 @@
         start = events + GROUP_ROWS * g
         owner_rows.append(jnp.pad(rows_sent[g], (start, cands - start - cap), constant_values=-1))
     owners = jnp.concatenate(owner_rows)[:, None] == (jnp.arange(128, dtype=jnp.int32) % events)[None, :]
-    owners = owners.astype(F32)
-
-    tables, tails = [None] * groups, [None] * groups
-    for h in range(groups):
-        tables[h], tails[h] = call(
-            functools.partial(import_kernel, h, freq, events, cap, scale),
-            [((events * GROUP_ROWS, 128), F32), ((2 * GROUP_ROWS, 128), BF16)],
-            (lists, counts, got[h], dup, square, energy, table),
-            scratch=weight_scratch(half, freq),
-            specs=[smem] * 2 + vmem(5),
-            micros=3.0,
+    owners = owners.astype(BF16)
+
+    tables, tails = [None] * STAGES, [None] * STAGES
+    for g in range(STAGES):
+        tables[g], tails[g] = call(
+            functools.partial(import_kernel, g, arrivals, freq, events, cap, scale),
+            [((events * arrivals * GROUP_ROWS, 128), F32), ((arrivals * 2 * GROUP_ROWS, 128), BF16)],
+            (lists, counts, *got[g * arrivals : (g + 1) * arrivals], dup, square, energy, table),
+            scratch=weight_scratch(pairs, freq),
+            specs=[smem] * 2 + vmem(arrivals + 4),
+            micros=8.0,
         )
 
     weights, terms, geo = call(
@@ -502,7 +516,7 @@
         specs=[smem] + vmem(4),
         micros=3.0,
     )
-    shares = [shares[0]] + [shifted(shares[d], "sta", d) for d in range(1, 4)]
+    shares = [shares[0]] + [lax.ppermute(shares[d], "sta", [(i, i ^ d) for i in range(4)]) for d in range(1, 4)]
     sources = jnp.stack([me] + [jnp.asarray(receiver(g, me), jnp.int32) for g in range(groups)])
     normal, right = call(
         functools.partial(total_kernel, groups, events, slots),

time: 67.6 us -> 69.7 us (1.031)
  Pallas kernels: 42.5 us -> 32.4 us
  starting transfers between devices: 17.4 us -> 22.7 us
  other arithmetic: 2.59 us -> 7.28 us
  waiting for transfers between devices: 2.16 us -> 4.26 us
    pallas_call x11 -> x7, Pallas kernels: 42.5 us -> 32.4 us  [call(): pl.pallas_call(kernel, out_shape=shapes, in_specs=specs if specs is not N...]
    all_to_all x1, starting transfers between devices: 3.28 us -> 9.62 us  [on_device(): lax.all_to_all(terms.reshape(4 * clusters, 8, 128), ('sta', 'clu'), split...]
    reduce_sum x1, other arithmetic: 0.47 us -> 5.14 us  [on_device(): jnp.sum(jnp.where(spot[:, None, :] == jnp.arange(longest, dtype=jnp.int32...]
    ppermute x3, waiting for transfers between devices: 2.13 us -> 4.24 us  [on_device(): lax.ppermute(shares[d], 'sta', [(i, i ^ d) for i in range(4)])]
    ppermute x3, starting transfers between devices: 4.75 us -> 3.55 us  [on_device(): lax.ppermute(shares[d], 'sta', [(i, i ^ d) for i in range(4)])]
  transfers between devices with their start and end apart: 10 -> 10, of which waited for: 2 -> 3; matrix products, arithmetic and copies ran while one was open for 6% -> 12% of each run, Pallas kernels for 47% -> 27%
where the time goes in v5:
time: 69.7 us; the launch traced here: 69.1 us
  Pallas kernels  32.4 us (46%)
  starting transfers between devices  22.7 us (33%)
  other arithmetic  7.28 us (10%)
  waiting for transfers between devices  4.26 us (6%)
  local copies, waits for them, and re-layouts  1.28 us (2%)
  between operations  1.12 us (2%)
    pallas_call x7, Pallas kernels, call(): pl.pallas_call(kernel, out_shape=shapes, in_specs=specs if specs is not N...  32.4 us
    all_to_all x1, starting transfers between devices, on_device(): lax.all_to_all(terms.reshape(4 * clusters, 8, 128), ('sta', 'clu'), split...  9.62 us
    ppermute x6, starting transfers between devices, on_device(): got[g] = lax.ppermute(outgoing[g], 'clu', routes[g])  9.56 us
    reduce_sum x1, other arithmetic, on_device(): jnp.sum(jnp.where(spot[:, None, :] == jnp.arange(longest, dtype=jnp.int32...  5.14 us
    ppermute x3, waiting for transfers between devices, on_device(): lax.ppermute(shares[d], 'sta', [(i, i ^ d) for i in range(4)])  4.24 us
    ppermute x3, starting transfers between devices, on_device(): lax.ppermute(shares[d], 'sta', [(i, i ^ d) for i in range(4)])  3.55 us
  transfers between devices with their start and end apart: 10, of which 3 were waited for; matrix products, arithmetic and copies ran while one was open for 12% of the time, Pallas kernels for 27%

profile of v5, /device:TPU:0, one launch (start us, length us, event | category | flops | bytes accessed | tf_op | source)
XLA Modules:
  0.0 69.1 jit_solution(11996222911738991312)
XLA Ops:
  0.6 0.0 copy-start.6
  0.7 2.3 %shard_map.122 = (bf16[800,128]{1,0:T(8,128)(2,1)}, bf16[800,128]{1,0:T(8,128)(2,1)}, bf16[800,128]{1,0:T(8,128)(2,1)}, bf16[800,128]{1,0:T(8,128)(2,1)}, bf16[8...) custom-call(s32[6,12]{1,0:T(8,128)} %exports_ref.1, bf16[32,64,128]{2,1,0:T(8,128)(2,1)} %spec_ref.1, bf16[32,4,64]{2,1,0:T(4,128)(2,1)} %partials.3), custom_call_target="tpu_custom_call" | custom-call | flops 2000000000 | bytes 1024 | tf_op jit(solution)/shard_map/pallas_call | solution.py:366
  3.0 0.5 collective-permute-start
  3.5 3.7 %collective-permute-start.3 = (bf16[800,128]{1,0:T(8,128)(2,1)}, bf16[800,128]{1,0:T(8,128)(2,1)S(1)}, u32[]{:S(2)}, u32[]{:S(2)}) collective-permute-start(bf16[800,128]{1,0:T(8,128)(2,1)} %get-tuple-element.37), channel_id=1, source_target_pairs={{0,5},{1,4},{2,7},{3,6},{4,1},{5,0},{6,3},{7,2},{8,13},{9,12},{10,... | collective-permute-start | bytes 614408 | tf_op jit(solution)/shard_map/ppermute | solution.py:425
  7.3 1.4 %collective-permute-start.4 = (bf16[800,128]{1,0:T(8,128)(2,1)}, bf16[800,128]{1,0:T(8,128)(2,1)S(1)}, u32[]{:S(2)}, u32[]{:S(2)}) collective-permute-start(bf16[800,128]{1,0:T(8,128)(2,1)} %get-tuple-element.38), channel_id=1, source_target_pairs={{0,6},{1,7},{2,4},{3,5},{4,2},{5,3},{6,0},{7,1},{8,14},{9,15},{10,... | collective-permute-start | bytes 614408 | tf_op jit(solution)/shard_map/ppermute | solution.py:425
  8.6 1.9 %collective-permute-start.5 = (bf16[800,128]{1,0:T(8,128)(2,1)}, bf16[800,128]{1,0:T(8,128)(2,1)S(1)}, u32[]{:S(2)}, u32[]{:S(2)}) collective-permute-start(bf16[800,128]{1,0:T(8,128)(2,1)} %get-tuple-element.39), channel_id=1, source_target_pairs={{0,7},{1,6},{2,5},{3,4},{4,3},{5,2},{6,1},{7,0},{8,15},{9,14},{10,... | collective-permute-start | bytes 614408 | tf_op jit(solution)/shard_map/ppermute | solution.py:425
  10.5 0.1 stack.80
  10.6 0.1 select_reduce_fusion
  10.7 0.7 %fusion.3 = pred[32,36]{0,1:T(8,128)(4,1)S(1)} fusion(s32[32,50]{1,0:T(8,128)S(1)} %get-tuple-element.52), kind=kLoop, calls=%fused_computation.8 | loop fusion | flops 114048 | bytes 7552 | tf_op jit(solution)/shard_map/reduce_or | solution.py:453
  11.4 0.1 convert_reduce_fusion
  11.6 0.1 eq.112
  11.7 0.3 fusion.1.hot
  12.0 0.1 fusion.2.hot_turned
  12.2 0.1 ceil.11
  12.3 0.1 copy.13
  12.4 0.1 multiply_reduce_fusion
  12.5 0.1 broadcast_add_fusion
  12.6 0.1 add_select_fusion
  12.7 0.1 broadcast_in_dim.87
  12.8 0.1 eq.122
  12.9 5.1 %fusion = s32[2,300]{0,1:T(8,128)S(1)} fusion(s32[2,576]{1,0:T(2,128)S(1)} %broadcast_in_dim.87, s32[2,576]{1,0:T(2,128)S(1)} %eq.122), kind=kLoop, calls=%fused_computation.1 | loop fusion | flops 1036200 | bytes 11616 | tf_op jit(solution)/shard_map/reduce_sum | solution.py:468
  18.0 0.1 copy.14.ids
  18.1 0.1 reduce_sum.58
  18.3 0.1 stack.87
  18.4 0.1 iota_compare_fusion.3
  18.5 0.1 select_reduce_fusion.1
  18.6 0.1 constant_dynamic-update-slice_fusion.5
  18.7 0.1 constant_dynamic-update-slice_fusion.4
  18.8 0.1 constant_dynamic-update-slice_fusion.3
  18.9 0.1 constant_dynamic-update-slice_fusion.2
  18.9 0.1 constant_dynamic-update-slice_fusion.1
  19.0 0.1 constant_dynamic-update-slice_fusion
  19.1 2.1 %collective-permute-start.2 = (bf16[800,128]{1,0:T(8,128)(2,1)S(1)}, bf16[800,128]{1,0:T(8,128)(2,1)S(1)}, u32[]{:S(2)}, u32[]{:S(2)}) collective-permute-start(bf16[800,128]{1,0:T(8,128)(2,1)S(1)} %copy-done.9), channel_id=1, source_target_pairs={{0,3},{1,2},{2,1},{3,0},{4,7},{5,6},{6,5},{7,4},{8,11},{9,10},{10,... | collective-permute-start | bytes 614408 | tf_op jit(solution)/shard_map/ppermute | solution.py:425
  21.2 9.6 %shard_map.123 = (f32[1024,128]{1,0:T(8,128)S(1)}, f32[32,128,128]{2,1,0:T(8,128)S(1)}, f32[32,64,128]{2,1,0:T(8,128)S(1)}, f32[32,128]{1,0:T(8,128)S(1)}) custom-call(s32[148]{0:T(256)S(1)} %copy-done.4, bf16[16,128,128]{2,1,0:T(8,128)(2,1)S(1)} %bitcast.45, bf16[80,64]{1,0:T(8,128)(2,1)S(1)} %copy-done.3), custom_call_target="tpu_custom_call" | custom-call | flops 8000000000 | bytes 1024 | tf_op jit(solution)/shard_map/pallas_call | solution.py:366
  30.9 7.4 %shard_map.125 = (f32[1536,128]{1,0:T(8,128)S(1)}, bf16[96,128]{1,0:T(8,128)(2,1)S(1)}) custom-call(s32[2,300]{1,0:T(2,128)S(1)} %copy.14.ids, s32[2]{0:T(128)S(1)} %convert_element_type.35.counts, bf16[800,128]{1,0:T(8,128)(2,1)S(1)} %collective-permute-done.3.refs_0_, bf16[800,128]{1,0:T(8,128)(2,1)S(1)} %collective-permute-done.4.refs_1_, ...), custom_call_target="tpu_custom_call" | custom-call | flops 8000000000 | bytes 1024 | tf_op jit(solution)/shard_map/pallas_call | solution.py:366
  38.4 7.4 %shard_map.124 = (f32[1536,128]{1,0:T(8,128)S(1)}, bf16[96,128]{1,0:T(8,128)(2,1)S(1)}) custom-call(s32[2,300]{1,0:T(2,128)S(1)} %copy.14.ids, s32[2]{0:T(128)S(1)} %convert_element_type.35.counts, bf16[800,128]{1,0:T(8,128)(2,1)S(1)} %collective-permute-done.refs_0_, bf16[800,128]{1,0:T(8,128)(2,1)S(1)} %collective-permute-done.1.refs_1_, ...), custom_call_target="tpu_custom_call" | custom-call | flops 8000000000 | bytes 1024 | tf_op jit(solution)/shard_map/pallas_call | solution.py:366
  45.8 2.4 %shard_map.126 = (bf16[2048,128]{1,0:T(8,128)(2,1)S(1)}, f32[4,8,8,128]{3,2,1,0:T(8,128)}, bf16[128,256]{1,0:T(8,128)(2,1)S(1)}) custom-call(bf16[2048,128]{1,0:T(8,128)(2,1)S(1)} %fusion.1.hot, bf16[128,2048]{1,0:T(8,128)(2,1)S(1)} %fusion.2.hot_turned, s32[1600,64]{1,0:T(8,128)S(1)} %bitcast.44, bf16[32,4,64]{2,1,0:T(4,128)(2,1)S(1)} %copy-done.2, ...), custom_call_target="tpu_custom_call" | custom-call | flops 2000000000 | bytes 1024 | tf_op jit(solution)/shard_map/pallas_call | solution.py:366
  48.3 9.6 %all-to-all-start = ((f32[32,8,128]{2,1,0:T(8,128)}), f32[32,8,128]{2,1,0:T(8,128)S(1)}, u32[]{:S(2)}, u32[]{:S(2)}) async-start(f32[32,8,128]{2,1,0:T(8,128)} %bitcast.19), calls=%async_computation | async-start | bytes 262144 | tf_op jit(solution)/shard_map/all_to_all | solution.py:506
  57.9 1.7 %shard_map.127 = (f32[56,128]{1,0:T(8,128)S(1)}, f32[56,128]{1,0:T(8,128)S(1)}, f32[56,128]{1,0:T(8,128)S(1)}, f32[56,128]{1,0:T(8,128)S(1)}) custom-call(s32[1]{0:T(128)} %bitcast.7.place, bf16[2048,128]{1,0:T(8,128)(2,1)S(1)} %fusion.1.hot, bf16[2048,128]{1,0:T(8,128)(2,1)S(1)} %get-tuple-element.43.slots, bf16[128,256]{1,0:T(8,128)(2,1)S(1)} %get-tuple-element.44.geo, ...), custom_call_target="tpu_custom_call" | custom-call | flops 3000000000 | bytes 1024 | tf_op jit(solution)/shard_map/pallas_call | solution.py:366
  59.6 1.8 %collective-permute-start.6 = (f32[56,128]{1,0:T(8,128)S(1)}, f32[56,128]{1,0:T(8,128)S(1)}, u32[]{:S(2)}, u32[]{:S(2)}) collective-permute-start(f32[56,128]{1,0:T(8,128)S(1)} %get-tuple-element.46), channel_id=1, source_target_pairs={{0,8},{8,0},{16,24},{24,16},{1,9},{9,1},{17,25},{25,17},{2,10},{10... | collective-permute-start | bytes 86024 | tf_op jit(solution)/shard_map/ppermute | solution.py:519
  61.4 1.5 %collective-permute-start.7 = (f32[56,128]{1,0:T(8,128)S(1)}, f32[56,128]{1,0:T(8,128)S(1)}, u32[]{:S(2)}, u32[]{:S(2)}) collective-permute-start(f32[56,128]{1,0:T(8,128)S(1)} %get-tuple-element.47), channel_id=1, source_target_pairs={{0,16},{8,24},{16,0},{24,8},{1,17},{9,25},{17,1},{25,9},{2,18},{10... | collective-permute-start | bytes 86024 | tf_op jit(solution)/shard_map/ppermute | solution.py:519
  62.9 0.3 collective-permute-start.8
  63.2 0.2 compare_convert_fusion.owners
  63.3 0.1 stack.73.clusters
  63.4 0.2 collective-permute-done.6.one
  63.7 1.8 %collective-permute-done.7.two = f32[56,128]{1,0:T(8,128)S(1)} collective-permute-done((f32[56,128]{1,0:T(8,128)S(1)}, f32[56,128]{1,0:T(8,128)S(1)}, u32[]{:S(2)}, u32[]{:S(2)}) %collective-permute-start.7) | collective-permute-done | bytes 28704 | tf_op jit(solution)/shard_map/ppermute | solution.py:519
  65.4 2.2 %collective-permute-done.8.three = f32[56,128]{1,0:T(8,128)S(1)} collective-permute-done((f32[56,128]{1,0:T(8,128)S(1)}, f32[56,128]{1,0:T(8,128)S(1)}, u32[]{:S(2)}, u32[]{:S(2)}) %collective-permute-start.8) | collective-permute-done | bytes 28704 | tf_op jit(solution)/shard_map/ppermute | solution.py:519
  67.7 1.5 %shard_map.128 = (f32[4,32,51]{2,1,0:T(8,128)}, f32[1,32]{1,0:T(1,128)}) custom-call(s32[7]{0:T(128)S(1)} %stack.73.clusters, f32[56,128]{1,0:T(8,128)S(1)} %get-tuple-element.45.own, f32[56,128]{1,0:T(8,128)S(1)} %collective-permute-done.6.one, f32[56,128]{1,0:T(8,128)S(1)} %collective-permute-done.7.two, f32[56,128]{1,0:T(8,128)S(1)} %collective-permute-done.8.three, ...), custom_call_target="tpu_custom_call" | custom-call | flops 1000000000 | bytes 1024 | tf_op jit(solution)/shard_map/pallas_call | solution.py:366
  (44 shorter events, 0.2 us)
Async XLA Ops:
  0.6 11.8 %copy-start.6 = (f32[18,18]{1,0:T(8,128)S(1)}, f32[18,18]{1,0:T(8,128)}, u32[]{:S(2)}) copy-start(f32[18,18]{1,0:T(8,128)} %constant.148.clone) | copy-start | bytes 3892
  0.6 9.8 %copy-start.5 = (s32[32,50]{1,0:T(8,128)S(1)}, s32[32,50]{1,0:T(8,128)}, u32[]{:S(2)}) copy-start(s32[32,50]{1,0:T(8,128)} %param.13) | copy-start | bytes 19204
  3.0 9.6 %copy-start.8 = (s32[18]{0:T(128)S(1)}, s32[18]{0:T(128)}, u32[]{:S(2)}) copy-start(s32[18]{0:T(128)} %constant.149.clone) | copy-start | bytes 220
  3.0 9.6 %copy-start.10 = (bf16[32,32,1]{1,0,2:T(8,128)(2,1)S(1)}, bf16[32,32,1]{1,0,2:T(8,128)(2,1)}, u32[]{:S(2)}) copy-start(bf16[32,32,1]{1,0,2:T(8,128)(2,1)} %constant.203) | copy-start | bytes 6148
  3.0 15.5 %copy-start.7 = (s32[6,12]{1,0:T(8,128)S(1)}, s32[6,12]{1,0:T(8,128)}, u32[]{:S(2)}) copy-start(s32[6,12]{1,0:T(8,128)} %exports_ref.1) | copy-start | bytes 868
  3.0 15.6 %copy-start.11 = (s32[128]{0:T(128)S(1)}, s32[128]{0:T(128)}, u32[]{:S(2)}) copy-start(s32[128]{0:T(128)} %constant.150.clone) | copy-start | bytes 1540
  3.0 16.1 %copy-start.9 = (bf16[800,128]{1,0:T(8,128)(2,1)S(1)}, bf16[800,128]{1,0:T(8,128)(2,1)}, u32[]{:S(2)}) copy-start(bf16[800,128]{1,0:T(8,128)(2,1)} %get-tuple-element.32) | copy-start | bytes 614404
  3.0 18.2 %copy-start.1 = (bf16[32,64,128]{2,1,0:T(8,128)(2,1)S(1)}, bf16[32,64,128]{2,1,0:T(8,128)(2,1)}, u32[]{:S(2)}) copy-start(bf16[32,64,128]{2,1,0:T(8,128)(2,1)} %spec_ref.1) | copy-start | bytes 1572868
  3.0 18.2 %copy-start.3 = (bf16[80,64]{1,0:T(8,128)(2,1)S(1)}, bf16[80,64]{1,0:T(8,128)(2,1)}, u32[]{:S(2)}) copy-start(bf16[80,64]{1,0:T(8,128)(2,1)} %constant.166.table.refs_6_) | copy-start | bytes 30724
  3.0 18.2 %copy-start.4 = (s32[148]{0:T(256)S(1)}, s32[148]{0:T(256)}, u32[]{:S(2)}) copy-start(s32[148]{0:T(256)} %constant.146.clone.ids) | copy-start | bytes 1780
  3.0 16.1 %collective-permute-start = (bf16[800,128]{1,0:T(8,128)(2,1)}, bf16[800,128]{1,0:T(8,128)(2,1)S(1)}, u32[]{:S(2)}, u32[]{:S(2)}) collective-permute-start(bf16[800,128]{1,0:T(8,128)(2,1)} %get-tuple-element.27), channel_id=1, source_target_pairs={{0,1},{1,0},{2,3},{3,2},{4,5},{5,4},{6,7},{7,6},{8,9},{9,8},{10,11... | collective-permute-start | bytes 614408 | tf_op jit(solution)/shard_map/ppermute | solution.py:425
  3.5 27.3 %collective-permute-start.3 = (bf16[800,128]{1,0:T(8,128)(2,1)}, bf16[800,128]{1,0:T(8,128)(2,1)S(1)}, u32[]{:S(2)}, u32[]{:S(2)}) collective-permute-start(bf16[800,128]{1,0:T(8,128)(2,1)} %get-tuple-element.37), channel_id=1, source_target_pairs={{0,5},{1,4},{2,7},{3,6},{4,1},{5,0},{6,3},{7,2},{8,13},{9,12},{10,... | collective-permute-start | bytes 614408 | tf_op jit(solution)/shard_map/ppermute | solution.py:425
  7.3 23.6 %collective-permute-start.4 = (bf16[800,128]{1,0:T(8,128)(2,1)}, bf16[800,128]{1,0:T(8,128)(2,1)S(1)}, u32[]{:S(2)}, u32[]{:S(2)}) collective-permute-start(bf16[800,128]{1,0:T(8,128)(2,1)} %get-tuple-element.38), channel_id=1, source_target_pairs={{0,6},{1,7},{2,4},{3,5},{4,2},{5,3},{6,0},{7,1},{8,14},{9,15},{10,... | collective-permute-start | bytes 614408 | tf_op jit(solution)/shard_map/ppermute | solution.py:425
  8.6 22.3 %collective-permute-start.5 = (bf16[800,128]{1,0:T(8,128)(2,1)}, bf16[800,128]{1,0:T(8,128)(2,1)S(1)}, u32[]{:S(2)}, u32[]{:S(2)}) collective-permute-start(bf16[800,128]{1,0:T(8,128)(2,1)} %get-tuple-element.39), channel_id=1, source_target_pairs={{0,7},{1,6},{2,5},{3,4},{4,3},{5,2},{6,1},{7,0},{8,15},{9,14},{10,... | collective-permute-start | bytes 614408 | tf_op jit(solution)/shard_map/ppermute | solution.py:425
  10.5 27.9 %collective-permute-start.1 = (bf16[800,128]{1,0:T(8,128)(2,1)}, bf16[800,128]{1,0:T(8,128)(2,1)S(1)}, u32[]{:S(2)}, u32[]{:S(2)}) collective-permute-start(bf16[800,128]{1,0:T(8,128)(2,1)} %get-tuple-element.31), channel_id=1, source_target_pairs={{0,2},{1,3},{2,0},{3,1},{4,6},{5,7},{6,4},{7,5},{8,10},{9,11},{10,... | collective-permute-start | bytes 614408 | tf_op jit(solution)/shard_map/ppermute | solution.py:425
  19.1 19.3 %collective-permute-start.2 = (bf16[800,128]{1,0:T(8,128)(2,1)S(1)}, bf16[800,128]{1,0:T(8,128)(2,1)S(1)}, u32[]{:S(2)}, u32[]{:S(2)}) collective-permute-start(bf16[800,128]{1,0:T(8,128)(2,1)S(1)} %copy-done.9), channel_id=1, source_target_pairs={{0,3},{1,2},{2,1},{3,0},{4,7},{5,6},{6,5},{7,4},{8,11},{9,10},{10,... | collective-permute-start | bytes 614408 | tf_op jit(solution)/shard_map/ppermute | solution.py:425
  38.3 7.5 %copy-start = (s32[32,50,64]{2,0,1:T(8,128)S(1)}, s32[32,50,64]{2,0,1:T(8,128)}, u32[]{:S(2)}) copy-start(s32[32,50,64]{2,0,1:T(8,128)} %param.14) | copy-start | bytes 1228804
  38.4 7.5 %copy-start.2 = (bf16[32,4,64]{2,1,0:T(4,128)(2,1)S(1)}, bf16[32,4,64]{2,1,0:T(4,128)(2,1)}, u32[]{:S(2)}) copy-start(bf16[32,4,64]{2,1,0:T(4,128)(2,1)} %partials.3) | copy-start | bytes 49156
  48.3 19.4 %all-to-all-start = ((f32[32,8,128]{2,1,0:T(8,128)}), f32[32,8,128]{2,1,0:T(8,128)S(1)}, u32[]{:S(2)}, u32[]{:S(2)}) async-start(f32[32,8,128]{2,1,0:T(8,128)} %bitcast.19), calls=%async_computation | async-start | bytes 262144 | tf_op jit(solution)/shard_map/all_to_all | solution.py:506
  59.6 4.1 %collective-permute-start.6 = (f32[56,128]{1,0:T(8,128)S(1)}, f32[56,128]{1,0:T(8,128)S(1)}, u32[]{:S(2)}, u32[]{:S(2)}) collective-permute-start(f32[56,128]{1,0:T(8,128)S(1)} %get-tuple-element.46), channel_id=1, source_target_pairs={{0,8},{8,0},{16,24},{24,16},{1,9},{9,1},{17,25},{25,17},{2,10},{10... | collective-permute-start | bytes 86024 | tf_op jit(solution)/shard_map/ppermute | solution.py:519
  61.4 4.0 %collective-permute-start.7 = (f32[56,128]{1,0:T(8,128)S(1)}, f32[56,128]{1,0:T(8,128)S(1)}, u32[]{:S(2)}, u32[]{:S(2)}) collective-permute-start(f32[56,128]{1,0:T(8,128)S(1)} %get-tuple-element.47), channel_id=1, source_target_pairs={{0,16},{8,24},{16,0},{24,8},{1,17},{9,25},{17,1},{25,9},{2,18},{10... | collective-permute-start | bytes 86024 | tf_op jit(solution)/shard_map/ppermute | solution.py:519
  62.9 4.8 %collective-permute-start.8 = (f32[56,128]{1,0:T(8,128)S(1)}, f32[56,128]{1,0:T(8,128)S(1)}, u32[]{:S(2)}, u32[]{:S(2)}) collective-permute-start(f32[56,128]{1,0:T(8,128)S(1)} %get-tuple-element.48), channel_id=1, source_target_pairs={{0,24},{8,16},{16,8},{24,0},{1,25},{9,17},{17,9},{25,1},{2,26},{10... | collective-permute-start | bytes 86024 | tf_op jit(solution)/shard_map/ppermute | solution.py:519

commit v6 on v5

--- a/solution.py
+++ b/solution.py
@@ -17,7 +17,7 @@
 BATCH = 8
 WIDE = 4
 UNROLL = 8
-STAGES = 2
+STAGE_SIZES = (3, 2, 1)
 
 
 def moment_table(freq_count):
@@ -30,9 +30,13 @@
         out[live] = -freq_count * sign / np.tan(np.pi * k[live] / (2 * freq_count))
         return out
 
-    table = np.zeros((freq_count + 16, freq_count), np.float32)
-    table[:freq_count] = -(edge(f[:, None] + f[None, :]) + edge(f[None, :] - f[:, None]))
-    table[freq_count] = (1.0 - 2.0 * (f % 2)) * f * math.pi / freq_count
+    w = f * math.pi / freq_count
+    table = np.zeros((freq_count + 16, 2 * freq_count), np.float32)
+    table[:freq_count, :freq_count] = -(edge(f[:, None] + f[None, :]) + edge(f[None, :] - f[:, None]))
+    table[freq_count, :freq_count] = (1.0 - 2.0 * (f % 2)) * w
+    high = (w * w).astype(jnp.bfloat16).astype(np.float64)
+    table[freq_count + 1, freq_count:] = high
+    table[freq_count + 2, freq_count:] = w * w - high
     return jnp.asarray(table, F32).astype(BF16)
 
 
@@ -76,21 +80,19 @@
         eb[j : j + 1, :] = jnp.sum(square, axis=0, keepdims=True)
 
 
-def listed_pairs(ids, batches, da, sq, ea, bp, bb, eb, table, work, store, freq, scale):
-    xs, reals, rm, rs, rt, rb, rz, re = work
+def listed_pairs(fetch, batches, da, sq, ea, bp, bb, eb, table, work, store, freq, scale):
+    xs, reals, rm, rs, rt, rz, re = work
     lead = lax.broadcasted_iota(jnp.int32, (8, 1), 0) == 0
-    step = lax.broadcasted_iota(jnp.int32, (8, 1), 0).astype(F32)
     low = low_half((8, 128))
-    unit = (math.pi / freq) ** 2
 
     def split(t, d):
-        code = ids[t * (BATCH // 2) + d]
+        code = fetch(t * (BATCH // 2) + d)
         return (code >> 12) & 31, code >> 17, ((code >> 6) & 63, code & 63)
 
     def cross_stage(t, slot):
         for d in range(BATCH // 2):
             j, _, duo = split(t, d)
-            squares, sums = [[], []], [None, None]
+            totals, sums = [None, None], [None, None]
             for v in range(0, freq, 16):
                 br, bi = bp[j, v : v + 16, :], bp[j, freq + v : freq + v + 16, :]
                 b2 = bb[j, v : v + 16, :]
@@ -102,24 +104,18 @@
                     u = 2 * d + i
                     lanes = slice(u * 128, (u + 1) * 128)
                     xs[slot, v : v + 16, lanes] = ci.astype(BF16)
+                    xs[slot, freq + v : freq + v + 16, lanes] = both.astype(BF16)
                     reals[slot, v : v + 16, lanes] = cr.astype(BF16)
-                    squares[i] += [both[:8], both[8:]]
-                    part = cr[:8] + cr[8:]
-                    sums[i] = part if v == 0 else sums[i] + part
+                    square, real = both[:8] + both[8:], cr[:8] + cr[8:]
                     if v == 0:
                         edge = cr[:8] * cr[:8] - ci[:8] * ci[:8]
-                        rs[slot, u * 8 : u * 8 + 8, :] = jnp.where(lead, edge, 0.0)
+                        totals[i], sums[i] = square + jnp.where(lead, edge, 0.0), real
+                    else:
+                        totals[i], sums[i] = totals[i] + square, sums[i] + real
             for i, e in enumerate(duo):
                 u = 2 * d + i
                 rows = slice(u * 8, u * 8 + 8)
-                zero, one, two = squares[i][-1], squares[i][-1], squares[i][-1]
-                for v in range(freq // 8 - 2, 0, -1):
-                    zero = zero + squares[i][v]
-                    one = one + zero
-                    two = two + one
-                zero = zero + squares[i][0]
-                rs[slot, rows, :] += zero
-                rb[slot, rows, :] = unit * (64.0 * (2.0 * two - one) + step * (16.0 * one + step * zero))
+                rs[slot, rows, :] = totals[i]
                 rt[slot, rows, :] = sums[i]
                 re[slot, u : u + 1, :] = ea[pl.ds(e, 1), :] * eb[pl.ds(j, 1), :]
 
@@ -138,13 +134,13 @@
         def pick(ref, k):
             return ref[slot, pl.ds(k, 8, stride=8), :]
 
-        moment, total, alternate, bend = pick(rm, 0), pick(rs, 0), pick(rt, 0), pick(rb, 0)
+        moment, total, alternate = pick(rm, 0), pick(rs, 0), pick(rt, 0)
         for k in range(1, 8):
             moment = moment + pick(rm, k)
             total = total + pick(rs, k)
-            bend = bend + pick(rb, k)
             alternate = alternate + pick(rt, k) if k % 2 == 0 else alternate - pick(rt, k)
         tilt = pick(rz, 0)
+        bend = pick(rz, 1) + pick(rz, 2)
         inverse = 1.0 / (re[slot] + 1e-06)
         power = (freq * total - alternate * alternate) * inverse
         rough = (freq * bend - tilt * tilt) * inverse
@@ -203,10 +199,10 @@
         out[pl.ds(column * events + e, 1), :] = jnp.where(row, even, -even)
         out[pl.ds((column + 1) * events + e, 1), :] = jnp.where(row, odd, -odd)
 
-    listed_pairs(ids, batches, da, sq, ea, bp, bb, eb, table, work, store, freq, scale)
-
-
-def import_kernel(stage, arrivals, freq, events, cap, scale, ids, counts, *refs):
+    listed_pairs(lambda n: ids[n], batches, da, sq, ea, bp, bb, eb, table, work, store, freq, scale)
+
+
+def import_kernel(begin, arrivals, freq, events, cap, scale, ids, counts, *refs):
     got, (da, sq, ea, table, out, tail, bp, bb, eb), work = refs[:arrivals], refs[arrivals : arrivals + 9], refs[arrivals + 9 :]
     pairs = cap // 2
 
@@ -222,8 +218,19 @@
         out[pl.ds(e * arrivals * GROUP_ROWS + column, 1), :] = even
         out[pl.ds(e * arrivals * GROUP_ROWS + column + 1, 1), :] = odd
 
-    batches = (counts[stage] + BATCH // 2 - 1) // (BATCH // 2)
-    listed_pairs(ids.at[stage], batches, da, sq, ea, bp, bb, eb, table, work, store, freq, scale)
+    ends = [counts[begin]]
+    for g in range(1, arrivals):
+        ends.append(ends[-1] + counts[begin + g])
+
+    def fetch(n):
+        group, start = 0, 0
+        for end in ends[:-1]:
+            group = group + jnp.where(n >= end, 1, 0)
+            start = jnp.where(n >= end, end, start)
+        return ids[begin + group, n - start]
+
+    batches = (ends[-1] + BATCH // 2 - 1) // (BATCH // 2)
+    listed_pairs(fetch, batches, da, sq, ea, bp, bb, eb, table, work, store, freq, scale)
 
 
 def weight_scratch(pairs, freq):
@@ -232,10 +239,10 @@
             pltpu.VMEM((pairs, 2 * freq, 128), F32),
             pltpu.VMEM((pairs, freq, 128), F32),
             pltpu.VMEM((-(-pairs // 8) * 8, 128), F32),
-            pltpu.VMEM((2, freq, BATCH * 128), BF16),
+            pltpu.VMEM((2, 2 * freq, BATCH * 128), BF16),
             pltpu.VMEM((2, freq, BATCH * 128), BF16),
         ]
-        + [pltpu.VMEM((2, BATCH * 8, 128), F32)] * 5
+        + [pltpu.VMEM((2, BATCH * 8, 128), F32)] * 4
         + [pltpu.VMEM((2, BATCH, 128), F32)]
     )
 
@@ -245,44 +252,65 @@
     return high, (x - high.astype(F32)).astype(BF16)
 
 
-def sums_kernel(groups, events, slots, hot, hot_turned, mask, partials, *refs):
-    tables, tails = refs[: STAGES + 1], refs[STAGES + 1 : 2 * STAGES + 1]
-    slots_out, terms_out, geo_out, own, own_geo = refs[2 * STAGES + 1 :]
-    import_rows = groups // STAGES * GROUP_ROWS
-    cands = hot.shape[1]
+def slots_kernel(events, slots, place, hot, mask, partials, *refs):
+    stages = len(STAGE_SIZES)
+    tables, tails = refs[: stages + 1], refs[stages + 1 : 2 * stages + 1]
+    outs, (slots_out, geo_out, own, own_geo, turned) = refs[2 * stages + 1 : -5], refs[-5:]
     rest = jnp.zeros((SLOT_ROWS - slots, 128), F32)
+    for e in range(events):
+        geo = partials[e].astype(F32)
+        own_geo[e : e + 1, :] = jnp.concatenate([geo[0:1], geo[1:2]], axis=1)
+        own_geo[events + e : events + e + 1, :] = jnp.concatenate([geo[2:3], geo[3:4]], axis=1)
+    ends = [t[start : start + 2 * GROUP_ROWS, :] for t in tails for start in range(0, t.shape[0], 2 * GROUP_ROWS)]
+    geo_out[:, :128] = jnp.concatenate([own_geo[:events].astype(BF16)] + [t[:GROUP_ROWS] for t in ends], axis=0)
+    geo_out[:, 128:] = jnp.concatenate([own_geo[events:].astype(BF16)] + [t[GROUP_ROWS:] for t in ends], axis=0)
+    turned[...] = jnp.zeros_like(turned)
+    low = low_half((SLOT_ROWS, 128))
+    column = lax.broadcasted_iota(jnp.int32, (16, 128), 0) % 4
+    block = lax.broadcasted_iota(jnp.int32, (16, 128), 1) // 64
 
     @pl.loop(0, events // UNROLL)
     def _(step):
         for u in range(UNROLL):
             e = step * UNROLL + u
             parts = [tables[0][pl.ds(pl.multiple_of(e * events, 8), events), :]]
-            for t in tables[1:]:
-                parts.append(t[pl.ds(pl.multiple_of(e * import_rows, 8), import_rows), :])
+            for t, size in zip(tables[1:], STAGE_SIZES):
+                rows = size * GROUP_ROWS
+                parts.append(t[pl.ds(pl.multiple_of(e * rows, 8), rows), :])
             every = jnp.concatenate(parts, axis=0).astype(BF16)
             rows = pl.ds(pl.multiple_of(e * SLOT_ROWS, SLOT_ROWS), SLOT_ROWS)
             live = mask[pl.ds(e, slots, stride=events), :].astype(F32)
             live = jnp.concatenate([jnp.concatenate([live, live], axis=1), rest], axis=0)
             picked = jnp.dot(hot[rows, :], every, preferred_element_type=F32) * live
+            partner = jnp.dot(hot[rows, :], geo_out[...], preferred_element_type=F32)
             slots_out[rows, :] = picked.astype(BF16)
             own[pl.ds(e, 1), :] = jnp.sum(picked, axis=0, keepdims=True)
+            weights = jnp.where(low, picked, pltpu.roll(picked, 64, 1))
+            weighted = jnp.concatenate([weights * partner[:, :128], weights * partner[:, 128:]], axis=1).astype(BF16)
             geo = partials[e].astype(F32)
-            own_geo[pl.ds(e, 1), :] = jnp.concatenate([geo[0:1], geo[1:2]], axis=1)
-            own_geo[pl.ds(events + e, 1), :] = jnp.concatenate([geo[2:3], geo[3:4]], axis=1)
-
-    gathered = jnp.dot(hot_turned[...], slots_out[...], preferred_element_type=F32)
+            geo = jnp.concatenate([geo, geo], axis=1)
+            geo = jnp.concatenate([jnp.broadcast_to(-geo[i : i + 1], (4, 128)) for i in range(4)], axis=0)
+            left = [jnp.where(column == block, geo, 0.0), jnp.where(column == block + 2, geo, 0.0)]
+            left = jnp.concatenate(left, axis=1).astype(BF16)
+            entry = lax.dot_general(left, weighted, (((1,), (1,)), ((), ())), preferred_element_type=F32)
+            turned[pl.ds(e, 16, stride=events), 0:SLOT_ROWS] = entry
+
+    for d, out in enumerate(outs):
+        share = place[0] ^ d
+        rows = pl.ds(pl.multiple_of(share * 4 * events, 128), 4 * events)
+        out[...] = turned[rows, :].T[: out.shape[0]]
+
+
+def terms_kernel(events, hot_turned, slots, geo, own, terms_out):
+    cands = geo.shape[0]
+    gathered = jnp.dot(hot_turned[...], slots[...], preferred_element_type=F32)
     low = low_half((cands, 128))
     gathered = jnp.where(low, gathered, -gathered)
     totals = jnp.concatenate([gathered[:events] + own[...], gathered[events:]], axis=0)
     turned = pltpu.roll(totals, 64, 1)
     weights = jnp.where(low, totals, turned)
     moves = jnp.where(low, turned, totals)
-    ends = [t[start : start + 2 * GROUP_ROWS, :] for t in tails for start in range(0, 2 * import_rows, 2 * GROUP_ROWS)]
-    first = jnp.concatenate([own_geo[:events].astype(BF16)] + [t[:GROUP_ROWS] for t in ends], axis=0)
-    second = jnp.concatenate([own_geo[events:].astype(BF16)] + [t[GROUP_ROWS:] for t in ends], axis=0)
-    geo_out[:, :128] = first
-    geo_out[:, 128:] = second
-    blocks = [first.astype(F32), second.astype(F32)]
+    blocks = [geo[:, :128].astype(F32), geo[:, 128:].astype(F32)]
     singles = []
     for block in blocks:
         other = pltpu.roll(block, 64, 1)
@@ -303,36 +331,6 @@
         share = jnp.concatenate(rows + [jnp.zeros((3, 128), F32)], axis=0)
         for q in range(terms_out.shape[1]):
             terms_out[i, q] = share
-
-
-def blocks_kernel(events, place, hot, slots, geo, partials, *refs):
-    outs, turned = refs[:-1], refs[-1]
-    turned[...] = jnp.zeros_like(turned)
-    low = low_half((SLOT_ROWS, 128))
-    column = lax.broadcasted_iota(jnp.int32, (16, 128), 0) % 4
-    block = lax.broadcasted_iota(jnp.int32, (16, 128), 1) // 64
-
-    @pl.loop(0, events // UNROLL)
-    def _(step):
-        for u in range(UNROLL):
-            e = step * UNROLL + u
-            rows = pl.ds(pl.multiple_of(e * SLOT_ROWS, SLOT_ROWS), SLOT_ROWS)
-            partner = jnp.dot(hot[rows, :], geo[...], preferred_element_type=F32)
-            pair = slots[rows, :].astype(F32)
-            weights = jnp.where(low, pair, pltpu.roll(pair, 64, 1))
-            weighted = jnp.concatenate([weights * partner[:, :128], weights * partner[:, 128:]], axis=1).astype(BF16)
-            own = partials[e].astype(F32)
-            own = jnp.concatenate([own, own], axis=1)
-            own = jnp.concatenate([jnp.broadcast_to(-own[i : i + 1], (4, 128)) for i in range(4)], axis=0)
-            left = [jnp.where(column == block, own, 0.0), jnp.where(column == block + 2, own, 0.0)]
-            left = jnp.concatenate(left, axis=1).astype(BF16)
-            entry = lax.dot_general(left, weighted, (((1,), (1,)), ((), ())), preferred_element_type=F32)
-            turned[pl.ds(e, 16, stride=events), 0:SLOT_ROWS] = entry
-
-    for d, out in enumerate(outs):
-        share = place[0] ^ d
-        rows = pl.ds(pl.multiple_of(share * 4 * events, 128), 4 * events)
-        out[...] = turned[rows, :].T[: out.shape[0]]
 
 
 def total_kernel(groups, events, slots, clusters, own, one, two, three, received, owners, normal, right):
@@ -451,20 +449,19 @@
     entry = far % cap
     named = jnp.where(pair_list < events, -1, arrival * half + entry // 2)
     wanted = jnp.any(named[:, :, None] == jnp.arange(groups * half, dtype=jnp.int32)[None, None, :], axis=1)
-    arrivals = groups // STAGES
-    pairs = arrivals * half
-    wanted = wanted.astype(F32).T.reshape(STAGES, pairs, events)
+    wanted = wanted.astype(F32).T.reshape(groups, half, events)
     ranks = np.arange(events)
     rank = jnp.einsum("gje,ef->gjf", wanted, jnp.asarray(ranks[:, None] < ranks[None, :], F32))
     rounded = jnp.ceil(jnp.sum(wanted, axis=2) * 0.5)
-    ranks = np.arange(pairs)
+    ranks = np.arange(half)
     start = jnp.sum(rounded[:, :, None] * jnp.asarray(ranks[:, None] < ranks[None, :], F32)[None], axis=1)
     rank = rank.astype(jnp.int32)
-    spot = jnp.where(wanted > 0, start.astype(jnp.int32)[:, :, None] + (rank >> 1), -1).reshape(STAGES, pairs * events)
+    spot = jnp.where(wanted > 0, start.astype(jnp.int32)[:, :, None] + (rank >> 1), -1).reshape(groups, half * events)
     event_ids = jnp.arange(events, dtype=jnp.int32)[None, None, :]
-    pair_codes = jnp.asarray(((ranks // half * GROUP_ROWS + ranks % half * 2) << 17) + (ranks << 12), jnp.int32)
-    code = jnp.where(rank & 1 == 0, pair_codes[None, :, None] + (event_ids << 6), event_ids).reshape(STAGES, pairs * events)
-    longest = pairs * events // 2 + 3 * BATCH // 2
+    inside = np.concatenate([np.arange(size) for size in STAGE_SIZES])[:, None]
+    pair_codes = jnp.asarray(((inside * GROUP_ROWS + 2 * ranks) << 17) + ((inside * half + ranks) << 12), jnp.int32)
+    code = jnp.where(rank & 1 == 0, pair_codes[:, :, None] + (event_ids << 6), event_ids).reshape(groups, half * events)
+    longest = half * events // 2 + 4 * BATCH // 2
     lists = jnp.sum(
         jnp.where(spot[:, None, :] == jnp.arange(longest, dtype=jnp.int32)[None, :, None], code[:, None, :], 0), axis=2
     )
@@ -485,38 +482,42 @@
     owners = jnp.concatenate(owner_rows)[:, None] == (jnp.arange(128, dtype=jnp.int32) % events)[None, :]
     owners = owners.astype(BF16)
 
-    tables, tails = [None] * STAGES, [None] * STAGES
-    for g in range(STAGES):
-        tables[g], tails[g] = call(
-            functools.partial(import_kernel, g, arrivals, freq, events, cap, scale),
-            [((events * arrivals * GROUP_ROWS, 128), F32), ((arrivals * 2 * GROUP_ROWS, 128), BF16)],
-            (lists, counts, *got[g * arrivals : (g + 1) * arrivals], dup, square, energy, table),
-            scratch=weight_scratch(pairs, freq),
-            specs=[smem] * 2 + vmem(arrivals + 4),
-            micros=8.0,
+    tables, tails, begin = [], [], 0
+    for size in STAGE_SIZES:
+        if tables:
+            lists, tables[-1] = lax.optimization_barrier((lists, tables[-1]))
+        table_part, tail_part = call(
+            functools.partial(import_kernel, begin, size, freq, events, cap, scale),
+            [((events * size * GROUP_ROWS, 128), F32), ((size * 2 * GROUP_ROWS, 128), BF16)],
+            (lists, counts, *got[begin : begin + size], dup, square, energy, table),
+            scratch=weight_scratch(size * half, freq),
+            specs=[smem] * 2 + vmem(size + 4),
+            micros=1.0 + 2.3 * size,
         )
-
-    weights, terms, geo = call(
-        functools.partial(sums_kernel, groups, events, slots),
-        [((events * SLOT_ROWS, 128), BF16), ((4, clusters, 8, 128), F32), ((cands, 256), BF16)],
-        (hot, hot_turned, mask, partials, local, *tables, *tails),
-        scratch=[pltpu.VMEM((events, 128), F32), pltpu.VMEM((2 * events, 128), F32)],
-        micros=2.0,
+        tables.append(table_part)
+        tails.append(tail_part)
+        begin += size
+
+    message_rows = -(-(slots + 1) // 8) * 8
+    place = lax.axis_index("sta").astype(jnp.int32).reshape(1)
+    *shares, weights, geo, own = call(
+        functools.partial(slots_kernel, events, slots),
+        [((message_rows, 128), F32)] * 4
+        + [((events * SLOT_ROWS, 128), BF16), ((cands, 256), BF16), ((events, 128), F32)],
+        (place, hot, mask, partials, local, *tables, *tails),
+        scratch=[pltpu.VMEM((2 * events, 128), F32), pltpu.VMEM((16 * events, 128), F32)],
+        specs=[smem] + vmem(4 + 2 * len(STAGE_SIZES)),
+        micros=3.0,
+    )
+    shares = [shares[0]] + [lax.ppermute(shares[d], "sta", [(i, i ^ d) for i in range(4)]) for d in range(1, 4)]
+    (terms,) = call(
+        functools.partial(terms_kernel, events),
+        [((4, clusters, 8, 128), F32)],
+        (hot_turned, weights, geo, own),
     )
     terms = lax.all_to_all(
         terms.reshape(4 * clusters, 8, 128), ("sta", "clu"), split_axis=0, concat_axis=0, tiled=True
     )
-    message_rows = -(-(slots + 1) // 8) * 8
-    place = lax.axis_index("sta").astype(jnp.int32).reshape(1)
-    shares = call(
-        functools.partial(blocks_kernel, events),
-        [((message_rows, 128), F32)] * 4,
-        (place, hot, weights, geo, partials),
-        scratch=[pltpu.VMEM((16 * events, 128), F32)],
-        specs=[smem] + vmem(4),
-        micros=3.0,
-    )
-    shares = [shares[0]] + [lax.ppermute(shares[d], "sta", [(i, i ^ d) for i in range(4)]) for d in range(1, 4)]
     sources = jnp.stack([me] + [jnp.asarray(receiver(g, me), jnp.int32) for g in range(groups)])
     normal, right = call(
         functools.partial(total_kernel, groups, events, slots),

time: 69.7 us -> 69.7 us (level)
  Pallas kernels: 32.4 us -> 38.4 us
  other arithmetic: 7.28 us -> 2.51 us
  starting transfers between devices: 22.7 us -> 21.9 us
    pallas_call x7 -> x8, Pallas kernels: 32.4 us -> 38.4 us  [call(): pl.pallas_call(kernel, out_shape=shapes, in_specs=specs if specs is not N...]
    reduce_sum x1, other arithmetic: 5.14 us -> 0.47 us  [on_device(): jnp.sum(jnp.where(spot[:, None, :] == jnp.arange(longest, dtype=jnp.int32...]
  transfers between devices with their start and end apart: 10 -> 10, of which waited for: 3 -> 3; matrix products, arithmetic and copies ran while one was open for 12% -> 5% of each run, Pallas kernels for 27% -> 35%
where the time goes in v6:
time: 69.7 us; the launch traced here: 69.5 us
  Pallas kernels  38.4 us (55%)
  starting transfers between devices  21.9 us (31%)
  waiting for transfers between devices  4.35 us (6%)
  other arithmetic  2.51 us (4%)
  between operations  1.11 us (2%)
  local copies, waits for them, and re-layouts  1.07 us (2%)
    pallas_call x8, Pallas kernels, call(): pl.pallas_call(kernel, out_shape=shapes, in_specs=specs if specs is not N...  38.4 us
    ppermute x6, starting transfers between devices, on_device(): got[g] = lax.ppermute(outgoing[g], 'clu', routes[g])  9.23 us
    all_to_all x1, starting transfers between devices, on_device(): lax.all_to_all(terms.reshape(4 * clusters, 8, 128), ('sta', 'clu'), split...  9.15 us
    ppermute x3, waiting for transfers between devices, on_device(): lax.ppermute(shares[d], 'sta', [(i, i ^ d) for i in range(4)])  4.33 us
    ppermute x3, starting transfers between devices, on_device(): lax.ppermute(shares[d], 'sta', [(i, i ^ d) for i in range(4)])  3.49 us
  transfers between devices with their start and end apart: 10, of which 3 were waited for; matrix products, arithmetic and copies ran while one was open for 5% of the time, Pallas kernels for 35%

profile of v6, /device:TPU:0, one launch (start us, length us, event | category | flops | bytes accessed | tf_op | source)
XLA Modules:
  0.0 69.5 jit_solution(13405357182748565632)
XLA Ops:
  0.6 0.0 copy-start.6
  0.6 0.0 copy-start.8
  0.7 2.4 %shard_map.122 = (bf16[800,128]{1,0:T(8,128)(2,1)}, bf16[800,128]{1,0:T(8,128)(2,1)}, bf16[800,128]{1,0:T(8,128)(2,1)}, bf16[800,128]{1,0:T(8,128)(2,1)}, bf16[8...) custom-call(s32[6,12]{1,0:T(8,128)} %exports_ref.1, bf16[32,64,128]{2,1,0:T(8,128)(2,1)} %spec_ref.1, bf16[32,4,64]{2,1,0:T(4,128)(2,1)} %partials.1), custom_call_target="tpu_custom_call" | custom-call | flops 2000000000 | bytes 1024 | tf_op jit(solution)/shard_map/pallas_call | solution.py:364
  3.1 0.5 collective-permute-start
  3.6 2.6 %collective-permute-start.1 = (bf16[800,128]{1,0:T(8,128)(2,1)}, bf16[800,128]{1,0:T(8,128)(2,1)S(1)}, u32[]{:S(2)}, u32[]{:S(2)}) collective-permute-start(bf16[800,128]{1,0:T(8,128)(2,1)} %get-tuple-element.37), channel_id=1, source_target_pairs={{0,2},{1,3},{2,0},{3,1},{4,6},{5,7},{6,4},{7,5},{8,10},{9,11},{10,... | collective-permute-start | bytes 614408 | tf_op jit(solution)/shard_map/ppermute | solution.py:423
  6.1 0.1 collective-permute-start.2
  6.3 2.6 %collective-permute-start.3 = (bf16[800,128]{1,0:T(8,128)(2,1)}, bf16[800,128]{1,0:T(8,128)(2,1)S(1)}, u32[]{:S(2)}, u32[]{:S(2)}) collective-permute-start(bf16[800,128]{1,0:T(8,128)(2,1)} %get-tuple-element.45), channel_id=1, source_target_pairs={{0,5},{1,4},{2,7},{3,6},{4,1},{5,0},{6,3},{7,2},{8,13},{9,12},{10,... | collective-permute-start | bytes 614408 | tf_op jit(solution)/shard_map/ppermute | solution.py:423
  8.9 1.3 %collective-permute-start.4 = (bf16[800,128]{1,0:T(8,128)(2,1)}, bf16[800,128]{1,0:T(8,128)(2,1)S(1)}, u32[]{:S(2)}, u32[]{:S(2)}) collective-permute-start(bf16[800,128]{1,0:T(8,128)(2,1)} %get-tuple-element.46), channel_id=1, source_target_pairs={{0,6},{1,7},{2,4},{3,5},{4,2},{5,3},{6,0},{7,1},{8,14},{9,15},{10,... | collective-permute-start | bytes 614408 | tf_op jit(solution)/shard_map/ppermute | solution.py:423
  10.3 0.1 stack.80
  10.4 0.1 select_reduce_fusion.1
  10.5 0.7 fusion.2
  11.2 0.1 convert_reduce_fusion
  11.4 0.1 eq.112
  11.4 0.3 fusion.hot
  11.8 0.1 fusion.1.hot_turned
  12.0 0.1 ceil.11
  12.0 0.1 multiply_reduce_fusion
  12.2 0.1 add_select_fusion
  12.3 0.1 broadcast_in_dim.78
  12.4 0.1 eq.119
  12.5 0.1 reduce_sum.58
  12.7 0.1 stack.87
  12.7 0.1 iota_compare_fusion.4
  12.8 0.1 select_reduce_fusion.2
  12.9 0.1 constant_dynamic-update-slice_fusion.5
  13.0 0.1 constant_dynamic-update-slice_fusion.4
  13.1 0.1 constant_dynamic-update-slice_fusion.3
  13.2 0.1 constant_dynamic-update-slice_fusion.2
  13.3 0.1 constant_dynamic-update-slice_fusion.1
  13.3 0.5 select_reduce_fusion.ids
  13.8 2.1 %collective-permute-start.5 = (bf16[800,128]{1,0:T(8,128)(2,1)}, bf16[800,128]{1,0:T(8,128)(2,1)S(1)}, u32[]{:S(2)}, u32[]{:S(2)}) collective-permute-start(bf16[800,128]{1,0:T(8,128)(2,1)} %get-tuple-element.50), channel_id=1, source_target_pairs={{0,7},{1,6},{2,5},{3,4},{4,3},{5,2},{6,1},{7,0},{8,15},{9,14},{10,... | collective-permute-start | bytes 614408 | tf_op jit(solution)/shard_map/ppermute | solution.py:423
  15.9 10.0 %shard_map.123 = (f32[1024,128]{1,0:T(8,128)S(1)}, f32[32,128,128]{2,1,0:T(8,128)S(1)}, f32[32,64,128]{2,1,0:T(8,128)S(1)}, f32[32,128]{1,0:T(8,128)S(1)}) custom-call(s32[148]{0:T(256)S(1)} %copy-done.4, bf16[16,128,128]{2,1,0:T(8,128)(2,1)S(1)} %bitcast.45, bf16[80,128]{1,0:T(8,128)(2,1)S(1)} %copy-done.3), custom_call_target="tpu_custom_call" | custom-call | flops 8000000000 | bytes 1024 | tf_op jit(solution)/shard_map/pallas_call | solution.py:364
  25.9 8.6 %shard_map.124 = (f32[1536,128]{1,0:T(8,128)S(1)}, bf16[96,128]{1,0:T(8,128)(2,1)S(1)}) custom-call(s32[6,112]{1,0:T(8,128)S(1)} %select_reduce_fusion.ids, s32[6]{0:T(128)S(1)} %convert_element_type.34.counts, bf16[800,128]{1,0:T(8,128)(2,1)S(1)} %collective-permute-done.refs_0_, bf16[800,128]{1,0:T(8,128)(2,1)S(1)} %collective-permute-done.1.refs_1_, ...), custom_call_target="tpu_custom_call" | custom-call | flops 7899999744 | bytes 1024 | tf_op jit(solution)/shard_map/pallas_call | solution.py:364
  34.5 5.8 %shard_map.125 = (f32[1024,128]{1,0:T(8,128)S(1)}, bf16[64,128]{1,0:T(8,128)(2,1)S(1)}) custom-call(s32[6,112]{1,0:T(8,128)S(1)} %select_reduce_fusion.ids, s32[6]{0:T(128)S(1)} %convert_element_type.34.counts, bf16[800,128]{1,0:T(8,128)(2,1)S(1)} %collective-permute-done.3.refs_0_, bf16[800,128]{1,0:T(8,128)(2,1)S(1)} %collective-permute-done.4.refs_1_, ...), custom_call_target="tpu_custom_call" | custom-call | flops 5600000000 | bytes 1024 | tf_op jit(solution)/shard_map/pallas_call | solution.py:364
  40.3 3.1 %shard_map.126 = (f32[512,128]{1,0:T(8,128)S(1)}, bf16[32,128]{1,0:T(8,128)(2,1)S(1)}) custom-call(s32[6,112]{1,0:T(8,128)S(1)} %select_reduce_fusion.ids, s32[6]{0:T(128)S(1)} %convert_element_type.34.counts, bf16[800,128]{1,0:T(8,128)(2,1)S(1)} %collective-permute-done.5.refs_0_, f32[32,128,128]{2,1,0:T(8,128)S(1)} %get-tuple-element.39.refs_3_.refs_2_.refs_1_, ...), custom_call_target="tpu_custom_call" | custom-call | flops 3300000000 | bytes 1024 | tf_op jit(solution)/shard_map/pallas_call | solution.py:364
  43.4 5.9 %shard_map.127 = (f32[56,128]{1,0:T(8,128)S(1)}, f32[56,128]{1,0:T(8,128)S(1)}, f32[56,128]{1,0:T(8,128)S(1)}, f32[56,128]{1,0:T(8,128)S(1)}, bf16[2048,128]{1,0...) custom-call(s32[1]{0:T(128)} %bitcast.7.place, bf16[2048,128]{1,0:T(8,128)(2,1)S(1)} %fusion.hot, ...), custom_call_target="tpu_custom_call" | custom-call | flops 3000000000 | bytes 1024 | tf_op jit(solution)/shard_map/pallas_call | solution.py:364
  49.4 1.3 %shard_map.128 = f32[4,8,8,128]{3,2,1,0:T(8,128)} custom-call(bf16[128,2048]{1,0:T(8,128)(2,1)S(1)} %fusion.1.hot_turned, bf16[2048,128]{1,0:T(8,128)(2,1)S(1)} %get-tuple-element.59.slots, bf16[128,256]{1,0:T(8,128)(2,1)S(1)} %get-tuple-element.60.geo, f32[32,128]{1,0:T(8,128)S(1)} %get-tuple-element.61.own), custom_call_target="tpu_custom_call" | custom-call | flops 1000000000 | bytes 1024 | tf_op jit(solution)/shard_map/pallas_call | solution.py:364
  50.7 9.1 %all-to-all-start = ((f32[32,8,128]{2,1,0:T(8,128)}), f32[32,8,128]{2,1,0:T(8,128)S(1)}, u32[]{:S(2)}, u32[]{:S(2)}) async-start(f32[32,8,128]{2,1,0:T(8,128)} %bitcast.19), calls=%async_computation | async-start | bytes 262144 | tf_op jit(solution)/shard_map/all_to_all | solution.py:518
  59.8 0.1 constant_dynamic-update-slice_fusion
  59.9 1.8 %collective-permute-start.6 = (f32[56,128]{1,0:T(8,128)S(1)}, f32[56,128]{1,0:T(8,128)S(1)}, u32[]{:S(2)}, u32[]{:S(2)}) collective-permute-start(f32[56,128]{1,0:T(8,128)S(1)} %get-tuple-element.56), channel_id=1, source_target_pairs={{0,8},{8,0},{16,24},{24,16},{1,9},{9,1},{17,25},{25,17},{2,10},{10... | collective-permute-start | bytes 86024 | tf_op jit(solution)/shard_map/ppermute | solution.py:512
  61.7 1.5 %collective-permute-start.7 = (f32[56,128]{1,0:T(8,128)S(1)}, f32[56,128]{1,0:T(8,128)S(1)}, u32[]{:S(2)}, u32[]{:S(2)}) collective-permute-start(f32[56,128]{1,0:T(8,128)S(1)} %get-tuple-element.57), channel_id=1, source_target_pairs={{0,16},{8,24},{16,0},{24,8},{1,17},{9,25},{17,1},{25,9},{2,18},{10... | collective-permute-start | bytes 86024 | tf_op jit(solution)/shard_map/ppermute | solution.py:512
  63.2 0.3 collective-permute-start.8
  63.4 0.2 compare_convert_fusion.owners
  63.6 0.1 stack.73.clusters
  63.7 0.3 collective-permute-done.6.one
  64.0 1.6 %collective-permute-done.7.two = f32[56,128]{1,0:T(8,128)S(1)} collective-permute-done((f32[56,128]{1,0:T(8,128)S(1)}, f32[56,128]{1,0:T(8,128)S(1)}, u32[]{:S(2)}, u32[]{:S(2)}) %collective-permute-start.7) | collective-permute-done | bytes 28704 | tf_op jit(solution)/shard_map/ppermute | solution.py:512
  65.6 2.4 %collective-permute-done.8.three = f32[56,128]{1,0:T(8,128)S(1)} collective-permute-done((f32[56,128]{1,0:T(8,128)S(1)}, f32[56,128]{1,0:T(8,128)S(1)}, u32[]{:S(2)}, u32[]{:S(2)}) %collective-permute-start.8) | collective-permute-done | bytes 28704 | tf_op jit(solution)/shard_map/ppermute | solution.py:512
  68.0 1.5 %shard_map.129 = (f32[4,32,51]{2,1,0:T(8,128)}, f32[1,32]{1,0:T(1,128)}) custom-call(s32[7]{0:T(128)S(1)} %stack.73.clusters, f32[56,128]{1,0:T(8,128)S(1)} %get-tuple-element.55.own, f32[56,128]{1,0:T(8,128)S(1)} %collective-permute-done.6.one, f32[56,128]{1,0:T(8,128)S(1)} %collective-permute-done.7.two, f32[56,128]{1,0:T(8,128)S(1)} %collective-permute-done.8.three, ...), custom_call_target="tpu_custom_call" | custom-call | flops 1000000000 | bytes 1024 | tf_op jit(solution)/shard_map/pallas_call | solution.py:364
  (40 shorter events, 0.2 us)
Async XLA Ops:
  0.6 11.4 %copy-start.6 = (f32[6,6]{1,0:T(8,128)S(1)}, f32[6,6]{1,0:T(8,128)}, u32[]{:S(2)}) copy-start(f32[6,6]{1,0:T(8,128)} %constant.148.clone) | copy-start | bytes 436
  0.6 11.5 %copy-start.8 = (bf16[32,32,1]{1,0,2:T(8,128)(2,1)S(1)}, bf16[32,32,1]{1,0,2:T(8,128)(2,1)}, u32[]{:S(2)}) copy-start(bf16[32,32,1]{1,0,2:T(8,128)(2,1)} %constant.203) | copy-start | bytes 6148
  0.7 11.5 %copy-start.9 = (s32[6,6]{1,0:T(8,128)S(1)}, s32[6,6]{1,0:T(8,128)}, u32[]{:S(2)}) copy-start(s32[6,6]{1,0:T(8,128)} %constant.149.clone) | copy-start | bytes 436
  0.7 12.3 %copy-start.10 = (s32[128]{0:T(128)S(1)}, s32[128]{0:T(128)}, u32[]{:S(2)}) copy-start(s32[128]{0:T(128)} %constant.150.clone) | copy-start | bytes 1540
  0.7 15.2 %copy-start.3 = (bf16[80,128]{1,0:T(8,128)(2,1)S(1)}, bf16[80,128]{1,0:T(8,128)(2,1)}, u32[]{:S(2)}) copy-start(bf16[80,128]{1,0:T(8,128)(2,1)} %constant.166.table.refs_6_.refs_5_.refs_4_) | copy-start | bytes 61444
  0.7 15.2 %copy-start.4 = (s32[148]{0:T(256)S(1)}, s32[148]{0:T(256)}, u32[]{:S(2)}) copy-start(s32[148]{0:T(256)} %constant.146.clone.ids) | copy-start | bytes 1780
  0.7 15.2 %copy-start.1 = (bf16[32,64,128]{2,1,0:T(8,128)(2,1)S(1)}, bf16[32,64,128]{2,1,0:T(8,128)(2,1)}, u32[]{:S(2)}) copy-start(bf16[32,64,128]{2,1,0:T(8,128)(2,1)} %spec_ref.1) | copy-start | bytes 1572868
  0.7 12.1 %copy-start.7 = (s32[6,12]{1,0:T(8,128)S(1)}, s32[6,12]{1,0:T(8,128)}, u32[]{:S(2)}) copy-start(s32[6,12]{1,0:T(8,128)} %exports_ref.1) | copy-start | bytes 868
  0.7 9.5 %copy-start.5 = (s32[32,50]{1,0:T(8,128)S(1)}, s32[32,50]{1,0:T(8,128)}, u32[]{:S(2)}) copy-start(s32[32,50]{1,0:T(8,128)} %param.13) | copy-start | bytes 19204
  3.1 10.7 %collective-permute-start = (bf16[800,128]{1,0:T(8,128)(2,1)}, bf16[800,128]{1,0:T(8,128)(2,1)S(1)}, u32[]{:S(2)}, u32[]{:S(2)}) collective-permute-start(bf16[800,128]{1,0:T(8,128)(2,1)} %get-tuple-element.33), channel_id=1, source_target_pairs={{0,1},{1,0},{2,3},{3,2},{4,5},{5,4},{6,7},{7,6},{8,9},{9,8},{10,11... | collective-permute-start | bytes 614408 | tf_op jit(solution)/shard_map/ppermute | solution.py:423
  3.6 22.3 %collective-permute-start.1 = (bf16[800,128]{1,0:T(8,128)(2,1)}, bf16[800,128]{1,0:T(8,128)(2,1)S(1)}, u32[]{:S(2)}, u32[]{:S(2)}) collective-permute-start(bf16[800,128]{1,0:T(8,128)(2,1)} %get-tuple-element.37), channel_id=1, source_target_pairs={{0,2},{1,3},{2,0},{3,1},{4,6},{5,7},{6,4},{7,5},{8,10},{9,11},{10,... | collective-permute-start | bytes 614408 | tf_op jit(solution)/shard_map/ppermute | solution.py:423
  6.1 19.8 %collective-permute-start.2 = (bf16[800,128]{1,0:T(8,128)(2,1)}, bf16[800,128]{1,0:T(8,128)(2,1)S(1)}, u32[]{:S(2)}, u32[]{:S(2)}) collective-permute-start(bf16[800,128]{1,0:T(8,128)(2,1)} %get-tuple-element.38), channel_id=1, source_target_pairs={{0,3},{1,2},{2,1},{3,0},{4,7},{5,6},{6,5},{7,4},{8,11},{9,10},{10,... | collective-permute-start | bytes 614408 | tf_op jit(solution)/shard_map/ppermute | solution.py:423
  6.3 28.2 %collective-permute-start.3 = (bf16[800,128]{1,0:T(8,128)(2,1)}, bf16[800,128]{1,0:T(8,128)(2,1)S(1)}, u32[]{:S(2)}, u32[]{:S(2)}) collective-permute-start(bf16[800,128]{1,0:T(8,128)(2,1)} %get-tuple-element.45), channel_id=1, source_target_pairs={{0,5},{1,4},{2,7},{3,6},{4,1},{5,0},{6,3},{7,2},{8,13},{9,12},{10,... | collective-permute-start | bytes 614408 | tf_op jit(solution)/shard_map/ppermute | solution.py:423
  8.9 25.6 %collective-permute-start.4 = (bf16[800,128]{1,0:T(8,128)(2,1)}, bf16[800,128]{1,0:T(8,128)(2,1)S(1)}, u32[]{:S(2)}, u32[]{:S(2)}) collective-permute-start(bf16[800,128]{1,0:T(8,128)(2,1)} %get-tuple-element.46), channel_id=1, source_target_pairs={{0,6},{1,7},{2,4},{3,5},{4,2},{5,3},{6,0},{7,1},{8,14},{9,15},{10,... | collective-permute-start | bytes 614408 | tf_op jit(solution)/shard_map/ppermute | solution.py:423
  13.8 26.5 %collective-permute-start.5 = (bf16[800,128]{1,0:T(8,128)(2,1)}, bf16[800,128]{1,0:T(8,128)(2,1)S(1)}, u32[]{:S(2)}, u32[]{:S(2)}) collective-permute-start(bf16[800,128]{1,0:T(8,128)(2,1)} %get-tuple-element.50), channel_id=1, source_target_pairs={{0,7},{1,6},{2,5},{3,4},{4,3},{5,2},{6,1},{7,0},{8,15},{9,14},{10,... | collective-permute-start | bytes 614408 | tf_op jit(solution)/shard_map/ppermute | solution.py:423
  40.3 3.1 %copy-start = (s32[32,50,64]{2,0,1:T(8,128)S(1)}, s32[32,50,64]{2,0,1:T(8,128)}, u32[]{:S(2)}) copy-start(s32[32,50,64]{2,0,1:T(8,128)} %param.14) | copy-start | bytes 1228804
  40.3 3.1 %copy-start.2 = (bf16[32,4,64]{2,1,0:T(4,128)(2,1)S(1)}, bf16[32,4,64]{2,1,0:T(4,128)(2,1)}, u32[]{:S(2)}) copy-start(bf16[32,4,64]{2,1,0:T(4,128)(2,1)} %partials.1) | copy-start | bytes 49156
  50.7 17.3 %all-to-all-start = ((f32[32,8,128]{2,1,0:T(8,128)}), f32[32,8,128]{2,1,0:T(8,128)S(1)}, u32[]{:S(2)}, u32[]{:S(2)}) async-start(f32[32,8,128]{2,1,0:T(8,128)} %bitcast.19), calls=%async_computation | async-start | bytes 262144 | tf_op jit(solution)/shard_map/all_to_all | solution.py:518
  59.9 4.1 %collective-permute-start.6 = (f32[56,128]{1,0:T(8,128)S(1)}, f32[56,128]{1,0:T(8,128)S(1)}, u32[]{:S(2)}, u32[]{:S(2)}) collective-permute-start(f32[56,128]{1,0:T(8,128)S(1)} %get-tuple-element.56), channel_id=1, source_target_pairs={{0,8},{8,0},{16,24},{24,16},{1,9},{9,1},{17,25},{25,17},{2,10},{10... | collective-permute-start | bytes 86024 | tf_op jit(solution)/shard_map/ppermute | solution.py:512
  61.7 3.9 %collective-permute-start.7 = (f32[56,128]{1,0:T(8,128)S(1)}, f32[56,128]{1,0:T(8,128)S(1)}, u32[]{:S(2)}, u32[]{:S(2)}) collective-permute-start(f32[56,128]{1,0:T(8,128)S(1)} %get-tuple-element.57), channel_id=1, source_target_pairs={{0,16},{8,24},{16,0},{24,8},{1,17},{9,25},{17,1},{25,9},{2,18},{10... | collective-permute-start | bytes 86024 | tf_op jit(solution)/shard_map/ppermute | solution.py:512
  63.2 4.9 %collective-permute-start.8 = (f32[56,128]{1,0:T(8,128)S(1)}, f32[56,128]{1,0:T(8,128)S(1)}, u32[]{:S(2)}, u32[]{:S(2)}) collective-permute-start(f32[56,128]{1,0:T(8,128)S(1)} %get-tuple-element.58), channel_id=1, source_target_pairs={{0,24},{8,16},{16,8},{24,0},{1,25},{9,17},{17,9},{25,1},{2,26},{10... | collective-permute-start | bytes 86024 | tf_op jit(solution)/shard_map/ppermute | solution.py:512

commit v7 on v5

--- a/solution.py
+++ b/solution.py
@@ -17,7 +17,7 @@
 BATCH = 8
 WIDE = 4
 UNROLL = 8
-STAGES = 2
+STAGE_SIZES = (2, 2, 2)
 
 
 def moment_table(freq_count):
@@ -76,7 +76,7 @@
         eb[j : j + 1, :] = jnp.sum(square, axis=0, keepdims=True)
 
 
-def listed_pairs(ids, batches, da, sq, ea, bp, bb, eb, table, work, store, freq, scale):
+def listed_pairs(fetch, batches, da, sq, ea, bp, bb, eb, table, work, store, freq, scale):
     xs, reals, rm, rs, rt, rb, rz, re = work
     lead = lax.broadcasted_iota(jnp.int32, (8, 1), 0) == 0
     step = lax.broadcasted_iota(jnp.int32, (8, 1), 0).astype(F32)
@@ -84,7 +84,7 @@
     unit = (math.pi / freq) ** 2
 
     def split(t, d):
-        code = ids[t * (BATCH // 2) + d]
+        code = fetch(t * (BATCH // 2) + d)
         return (code >> 12) & 31, code >> 17, ((code >> 6) & 63, code & 63)
 
     def cross_stage(t, slot):
@@ -203,10 +203,10 @@
         out[pl.ds(column * events + e, 1), :] = jnp.where(row, even, -even)
         out[pl.ds((column + 1) * events + e, 1), :] = jnp.where(row, odd, -odd)
 
-    listed_pairs(ids, batches, da, sq, ea, bp, bb, eb, table, work, store, freq, scale)
-
-
-def import_kernel(stage, arrivals, freq, events, cap, scale, ids, counts, *refs):
+    listed_pairs(lambda n: ids[n], batches, da, sq, ea, bp, bb, eb, table, work, store, freq, scale)
+
+
+def import_kernel(begin, arrivals, freq, events, cap, scale, ids, counts, *refs):
     got, (da, sq, ea, table, out, tail, bp, bb, eb), work = refs[:arrivals], refs[arrivals : arrivals + 9], refs[arrivals + 9 :]
     pairs = cap // 2
 
@@ -222,8 +222,19 @@
         out[pl.ds(e * arrivals * GROUP_ROWS + column, 1), :] = even
         out[pl.ds(e * arrivals * GROUP_ROWS + column + 1, 1), :] = odd
 
-    batches = (counts[stage] + BATCH // 2 - 1) // (BATCH // 2)
-    listed_pairs(ids.at[stage], batches, da, sq, ea, bp, bb, eb, table, work, store, freq, scale)
+    ends = [counts[begin]]
+    for g in range(1, arrivals):
+        ends.append(ends[-1] + counts[begin + g])
+
+    def fetch(n):
+        group, start = 0, 0
+        for end in ends[:-1]:
+            group = group + jnp.where(n >= end, 1, 0)
+            start = jnp.where(n >= end, end, start)
+        return ids[begin + group, n - start]
+
+    batches = (ends[-1] + BATCH // 2 - 1) // (BATCH // 2)
+    listed_pairs(fetch, batches, da, sq, ea, bp, bb, eb, table, work, store, freq, scale)
 
 
 def weight_scratch(pairs, freq):
@@ -246,9 +257,9 @@
 
 
 def sums_kernel(groups, events, slots, hot, hot_turned, mask, partials, *refs):
-    tables, tails = refs[: STAGES + 1], refs[STAGES + 1 : 2 * STAGES + 1]
-    slots_out, terms_out, geo_out, own, own_geo = refs[2 * STAGES + 1 :]
-    import_rows = groups // STAGES * GROUP_ROWS
+    stages = len(STAGE_SIZES)
+    tables, tails = refs[: stages + 1], refs[stages + 1 : 2 * stages + 1]
+    slots_out, terms_out, geo_out, own, own_geo = refs[2 * stages + 1 :]
     cands = hot.shape[1]
     rest = jnp.zeros((SLOT_ROWS - slots, 128), F32)
 
@@ -257,8 +268,9 @@
         for u in range(UNROLL):
             e = step * UNROLL + u
             parts = [tables[0][pl.ds(pl.multiple_of(e * events, 8), events), :]]
-            for t in tables[1:]:
-                parts.append(t[pl.ds(pl.multiple_of(e * import_rows, 8), import_rows), :])
+            for t, size in zip(tables[1:], STAGE_SIZES):
+                rows = size * GROUP_ROWS
+                parts.append(t[pl.ds(pl.multiple_of(e * rows, 8), rows), :])
             every = jnp.concatenate(parts, axis=0).astype(BF16)
             rows = pl.ds(pl.multiple_of(e * SLOT_ROWS, SLOT_ROWS), SLOT_ROWS)
             live = mask[pl.ds(e, slots, stride=events), :].astype(F32)
@@ -277,7 +289,7 @@
     turned = pltpu.roll(totals, 64, 1)
     weights = jnp.where(low, totals, turned)
     moves = jnp.where(low, turned, totals)
-    ends = [t[start : start + 2 * GROUP_ROWS, :] for t in tails for start in range(0, 2 * import_rows, 2 * GROUP_ROWS)]
+    ends = [t[start : start + 2 * GROUP_ROWS, :] for t in tails for start in range(0, t.shape[0], 2 * GROUP_ROWS)]
     first = jnp.concatenate([own_geo[:events].astype(BF16)] + [t[:GROUP_ROWS] for t in ends], axis=0)
     second = jnp.concatenate([own_geo[events:].astype(BF16)] + [t[GROUP_ROWS:] for t in ends], axis=0)
     geo_out[:, :128] = first
@@ -451,20 +463,19 @@
     entry = far % cap
     named = jnp.where(pair_list < events, -1, arrival * half + entry // 2)
     wanted = jnp.any(named[:, :, None] == jnp.arange(groups * half, dtype=jnp.int32)[None, None, :], axis=1)
-    arrivals = groups // STAGES
-    pairs = arrivals * half
-    wanted = wanted.astype(F32).T.reshape(STAGES, pairs, events)
+    wanted = wanted.astype(F32).T.reshape(groups, half, events)
     ranks = np.arange(events)
     rank = jnp.einsum("gje,ef->gjf", wanted, jnp.asarray(ranks[:, None] < ranks[None, :], F32))
     rounded = jnp.ceil(jnp.sum(wanted, axis=2) * 0.5)
-    ranks = np.arange(pairs)
+    ranks = np.arange(half)
     start = jnp.sum(rounded[:, :, None] * jnp.asarray(ranks[:, None] < ranks[None, :], F32)[None], axis=1)
     rank = rank.astype(jnp.int32)
-    spot = jnp.where(wanted > 0, start.astype(jnp.int32)[:, :, None] + (rank >> 1), -1).reshape(STAGES, pairs * events)
+    spot = jnp.where(wanted > 0, start.astype(jnp.int32)[:, :, None] + (rank >> 1), -1).reshape(groups, half * events)
     event_ids = jnp.arange(events, dtype=jnp.int32)[None, None, :]
-    pair_codes = jnp.asarray(((ranks // half * GROUP_ROWS + ranks % half * 2) << 17) + (ranks << 12), jnp.int32)
-    code = jnp.where(rank & 1 == 0, pair_codes[None, :, None] + (event_ids << 6), event_ids).reshape(STAGES, pairs * events)
-    longest = pairs * events // 2 + 3 * BATCH // 2
+    inside = np.concatenate([np.arange(size) for size in STAGE_SIZES])[:, None]
+    pair_codes = jnp.asarray(((inside * GROUP_ROWS + 2 * ranks) << 17) + ((inside * half + ranks) << 12), jnp.int32)
+    code = jnp.where(rank & 1 == 0, pair_codes[:, :, None] + (event_ids << 6), event_ids).reshape(groups, half * events)
+    longest = half * events // 2 + 4 * BATCH // 2
     lists = jnp.sum(
         jnp.where(spot[:, None, :] == jnp.arange(longest, dtype=jnp.int32)[None, :, None], code[:, None, :], 0), axis=2
     )
@@ -485,26 +496,28 @@
     owners = jnp.concatenate(owner_rows)[:, None] == (jnp.arange(128, dtype=jnp.int32) % events)[None, :]
     owners = owners.astype(BF16)
 
-    tables, tails = [None] * STAGES, [None] * STAGES
-    for g in range(STAGES):
-        tables[g], tails[g] = call(
-            functools.partial(import_kernel, g, arrivals, freq, events, cap, scale),
-            [((events * arrivals * GROUP_ROWS, 128), F32), ((arrivals * 2 * GROUP_ROWS, 128), BF16)],
-            (lists, counts, *got[g * arrivals : (g + 1) * arrivals], dup, square, energy, table),
-            scratch=weight_scratch(pairs, freq),
-            specs=[smem] * 2 + vmem(arrivals + 4),
-            micros=8.0,
+    tables, tails, begin = [], [], 0
+    for size in STAGE_SIZES:
+        if tables:
+            lists, tables[-1] = lax.optimization_barrier((lists, tables[-1]))
+        table_part, tail_part = call(
+            functools.partial(import_kernel, begin, size, freq, events, cap, scale),
+            [((events * size * GROUP_ROWS, 128), F32), ((size * 2 * GROUP_ROWS, 128), BF16)],
+            (lists, counts, *got[begin : begin + size], dup, square, energy, table),
+            scratch=weight_scratch(size * half, freq),
+            specs=[smem] * 2 + vmem(size + 4),
+            micros=1.0 + 2.3 * size,
         )
+        tables.append(table_part)
+        tails.append(tail_part)
+        begin += size
 
     weights, terms, geo = call(
         functools.partial(sums_kernel, groups, events, slots),
         [((events * SLOT_ROWS, 128), BF16), ((4, clusters, 8, 128), F32), ((cands, 256), BF16)],
         (hot, hot_turned, mask, partials, local, *tables, *tails),
         scratch=[pltpu.VMEM((events, 128), F32), pltpu.VMEM((2 * events, 128), F32)],
-        micros=2.0,
-    )
-    terms = lax.all_to_all(
-        terms.reshape(4 * clusters, 8, 128), ("sta", "clu"), split_axis=0, concat_axis=0, tiled=True
+        micros=2.4,
     )
     message_rows = -(-(slots + 1) // 8) * 8
     place = lax.axis_index("sta").astype(jnp.int32).reshape(1)
@@ -514,9 +527,13 @@
         (place, hot, weights, geo, partials),
         scratch=[pltpu.VMEM((16 * events, 128), F32)],
         specs=[smem] + vmem(4),
-        micros=3.0,
+        micros=1.7,
     )
     shares = [shares[0]] + [lax.ppermute(shares[d], "sta", [(i, i ^ d) for i in range(4)]) for d in range(1, 4)]
+    terms, shares[1] = lax.optimization_barrier((terms, shares[1]))
+    terms = lax.all_to_all(
+        terms.reshape(4 * clusters, 8, 128), ("sta", "clu"), split_axis=0, concat_axis=0, tiled=True
+    )
     sources = jnp.stack([me] + [jnp.asarray(receiver(g, me), jnp.int32) for g in range(groups)])
     normal, right = call(
         functools.partial(total_kernel, groups, events, slots),

time: 69.7 us -> 64.9 us (0.931)
  other arithmetic: 7.28 us -> 2.51 us
  starting transfers between devices: 22.7 us -> 19.2 us
  waiting for transfers between devices: 4.26 us -> 6.89 us
  Pallas kernels: 32.4 us -> 33.8 us
    reduce_sum x1, other arithmetic: 5.14 us -> 0.47 us  [on_device(): jnp.sum(jnp.where(spot[:, None, :] == jnp.arange(longest, dtype=jnp.int32...]
    all_to_all x1, starting transfers between devices: 9.62 us -> 5.18 us  [on_device(): lax.all_to_all(terms.reshape(4 * clusters, 8, 128), ('sta', 'clu'), split...]
    pallas_call x7 -> x8, Pallas kernels: 32.4 us -> 33.8 us  [call(): pl.pallas_call(kernel, out_shape=shapes, in_specs=specs if specs is not N...]
    all_to_all x1, waiting for transfers between devices: 0.01 us -> 1.39 us  [on_device(): lax.all_to_all(terms.reshape(4 * clusters, 8, 128), ('sta', 'clu'), split...]
    ppermute x3, waiting for transfers between devices: 4.24 us -> 5.49 us  [on_device(): lax.ppermute(shares[d], 'sta', [(i, i ^ d) for i in range(4)])]
    ppermute x3, starting transfers between devices: 3.55 us -> 4.8 us  [on_device(): lax.ppermute(shares[d], 'sta', [(i, i ^ d) for i in range(4)])]
  transfers between devices with their start and end apart: 10 -> 10, of which waited for: 3 -> 4; matrix products, arithmetic and copies ran while one was open for 12% -> 6% of each run, Pallas kernels for 27% -> 31%
where the time goes in v7:
time: 64.9 us; the launch traced here: 64.7 us
  Pallas kernels  33.8 us (52%)
  starting transfers between devices  19.2 us (30%)
  waiting for transfers between devices  6.89 us (11%)
  other arithmetic  2.51 us (4%)
  between operations  1.11 us (2%)
  local copies, waits for them, and re-layouts  1.06 us (2%)
    pallas_call x8, Pallas kernels, call(): pl.pallas_call(kernel, out_shape=shapes, in_specs=specs if specs is not N...  33.8 us
    ppermute x6, starting transfers between devices, on_device(): got[g] = lax.ppermute(outgoing[g], 'clu', routes[g])  9.23 us
    ppermute x3, waiting for transfers between devices, on_device(): lax.ppermute(shares[d], 'sta', [(i, i ^ d) for i in range(4)])  5.49 us
    all_to_all x1, starting transfers between devices, on_device(): lax.all_to_all(terms.reshape(4 * clusters, 8, 128), ('sta', 'clu'), split...  5.18 us
    ppermute x3, starting transfers between devices, on_device(): lax.ppermute(shares[d], 'sta', [(i, i ^ d) for i in range(4)])  4.8 us
    all_to_all x1, waiting for transfers between devices, on_device(): lax.all_to_all(terms.reshape(4 * clusters, 8, 128), ('sta', 'clu'), split...  1.39 us
  transfers between devices with their start and end apart: 10, of which 4 were waited for; matrix products, arithmetic and copies ran while one was open for 6% of the time, Pallas kernels for 31%

profile of v7, /device:TPU:0, one launch (start us, length us, event | category | flops | bytes accessed | tf_op | source)
XLA Modules:
  0.0 64.7 jit_solution(6646278349139626156)
XLA Ops:
  0.6 0.0 copy-start.6
  0.7 2.4 %shard_map.122 = (bf16[800,128]{1,0:T(8,128)(2,1)}, bf16[800,128]{1,0:T(8,128)(2,1)}, bf16[800,128]{1,0:T(8,128)(2,1)}, bf16[800,128]{1,0:T(8,128)(2,1)}, bf16[8...) custom-call(s32[6,12]{1,0:T(8,128)} %exports_ref.1, bf16[32,64,128]{2,1,0:T(8,128)(2,1)} %spec_ref.1, bf16[32,4,64]{2,1,0:T(4,128)(2,1)} %partials.3), custom_call_target="tpu_custom_call" | custom-call | flops 2000000000 | bytes 1024 | tf_op jit(solution)/shard_map/pallas_call | solution.py:378
  3.1 0.5 collective-permute-start
  3.6 2.6 %collective-permute-start.1 = (bf16[800,128]{1,0:T(8,128)(2,1)}, bf16[800,128]{1,0:T(8,128)(2,1)S(1)}, u32[]{:S(2)}, u32[]{:S(2)}) collective-permute-start(bf16[800,128]{1,0:T(8,128)(2,1)} %get-tuple-element.39), channel_id=1, source_target_pairs={{0,2},{1,3},{2,0},{3,1},{4,6},{5,7},{6,4},{7,5},{8,10},{9,11},{10,... | collective-permute-start | bytes 614408 | tf_op jit(solution)/shard_map/ppermute | solution.py:437
  6.1 0.1 collective-permute-start.2
  6.3 2.6 %collective-permute-start.3 = (bf16[800,128]{1,0:T(8,128)(2,1)}, bf16[800,128]{1,0:T(8,128)(2,1)S(1)}, u32[]{:S(2)}, u32[]{:S(2)}) collective-permute-start(bf16[800,128]{1,0:T(8,128)(2,1)} %get-tuple-element.47), channel_id=1, source_target_pairs={{0,5},{1,4},{2,7},{3,6},{4,1},{5,0},{6,3},{7,2},{8,13},{9,12},{10,... | collective-permute-start | bytes 614408 | tf_op jit(solution)/shard_map/ppermute | solution.py:437
  8.9 1.3 %collective-permute-start.4 = (bf16[800,128]{1,0:T(8,128)(2,1)}, bf16[800,128]{1,0:T(8,128)(2,1)S(1)}, u32[]{:S(2)}, u32[]{:S(2)}) collective-permute-start(bf16[800,128]{1,0:T(8,128)(2,1)} %get-tuple-element.51), channel_id=1, source_target_pairs={{0,6},{1,7},{2,4},{3,5},{4,2},{5,3},{6,0},{7,1},{8,14},{9,15},{10,... | collective-permute-start | bytes 614408 | tf_op jit(solution)/shard_map/ppermute | solution.py:437
  10.3 0.1 stack.80
  10.4 0.1 select_reduce_fusion.1
  10.5 0.7 %fusion.2 = pred[32,36]{0,1:T(8,128)(4,1)S(1)} fusion(s32[32,50]{1,0:T(8,128)S(1)} %get-tuple-element.68), kind=kLoop, calls=%fused_computation.8 | loop fusion | flops 114048 | bytes 7552 | tf_op jit(solution)/shard_map/reduce_or | solution.py:465
  11.2 0.1 convert_reduce_fusion
  11.4 0.1 eq.112
  11.4 0.3 fusion.hot
  11.8 0.1 fusion.1.hot_turned
  12.0 0.1 ceil.11
  12.0 0.1 multiply_reduce_fusion
  12.2 0.1 add_select_fusion
  12.4 0.1 broadcast_in_dim.78
  12.4 0.1 eq.122
  12.5 0.1 reduce_sum.58
  12.7 0.1 stack.87
  12.7 0.1 iota_compare_fusion.4
  12.8 0.1 select_reduce_fusion.2
  13.0 0.1 constant_dynamic-update-slice_fusion.5
  13.0 0.1 constant_dynamic-update-slice_fusion.4
  13.1 0.1 constant_dynamic-update-slice_fusion.3
  13.2 0.1 constant_dynamic-update-slice_fusion.2
  13.3 0.5 select_reduce_fusion.ids
  13.8 2.1 %collective-permute-start.5 = (bf16[800,128]{1,0:T(8,128)(2,1)}, bf16[800,128]{1,0:T(8,128)(2,1)S(1)}, u32[]{:S(2)}, u32[]{:S(2)}) collective-permute-start(bf16[800,128]{1,0:T(8,128)(2,1)} %get-tuple-element.52), channel_id=1, source_target_pairs={{0,7},{1,6},{2,5},{3,4},{4,3},{5,2},{6,1},{7,0},{8,15},{9,14},{10,... | collective-permute-start | bytes 614408 | tf_op jit(solution)/shard_map/ppermute | solution.py:437
  15.9 9.2 %shard_map.123 = (f32[1024,128]{1,0:T(8,128)S(1)}, f32[32,128,128]{2,1,0:T(8,128)S(1)}, f32[32,64,128]{2,1,0:T(8,128)S(1)}, f32[32,128]{1,0:T(8,128)S(1)}) custom-call(s32[148]{0:T(256)S(1)} %copy-done.4, bf16[16,128,128]{2,1,0:T(8,128)(2,1)S(1)} %bitcast.45, bf16[80,64]{1,0:T(8,128)(2,1)S(1)} %copy-done.3), custom_call_target="tpu_custom_call" | custom-call | flops 8000000000 | bytes 1024 | tf_op jit(solution)/shard_map/pallas_call | solution.py:378
  25.1 6.0 %shard_map.124 = (f32[1024,128]{1,0:T(8,128)S(1)}, bf16[64,128]{1,0:T(8,128)(2,1)S(1)}) custom-call(s32[6,112]{1,0:T(8,128)S(1)} %select_reduce_fusion.ids, s32[6]{0:T(128)S(1)} %convert_element_type.35.counts, bf16[800,128]{1,0:T(8,128)(2,1)S(1)} %collective-permute-done.refs_0_, bf16[800,128]{1,0:T(8,128)(2,1)S(1)} %collective-permute-done.1.refs_1_, ...), custom_call_target="tpu_custom_call" | custom-call | flops 5600000000 | bytes 1024 | tf_op jit(solution)/shard_map/pallas_call | solution.py:378
  31.2 5.1 %shard_map.125 = (f32[1024,128]{1,0:T(8,128)S(1)}, bf16[64,128]{1,0:T(8,128)(2,1)S(1)}) custom-call(s32[6,112]{1,0:T(8,128)S(1)} %select_reduce_fusion.ids, s32[6]{0:T(128)S(1)} %convert_element_type.35.counts, bf16[800,128]{1,0:T(8,128)(2,1)S(1)} %collective-permute-done.2.refs_0_, bf16[800,128]{1,0:T(8,128)(2,1)S(1)} %collective-permute-done.3.refs_1_, ...), custom_call_target="tpu_custom_call" | custom-call | flops 5600000000 | bytes 1024 | tf_op jit(solution)/shard_map/pallas_call | solution.py:378
  36.3 5.6 %shard_map.126 = (f32[1024,128]{1,0:T(8,128)S(1)}, bf16[64,128]{1,0:T(8,128)(2,1)S(1)}) custom-call(s32[6,112]{1,0:T(8,128)S(1)} %select_reduce_fusion.ids, s32[6]{0:T(128)S(1)} %convert_element_type.35.counts, bf16[800,128]{1,0:T(8,128)(2,1)S(1)} %collective-permute-done.4.refs_0_, bf16[800,128]{1,0:T(8,128)(2,1)S(1)} %collective-permute-done.5.refs_1_, ...), custom_call_target="tpu_custom_call" | custom-call | flops 5600000000 | bytes 1024 | tf_op jit(solution)/shard_map/pallas_call | solution.py:378
  41.9 2.4 %shard_map.127 = (bf16[2048,128]{1,0:T(8,128)(2,1)S(1)}, f32[4,8,8,128]{3,2,1,0:T(8,128)}, bf16[128,256]{1,0:T(8,128)(2,1)S(1)}) custom-call(bf16[2048,128]{1,0:T(8,128)(2,1)S(1)} %fusion.hot, bf16[128,2048]{1,0:T(8,128)(2,1)S(1)} %fusion.1.hot_turned, s32[1600,64]{1,0:T(8,128)S(1)} %bitcast.44, bf16[32,4,64]{2,1,0:T(4,128)(2,1)S(1)} %copy-done.2, ...), custom_call_target="tpu_custom_call" | custom-call | flops 2400000000 | bytes 1024 | tf_op jit(solution)/shard_map/pallas_call | solution.py:378
  44.3 1.7 %shard_map.128 = (f32[56,128]{1,0:T(8,128)S(1)}, f32[56,128]{1,0:T(8,128)S(1)}, f32[56,128]{1,0:T(8,128)S(1)}, f32[56,128]{1,0:T(8,128)S(1)}) custom-call(s32[1]{0:T(128)} %bitcast.7.place, bf16[2048,128]{1,0:T(8,128)(2,1)S(1)} %fusion.hot, bf16[2048,128]{1,0:T(8,128)(2,1)S(1)} %get-tuple-element.57.slots, bf16[128,256]{1,0:T(8,128)(2,1)S(1)} %get-tuple-element.58.geo, ...), custom_call_target="tpu_custom_call" | custom-call | flops 1700000000 | bytes 1024 | tf_op jit(solution)/shard_map/pallas_call | solution.py:378
  46.0 1.6 %collective-permute-start.6 = (f32[56,128]{1,0:T(8,128)S(1)}, f32[56,128]{1,0:T(8,128)S(1)}, u32[]{:S(2)}, u32[]{:S(2)}) collective-permute-start(f32[56,128]{1,0:T(8,128)S(1)} %get-tuple-element.61), channel_id=1, source_target_pairs={{0,8},{8,0},{16,24},{24,16},{1,9},{9,1},{17,25},{25,17},{2,10},{10... | collective-permute-start | bytes 86024 | tf_op jit(solution)/shard_map/ppermute | solution.py:532
  47.5 0.1 constant_dynamic-update-slice_fusion.1
  47.6 2.3 %collective-permute-done.6.one = f32[56,128]{1,0:T(8,128)S(1)} collective-permute-done((f32[56,128]{1,0:T(8,128)S(1)}, f32[56,128]{1,0:T(8,128)S(1)}, u32[]{:S(2)}, u32[]{:S(2)}) %collective-permute-start.6) | collective-permute-done | bytes 28704 | tf_op jit(solution)/shard_map/ppermute | solution.py:532
  49.9 5.2 %all-to-all-start = ((f32[32,8,128]{2,1,0:T(8,128)}), f32[32,8,128]{2,1,0:T(8,128)S(1)}, u32[]{:S(2)}, u32[]{:S(2)}) async-start(f32[32,8,128]{2,1,0:T(8,128)} %bitcast.19), calls=%async_computation | async-start | bytes 262144 | tf_op jit(solution)/shard_map/all_to_all | solution.py:534
  55.1 0.1 constant_dynamic-update-slice_fusion
  55.2 1.8 %collective-permute-start.7 = (f32[56,128]{1,0:T(8,128)S(1)}, f32[56,128]{1,0:T(8,128)S(1)}, u32[]{:S(2)}, u32[]{:S(2)}) collective-permute-start(f32[56,128]{1,0:T(8,128)S(1)} %get-tuple-element.63), channel_id=1, source_target_pairs={{0,16},{8,24},{16,0},{24,8},{1,17},{9,25},{17,1},{25,9},{2,18},{10... | collective-permute-start | bytes 86024 | tf_op jit(solution)/shard_map/ppermute | solution.py:532
  56.9 1.5 %collective-permute-start.8 = (f32[56,128]{1,0:T(8,128)S(1)}, f32[56,128]{1,0:T(8,128)S(1)}, u32[]{:S(2)}, u32[]{:S(2)}) collective-permute-start(f32[56,128]{1,0:T(8,128)S(1)} %get-tuple-element.64), channel_id=1, source_target_pairs={{0,24},{8,16},{16,8},{24,0},{1,25},{9,17},{17,9},{25,1},{2,26},{10... | collective-permute-start | bytes 86024 | tf_op jit(solution)/shard_map/ppermute | solution.py:532
  58.4 0.2 compare_convert_fusion.owners
  58.6 0.1 stack.73.clusters
  58.7 0.5 collective-permute-done.7.two
  59.2 2.7 %collective-permute-done.8.three = f32[56,128]{1,0:T(8,128)S(1)} collective-permute-done((f32[56,128]{1,0:T(8,128)S(1)}, f32[56,128]{1,0:T(8,128)S(1)}, u32[]{:S(2)}, u32[]{:S(2)}) %collective-permute-start.8) | collective-permute-done | bytes 28704 | tf_op jit(solution)/shard_map/ppermute | solution.py:532
  61.9 1.4 %all-to-all-done.received = f32[32,8,128]{2,1,0:T(8,128)S(1)} async-done(((f32[32,8,128]{2,1,0:T(8,128)}), f32[32,8,128]{2,1,0:T(8,128)S(1)}, u32[]{:S(2)}, u32[]{:S(2)}) %all-to-all-start) | async-done | bytes 131104 | tf_op jit(solution)/shard_map/all_to_all | solution.py:534
  63.3 1.5 %shard_map.129 = (f32[4,32,51]{2,1,0:T(8,128)}, f32[1,32]{1,0:T(1,128)}) custom-call(s32[7]{0:T(128)S(1)} %stack.73.clusters, f32[56,128]{1,0:T(8,128)S(1)} %get-tuple-element.59.own, f32[56,128]{1,0:T(8,128)S(1)} %collective-permute-done.6.one, f32[56,128]{1,0:T(8,128)S(1)} %collective-permute-done.7.two, f32[56,128]{1,0:T(8,128)S(1)} %collective-permute-done.8.three, ...), custom_call_target="tpu_custom_call" | custom-call | flops 1000000000 | bytes 1024 | tf_op jit(solution)/shard_map/pallas_call | solution.py:378
  (40 shorter events, 0.2 us)
Async XLA Ops:
  0.6 11.4 %copy-start.6 = (f32[6,6]{1,0:T(8,128)S(1)}, f32[6,6]{1,0:T(8,128)}, u32[]{:S(2)}) copy-start(f32[6,6]{1,0:T(8,128)} %constant.148.clone) | copy-start | bytes 436
  0.6 11.6 %copy-start.8 = (bf16[32,32,1]{1,0,2:T(8,128)(2,1)S(1)}, bf16[32,32,1]{1,0,2:T(8,128)(2,1)}, u32[]{:S(2)}) copy-start(bf16[32,32,1]{1,0,2:T(8,128)(2,1)} %constant.203) | copy-start | bytes 6148
  0.7 11.5 %copy-start.9 = (s32[6,6]{1,0:T(8,128)S(1)}, s32[6,6]{1,0:T(8,128)}, u32[]{:S(2)}) copy-start(s32[6,6]{1,0:T(8,128)} %constant.149.clone) | copy-start | bytes 436
  0.7 12.3 %copy-start.10 = (s32[128]{0:T(128)S(1)}, s32[128]{0:T(128)}, u32[]{:S(2)}) copy-start(s32[128]{0:T(128)} %constant.150.clone) | copy-start | bytes 1540
  0.7 15.2 %copy-start.3 = (bf16[80,64]{1,0:T(8,128)(2,1)S(1)}, bf16[80,64]{1,0:T(8,128)(2,1)}, u32[]{:S(2)}) copy-start(bf16[80,64]{1,0:T(8,128)(2,1)} %constant.166.table.refs_5_) | copy-start | bytes 30724
  0.7 15.2 %copy-start.4 = (s32[148]{0:T(256)S(1)}, s32[148]{0:T(256)}, u32[]{:S(2)}) copy-start(s32[148]{0:T(256)} %constant.146.clone.ids) | copy-start | bytes 1780
  0.7 15.1 %copy-start.1 = (bf16[32,64,128]{2,1,0:T(8,128)(2,1)S(1)}, bf16[32,64,128]{2,1,0:T(8,128)(2,1)}, u32[]{:S(2)}) copy-start(bf16[32,64,128]{2,1,0:T(8,128)(2,1)} %spec_ref.1) | copy-start | bytes 1572868
  0.7 12.1 %copy-start.7 = (s32[6,12]{1,0:T(8,128)S(1)}, s32[6,12]{1,0:T(8,128)}, u32[]{:S(2)}) copy-start(s32[6,12]{1,0:T(8,128)} %exports_ref.1) | copy-start | bytes 868
  0.7 9.5 %copy-start.5 = (s32[32,50]{1,0:T(8,128)S(1)}, s32[32,50]{1,0:T(8,128)}, u32[]{:S(2)}) copy-start(s32[32,50]{1,0:T(8,128)} %param.13) | copy-start | bytes 19204
  3.1 10.6 %collective-permute-start = (bf16[800,128]{1,0:T(8,128)(2,1)}, bf16[800,128]{1,0:T(8,128)(2,1)S(1)}, u32[]{:S(2)}, u32[]{:S(2)}) collective-permute-start(bf16[800,128]{1,0:T(8,128)(2,1)} %get-tuple-element.35), channel_id=1, source_target_pairs={{0,1},{1,0},{2,3},{3,2},{4,5},{5,4},{6,7},{7,6},{8,9},{9,8},{10,11... | collective-permute-start | bytes 614408 | tf_op jit(solution)/shard_map/ppermute | solution.py:437
  3.6 21.5 %collective-permute-start.1 = (bf16[800,128]{1,0:T(8,128)(2,1)}, bf16[800,128]{1,0:T(8,128)(2,1)S(1)}, u32[]{:S(2)}, u32[]{:S(2)}) collective-permute-start(bf16[800,128]{1,0:T(8,128)(2,1)} %get-tuple-element.39), channel_id=1, source_target_pairs={{0,2},{1,3},{2,0},{3,1},{4,6},{5,7},{6,4},{7,5},{8,10},{9,11},{10,... | collective-permute-start | bytes 614408 | tf_op jit(solution)/shard_map/ppermute | solution.py:437
  6.1 25.0 %collective-permute-start.2 = (bf16[800,128]{1,0:T(8,128)(2,1)}, bf16[800,128]{1,0:T(8,128)(2,1)S(1)}, u32[]{:S(2)}, u32[]{:S(2)}) collective-permute-start(bf16[800,128]{1,0:T(8,128)(2,1)} %get-tuple-element.46), channel_id=1, source_target_pairs={{0,3},{1,2},{2,1},{3,0},{4,7},{5,6},{6,5},{7,4},{8,11},{9,10},{10,... | collective-permute-start | bytes 614408 | tf_op jit(solution)/shard_map/ppermute | solution.py:437
  6.3 24.9 %collective-permute-start.3 = (bf16[800,128]{1,0:T(8,128)(2,1)}, bf16[800,128]{1,0:T(8,128)(2,1)S(1)}, u32[]{:S(2)}, u32[]{:S(2)}) collective-permute-start(bf16[800,128]{1,0:T(8,128)(2,1)} %get-tuple-element.47), channel_id=1, source_target_pairs={{0,5},{1,4},{2,7},{3,6},{4,1},{5,0},{6,3},{7,2},{8,13},{9,12},{10,... | collective-permute-start | bytes 614408 | tf_op jit(solution)/shard_map/ppermute | solution.py:437
  8.9 27.4 %collective-permute-start.4 = (bf16[800,128]{1,0:T(8,128)(2,1)}, bf16[800,128]{1,0:T(8,128)(2,1)S(1)}, u32[]{:S(2)}, u32[]{:S(2)}) collective-permute-start(bf16[800,128]{1,0:T(8,128)(2,1)} %get-tuple-element.51), channel_id=1, source_target_pairs={{0,6},{1,7},{2,4},{3,5},{4,2},{5,3},{6,0},{7,1},{8,14},{9,15},{10,... | collective-permute-start | bytes 614408 | tf_op jit(solution)/shard_map/ppermute | solution.py:437
  13.8 22.5 %collective-permute-start.5 = (bf16[800,128]{1,0:T(8,128)(2,1)}, bf16[800,128]{1,0:T(8,128)(2,1)S(1)}, u32[]{:S(2)}, u32[]{:S(2)}) collective-permute-start(bf16[800,128]{1,0:T(8,128)(2,1)} %get-tuple-element.52), channel_id=1, source_target_pairs={{0,7},{1,6},{2,5},{3,4},{4,3},{5,2},{6,1},{7,0},{8,15},{9,14},{10,... | collective-permute-start | bytes 614408 | tf_op jit(solution)/shard_map/ppermute | solution.py:437
  36.2 5.6 %copy-start = (s32[32,50,64]{2,0,1:T(8,128)S(1)}, s32[32,50,64]{2,0,1:T(8,128)}, u32[]{:S(2)}) copy-start(s32[32,50,64]{2,0,1:T(8,128)} %param.14) | copy-start | bytes 1228804
  36.2 5.6 %copy-start.2 = (bf16[32,4,64]{2,1,0:T(4,128)(2,1)S(1)}, bf16[32,4,64]{2,1,0:T(4,128)(2,1)}, u32[]{:S(2)}) copy-start(bf16[32,4,64]{2,1,0:T(4,128)(2,1)} %partials.3) | copy-start | bytes 49156
  46.0 3.9 %collective-permute-start.6 = (f32[56,128]{1,0:T(8,128)S(1)}, f32[56,128]{1,0:T(8,128)S(1)}, u32[]{:S(2)}, u32[]{:S(2)}) collective-permute-start(f32[56,128]{1,0:T(8,128)S(1)} %get-tuple-element.61), channel_id=1, source_target_pairs={{0,8},{8,0},{16,24},{24,16},{1,9},{9,1},{17,25},{25,17},{2,10},{10... | collective-permute-start | bytes 86024 | tf_op jit(solution)/shard_map/ppermute | solution.py:532
  49.9 13.4 %all-to-all-start = ((f32[32,8,128]{2,1,0:T(8,128)}), f32[32,8,128]{2,1,0:T(8,128)S(1)}, u32[]{:S(2)}, u32[]{:S(2)}) async-start(f32[32,8,128]{2,1,0:T(8,128)} %bitcast.19), calls=%async_computation | async-start | bytes 262144 | tf_op jit(solution)/shard_map/all_to_all | solution.py:534
  55.2 4.1 %collective-permute-start.7 = (f32[56,128]{1,0:T(8,128)S(1)}, f32[56,128]{1,0:T(8,128)S(1)}, u32[]{:S(2)}, u32[]{:S(2)}) collective-permute-start(f32[56,128]{1,0:T(8,128)S(1)} %get-tuple-element.63), channel_id=1, source_target_pairs={{0,16},{8,24},{16,0},{24,8},{1,17},{9,25},{17,1},{25,9},{2,18},{10... | collective-permute-start | bytes 86024 | tf_op jit(solution)/shard_map/ppermute | solution.py:532
  56.9 4.9 %collective-permute-start.8 = (f32[56,128]{1,0:T(8,128)S(1)}, f32[56,128]{1,0:T(8,128)S(1)}, u32[]{:S(2)}, u32[]{:S(2)}) collective-permute-start(f32[56,128]{1,0:T(8,128)S(1)} %get-tuple-element.64), channel_id=1, source_target_pairs={{0,24},{8,16},{16,8},{24,0},{1,25},{9,17},{17,9},{25,1},{2,26},{10... | collective-permute-start | bytes 86024 | tf_op jit(solution)/shard_map/ppermute | solution.py:532

commit v8 on v7

--- a/solution.py
+++ b/solution.py
@@ -18,6 +18,7 @@
 WIDE = 4
 UNROLL = 8
 STAGE_SIZES = (2, 2, 2)
+LATE = 2
 
 
 def moment_table(freq_count):
@@ -434,7 +435,10 @@
     )
     got = [None] * groups
     for g in [0] + list(range(groups - 1, 0, -1)):
-        got[g] = lax.ppermute(outgoing[g], "clu", routes[g])
+        block = outgoing[g]
+        if g == LATE:
+            block, got[0] = lax.optimization_barrier((block, got[0]))
+        got[g] = lax.ppermute(block, "clu", routes[g])
     me = lax.axis_index("clu").astype(jnp.int32)
     sent = jnp.stack([jnp.asarray(send_group(g, me), jnp.int32) for g in range(groups)])
     came = jnp.stack([jnp.asarray(receive_group(g, me), jnp.int32) for g in range(groups)])
@@ -530,7 +534,6 @@
         micros=1.7,
     )
     shares = [shares[0]] + [lax.ppermute(shares[d], "sta", [(i, i ^ d) for i in range(4)]) for d in range(1, 4)]
-    terms, shares[1] = lax.optimization_barrier((terms, shares[1]))
     terms = lax.all_to_all(
         terms.reshape(4 * clusters, 8, 128), ("sta", "clu"), split_axis=0, concat_axis=0, tiled=True
     )

time: 64.9 us -> 61.2 us (0.943)
  waiting for transfers between devices: 6.89 us -> 5.1 us
  starting transfers between devices: 19.2 us -> 17.5 us
    all_to_all x1, waiting for transfers between devices: 1.39 us -> 0.01 us  [on_device(): lax.all_to_all(terms.reshape(4 * clusters, 8, 128), ('sta', 'clu'), split...]
    ppermute x3, waiting for transfers between devices: 5.49 us -> 4.24 us  [on_device(): lax.ppermute(shares[d], 'sta', [(i, i ^ d) for i in range(4)])]
    ppermute x3, starting transfers between devices: 4.8 us -> 3.55 us  [on_device(): lax.ppermute(shares[d], 'sta', [(i, i ^ d) for i in range(4)])]
    ppermute x6, waiting for transfers between devices: 0.02 us -> 0.86 us  [on_device(): got[g] = lax.ppermute(block, 'clu', routes[g])]
  transfers between devices with their start and end apart: 10 -> 10, of which waited for: 4 -> 4; matrix products, arithmetic and copies ran while one was open for 6% -> 6% of each run, Pallas kernels for 31% -> 37%
where the time goes in v8:
time: 61.2 us
  Pallas kernels  33.8 us (55%)
  starting transfers between devices  17.5 us (29%)
  waiting for transfers between devices  5.1 us (8%)
  other arithmetic  2.52 us (4%)
  between operations  1.14 us (2%)
  local copies, waits for them, and re-layouts  1.07 us (2%)
    pallas_call x8, Pallas kernels, call(): pl.pallas_call(kernel, out_shape=shapes, in_specs=specs if specs is not N...  33.8 us
    ppermute x6, starting transfers between devices, on_device(): got[g] = lax.ppermute(block, 'clu', routes[g])  8.95 us
    all_to_all x1, starting transfers between devices, on_device(): lax.all_to_all(terms.reshape(4 * clusters, 8, 128), ('sta', 'clu'), split...  4.98 us
    ppermute x3, waiting for transfers between devices, on_device(): lax.ppermute(shares[d], 'sta', [(i, i ^ d) for i in range(4)])  4.24 us
    ppermute x3, starting transfers between devices, on_device(): lax.ppermute(shares[d], 'sta', [(i, i ^ d) for i in range(4)])  3.55 us
  transfers between devices with their start and end apart: 10, of which 4 were waited for; matrix products, arithmetic and copies ran while one was open for 6% of the time, Pallas kernels for 37%

profile of v8, /device:TPU:0, one launch (start us, length us, event | category | flops | bytes accessed | tf_op | source)
XLA Modules:
  0.0 61.2 jit_solution(15886424906168986268)
XLA Ops:
  0.6 0.0 copy-start.6
  0.7 2.4 %shard_map.122 = (bf16[800,128]{1,0:T(8,128)(2,1)}, bf16[800,128]{1,0:T(8,128)(2,1)}, bf16[800,128]{1,0:T(8,128)(2,1)}, bf16[800,128]{1,0:T(8,128)(2,1)}, bf16[8...) custom-call(s32[6,12]{1,0:T(8,128)} %exports_ref.1, bf16[32,64,128]{2,1,0:T(8,128)(2,1)} %spec_ref.1, bf16[32,4,64]{2,1,0:T(4,128)(2,1)} %partials.3), custom_call_target="tpu_custom_call" | custom-call | flops 2000000000 | bytes 1024 | tf_op jit(solution)/shard_map/pallas_call | solution.py:379
  3.1 0.5 collective-permute-start
  3.6 2.6 %collective-permute-start.1 = (bf16[800,128]{1,0:T(8,128)(2,1)}, bf16[800,128]{1,0:T(8,128)(2,1)S(1)}, u32[]{:S(2)}, u32[]{:S(2)}) collective-permute-start(bf16[800,128]{1,0:T(8,128)(2,1)} %get-tuple-element.41), channel_id=1, source_target_pairs={{0,2},{1,3},{2,0},{3,1},{4,6},{5,7},{6,4},{7,5},{8,10},{9,11},{10,... | collective-permute-start | bytes 614408 | tf_op jit(solution)/shard_map/ppermute | solution.py:441
  6.1 2.4 %collective-permute-start.3 = (bf16[800,128]{1,0:T(8,128)(2,1)}, bf16[800,128]{1,0:T(8,128)(2,1)S(1)}, u32[]{:S(2)}, u32[]{:S(2)}) collective-permute-start(bf16[800,128]{1,0:T(8,128)(2,1)} %get-tuple-element.49), channel_id=1, source_target_pairs={{0,5},{1,4},{2,7},{3,6},{4,1},{5,0},{6,3},{7,2},{8,13},{9,12},{10,... | collective-permute-start | bytes 614408 | tf_op jit(solution)/shard_map/ppermute | solution.py:441
  8.6 0.1 collective-permute-start.4
  8.6 3.4 %collective-permute-start.5 = (bf16[800,128]{1,0:T(8,128)(2,1)}, bf16[800,128]{1,0:T(8,128)(2,1)S(1)}, u32[]{:S(2)}, u32[]{:S(2)}) collective-permute-start(bf16[800,128]{1,0:T(8,128)(2,1)} %get-tuple-element.54), channel_id=1, source_target_pairs={{0,7},{1,6},{2,5},{3,4},{4,3},{5,2},{6,1},{7,0},{8,15},{9,14},{10,... | collective-permute-start | bytes 614408 | tf_op jit(solution)/shard_map/ppermute | solution.py:441
  12.0 0.1 stack.80
  12.1 0.1 select_reduce_fusion.1
  12.3 0.7 %fusion.2 = pred[32,36]{0,1:T(8,128)(4,1)S(1)} fusion(s32[32,50]{1,0:T(8,128)S(1)} %get-tuple-element.68), kind=kLoop, calls=%fused_computation.8 | loop fusion | flops 114048 | bytes 7552 | tf_op jit(solution)/shard_map/reduce_or | solution.py:469
  13.0 0.1 convert_reduce_fusion
  13.1 0.1 eq.112
  13.2 0.3 fusion.hot
  13.5 0.1 fusion.1.hot_turned
  13.7 0.1 ceil.11
  13.8 0.1 multiply_reduce_fusion
  14.0 0.1 add_select_fusion
  14.1 0.1 broadcast_in_dim.78
  14.2 0.1 eq.122
  14.2 0.1 reduce_sum.58
  14.4 0.1 stack.87
  14.5 0.1 iota_compare_fusion.4
  14.6 0.1 select_reduce_fusion.2
  14.7 0.1 constant_dynamic-update-slice_fusion.5
  14.8 0.1 constant_dynamic-update-slice_fusion.4
  14.9 0.1 constant_dynamic-update-slice_fusion.3
  14.9 0.1 constant_dynamic-update-slice_fusion.2
  15.0 0.1 constant_dynamic-update-slice_fusion.1
  15.1 0.1 constant_dynamic-update-slice_fusion
  15.2 0.5 select_reduce_fusion.ids
  15.7 0.1 collective-permute-start.2
  15.8 9.2 %shard_map.123 = (f32[1024,128]{1,0:T(8,128)S(1)}, f32[32,128,128]{2,1,0:T(8,128)S(1)}, f32[32,64,128]{2,1,0:T(8,128)S(1)}, f32[32,128]{1,0:T(8,128)S(1)}) custom-call(s32[148]{0:T(256)S(1)} %copy-done.4, bf16[16,128,128]{2,1,0:T(8,128)(2,1)S(1)} %bitcast.45, bf16[80,64]{1,0:T(8,128)(2,1)S(1)} %copy-done.3), custom_call_target="tpu_custom_call" | custom-call | flops 8000000000 | bytes 1024 | tf_op jit(solution)/shard_map/pallas_call | solution.py:379
  25.0 6.0 %shard_map.124 = (f32[1024,128]{1,0:T(8,128)S(1)}, bf16[64,128]{1,0:T(8,128)(2,1)S(1)}) custom-call(s32[6,112]{1,0:T(8,128)S(1)} %select_reduce_fusion.ids, s32[6]{0:T(128)S(1)} %convert_element_type.35.counts, bf16[800,128]{1,0:T(8,128)(2,1)S(1)} %collective-permute-done.refs_0_, bf16[800,128]{1,0:T(8,128)(2,1)S(1)} %collective-permute-done.1.refs_1_, ...), custom_call_target="tpu_custom_call" | custom-call | flops 5600000000 | bytes 1024 | tf_op jit(solution)/shard_map/pallas_call | solution.py:379
  31.1 0.8 %collective-permute-done.2.refs_0_ = bf16[800,128]{1,0:T(8,128)(2,1)S(1)} collective-permute-done((bf16[800,128]{1,0:T(8,128)(2,1)}, bf16[800,128]{1,0:T(8,128)(2,1)S(1)}, u32[]{:S(2)}, u32[]{:S(2)}) %collective-permute-start.2) | collective-permute-done | bytes 204832 | tf_op jit(solution)/shard_map/ppermute | solution.py:441
  31.9 5.5 %shard_map.125 = (f32[1024,128]{1,0:T(8,128)S(1)}, bf16[64,128]{1,0:T(8,128)(2,1)S(1)}) custom-call(s32[6,112]{1,0:T(8,128)S(1)} %select_reduce_fusion.ids, s32[6]{0:T(128)S(1)} %convert_element_type.35.counts, bf16[800,128]{1,0:T(8,128)(2,1)S(1)} %collective-permute-done.2.refs_0_, bf16[800,128]{1,0:T(8,128)(2,1)S(1)} %collective-permute-done.3.refs_1_, ...), custom_call_target="tpu_custom_call" | custom-call | flops 5600000000 | bytes 1024 | tf_op jit(solution)/shard_map/pallas_call | solution.py:379
  37.5 5.1 %shard_map.126 = (f32[1024,128]{1,0:T(8,128)S(1)}, bf16[64,128]{1,0:T(8,128)(2,1)S(1)}) custom-call(s32[6,112]{1,0:T(8,128)S(1)} %select_reduce_fusion.ids, s32[6]{0:T(128)S(1)} %convert_element_type.35.counts, bf16[800,128]{1,0:T(8,128)(2,1)S(1)} %collective-permute-done.4.refs_0_, bf16[800,128]{1,0:T(8,128)(2,1)S(1)} %collective-permute-done.5.refs_1_, ...), custom_call_target="tpu_custom_call" | custom-call | flops 5600000000 | bytes 1024 | tf_op jit(solution)/shard_map/pallas_call | solution.py:379
  42.6 2.4 %shard_map.127 = (bf16[2048,128]{1,0:T(8,128)(2,1)S(1)}, f32[4,8,8,128]{3,2,1,0:T(8,128)}, bf16[128,256]{1,0:T(8,128)(2,1)S(1)}) custom-call(bf16[2048,128]{1,0:T(8,128)(2,1)S(1)} %fusion.hot, bf16[128,2048]{1,0:T(8,128)(2,1)S(1)} %fusion.1.hot_turned, s32[1600,64]{1,0:T(8,128)S(1)} %bitcast.44, bf16[32,4,64]{2,1,0:T(4,128)(2,1)S(1)} %copy-done.2, ...), custom_call_target="tpu_custom_call" | custom-call | flops 2400000000 | bytes 1024 | tf_op jit(solution)/shard_map/pallas_call | solution.py:379
  45.0 5.0 %all-to-all-start = ((f32[32,8,128]{2,1,0:T(8,128)}), f32[32,8,128]{2,1,0:T(8,128)S(1)}, u32[]{:S(2)}, u32[]{:S(2)}) async-start(f32[32,8,128]{2,1,0:T(8,128)} %bitcast.19), calls=%async_computation | async-start | bytes 262144 | tf_op jit(solution)/shard_map/all_to_all | solution.py:537
  49.9 1.7 %shard_map.128 = (f32[56,128]{1,0:T(8,128)S(1)}, f32[56,128]{1,0:T(8,128)S(1)}, f32[56,128]{1,0:T(8,128)S(1)}, f32[56,128]{1,0:T(8,128)S(1)}) custom-call(s32[1]{0:T(128)} %bitcast.7.place, bf16[2048,128]{1,0:T(8,128)(2,1)S(1)} %fusion.hot, bf16[2048,128]{1,0:T(8,128)(2,1)S(1)} %get-tuple-element.59.slots, bf16[128,256]{1,0:T(8,128)(2,1)S(1)} %get-tuple-element.60.geo, ...), custom_call_target="tpu_custom_call" | custom-call | flops 1700000000 | bytes 1024 | tf_op jit(solution)/shard_map/pallas_call | solution.py:379
  51.7 1.8 %collective-permute-start.6 = (f32[56,128]{1,0:T(8,128)S(1)}, f32[56,128]{1,0:T(8,128)S(1)}, u32[]{:S(2)}, u32[]{:S(2)}) collective-permute-start(f32[56,128]{1,0:T(8,128)S(1)} %get-tuple-element.62), channel_id=1, source_target_pairs={{0,8},{8,0},{16,24},{24,16},{1,9},{9,1},{17,25},{25,17},{2,10},{10... | collective-permute-start | bytes 86024 | tf_op jit(solution)/shard_map/ppermute | solution.py:536
  53.5 1.5 %collective-permute-start.7 = (f32[56,128]{1,0:T(8,128)S(1)}, f32[56,128]{1,0:T(8,128)S(1)}, u32[]{:S(2)}, u32[]{:S(2)}) collective-permute-start(f32[56,128]{1,0:T(8,128)S(1)} %get-tuple-element.63), channel_id=1, source_target_pairs={{0,16},{8,24},{16,0},{24,8},{1,17},{9,25},{17,1},{25,9},{2,18},{10... | collective-permute-start | bytes 86024 | tf_op jit(solution)/shard_map/ppermute | solution.py:536
  55.0 0.3 collective-permute-start.8
  55.2 0.2 compare_convert_fusion.owners
  55.4 0.1 stack.73.clusters
  55.5 0.2 collective-permute-done.6.one
  55.7 1.8 %collective-permute-done.7.two = f32[56,128]{1,0:T(8,128)S(1)} collective-permute-done((f32[56,128]{1,0:T(8,128)S(1)}, f32[56,128]{1,0:T(8,128)S(1)}, u32[]{:S(2)}, u32[]{:S(2)}) %collective-permute-start.7) | collective-permute-done | bytes 28704 | tf_op jit(solution)/shard_map/ppermute | solution.py:536
  57.5 2.2 %collective-permute-done.8.three = f32[56,128]{1,0:T(8,128)S(1)} collective-permute-done((f32[56,128]{1,0:T(8,128)S(1)}, f32[56,128]{1,0:T(8,128)S(1)}, u32[]{:S(2)}, u32[]{:S(2)}) %collective-permute-start.8) | collective-permute-done | bytes 28704 | tf_op jit(solution)/shard_map/ppermute | solution.py:536
  59.7 1.5 %shard_map.129 = (f32[4,32,51]{2,1,0:T(8,128)}, f32[1,32]{1,0:T(1,128)}) custom-call(s32[7]{0:T(128)S(1)} %stack.73.clusters, f32[56,128]{1,0:T(8,128)S(1)} %get-tuple-element.61.own, f32[56,128]{1,0:T(8,128)S(1)} %collective-permute-done.6.one, f32[56,128]{1,0:T(8,128)S(1)} %collective-permute-done.7.two, f32[56,128]{1,0:T(8,128)S(1)} %collective-permute-done.8.three, ...), custom_call_target="tpu_custom_call" | custom-call | flops 1000000000 | bytes 1024 | tf_op jit(solution)/shard_map/pallas_call | solution.py:379
  (40 shorter events, 0.2 us)
Async XLA Ops:
  0.6 13.2 %copy-start.6 = (f32[6,6]{1,0:T(8,128)S(1)}, f32[6,6]{1,0:T(8,128)}, u32[]{:S(2)}) copy-start(f32[6,6]{1,0:T(8,128)} %constant.148.clone) | copy-start | bytes 436
  0.6 13.3 %copy-start.8 = (bf16[32,32,1]{1,0,2:T(8,128)(2,1)S(1)}, bf16[32,32,1]{1,0,2:T(8,128)(2,1)}, u32[]{:S(2)}) copy-start(bf16[32,32,1]{1,0,2:T(8,128)(2,1)} %constant.203) | copy-start | bytes 6148
  0.7 13.3 %copy-start.9 = (s32[6,6]{1,0:T(8,128)S(1)}, s32[6,6]{1,0:T(8,128)}, u32[]{:S(2)}) copy-start(s32[6,6]{1,0:T(8,128)} %constant.149.clone) | copy-start | bytes 436
  0.7 14.0 %copy-start.10 = (s32[128]{0:T(128)S(1)}, s32[128]{0:T(128)}, u32[]{:S(2)}) copy-start(s32[128]{0:T(128)} %constant.150.clone) | copy-start | bytes 1540
  0.7 15.1 %copy-start.3 = (bf16[80,64]{1,0:T(8,128)(2,1)S(1)}, bf16[80,64]{1,0:T(8,128)(2,1)}, u32[]{:S(2)}) copy-start(bf16[80,64]{1,0:T(8,128)(2,1)} %constant.166.table.refs_5_) | copy-start | bytes 30724
  0.7 15.1 %copy-start.4 = (s32[148]{0:T(256)S(1)}, s32[148]{0:T(256)}, u32[]{:S(2)}) copy-start(s32[148]{0:T(256)} %constant.146.clone.ids) | copy-start | bytes 1780
  0.7 15.1 %copy-start.1 = (bf16[32,64,128]{2,1,0:T(8,128)(2,1)S(1)}, bf16[32,64,128]{2,1,0:T(8,128)(2,1)}, u32[]{:S(2)}) copy-start(bf16[32,64,128]{2,1,0:T(8,128)(2,1)} %spec_ref.1) | copy-start | bytes 1572868
  0.7 13.9 %copy-start.7 = (s32[6,12]{1,0:T(8,128)S(1)}, s32[6,12]{1,0:T(8,128)}, u32[]{:S(2)}) copy-start(s32[6,12]{1,0:T(8,128)} %exports_ref.1) | copy-start | bytes 868
  0.7 11.3 %copy-start.5 = (s32[32,50]{1,0:T(8,128)S(1)}, s32[32,50]{1,0:T(8,128)}, u32[]{:S(2)}) copy-start(s32[32,50]{1,0:T(8,128)} %param.13) | copy-start | bytes 19204
  3.1 12.5 %collective-permute-start = (bf16[800,128]{1,0:T(8,128)(2,1)}, bf16[800,128]{1,0:T(8,128)(2,1)S(1)}, u32[]{:S(2)}, u32[]{:S(2)}) collective-permute-start(bf16[800,128]{1,0:T(8,128)(2,1)} %get-tuple-element.36), channel_id=1, source_target_pairs={{0,1},{1,0},{2,3},{3,2},{4,5},{5,4},{6,7},{7,6},{8,9},{9,8},{10,11... | collective-permute-start | bytes 614408 | tf_op jit(solution)/shard_map/ppermute | solution.py:441
  3.6 21.5 %collective-permute-start.1 = (bf16[800,128]{1,0:T(8,128)(2,1)}, bf16[800,128]{1,0:T(8,128)(2,1)S(1)}, u32[]{:S(2)}, u32[]{:S(2)}) collective-permute-start(bf16[800,128]{1,0:T(8,128)(2,1)} %get-tuple-element.41), channel_id=1, source_target_pairs={{0,2},{1,3},{2,0},{3,1},{4,6},{5,7},{6,4},{7,5},{8,10},{9,11},{10,... | collective-permute-start | bytes 614408 | tf_op jit(solution)/shard_map/ppermute | solution.py:441
  6.1 24.9 %collective-permute-start.3 = (bf16[800,128]{1,0:T(8,128)(2,1)}, bf16[800,128]{1,0:T(8,128)(2,1)S(1)}, u32[]{:S(2)}, u32[]{:S(2)}) collective-permute-start(bf16[800,128]{1,0:T(8,128)(2,1)} %get-tuple-element.49), channel_id=1, source_target_pairs={{0,5},{1,4},{2,7},{3,6},{4,1},{5,0},{6,3},{7,2},{8,13},{9,12},{10,... | collective-permute-start | bytes 614408 | tf_op jit(solution)/shard_map/ppermute | solution.py:441
  8.6 28.9 %collective-permute-start.4 = (bf16[800,128]{1,0:T(8,128)(2,1)}, bf16[800,128]{1,0:T(8,128)(2,1)S(1)}, u32[]{:S(2)}, u32[]{:S(2)}) collective-permute-start(bf16[800,128]{1,0:T(8,128)(2,1)} %get-tuple-element.53), channel_id=1, source_target_pairs={{0,6},{1,7},{2,4},{3,5},{4,2},{5,3},{6,0},{7,1},{8,14},{9,15},{10,... | collective-permute-start | bytes 614408 | tf_op jit(solution)/shard_map/ppermute | solution.py:441
  8.6 28.9 %collective-permute-start.5 = (bf16[800,128]{1,0:T(8,128)(2,1)}, bf16[800,128]{1,0:T(8,128)(2,1)S(1)}, u32[]{:S(2)}, u32[]{:S(2)}) collective-permute-start(bf16[800,128]{1,0:T(8,128)(2,1)} %get-tuple-element.54), channel_id=1, source_target_pairs={{0,7},{1,6},{2,5},{3,4},{4,3},{5,2},{6,1},{7,0},{8,15},{9,14},{10,... | collective-permute-start | bytes 614408 | tf_op jit(solution)/shard_map/ppermute | solution.py:441
  15.7 16.2 %collective-permute-start.2 = (bf16[800,128]{1,0:T(8,128)(2,1)}, bf16[800,128]{1,0:T(8,128)(2,1)S(1)}, u32[]{:S(2)}, u32[]{:S(2)}) collective-permute-start(bf16[800,128]{1,0:T(8,128)(2,1)} %get-tuple-element.48), channel_id=1, source_target_pairs={{0,3},{1,2},{2,1},{3,0},{4,7},{5,6},{6,5},{7,4},{8,11},{9,10},{10,... | collective-permute-start | bytes 614408 | tf_op jit(solution)/shard_map/ppermute | solution.py:441
  37.4 5.1 %copy-start = (s32[32,50,64]{2,0,1:T(8,128)S(1)}, s32[32,50,64]{2,0,1:T(8,128)}, u32[]{:S(2)}) copy-start(s32[32,50,64]{2,0,1:T(8,128)} %param.14) | copy-start | bytes 1228804
  37.5 5.1 %copy-start.2 = (bf16[32,4,64]{2,1,0:T(4,128)(2,1)S(1)}, bf16[32,4,64]{2,1,0:T(4,128)(2,1)}, u32[]{:S(2)}) copy-start(bf16[32,4,64]{2,1,0:T(4,128)(2,1)} %partials.3) | copy-start | bytes 49156
  45.0 14.8 %all-to-all-start = ((f32[32,8,128]{2,1,0:T(8,128)}), f32[32,8,128]{2,1,0:T(8,128)S(1)}, u32[]{:S(2)}, u32[]{:S(2)}) async-start(f32[32,8,128]{2,1,0:T(8,128)} %bitcast.19), calls=%async_computation | async-start | bytes 262144 | tf_op jit(solution)/shard_map/all_to_all | solution.py:537
  51.7 4.0 %collective-permute-start.6 = (f32[56,128]{1,0:T(8,128)S(1)}, f32[56,128]{1,0:T(8,128)S(1)}, u32[]{:S(2)}, u32[]{:S(2)}) collective-permute-start(f32[56,128]{1,0:T(8,128)S(1)} %get-tuple-element.62), channel_id=1, source_target_pairs={{0,8},{8,0},{16,24},{24,16},{1,9},{9,1},{17,25},{25,17},{2,10},{10... | collective-permute-start | bytes 86024 | tf_op jit(solution)/shard_map/ppermute | solution.py:536
  53.5 4.0 %collective-permute-start.7 = (f32[56,128]{1,0:T(8,128)S(1)}, f32[56,128]{1,0:T(8,128)S(1)}, u32[]{:S(2)}, u32[]{:S(2)}) collective-permute-start(f32[56,128]{1,0:T(8,128)S(1)} %get-tuple-element.63), channel_id=1, source_target_pairs={{0,16},{8,24},{16,0},{24,8},{1,17},{9,25},{17,1},{25,9},{2,18},{10... | collective-permute-start | bytes 86024 | tf_op jit(solution)/shard_map/ppermute | solution.py:536
  55.0 4.8 %collective-permute-start.8 = (f32[56,128]{1,0:T(8,128)S(1)}, f32[56,128]{1,0:T(8,128)S(1)}, u32[]{:S(2)}, u32[]{:S(2)}) collective-permute-start(f32[56,128]{1,0:T(8,128)S(1)} %get-tuple-element.64), channel_id=1, source_target_pairs={{0,24},{8,16},{16,8},{24,0},{1,25},{9,17},{17,9},{25,1},{2,26},{10... | collective-permute-start | bytes 86024 | tf_op jit(solution)/shard_map/ppermute | solution.py:536

commit v9 on v8

--- a/solution.py
+++ b/solution.py
@@ -348,7 +348,7 @@
         out[...] = turned[rows, :].T[: out.shape[0]]
 
 
-def total_kernel(groups, events, slots, clusters, own, one, two, three, received, owners, normal, right):
+def spread_kernel(groups, clusters, received, owners, out):
     parts = []
     for g in range(groups + 1):
         part = received[clusters[g]]
@@ -356,11 +356,14 @@
             part = part + received[t * (received.shape[0] // 4) + clusters[g]]
         parts.append(part)
     high, low = two_parts(jnp.concatenate(parts, axis=1))
-    spread = jnp.dot(high, owners[...], preferred_element_type=F32) + jnp.dot(low, owners[...], preferred_element_type=F32)
+    out[...] = jnp.dot(high, owners[...], preferred_element_type=F32) + jnp.dot(low, owners[...], preferred_element_type=F32)
+
+
+def total_kernel(events, slots, own, one, two, three, spread, normal, right):
     block = lax.broadcasted_iota(jnp.int32, (1, 128), 1) // events
     diagonal = jnp.zeros((1, 128), F32)
     for j in range(4):
-        diagonal = jnp.where(block == j, spread[j : j + 1], diagonal)
+        diagonal = jnp.where(block == j, spread[j : j + 1, :], diagonal)
     right[...] = spread[4:5, :events]
     total = pltpu.roll((own[...] + one[...]) + (two[...] + three[...]), 1, 0)
     top = lax.broadcasted_iota(jnp.int32, total.shape, 0) == 0
@@ -458,7 +461,7 @@
         (jnp.asarray(duos, jnp.int32), natural.reshape(events // 2, 2 * stations, two_freq), table),
         scratch=weight_scratch(events // 2, freq),
         specs=[smem] + vmem(2),
-        micros=8.0,
+        micros=0.5,
     )
 
     far = jnp.maximum(pair_list - events, 0)
@@ -487,9 +490,6 @@
 
     column = jnp.where(pair_list < events, pair_list, events + GROUP_ROWS * arrival + entry)
     column = jnp.pad(column, ((0, 0), (0, SLOT_ROWS - slots)), constant_values=-1).reshape(-1)
-    cand_ids = jnp.arange(cands, dtype=jnp.int32)
-    hot = (column[:, None] == cand_ids[None, :]).astype(BF16)
-    hot_turned = (cand_ids[:, None] == column[None, :]).astype(BF16)
     mask = station_mask.transpose(1, 0, 2).reshape(slots * events, stations)
     owner_rows = [jnp.asarray(np.where(np.arange(cands) < events, np.arange(cands), -1), jnp.int32)]
     hot_sent = sent[:, None] == jnp.arange(groups, dtype=jnp.int32)[None, :]
@@ -503,19 +503,22 @@
     tables, tails, begin = [], [], 0
     for size in STAGE_SIZES:
         if tables:
-            lists, tables[-1] = lax.optimization_barrier((lists, tables[-1]))
+            lists, column, tables[-1] = lax.optimization_barrier((lists, column, tables[-1]))
         table_part, tail_part = call(
             functools.partial(import_kernel, begin, size, freq, events, cap, scale),
             [((events * size * GROUP_ROWS, 128), F32), ((size * 2 * GROUP_ROWS, 128), BF16)],
             (lists, counts, *got[begin : begin + size], dup, square, energy, table),
             scratch=weight_scratch(size * half, freq),
             specs=[smem] * 2 + vmem(size + 4),
-            micros=1.0 + 2.3 * size,
+            micros=0.5,
         )
         tables.append(table_part)
         tails.append(tail_part)
         begin += size
 
+    cand_ids = jnp.arange(cands, dtype=jnp.int32)
+    hot = (column[:, None] == cand_ids[None, :]).astype(BF16)
+    hot_turned = (cand_ids[:, None] == column[None, :]).astype(BF16)
     weights, terms, geo = call(
         functools.partial(sums_kernel, groups, events, slots),
         [((events * SLOT_ROWS, 128), BF16), ((4, clusters, 8, 128), F32), ((cands, 256), BF16)],
@@ -538,11 +541,16 @@
         terms.reshape(4 * clusters, 8, 128), ("sta", "clu"), split_axis=0, concat_axis=0, tiled=True
     )
     sources = jnp.stack([me] + [jnp.asarray(receiver(g, me), jnp.int32) for g in range(groups)])
+    (spread,) = call(
+        functools.partial(spread_kernel, groups),
+        [((8, 128), F32)],
+        (sources, terms, owners),
+        specs=[smem] + vmem(2),
+    )
     normal, right = call(
-        functools.partial(total_kernel, groups, events, slots),
+        functools.partial(total_kernel, events, slots),
         [((4, events, slots + 1), F32), ((1, events), F32)],
-        (sources, *shares, terms, owners),
-        specs=[smem] + vmem(6),
+        (*shares, spread),
     )
     return (normal.transpose(0, 2, 1), right)
 

time: 61.2 us -> 61.6 us (level)
  Pallas kernels: 33.8 us -> 35 us
  waiting for transfers between devices: 5.1 us -> 4.46 us
    ppermute x3, waiting for transfers between devices: 4.24 us -> 1.17 us  [on_device(): lax.ppermute(shares[d], 'sta', [(i, i ^ d) for i in range(4)])]
    all_to_all x1, waiting for transfers between devices: 0.01 us -> 2.62 us  [on_device(): lax.all_to_all(terms.reshape(4 * clusters, 8, 128), ('sta', 'clu'), split...]
    pallas_call x8 -> x9, Pallas kernels: 33.8 us -> 35 us  [call(): pl.pallas_call(kernel, out_shape=shapes, in_specs=specs if specs is not N...]
  transfers between devices with their start and end apart: 10 -> 10, of which waited for: 4 -> 3; matrix products, arithmetic and copies ran while one was open for 6% -> 6% of each run, Pallas kernels for 37% -> 39%
where the time goes in v9:
time: 61.6 us; the launch traced here: 61.1 us
  Pallas kernels  35 us (57%)
  starting transfers between devices  16.9 us (27%)
  waiting for transfers between devices  4.46 us (7%)
  other arithmetic  2.53 us (4%)
  between operations  1.09 us (2%)
  local copies, waits for them, and re-layouts  1.06 us (2%)
    pallas_call x9, Pallas kernels, call(): pl.pallas_call(kernel, out_shape=shapes, in_specs=specs if specs is not N...  35 us
    ppermute x6, starting transfers between devices, on_device(): got[g] = lax.ppermute(block, 'clu', routes[g])  8.9 us
    all_to_all x1, starting transfers between devices, on_device(): lax.all_to_all(terms.reshape(4 * clusters, 8, 128), ('sta', 'clu'), split...  4.41 us
    ppermute x3, starting transfers between devices, on_device(): lax.ppermute(shares[d], 'sta', [(i, i ^ d) for i in range(4)])  3.55 us
    all_to_all x1, waiting for transfers between devices, on_device(): lax.all_to_all(terms.reshape(4 * clusters, 8, 128), ('sta', 'clu'), split...  2.62 us
  transfers between devices with their start and end apart: 10, of which 3 were waited for; matrix products, arithmetic and copies ran while one was open for 6% of the time, Pallas kernels for 39%

profile of v9, /device:TPU:0, one launch (start us, length us, event | category | flops | bytes accessed | tf_op | source)
XLA Modules:
  0.0 61.1 jit_solution(16785197265730157848)
XLA Ops:
  0.6 0.0 copy-start.6
  0.7 2.4 %shard_map.122 = (bf16[800,128]{1,0:T(8,128)(2,1)}, bf16[800,128]{1,0:T(8,128)(2,1)}, bf16[800,128]{1,0:T(8,128)(2,1)}, bf16[800,128]{1,0:T(8,128)(2,1)}, bf16[8...) custom-call(s32[6,12]{1,0:T(8,128)} %exports_ref.1, bf16[32,64,128]{2,1,0:T(8,128)(2,1)} %spec_ref.1, bf16[32,4,64]{2,1,0:T(4,128)(2,1)} %partials.3), custom_call_target="tpu_custom_call" | custom-call | flops 2000000000 | bytes 1024 | tf_op jit(solution)/shard_map/pallas_call | solution.py:382
  3.1 0.5 collective-permute-start
  3.6 2.6 %collective-permute-start.1 = (bf16[800,128]{1,0:T(8,128)(2,1)}, bf16[800,128]{1,0:T(8,128)(2,1)S(1)}, u32[]{:S(2)}, u32[]{:S(2)}) collective-permute-start(bf16[800,128]{1,0:T(8,128)(2,1)} %get-tuple-element.41), channel_id=1, source_target_pairs={{0,2},{1,3},{2,0},{3,1},{4,6},{5,7},{6,4},{7,5},{8,10},{9,11},{10,... | collective-permute-start | bytes 614408 | tf_op jit(solution)/shard_map/ppermute | solution.py:444
  6.1 2.4 %collective-permute-start.3 = (bf16[800,128]{1,0:T(8,128)(2,1)}, bf16[800,128]{1,0:T(8,128)(2,1)S(1)}, u32[]{:S(2)}, u32[]{:S(2)}) collective-permute-start(bf16[800,128]{1,0:T(8,128)(2,1)} %get-tuple-element.50), channel_id=1, source_target_pairs={{0,5},{1,4},{2,7},{3,6},{4,1},{5,0},{6,3},{7,2},{8,13},{9,12},{10,... | collective-permute-start | bytes 614408 | tf_op jit(solution)/shard_map/ppermute | solution.py:444
  8.6 0.1 collective-permute-start.4
  8.6 3.4 %collective-permute-start.5 = (bf16[800,128]{1,0:T(8,128)(2,1)}, bf16[800,128]{1,0:T(8,128)(2,1)S(1)}, u32[]{:S(2)}, u32[]{:S(2)}) collective-permute-start(bf16[800,128]{1,0:T(8,128)(2,1)} %get-tuple-element.58), channel_id=1, source_target_pairs={{0,7},{1,6},{2,5},{3,4},{4,3},{5,2},{6,1},{7,0},{8,15},{9,14},{10,... | collective-permute-start | bytes 614408 | tf_op jit(solution)/shard_map/ppermute | solution.py:444
  12.0 0.1 stack.72
  12.1 0.1 select_reduce_fusion.1
  12.3 0.7 %fusion.2 = pred[32,36]{0,1:T(8,128)(4,1)S(1)} fusion(s32[32,50]{1,0:T(8,128)S(1)} %get-tuple-element.73), kind=kLoop, calls=%fused_computation.8 | loop fusion | flops 114048 | bytes 7552 | tf_op jit(solution)/shard_map/reduce_or | solution.py:472
  13.0 0.1 convert_reduce_fusion
  13.2 0.1 ceil.11
  13.3 0.1 multiply_reduce_fusion
  13.4 0.1 add_select_fusion
  13.6 0.1 broadcast_in_dim.83
  13.6 0.1 eq.113
  13.7 0.1 stack.87
  13.8 0.1 iota_compare_fusion.4
  13.9 0.1 select_reduce_fusion.2
  14.0 0.5 select_reduce_fusion.ids
  14.5 0.1 constant_dynamic-update-slice_fusion.5
  14.6 0.1 constant_dynamic-update-slice_fusion.4
  14.6 0.1 constant_dynamic-update-slice_fusion.3
  14.7 0.1 constant_dynamic-update-slice_fusion.2
  14.8 0.1 constant_dynamic-update-slice_fusion.1
  14.9 0.1 reduce_sum.58
  15.0 0.1 reshape.86
  15.1 0.0 collective-permute-start.2
  15.1 0.1 constant_dynamic-update-slice_fusion
  15.2 9.7 %shard_map.123 = (f32[1024,128]{1,0:T(8,128)S(1)}, f32[32,128,128]{2,1,0:T(8,128)S(1)}, f32[32,64,128]{2,1,0:T(8,128)S(1)}, f32[32,128]{1,0:T(8,128)S(1)}) custom-call(s32[148]{0:T(256)S(1)} %copy-done.4, bf16[16,128,128]{2,1,0:T(8,128)(2,1)S(1)} %bitcast.45, bf16[80,64]{1,0:T(8,128)(2,1)S(1)} %copy-done), custom_call_target="tpu_custom_call" | custom-call | flops 500000000 | bytes 1024 | tf_op jit(solution)/shard_map/pallas_call | solution.py:382
  25.0 5.8 %shard_map.124 = (f32[1024,128]{1,0:T(8,128)S(1)}, bf16[64,128]{1,0:T(8,128)(2,1)S(1)}) custom-call(s32[6,112]{1,0:T(8,128)S(1)} %select_reduce_fusion.ids, s32[6]{0:T(128)S(1)} %convert_element_type.32.counts, bf16[800,128]{1,0:T(8,128)(2,1)S(1)} %collective-permute-done.refs_0_, bf16[800,128]{1,0:T(8,128)(2,1)S(1)} %collective-permute-done.1.refs_1_, ...), custom_call_target="tpu_custom_call" | custom-call | flops 500000000 | bytes 1024 | tf_op jit(solution)/shard_map/pallas_call | solution.py:382
  30.8 0.7 %collective-permute-done.2.refs_0_ = bf16[800,128]{1,0:T(8,128)(2,1)S(1)} collective-permute-done((bf16[800,128]{1,0:T(8,128)(2,1)}, bf16[800,128]{1,0:T(8,128)(2,1)S(1)}, u32[]{:S(2)}, u32[]{:S(2)}) %collective-permute-start.2) | collective-permute-done | bytes 204832 | tf_op jit(solution)/shard_map/ppermute | solution.py:444
  31.4 5.8 %shard_map.125 = (f32[1024,128]{1,0:T(8,128)S(1)}, bf16[64,128]{1,0:T(8,128)(2,1)S(1)}) custom-call(s32[6,112]{1,0:T(8,128)S(1)} %select_reduce_fusion.ids, s32[6]{0:T(128)S(1)} %convert_element_type.32.counts, bf16[800,128]{1,0:T(8,128)(2,1)S(1)} %collective-permute-done.2.refs_0_, bf16[800,128]{1,0:T(8,128)(2,1)S(1)} %collective-permute-done.3.refs_1_, ...), custom_call_target="tpu_custom_call" | custom-call | flops 500000000 | bytes 1024 | tf_op jit(solution)/shard_map/pallas_call | solution.py:382
  37.2 0.3 fusion.hot
  37.6 0.1 fusion.1.hot_turned
  37.7 5.8 %shard_map.126 = (f32[1024,128]{1,0:T(8,128)S(1)}, bf16[64,128]{1,0:T(8,128)(2,1)S(1)}) custom-call(s32[6,112]{1,0:T(8,128)S(1)} %select_reduce_fusion.ids, s32[6]{0:T(128)S(1)} %convert_element_type.32.counts, bf16[800,128]{1,0:T(8,128)(2,1)S(1)} %collective-permute-done.4.refs_0_, bf16[800,128]{1,0:T(8,128)(2,1)S(1)} %collective-permute-done.5.refs_1_, ...), custom_call_target="tpu_custom_call" | custom-call | flops 500000000 | bytes 1024 | tf_op jit(solution)/shard_map/pallas_call | solution.py:382
  43.5 2.4 %shard_map.127 = (bf16[2048,128]{1,0:T(8,128)(2,1)S(1)}, f32[4,8,8,128]{3,2,1,0:T(8,128)}, bf16[128,256]{1,0:T(8,128)(2,1)S(1)}) custom-call(bf16[2048,128]{1,0:T(8,128)(2,1)S(1)} %fusion.hot, bf16[128,2048]{1,0:T(8,128)(2,1)S(1)} %fusion.1.hot_turned, s32[1600,64]{1,0:T(8,128)S(1)} %bitcast.44, bf16[32,4,64]{2,1,0:T(4,128)(2,1)S(1)} %copy-done.3, ...), custom_call_target="tpu_custom_call" | custom-call | flops 2400000000 | bytes 1024 | tf_op jit(solution)/shard_map/pallas_call | solution.py:382
  45.9 4.4 %all-to-all-start = ((f32[32,8,128]{2,1,0:T(8,128)}), f32[32,8,128]{2,1,0:T(8,128)S(1)}, u32[]{:S(2)}, u32[]{:S(2)}) async-start(f32[32,8,128]{2,1,0:T(8,128)} %bitcast.19), calls=%async_computation | async-start | bytes 262144 | tf_op jit(solution)/shard_map/all_to_all | solution.py:540
  50.3 0.2 compare_convert_fusion.owners
  50.5 0.1 stack.80.clusters
  50.6 1.7 %shard_map.128 = (f32[56,128]{1,0:T(8,128)S(1)}, f32[56,128]{1,0:T(8,128)S(1)}, f32[56,128]{1,0:T(8,128)S(1)}, f32[56,128]{1,0:T(8,128)S(1)}) custom-call(s32[1]{0:T(128)} %bitcast.place, bf16[2048,128]{1,0:T(8,128)(2,1)S(1)} %fusion.hot, bf16[2048,128]{1,0:T(8,128)(2,1)S(1)} %get-tuple-element.63.slots, bf16[128,256]{1,0:T(8,128)(2,1)S(1)} %get-tuple-element.64.geo, ...), custom_call_target="tpu_custom_call" | custom-call | flops 1700000000 | bytes 1024 | tf_op jit(solution)/shard_map/pallas_call | solution.py:382
  52.3 1.8 %collective-permute-start.6 = (f32[56,128]{1,0:T(8,128)S(1)}, f32[56,128]{1,0:T(8,128)S(1)}, u32[]{:S(2)}, u32[]{:S(2)}) collective-permute-start(f32[56,128]{1,0:T(8,128)S(1)} %get-tuple-element.66), channel_id=1, source_target_pairs={{0,8},{8,0},{16,24},{24,16},{1,9},{9,1},{17,25},{25,17},{2,10},{10... | collective-permute-start | bytes 86024 | tf_op jit(solution)/shard_map/ppermute | solution.py:539
  54.2 1.5 %collective-permute-start.7 = (f32[56,128]{1,0:T(8,128)S(1)}, f32[56,128]{1,0:T(8,128)S(1)}, u32[]{:S(2)}, u32[]{:S(2)}) collective-permute-start(f32[56,128]{1,0:T(8,128)S(1)} %get-tuple-element.67), channel_id=1, source_target_pairs={{0,16},{8,24},{16,0},{24,8},{1,17},{9,25},{17,1},{25,9},{2,18},{10... | collective-permute-start | bytes 86024 | tf_op jit(solution)/shard_map/ppermute | solution.py:539
  55.6 0.3 collective-permute-start.8
  55.9 2.6 %all-to-all-done.received = f32[32,8,128]{2,1,0:T(8,128)S(1)} async-done(((f32[32,8,128]{2,1,0:T(8,128)}), f32[32,8,128]{2,1,0:T(8,128)S(1)}, u32[]{:S(2)}, u32[]{:S(2)}) %all-to-all-start) | async-done | bytes 131104 | tf_op jit(solution)/shard_map/all_to_all | solution.py:540
  58.5 0.7 %shard_map.129.spread = f32[8,128]{1,0:T(8,128)S(1)} custom-call(s32[7]{0:T(128)S(1)} %stack.80.clusters, f32[32,8,128]{2,1,0:T(8,128)S(1)} %all-to-all-done.received, bf16[896,128]{1,0:T(8,128)(2,1)S(1)} %compare_convert_fusion.owners), custom_call_target="tpu_custom_call" | custom-call | flops 1000000000 | bytes 1024 | tf_op jit(solution)/shard_map/pallas_call | solution.py:382
  59.2 1.2 %collective-permute-done.8.three = f32[56,128]{1,0:T(8,128)S(1)} collective-permute-done((f32[56,128]{1,0:T(8,128)S(1)}, f32[56,128]{1,0:T(8,128)S(1)}, u32[]{:S(2)}, u32[]{:S(2)}) %collective-permute-start.8) | collective-permute-done | bytes 28704 | tf_op jit(solution)/shard_map/ppermute | solution.py:539
  60.4 0.7 %shard_map.130 = (f32[4,32,51]{2,1,0:T(8,128)}, f32[1,32]{1,0:T(1,128)}) custom-call(f32[56,128]{1,0:T(8,128)S(1)} %get-tuple-element.65.own, f32[56,128]{1,0:T(8,128)S(1)} %collective-permute-done.6.one, f32[56,128]{1,0:T(8,128)S(1)} %collective-permute-done.7.two, f32[56,128]{1,0:T(8,128)S(1)} %collective-permute-done.8.three, f32[8,128]{1,0:T(8,128)S(1)} %shard_map.129.spread), custom_call_target="tpu_custom_call" | custom-call | flops 1000000000 | bytes 1024 | tf_op jit(solution)/shard_map/pallas_call | solution.py:382
  (41 shorter events, 0.2 us)
Async XLA Ops:
  0.6 12.6 %copy-start.6 = (f32[6,6]{1,0:T(8,128)S(1)}, f32[6,6]{1,0:T(8,128)}, u32[]{:S(2)}) copy-start(f32[6,6]{1,0:T(8,128)} %constant.148.clone) | copy-start | bytes 436
  0.6 12.8 %copy-start.8 = (bf16[32,32,1]{1,0,2:T(8,128)(2,1)S(1)}, bf16[32,32,1]{1,0,2:T(8,128)(2,1)}, u32[]{:S(2)}) copy-start(bf16[32,32,1]{1,0,2:T(8,128)(2,1)} %constant.203) | copy-start | bytes 6148
  0.7 12.8 %copy-start.9 = (s32[6,6]{1,0:T(8,128)S(1)}, s32[6,6]{1,0:T(8,128)}, u32[]{:S(2)}) copy-start(s32[6,6]{1,0:T(8,128)} %constant.149.clone) | copy-start | bytes 436
  0.7 13.8 %copy-start.10 = (s32[128]{0:T(128)S(1)}, s32[128]{0:T(128)}, u32[]{:S(2)}) copy-start(s32[128]{0:T(128)} %constant.150.clone) | copy-start | bytes 1540
  0.7 14.5 %copy-start = (bf16[80,64]{1,0:T(8,128)(2,1)S(1)}, bf16[80,64]{1,0:T(8,128)(2,1)}, u32[]{:S(2)}) copy-start(bf16[80,64]{1,0:T(8,128)(2,1)} %constant.166.table.refs_5_) | copy-start | bytes 30724
  0.7 14.5 %copy-start.4 = (s32[148]{0:T(256)S(1)}, s32[148]{0:T(256)}, u32[]{:S(2)}) copy-start(s32[148]{0:T(256)} %constant.146.clone.ids) | copy-start | bytes 1780
  0.7 14.5 %copy-start.2 = (bf16[32,64,128]{2,1,0:T(8,128)(2,1)S(1)}, bf16[32,64,128]{2,1,0:T(8,128)(2,1)}, u32[]{:S(2)}) copy-start(bf16[32,64,128]{2,1,0:T(8,128)(2,1)} %spec_ref.1) | copy-start | bytes 1572868
  0.7 13.2 %copy-start.7 = (s32[6,12]{1,0:T(8,128)S(1)}, s32[6,12]{1,0:T(8,128)}, u32[]{:S(2)}) copy-start(s32[6,12]{1,0:T(8,128)} %exports_ref.1) | copy-start | bytes 868
  0.7 11.3 %copy-start.5 = (s32[32,50]{1,0:T(8,128)S(1)}, s32[32,50]{1,0:T(8,128)}, u32[]{:S(2)}) copy-start(s32[32,50]{1,0:T(8,128)} %param.13) | copy-start | bytes 19204
  3.1 12.0 %collective-permute-start = (bf16[800,128]{1,0:T(8,128)(2,1)}, bf16[800,128]{1,0:T(8,128)(2,1)S(1)}, u32[]{:S(2)}, u32[]{:S(2)}) collective-permute-start(bf16[800,128]{1,0:T(8,128)(2,1)} %get-tuple-element.38), channel_id=1, source_target_pairs={{0,1},{1,0},{2,3},{3,2},{4,5},{5,4},{6,7},{7,6},{8,9},{9,8},{10,11... | collective-permute-start | bytes 614408 | tf_op jit(solution)/shard_map/ppermute | solution.py:444
  3.6 21.4 %collective-permute-start.1 = (bf16[800,128]{1,0:T(8,128)(2,1)}, bf16[800,128]{1,0:T(8,128)(2,1)S(1)}, u32[]{:S(2)}, u32[]{:S(2)}) collective-permute-start(bf16[800,128]{1,0:T(8,128)(2,1)} %get-tuple-element.41), channel_id=1, source_target_pairs={{0,2},{1,3},{2,0},{3,1},{4,6},{5,7},{6,4},{7,5},{8,10},{9,11},{10,... | collective-permute-start | bytes 614408 | tf_op jit(solution)/shard_map/ppermute | solution.py:444
  6.1 24.6 %collective-permute-start.3 = (bf16[800,128]{1,0:T(8,128)(2,1)}, bf16[800,128]{1,0:T(8,128)(2,1)S(1)}, u32[]{:S(2)}, u32[]{:S(2)}) collective-permute-start(bf16[800,128]{1,0:T(8,128)(2,1)} %get-tuple-element.50), channel_id=1, source_target_pairs={{0,5},{1,4},{2,7},{3,6},{4,1},{5,0},{6,3},{7,2},{8,13},{9,12},{10,... | collective-permute-start | bytes 614408 | tf_op jit(solution)/shard_map/ppermute | solution.py:444
  8.6 29.1 %collective-permute-start.4 = (bf16[800,128]{1,0:T(8,128)(2,1)}, bf16[800,128]{1,0:T(8,128)(2,1)S(1)}, u32[]{:S(2)}, u32[]{:S(2)}) collective-permute-start(bf16[800,128]{1,0:T(8,128)(2,1)} %get-tuple-element.57), channel_id=1, source_target_pairs={{0,6},{1,7},{2,4},{3,5},{4,2},{5,3},{6,0},{7,1},{8,14},{9,15},{10,... | collective-permute-start | bytes 614408 | tf_op jit(solution)/shard_map/ppermute | solution.py:444
  8.6 29.1 %collective-permute-start.5 = (bf16[800,128]{1,0:T(8,128)(2,1)}, bf16[800,128]{1,0:T(8,128)(2,1)S(1)}, u32[]{:S(2)}, u32[]{:S(2)}) collective-permute-start(bf16[800,128]{1,0:T(8,128)(2,1)} %get-tuple-element.58), channel_id=1, source_target_pairs={{0,7},{1,6},{2,5},{3,4},{4,3},{5,2},{6,1},{7,0},{8,15},{9,14},{10,... | collective-permute-start | bytes 614408 | tf_op jit(solution)/shard_map/ppermute | solution.py:444
  15.1 16.3 %collective-permute-start.2 = (bf16[800,128]{1,0:T(8,128)(2,1)}, bf16[800,128]{1,0:T(8,128)(2,1)S(1)}, u32[]{:S(2)}, u32[]{:S(2)}) collective-permute-start(bf16[800,128]{1,0:T(8,128)(2,1)} %get-tuple-element.49), channel_id=1, source_target_pairs={{0,3},{1,2},{2,1},{3,0},{4,7},{5,6},{6,5},{7,4},{8,11},{9,10},{10,... | collective-permute-start | bytes 614408 | tf_op jit(solution)/shard_map/ppermute | solution.py:444
  37.6 5.9 %copy-start.1 = (s32[32,50,64]{2,0,1:T(8,128)S(1)}, s32[32,50,64]{2,0,1:T(8,128)}, u32[]{:S(2)}) copy-start(s32[32,50,64]{2,0,1:T(8,128)} %param.14) | copy-start | bytes 1228804
  37.6 5.9 %copy-start.3 = (bf16[32,4,64]{2,1,0:T(4,128)(2,1)S(1)}, bf16[32,4,64]{2,1,0:T(4,128)(2,1)}, u32[]{:S(2)}) copy-start(bf16[32,4,64]{2,1,0:T(4,128)(2,1)} %partials.3) | copy-start | bytes 49156
  45.9 12.6 %all-to-all-start = ((f32[32,8,128]{2,1,0:T(8,128)}), f32[32,8,128]{2,1,0:T(8,128)S(1)}, u32[]{:S(2)}, u32[]{:S(2)}) async-start(f32[32,8,128]{2,1,0:T(8,128)} %bitcast.19), calls=%async_computation | async-start | bytes 262144 | tf_op jit(solution)/shard_map/all_to_all | solution.py:540
  52.3 6.9 %collective-permute-start.6 = (f32[56,128]{1,0:T(8,128)S(1)}, f32[56,128]{1,0:T(8,128)S(1)}, u32[]{:S(2)}, u32[]{:S(2)}) collective-permute-start(f32[56,128]{1,0:T(8,128)S(1)} %get-tuple-element.66), channel_id=1, source_target_pairs={{0,8},{8,0},{16,24},{24,16},{1,9},{9,1},{17,25},{25,17},{2,10},{10... | collective-permute-start | bytes 86024 | tf_op jit(solution)/shard_map/ppermute | solution.py:539
  54.2 5.1 %collective-permute-start.7 = (f32[56,128]{1,0:T(8,128)S(1)}, f32[56,128]{1,0:T(8,128)S(1)}, u32[]{:S(2)}, u32[]{:S(2)}) collective-permute-start(f32[56,128]{1,0:T(8,128)S(1)} %get-tuple-element.67), channel_id=1, source_target_pairs={{0,16},{8,24},{16,0},{24,8},{1,17},{9,25},{17,1},{25,9},{2,18},{10... | collective-permute-start | bytes 86024 | tf_op jit(solution)/shard_map/ppermute | solution.py:539
  55.6 4.8 %collective-permute-start.8 = (f32[56,128]{1,0:T(8,128)S(1)}, f32[56,128]{1,0:T(8,128)S(1)}, u32[]{:S(2)}, u32[]{:S(2)}) collective-permute-start(f32[56,128]{1,0:T(8,128)S(1)} %get-tuple-element.68), channel_id=1, source_target_pairs={{0,24},{8,16},{16,8},{24,0},{1,25},{9,17},{17,9},{25,1},{2,26},{10... | collective-permute-start | bytes 86024 | tf_op jit(solution)/shard_map/ppermute | solution.py:539

commit v10 on v9

--- a/solution.py
+++ b/solution.py
@@ -461,7 +461,7 @@
         (jnp.asarray(duos, jnp.int32), natural.reshape(events // 2, 2 * stations, two_freq), table),
         scratch=weight_scratch(events // 2, freq),
         specs=[smem] + vmem(2),
-        micros=0.5,
+        micros=8.0,
     )
 
     far = jnp.maximum(pair_list - events, 0)
@@ -490,6 +490,9 @@
 
     column = jnp.where(pair_list < events, pair_list, events + GROUP_ROWS * arrival + entry)
     column = jnp.pad(column, ((0, 0), (0, SLOT_ROWS - slots)), constant_values=-1).reshape(-1)
+    cand_ids = jnp.arange(cands, dtype=jnp.int32)
+    hot = (column[:, None] == cand_ids[None, :]).astype(BF16)
+    hot_turned = (cand_ids[:, None] == column[None, :]).astype(BF16)
     mask = station_mask.transpose(1, 0, 2).reshape(slots * events, stations)
     owner_rows = [jnp.asarray(np.where(np.arange(cands) < events, np.arange(cands), -1), jnp.int32)]
     hot_sent = sent[:, None] == jnp.arange(groups, dtype=jnp.int32)[None, :]
@@ -503,22 +506,19 @@
     tables, tails, begin = [], [], 0
     for size in STAGE_SIZES:
         if tables:
-            lists, column, tables[-1] = lax.optimization_barrier((lists, column, tables[-1]))
+            lists, tables[-1] = lax.optimization_barrier((lists, tables[-1]))
         table_part, tail_part = call(
             functools.partial(import_kernel, begin, size, freq, events, cap, scale),
             [((events * size * GROUP_ROWS, 128), F32), ((size * 2 * GROUP_ROWS, 128), BF16)],
             (lists, counts, *got[begin : begin + size], dup, square, energy, table),
             scratch=weight_scratch(size * half, freq),
             specs=[smem] * 2 + vmem(size + 4),
-            micros=0.5,
+            micros=1.0 + 2.3 * size,
         )
         tables.append(table_part)
         tails.append(tail_part)
         begin += size
 
-    cand_ids = jnp.arange(cands, dtype=jnp.int32)
-    hot = (column[:, None] == cand_ids[None, :]).astype(BF16)
-    hot_turned = (cand_ids[:, None] == column[None, :]).astype(BF16)
     weights, terms, geo = call(
         functools.partial(sums_kernel, groups, events, slots),
         [((events * SLOT_ROWS, 128), BF16), ((4, clusters, 8, 128), F32), ((cands, 256), BF16)],

time: 61.6 us -> 60.3 us (0.979)
  Pallas kernels: 35 us -> 34.2 us
    pallas_call x9, Pallas kernels: 35 us -> 34.2 us  [call(): pl.pallas_call(kernel, out_shape=shapes, in_specs=specs if specs is not N...]
where the time goes in v10:
time: 60.3 us; the launch traced here: 60.1 us
  Pallas kernels  34.2 us (57%)
  starting transfers between devices  16.3 us (27%)
  waiting for transfers between devices  4.64 us (8%)
  other arithmetic  2.52 us (4%)
  between operations  1.14 us (2%)
  local copies, waits for them, and re-layouts  1.07 us (2%)
    pallas_call x9, Pallas kernels, call(): pl.pallas_call(kernel, out_shape=shapes, in_specs=specs if specs is not N...  34.2 us
    ppermute x6, starting transfers between devices, on_device(): got[g] = lax.ppermute(block, 'clu', routes[g])  8.95 us
    all_to_all x1, starting transfers between devices, on_device(): lax.all_to_all(terms.reshape(4 * clusters, 8, 128), ('sta', 'clu'), split...  3.84 us
    ppermute x3, starting transfers between devices, on_device(): lax.ppermute(shares[d], 'sta', [(i, i ^ d) for i in range(4)])  3.55 us
    all_to_all x1, waiting for transfers between devices, on_device(): lax.all_to_all(terms.reshape(4 * clusters, 8, 128), ('sta', 'clu'), split...  2.63 us
  transfers between devices with their start and end apart: 10, of which 3 were waited for; matrix products, arithmetic and copies ran while one was open for 6% of the time, Pallas kernels for 39%

profile of v10, /device:TPU:0, one launch (start us, length us, event | category | flops | bytes accessed | tf_op | source)
XLA Modules:
  0.0 60.1 jit_solution(3279962789207937825)
XLA Ops:
  0.6 0.0 copy-start.6
  0.7 2.4 %shard_map.122 = (bf16[800,128]{1,0:T(8,128)(2,1)}, bf16[800,128]{1,0:T(8,128)(2,1)}, bf16[800,128]{1,0:T(8,128)(2,1)}, bf16[800,128]{1,0:T(8,128)(2,1)}, bf16[8...) custom-call(s32[6,12]{1,0:T(8,128)} %exports_ref.1, bf16[32,64,128]{2,1,0:T(8,128)(2,1)} %spec_ref.1, bf16[32,4,64]{2,1,0:T(4,128)(2,1)} %partials.3), custom_call_target="tpu_custom_call" | custom-call | flops 2000000000 | bytes 1024 | tf_op jit(solution)/shard_map/pallas_call | solution.py:382
  3.1 0.4 collective-permute-start
  3.6 2.6 %collective-permute-start.1 = (bf16[800,128]{1,0:T(8,128)(2,1)}, bf16[800,128]{1,0:T(8,128)(2,1)S(1)}, u32[]{:S(2)}, u32[]{:S(2)}) collective-permute-start(bf16[800,128]{1,0:T(8,128)(2,1)} %get-tuple-element.41), channel_id=1, source_target_pairs={{0,2},{1,3},{2,0},{3,1},{4,6},{5,7},{6,4},{7,5},{8,10},{9,11},{10,... | collective-permute-start | bytes 614408 | tf_op jit(solution)/shard_map/ppermute | solution.py:444
  6.1 2.4 %collective-permute-start.3 = (bf16[800,128]{1,0:T(8,128)(2,1)}, bf16[800,128]{1,0:T(8,128)(2,1)S(1)}, u32[]{:S(2)}, u32[]{:S(2)}) collective-permute-start(bf16[800,128]{1,0:T(8,128)(2,1)} %get-tuple-element.49), channel_id=1, source_target_pairs={{0,5},{1,4},{2,7},{3,6},{4,1},{5,0},{6,3},{7,2},{8,13},{9,12},{10,... | collective-permute-start | bytes 614408 | tf_op jit(solution)/shard_map/ppermute | solution.py:444
  8.6 0.1 collective-permute-start.4
  8.6 3.4 %collective-permute-start.5 = (bf16[800,128]{1,0:T(8,128)(2,1)}, bf16[800,128]{1,0:T(8,128)(2,1)S(1)}, u32[]{:S(2)}, u32[]{:S(2)}) collective-permute-start(bf16[800,128]{1,0:T(8,128)(2,1)} %get-tuple-element.54), channel_id=1, source_target_pairs={{0,7},{1,6},{2,5},{3,4},{4,3},{5,2},{6,1},{7,0},{8,15},{9,14},{10,... | collective-permute-start | bytes 614408 | tf_op jit(solution)/shard_map/ppermute | solution.py:444
  12.0 0.1 stack.72
  12.1 0.1 select_reduce_fusion.1
  12.3 0.7 %fusion.2 = pred[32,36]{0,1:T(8,128)(4,1)S(1)} fusion(s32[32,50]{1,0:T(8,128)S(1)} %get-tuple-element.68), kind=kLoop, calls=%fused_computation.8 | loop fusion | flops 114048 | bytes 7552 | tf_op jit(solution)/shard_map/reduce_or | solution.py:472
  13.0 0.1 convert_reduce_fusion
  13.1 0.1 eq.112
  13.2 0.3 fusion.hot
  13.5 0.1 fusion.1.hot_turned
  13.7 0.1 ceil.11
  13.8 0.1 multiply_reduce_fusion
  14.0 0.1 add_select_fusion
  14.1 0.1 broadcast_in_dim.78
  14.2 0.1 eq.122
  14.2 0.1 reduce_sum.58
  14.4 0.1 stack.87
  14.5 0.1 iota_compare_fusion.4
  14.6 0.1 select_reduce_fusion.2
  14.7 0.1 constant_dynamic-update-slice_fusion.5
  14.8 0.1 constant_dynamic-update-slice_fusion.4
  14.9 0.1 constant_dynamic-update-slice_fusion.3
  14.9 0.1 constant_dynamic-update-slice_fusion.2
  15.0 0.1 constant_dynamic-update-slice_fusion.1
  15.1 0.1 constant_dynamic-update-slice_fusion
  15.2 0.5 select_reduce_fusion.ids
  15.7 0.1 collective-permute-start.2
  15.8 9.2 %shard_map.123 = (f32[1024,128]{1,0:T(8,128)S(1)}, f32[32,128,128]{2,1,0:T(8,128)S(1)}, f32[32,64,128]{2,1,0:T(8,128)S(1)}, f32[32,128]{1,0:T(8,128)S(1)}) custom-call(s32[148]{0:T(256)S(1)} %copy-done.4, bf16[16,128,128]{2,1,0:T(8,128)(2,1)S(1)} %bitcast.45, bf16[80,64]{1,0:T(8,128)(2,1)S(1)} %copy-done.3), custom_call_target="tpu_custom_call" | custom-call | flops 8000000000 | bytes 1024 | tf_op jit(solution)/shard_map/pallas_call | solution.py:382
  25.0 6.0 %shard_map.124 = (f32[1024,128]{1,0:T(8,128)S(1)}, bf16[64,128]{1,0:T(8,128)(2,1)S(1)}) custom-call(s32[6,112]{1,0:T(8,128)S(1)} %select_reduce_fusion.ids, s32[6]{0:T(128)S(1)} %convert_element_type.35.counts, bf16[800,128]{1,0:T(8,128)(2,1)S(1)} %collective-permute-done.refs_0_, bf16[800,128]{1,0:T(8,128)(2,1)S(1)} %collective-permute-done.1.refs_1_, ...), custom_call_target="tpu_custom_call" | custom-call | flops 5600000000 | bytes 1024 | tf_op jit(solution)/shard_map/pallas_call | solution.py:382
  31.1 0.8 %collective-permute-done.2.refs_0_ = bf16[800,128]{1,0:T(8,128)(2,1)S(1)} collective-permute-done((bf16[800,128]{1,0:T(8,128)(2,1)}, bf16[800,128]{1,0:T(8,128)(2,1)S(1)}, u32[]{:S(2)}, u32[]{:S(2)}) %collective-permute-start.2) | collective-permute-done | bytes 204832 | tf_op jit(solution)/shard_map/ppermute | solution.py:444
  31.9 5.5 %shard_map.125 = (f32[1024,128]{1,0:T(8,128)S(1)}, bf16[64,128]{1,0:T(8,128)(2,1)S(1)}) custom-call(s32[6,112]{1,0:T(8,128)S(1)} %select_reduce_fusion.ids, s32[6]{0:T(128)S(1)} %convert_element_type.35.counts, bf16[800,128]{1,0:T(8,128)(2,1)S(1)} %collective-permute-done.2.refs_0_, bf16[800,128]{1,0:T(8,128)(2,1)S(1)} %collective-permute-done.3.refs_1_, ...), custom_call_target="tpu_custom_call" | custom-call | flops 5600000000 | bytes 1024 | tf_op jit(solution)/shard_map/pallas_call | solution.py:382
  37.5 5.5 %shard_map.126 = (f32[1024,128]{1,0:T(8,128)S(1)}, bf16[64,128]{1,0:T(8,128)(2,1)S(1)}) custom-call(s32[6,112]{1,0:T(8,128)S(1)} %select_reduce_fusion.ids, s32[6]{0:T(128)S(1)} %convert_element_type.35.counts, bf16[800,128]{1,0:T(8,128)(2,1)S(1)} %collective-permute-done.4.refs_0_, bf16[800,128]{1,0:T(8,128)(2,1)S(1)} %collective-permute-done.5.refs_1_, ...), custom_call_target="tpu_custom_call" | custom-call | flops 5600000000 | bytes 1024 | tf_op jit(solution)/shard_map/pallas_call | solution.py:382
  43.0 2.4 %shard_map.127 = (bf16[2048,128]{1,0:T(8,128)(2,1)S(1)}, f32[4,8,8,128]{3,2,1,0:T(8,128)}, bf16[128,256]{1,0:T(8,128)(2,1)S(1)}) custom-call(bf16[2048,128]{1,0:T(8,128)(2,1)S(1)} %fusion.hot, bf16[128,2048]{1,0:T(8,128)(2,1)S(1)} %fusion.1.hot_turned, s32[1600,64]{1,0:T(8,128)S(1)} %bitcast.44, bf16[32,4,64]{2,1,0:T(4,128)(2,1)S(1)} %copy-done.2, ...), custom_call_target="tpu_custom_call" | custom-call | flops 2400000000 | bytes 1024 | tf_op jit(solution)/shard_map/pallas_call | solution.py:382
  45.4 3.8 %all-to-all-start = ((f32[32,8,128]{2,1,0:T(8,128)}), f32[32,8,128]{2,1,0:T(8,128)S(1)}, u32[]{:S(2)}, u32[]{:S(2)}) async-start(f32[32,8,128]{2,1,0:T(8,128)} %bitcast.19), calls=%async_computation | async-start | bytes 262144 | tf_op jit(solution)/shard_map/all_to_all | solution.py:540
  49.3 0.2 compare_convert_fusion.owners
  49.5 0.1 stack.80.clusters
  49.6 1.7 %shard_map.128 = (f32[56,128]{1,0:T(8,128)S(1)}, f32[56,128]{1,0:T(8,128)S(1)}, f32[56,128]{1,0:T(8,128)S(1)}, f32[56,128]{1,0:T(8,128)S(1)}) custom-call(s32[1]{0:T(128)} %bitcast.place, bf16[2048,128]{1,0:T(8,128)(2,1)S(1)} %fusion.hot, bf16[2048,128]{1,0:T(8,128)(2,1)S(1)} %get-tuple-element.59.slots, bf16[128,256]{1,0:T(8,128)(2,1)S(1)} %get-tuple-element.60.geo, ...), custom_call_target="tpu_custom_call" | custom-call | flops 1700000000 | bytes 1024 | tf_op jit(solution)/shard_map/pallas_call | solution.py:382
  51.3 1.8 %collective-permute-start.6 = (f32[56,128]{1,0:T(8,128)S(1)}, f32[56,128]{1,0:T(8,128)S(1)}, u32[]{:S(2)}, u32[]{:S(2)}) collective-permute-start(f32[56,128]{1,0:T(8,128)S(1)} %get-tuple-element.62), channel_id=1, source_target_pairs={{0,8},{8,0},{16,24},{24,16},{1,9},{9,1},{17,25},{25,17},{2,10},{10... | collective-permute-start | bytes 86024 | tf_op jit(solution)/shard_map/ppermute | solution.py:539
  53.1 1.5 %collective-permute-start.7 = (f32[56,128]{1,0:T(8,128)S(1)}, f32[56,128]{1,0:T(8,128)S(1)}, u32[]{:S(2)}, u32[]{:S(2)}) collective-permute-start(f32[56,128]{1,0:T(8,128)S(1)} %get-tuple-element.63), channel_id=1, source_target_pairs={{0,16},{8,24},{16,0},{24,8},{1,17},{9,25},{17,1},{25,9},{2,18},{10... | collective-permute-start | bytes 86024 | tf_op jit(solution)/shard_map/ppermute | solution.py:539
  54.6 0.3 collective-permute-start.8
  54.8 2.6 %all-to-all-done.received = f32[32,8,128]{2,1,0:T(8,128)S(1)} async-done(((f32[32,8,128]{2,1,0:T(8,128)}), f32[32,8,128]{2,1,0:T(8,128)S(1)}, u32[]{:S(2)}, u32[]{:S(2)}) %all-to-all-start) | async-done | bytes 131104 | tf_op jit(solution)/shard_map/all_to_all | solution.py:540
  57.5 0.7 %shard_map.129.spread = f32[8,128]{1,0:T(8,128)S(1)} custom-call(s32[7]{0:T(128)S(1)} %stack.80.clusters, f32[32,8,128]{2,1,0:T(8,128)S(1)} %all-to-all-done.received, bf16[896,128]{1,0:T(8,128)(2,1)S(1)} %compare_convert_fusion.owners), custom_call_target="tpu_custom_call" | custom-call | flops 1000000000 | bytes 1024 | tf_op jit(solution)/shard_map/pallas_call | solution.py:382
  58.2 1.2 %collective-permute-done.8.three = f32[56,128]{1,0:T(8,128)S(1)} collective-permute-done((f32[56,128]{1,0:T(8,128)S(1)}, f32[56,128]{1,0:T(8,128)S(1)}, u32[]{:S(2)}, u32[]{:S(2)}) %collective-permute-start.8) | collective-permute-done | bytes 28704 | tf_op jit(solution)/shard_map/ppermute | solution.py:539
  59.3 0.7 %shard_map.130 = (f32[4,32,51]{2,1,0:T(8,128)}, f32[1,32]{1,0:T(1,128)}) custom-call(f32[56,128]{1,0:T(8,128)S(1)} %get-tuple-element.61.own, f32[56,128]{1,0:T(8,128)S(1)} %collective-permute-done.6.one, f32[56,128]{1,0:T(8,128)S(1)} %collective-permute-done.7.two, f32[56,128]{1,0:T(8,128)S(1)} %collective-permute-done.8.three, f32[8,128]{1,0:T(8,128)S(1)} %shard_map.129.spread), custom_call_target="tpu_custom_call" | custom-call | flops 1000000000 | bytes 1024 | tf_op jit(solution)/shard_map/pallas_call | solution.py:382
  (41 shorter events, 0.2 us)
Async XLA Ops:
  0.6 13.2 %copy-start.6 = (f32[6,6]{1,0:T(8,128)S(1)}, f32[6,6]{1,0:T(8,128)}, u32[]{:S(2)}) copy-start(f32[6,6]{1,0:T(8,128)} %constant.148.clone) | copy-start | bytes 436
  0.6 13.3 %copy-start.8 = (bf16[32,32,1]{1,0,2:T(8,128)(2,1)S(1)}, bf16[32,32,1]{1,0,2:T(8,128)(2,1)}, u32[]{:S(2)}) copy-start(bf16[32,32,1]{1,0,2:T(8,128)(2,1)} %constant.203) | copy-start | bytes 6148
  0.7 13.3 %copy-start.9 = (s32[6,6]{1,0:T(8,128)S(1)}, s32[6,6]{1,0:T(8,128)}, u32[]{:S(2)}) copy-start(s32[6,6]{1,0:T(8,128)} %constant.149.clone) | copy-start | bytes 436
  0.7 14.0 %copy-start.10 = (s32[128]{0:T(128)S(1)}, s32[128]{0:T(128)}, u32[]{:S(2)}) copy-start(s32[128]{0:T(128)} %constant.150.clone) | copy-start | bytes 1540
  0.7 15.1 %copy-start.3 = (bf16[80,64]{1,0:T(8,128)(2,1)S(1)}, bf16[80,64]{1,0:T(8,128)(2,1)}, u32[]{:S(2)}) copy-start(bf16[80,64]{1,0:T(8,128)(2,1)} %constant.166.table.refs_5_) | copy-start | bytes 30724
  0.7 15.1 %copy-start.4 = (s32[148]{0:T(256)S(1)}, s32[148]{0:T(256)}, u32[]{:S(2)}) copy-start(s32[148]{0:T(256)} %constant.146.clone.ids) | copy-start | bytes 1780
  0.7 15.1 %copy-start.1 = (bf16[32,64,128]{2,1,0:T(8,128)(2,1)S(1)}, bf16[32,64,128]{2,1,0:T(8,128)(2,1)}, u32[]{:S(2)}) copy-start(bf16[32,64,128]{2,1,0:T(8,128)(2,1)} %spec_ref.1) | copy-start | bytes 1572868
  0.7 13.8 %copy-start.7 = (s32[6,12]{1,0:T(8,128)S(1)}, s32[6,12]{1,0:T(8,128)}, u32[]{:S(2)}) copy-start(s32[6,12]{1,0:T(8,128)} %exports_ref.1) | copy-start | bytes 868
  0.7 11.3 %copy-start.5 = (s32[32,50]{1,0:T(8,128)S(1)}, s32[32,50]{1,0:T(8,128)}, u32[]{:S(2)}) copy-start(s32[32,50]{1,0:T(8,128)} %param.13) | copy-start | bytes 19204
  3.1 12.5 %collective-permute-start = (bf16[800,128]{1,0:T(8,128)(2,1)}, bf16[800,128]{1,0:T(8,128)(2,1)S(1)}, u32[]{:S(2)}, u32[]{:S(2)}) collective-permute-start(bf16[800,128]{1,0:T(8,128)(2,1)} %get-tuple-element.36), channel_id=1, source_target_pairs={{0,1},{1,0},{2,3},{3,2},{4,5},{5,4},{6,7},{7,6},{8,9},{9,8},{10,11... | collective-permute-start | bytes 614408 | tf_op jit(solution)/shard_map/ppermute | solution.py:444
  3.6 21.5 %collective-permute-start.1 = (bf16[800,128]{1,0:T(8,128)(2,1)}, bf16[800,128]{1,0:T(8,128)(2,1)S(1)}, u32[]{:S(2)}, u32[]{:S(2)}) collective-permute-start(bf16[800,128]{1,0:T(8,128)(2,1)} %get-tuple-element.41), channel_id=1, source_target_pairs={{0,2},{1,3},{2,0},{3,1},{4,6},{5,7},{6,4},{7,5},{8,10},{9,11},{10,... | collective-permute-start | bytes 614408 | tf_op jit(solution)/shard_map/ppermute | solution.py:444
  6.1 24.9 %collective-permute-start.3 = (bf16[800,128]{1,0:T(8,128)(2,1)}, bf16[800,128]{1,0:T(8,128)(2,1)S(1)}, u32[]{:S(2)}, u32[]{:S(2)}) collective-permute-start(bf16[800,128]{1,0:T(8,128)(2,1)} %get-tuple-element.49), channel_id=1, source_target_pairs={{0,5},{1,4},{2,7},{3,6},{4,1},{5,0},{6,3},{7,2},{8,13},{9,12},{10,... | collective-permute-start | bytes 614408 | tf_op jit(solution)/shard_map/ppermute | solution.py:444
  8.6 28.9 %collective-permute-start.4 = (bf16[800,128]{1,0:T(8,128)(2,1)}, bf16[800,128]{1,0:T(8,128)(2,1)S(1)}, u32[]{:S(2)}, u32[]{:S(2)}) collective-permute-start(bf16[800,128]{1,0:T(8,128)(2,1)} %get-tuple-element.53), channel_id=1, source_target_pairs={{0,6},{1,7},{2,4},{3,5},{4,2},{5,3},{6,0},{7,1},{8,14},{9,15},{10,... | collective-permute-start | bytes 614408 | tf_op jit(solution)/shard_map/ppermute | solution.py:444
  8.6 28.9 %collective-permute-start.5 = (bf16[800,128]{1,0:T(8,128)(2,1)}, bf16[800,128]{1,0:T(8,128)(2,1)S(1)}, u32[]{:S(2)}, u32[]{:S(2)}) collective-permute-start(bf16[800,128]{1,0:T(8,128)(2,1)} %get-tuple-element.54), channel_id=1, source_target_pairs={{0,7},{1,6},{2,5},{3,4},{4,3},{5,2},{6,1},{7,0},{8,15},{9,14},{10,... | collective-permute-start | bytes 614408 | tf_op jit(solution)/shard_map/ppermute | solution.py:444
  15.7 16.2 %collective-permute-start.2 = (bf16[800,128]{1,0:T(8,128)(2,1)}, bf16[800,128]{1,0:T(8,128)(2,1)S(1)}, u32[]{:S(2)}, u32[]{:S(2)}) collective-permute-start(bf16[800,128]{1,0:T(8,128)(2,1)} %get-tuple-element.48), channel_id=1, source_target_pairs={{0,3},{1,2},{2,1},{3,0},{4,7},{5,6},{6,5},{7,4},{8,11},{9,10},{10,... | collective-permute-start | bytes 614408 | tf_op jit(solution)/shard_map/ppermute | solution.py:444
  37.4 5.6 %copy-start = (s32[32,50,64]{2,0,1:T(8,128)S(1)}, s32[32,50,64]{2,0,1:T(8,128)}, u32[]{:S(2)}) copy-start(s32[32,50,64]{2,0,1:T(8,128)} %param.14) | copy-start | bytes 1228804
  37.5 5.6 %copy-start.2 = (bf16[32,4,64]{2,1,0:T(4,128)(2,1)S(1)}, bf16[32,4,64]{2,1,0:T(4,128)(2,1)}, u32[]{:S(2)}) copy-start(bf16[32,4,64]{2,1,0:T(4,128)(2,1)} %partials.3) | copy-start | bytes 49156
  45.4 12.0 %all-to-all-start = ((f32[32,8,128]{2,1,0:T(8,128)}), f32[32,8,128]{2,1,0:T(8,128)S(1)}, u32[]{:S(2)}, u32[]{:S(2)}) async-start(f32[32,8,128]{2,1,0:T(8,128)} %bitcast.19), calls=%async_computation | async-start | bytes 262144 | tf_op jit(solution)/shard_map/all_to_all | solution.py:540
  51.3 6.9 %collective-permute-start.6 = (f32[56,128]{1,0:T(8,128)S(1)}, f32[56,128]{1,0:T(8,128)S(1)}, u32[]{:S(2)}, u32[]{:S(2)}) collective-permute-start(f32[56,128]{1,0:T(8,128)S(1)} %get-tuple-element.62), channel_id=1, source_target_pairs={{0,8},{8,0},{16,24},{24,16},{1,9},{9,1},{17,25},{25,17},{2,10},{10... | collective-permute-start | bytes 86024 | tf_op jit(solution)/shard_map/ppermute | solution.py:539
  53.1 5.1 %collective-permute-start.7 = (f32[56,128]{1,0:T(8,128)S(1)}, f32[56,128]{1,0:T(8,128)S(1)}, u32[]{:S(2)}, u32[]{:S(2)}) collective-permute-start(f32[56,128]{1,0:T(8,128)S(1)} %get-tuple-element.63), channel_id=1, source_target_pairs={{0,16},{8,24},{16,0},{24,8},{1,17},{9,25},{17,1},{25,9},{2,18},{10... | collective-permute-start | bytes 86024 | tf_op jit(solution)/shard_map/ppermute | solution.py:539
  54.6 4.8 %collective-permute-start.8 = (f32[56,128]{1,0:T(8,128)S(1)}, f32[56,128]{1,0:T(8,128)S(1)}, u32[]{:S(2)}, u32[]{:S(2)}) collective-permute-start(f32[56,128]{1,0:T(8,128)S(1)} %get-tuple-element.64), channel_id=1, source_target_pairs={{0,24},{8,16},{16,8},{24,0},{1,25},{9,17},{17,9},{25,1},{2,26},{10... | collective-permute-start | bytes 86024 | tf_op jit(solution)/shard_map/ppermute | solution.py:539
